TPU v7x, 32 devices: a whole 2x2x4 slice. The times are simulated.
32 devices in a mesh: dp: 8 (over z, x), opt: 4 (over y, core).
Axes of the slice: x: 2, y: 2, z: 4, core: 2. Of those that a mesh axis runs over, the one named last changes fastest.
Arguments:
- patches: bfloat16 [4, 8, 64, 49, 512], P('opt', 'dp'), may hold values from -6 to 6
- regions: bfloat16 [4, 8, 64, 512], P('opt', None, 'dp'), may hold values from -6 to 6
- image_ids: int32 [4, 8, 64], P('opt'), may hold values from 0 to 15, as said below
- attn_w: float32 [4, 512, 512], P('opt')
- mlp_in: float32 [512, 2048], P(None, 'opt'), may hold values from -0.25 to 0.25
- mlp_out: float32 [2048, 512], P('opt'), may hold values from -0.125 to 0.125
- vec_params: float32 [12, 512], replicated
- patch_cot: bfloat16 [4, 8, 64, 49, 512], P('opt', None, 'dp'), may hold values from -6 to 6
- region_cot: bfloat16 [4, 8, 64, 512], P('opt', None, 'dp'), may hold values from -6 to 6
- attn_mom: float32 [4, 512, 512], P('opt'), may hold values from -0.0078125 to 0.0078125
- mlp_in_mom: float32 [512, 2048], P(None, 'opt'), may hold values from -0.0078125 to 0.0078125
- mlp_out_mom: float32 [2048, 512], P('opt'), may hold values from -0.0078125 to 0.0078125
- adam_first: float32 [12, 512], replicated, may hold values from -0.001953125 to 0.001953125
- adam_second: float32 [12, 512], replicated, may hold values from 6.357829e-08 to 2.5431316e-07
Outputs:
- out_patches: bfloat16 [4, 8, 64, 49, 512], P('opt', None, 'dp')
- out_regions: bfloat16 [4, 8, 64, 512], P('opt', None, 'dp')
- d_patches: bfloat16 [4, 8, 64, 49, 512], P('opt', 'dp')
- d_regions: float32 [4, 8, 64, 512], P('opt', None, 'dp')
- new_attn_w: float32 [4, 512, 512], P('opt')
- new_attn_mom: float32 [4, 512, 512], P('opt')
- new_mlp_in: float32 [512, 2048], P(None, 'opt')
- new_mlp_in_mom: float32 [512, 2048], P(None, 'opt')
- new_mlp_out: float32 [2048, 512], P('opt')
- new_mlp_out_mom: float32 [2048, 512], P('opt')
- new_vec_params: float32 [12, 512], replicated
- new_adam_first: float32 [12, 512], replicated
- new_adam_second: float32 [12, 512], replicated
- grad_norm: float32 [], replicated
Inputs may be any that keep to these rules, and one draw needn't show every extreme that they name: `image_ids`: equal ids within one canvas mark one image; an image is a band of whole canvas rows or the left or right part of such a band; in every canvas some image covers all 64 window columns.
All inputs are finite; a program needn't handle non-finite values.
Results may differ from a plain program's by a relative error of at most 0.018.
Values may be sent and summed in bfloat16 or wider, within the bound.
No kernel may reach another device: no remote copies, remote signals or barrier semaphores. Data moves between devices by JAX's collectives and lax.ppermute only.
A program may use at most 384 MiB of HBM per device.

v0:
```python
from functools import partial

import jax
import jax.numpy as jnp
from jax import lax
from jax.sharding import PartitionSpec as P

D = 512
HEADS = 16
HEAD_DIM = 32
FF = 2048
PATCH = 49
OPT_STEP = 10


NORM_EPS = 1e-05
MASKED = -1e30
NS_FIRST = 3.4445
NS_SECOND = -4.775
NS_THIRD = 2.0315
MUON_RATE = 0.5
MUON_MOMENTUM = 0.5
MUON_DECAY = 0.01
ADAM_RATE = 0.5
BETA_FIRST = 0.9
BETA_SECOND = 0.95
ADAM_EPS = 1e-08
CLIP_LIMIT = 1.0


def layer_norm(values, gain, offset):
    centre = values - jnp.mean(values, axis=-1, keepdims=True)
    spread = jnp.mean(centre * centre, axis=-1, keepdims=True)
    return centre * lax.rsqrt(spread + NORM_EPS) * gain + offset


def split_heads(values):
    return values.reshape(values.shape[:-1] + (HEADS, HEAD_DIM))


def merge_heads(values):
    return values.reshape(values.shape[:-2] + (HEADS * HEAD_DIM,))


def project(low_rows, low_weight):
    return lax.dot_general(
        low_rows,
        low_weight,
        (((low_rows.ndim - 1,), (0,)), ((), ())),
        preferred_element_type=jnp.float32,
    )


def back_project(low_grads, low_weight):
    return lax.dot_general(
        low_grads,
        low_weight,
        (((low_grads.ndim - 1,), (1,)), ((), ())),
        preferred_element_type=jnp.float32,
    )


def weight_grad(low_rows, low_grads):
    flat_rows = low_rows.reshape(-1, low_rows.shape[-1])
    flat_grads = low_grads.reshape(-1, low_grads.shape[-1])
    return lax.dot_general(
        flat_rows, flat_grads, (((0,), (0,)), ((), ())), preferred_element_type=jnp.float32
    )


def column_sums(low_grads):
    return jnp.sum(low_grads.astype(jnp.float32).reshape(-1, low_grads.shape[-1]), axis=0)


def high_dot(left, right):
    return jnp.dot(left, right, precision=lax.Precision.HIGHEST)


def gram_wide(matrix):
    return lax.dot_general(
        matrix, matrix, (((1,), (1,)), ((), ())), precision=lax.Precision.HIGHEST
    )


def gram_tall(matrix):
    return lax.dot_general(
        matrix, matrix, (((0,), (0,)), ((), ())), precision=lax.Precision.HIGHEST
    )


def project_heads(normed_low, weights, bias_query, bias_value):
    queries = (project(normed_low, weights[0]) + bias_query).astype(jnp.bfloat16)
    keys_low = project(normed_low, weights[1]).astype(jnp.bfloat16)
    values_low = (project(normed_low, weights[2]) + bias_value).astype(jnp.bfloat16)
    return (queries, keys_low, values_low)


def attention_forward(queries, keys_in, values_in, same_image):
    scores = jnp.einsum(
        "...qhd,...khd->...hqk",
        split_heads(queries),
        split_heads(keys_in),
        preferred_element_type=jnp.float32,
    )
    scores = scores * HEAD_DIM ** (-0.5)
    if same_image is not None:
        scores = jnp.where(same_image, scores, MASKED)
    row_peak = jnp.max(scores, axis=-1, keepdims=True)
    raised = jnp.exp(scores - row_peak)
    row_total = jnp.sum(raised, axis=-1, keepdims=True)
    soft_weights = raised / row_total
    low_weights = soft_weights.astype(jnp.bfloat16)
    mixed = jnp.einsum(
        "...hqk,...khd->...qhd",
        low_weights,
        split_heads(values_in),
        preferred_element_type=jnp.float32,
    )
    return (merge_heads(mixed).astype(jnp.bfloat16), soft_weights, low_weights, row_peak, row_total)


def attention_backward(grad_mixed, keys_in, values_in, soft_weights):
    grad_weights = jnp.einsum(
        "...qhd,...khd->...hqk",
        split_heads(grad_mixed),
        split_heads(values_in),
        preferred_element_type=jnp.float32,
    )
    row_dot = jnp.sum(soft_weights * grad_weights, axis=-1, keepdims=True)
    grad_scores = (soft_weights * (grad_weights - row_dot)).astype(jnp.bfloat16)
    grad_queries = jnp.einsum(
        "...hqk,...khd->...qhd",
        grad_scores,
        split_heads(keys_in),
        preferred_element_type=jnp.float32,
    )
    return (merge_heads(grad_queries * HEAD_DIM ** (-0.5)), grad_scores, row_dot)


def key_terms(grad_scores, low_weights, queries, grad_mixed):
    grad_keys = jnp.einsum(
        "...hqk,...qhd->...khd",
        grad_scores,
        split_heads(queries),
        preferred_element_type=jnp.float32,
    )
    grad_values = jnp.einsum(
        "...hqk,...qhd->...khd",
        low_weights,
        split_heads(grad_mixed),
        preferred_element_type=jnp.float32,
    )
    return (merge_heads(grad_keys * HEAD_DIM ** (-0.5)), merge_heads(grad_values))


def projection_back(normed_low, grad_queries, grad_keys, grad_values, weights):
    low_query = grad_queries.astype(jnp.bfloat16)
    low_key = grad_keys.astype(jnp.bfloat16)
    low_value = grad_values.astype(jnp.bfloat16)
    grads = (
        weight_grad(normed_low, low_query),
        weight_grad(normed_low, low_key),
        weight_grad(normed_low, low_value),
        column_sums(low_query),
        column_sums(low_value),
    )
    grad_normed = (
        back_project(low_query, weights[0])
        + back_project(low_key, weights[1])
        + back_project(low_value, weights[2])
    )
    return (grads, grad_normed)


def output_back(grad_branch, mixed_low, w_output):
    low_grad = grad_branch.astype(jnp.bfloat16)
    return (
        weight_grad(mixed_low, low_grad),
        column_sums(low_grad),
        back_project(low_grad, w_output).astype(jnp.bfloat16),
    )


def orthogonalize(matrix):
    current = matrix / (jnp.sqrt(jnp.sum(matrix * matrix)) + 1e-07)
    for sweep_index in range(5):
        gram = gram_wide(current)
        poly = NS_SECOND * gram + NS_THIRD * high_dot(gram, gram)
        current = NS_FIRST * current + high_dot(poly, current)
    return current


def newton_schulz(wide, tall, combine):
    for sweep_index in range(5):
        wide_gram, tall_gram = combine(gram_wide(wide), gram_tall(tall))
        if sweep_index == 0:
            wide_factor = 1.0 / (jnp.sqrt(jnp.trace(wide_gram)) + 1e-07)
            tall_factor = 1.0 / (jnp.sqrt(jnp.trace(tall_gram)) + 1e-07)
            wide = wide * wide_factor
            tall = tall * tall_factor
            wide_gram = wide_gram * (wide_factor * wide_factor)
            tall_gram = tall_gram * (tall_factor * tall_factor)
        wide_poly = NS_SECOND * wide_gram + NS_THIRD * high_dot(wide_gram, wide_gram)
        tall_poly = NS_SECOND * tall_gram + NS_THIRD * high_dot(tall_gram, tall_gram)
        wide = NS_FIRST * wide + high_dot(wide_poly, wide)
        tall = NS_FIRST * tall + high_dot(tall, tall_poly)
    return (wide, tall)


def per_device(
    patches,
    regions,
    image_ids,
    attn_w,
    mlp_in,
    mlp_out,
    vec_params,
    patch_cot,
    region_cot,
    attn_mom,
    mlp_in_mom,
    mlp_out_mom,
    adam_first,
    adam_second,
):
    attn_all, w_first, w_second = (
        lax.all_gather(attn_w.astype(jnp.bfloat16), "opt", axis=0, tiled=True),
        lax.all_gather(mlp_in.astype(jnp.bfloat16), "opt", axis=1, tiled=True),
        lax.all_gather(mlp_out.astype(jnp.bfloat16), "opt", axis=0, tiled=True),
    )
    weights = (attn_all[0], attn_all[1], attn_all[2], attn_all[3])
    gain_one, shift_one, gain_two, shift_two = (
        vec_params[0],
        vec_params[1],
        vec_params[2],
        vec_params[3],
    )
    bias_query, bias_value, bias_output, bias_second = (
        vec_params[4],
        vec_params[5],
        vec_params[6],
        vec_params[7],
    )
    bias_first = vec_params[8:].reshape(FF)
    windows = lax.all_to_all(patches, "dp", split_axis=2, concat_axis=1, tiled=True)
    grid_rows = windows.shape[1]
    cols_dev = windows.shape[2]
    count_dev = grid_rows * cols_dev
    dp_size = lax.axis_size("dp")
    dp_index = lax.axis_index("dp")
    ids_group = image_ids[0]
    own_ids = lax.dynamic_slice_in_dim(ids_group, dp_index * cols_dev, cols_dev, 1).reshape(
        count_dev
    )
    all_ids = ids_group.reshape(grid_rows, dp_size, cols_dev).transpose(1, 0, 2).reshape(-1)
    same_image = (own_ids[:, None] == all_ids[None, :])[None]
    regional_in = regions.reshape(count_dev, D).astype(jnp.float32)
    reg_normed_f, reg_norm_pull = jax.vjp(layer_norm, regional_in, gain_one, shift_one)
    reg_normed = reg_normed_f.astype(jnp.bfloat16)
    reg_queries, reg_keys, reg_values = project_heads(reg_normed, weights, bias_query, bias_value)
    gathered = lax.all_gather(
        jnp.concatenate([reg_keys, reg_values], axis=-1), "dp", axis=0, tiled=True
    )
    keys_all = gathered[:, :D]
    values_all = gathered[:, D:]
    reg_mixed, reg_soft, reg_low_soft, reg_peak, reg_total = attention_forward(
        reg_queries, keys_all, values_all, same_image
    )
    regional_out = regional_in + (project(reg_mixed, weights[3]) + bias_output)
    window_in = jnp.concatenate(
        [
            regional_out.reshape(count_dev, 1, D),
            windows[0].reshape(count_dev, PATCH, D).astype(jnp.float32),
        ],
        axis=1,
    )
    win_normed_f, win_norm_pull = jax.vjp(layer_norm, window_in, gain_one, shift_one)
    win_normed = win_normed_f.astype(jnp.bfloat16)
    win_queries, win_keys, win_values = project_heads(win_normed, weights, bias_query, bias_value)
    win_mixed, win_soft, win_low_soft, win_peak, win_total = attention_forward(
        win_queries, win_keys, win_values, None
    )
    after_attention = window_in + (project(win_mixed, weights[3]) + bias_output)
    hidden_f, mlp_norm_pull = jax.vjp(layer_norm, after_attention, gain_two, shift_two)
    hidden = hidden_f.astype(jnp.bfloat16)
    active = project(hidden, w_first) + bias_first
    gelu_rows, gelu_pull = jax.vjp(partial(jax.nn.gelu, approximate=False), active)
    gelu_low = gelu_rows.astype(jnp.bfloat16)
    result = after_attention + (project(gelu_low, w_second) + bias_second)
    out_regions = result[:, 0].reshape(regions.shape).astype(jnp.bfloat16)
    out_patches = result[:, 1:].reshape(windows.shape).astype(jnp.bfloat16)
    grad_result = jnp.concatenate(
        [region_cot.reshape(count_dev, 1, D), patch_cot.reshape(count_dev, PATCH, D)], axis=1
    ).astype(jnp.float32)
    grad_mlp = grad_result.astype(jnp.bfloat16)
    d_w_second = weight_grad(gelu_low, grad_mlp)
    d_bias_second = column_sums(grad_mlp)
    d_gelu = back_project(grad_mlp, w_second)
    d_active = gelu_pull(d_gelu)[0].astype(jnp.bfloat16)
    d_w_first = weight_grad(hidden, d_active)
    d_bias_first = column_sums(d_active)
    d_hidden = back_project(d_active, w_first)
    d_after_norm, d_gain_two, d_shift_two = mlp_norm_pull(d_hidden)
    d_after = grad_result + d_after_norm
    d_w_output, d_bias_output, d_win_mixed = output_back(d_after, win_mixed, weights[3])
    d_win_queries, win_grad_scores, win_row_dot = attention_backward(
        d_win_mixed, win_keys, win_values, win_soft
    )
    d_win_keys, d_win_values = key_terms(win_grad_scores, win_low_soft, win_queries, d_win_mixed)
    win_grads, d_win_normed = projection_back(
        win_normed, d_win_queries, d_win_keys, d_win_values, weights
    )
    d_window_norm, d_gain_one, d_shift_one = win_norm_pull(d_win_normed)
    d_window_in = d_after + d_window_norm
    d_region_out = d_window_in[:, 0]
    d_patch_low = d_window_in[:, 1:].astype(jnp.bfloat16).reshape(windows.shape)
    d_patches = lax.all_to_all(d_patch_low, "dp", split_axis=1, concat_axis=2, tiled=True)
    d_reg_wout, d_reg_bout, d_reg_mixed = output_back(d_region_out, reg_mixed, weights[3])
    d_reg_queries, reg_grad_scores, reg_row_dot = attention_backward(
        d_reg_mixed, keys_all, values_all, reg_soft
    )
    part_keys, part_values = key_terms(reg_grad_scores, reg_low_soft, reg_queries, d_reg_mixed)
    own_terms = lax.psum_scatter(
        jnp.concatenate([part_keys, part_values], axis=-1), "dp", scatter_dimension=0, tiled=True
    )
    reg_grads, d_reg_normed = projection_back(
        reg_normed, d_reg_queries, own_terms[:, :D], own_terms[:, D:], weights
    )
    d_reg_norm, d_gain_reg, d_shift_reg = reg_norm_pull(d_reg_normed)
    d_regions = (d_region_out + d_reg_norm).reshape(regions.shape)
    grad_attn = jnp.stack(
        [
            win_grads[0] + reg_grads[0],
            win_grads[1] + reg_grads[1],
            win_grads[2] + reg_grads[2],
            d_w_output + d_reg_wout,
        ]
    )
    vector_rows = jnp.stack(
        [
            d_gain_one + d_gain_reg,
            d_shift_one + d_shift_reg,
            d_gain_two,
            d_shift_two,
            win_grads[3] + reg_grads[3],
            win_grads[4] + reg_grads[4],
            d_bias_output + d_reg_bout,
            d_bias_second,
        ]
    )
    grad_vec = jnp.concatenate([vector_rows, d_bias_first.reshape(FF // D, D)], axis=0)
    own_attn, own_first, own_second = (
        lax.psum_scatter(
            grad_attn.astype(jnp.bfloat16), "opt", scatter_dimension=0, tiled=True
        ).astype(jnp.float32),
        lax.psum_scatter(
            d_w_first.astype(jnp.bfloat16), "opt", scatter_dimension=1, tiled=True
        ).astype(jnp.float32),
        lax.psum_scatter(
            d_w_second.astype(jnp.bfloat16), "opt", scatter_dimension=0, tiled=True
        ).astype(jnp.float32),
    )
    own_attn, own_first, own_second, grad_vec = lax.psum(
        (own_attn, own_first, own_second, grad_vec), "dp"
    )
    owned_squares = (
        jnp.sum(own_attn * own_attn)
        + jnp.sum(own_first * own_first)
        + jnp.sum(own_second * own_second)
    )
    total_squares, grad_vec = lax.psum((owned_squares, grad_vec), "opt")
    grad_norm = jnp.sqrt(total_squares + jnp.sum(grad_vec * grad_vec))
    clip = jnp.minimum(1.0, CLIP_LIMIT / (grad_norm + 1e-06))
    decay_keep = 1.0 - MUON_RATE * MUON_DECAY
    attn_mom_new = MUON_MOMENTUM * attn_mom + clip * own_attn
    new_attn = attn_w * decay_keep - MUON_RATE * jax.vmap(orthogonalize)(attn_mom_new)
    first_mom_new = MUON_MOMENTUM * mlp_in_mom + clip * own_first
    second_mom_new = MUON_MOMENTUM * mlp_out_mom + clip * own_second

    def sum_grams(wide_gram, tall_gram):
        return (
            lax.psum(wide_gram.astype(jnp.bfloat16), "opt").astype(jnp.float32),
            lax.psum(tall_gram.astype(jnp.bfloat16), "opt").astype(jnp.float32),
        )

    wide_ortho, tall_ortho = newton_schulz(first_mom_new, second_mom_new, sum_grams)
    tall_scale = max(1.0, FF / D) ** 0.5
    new_first = mlp_in * decay_keep - MUON_RATE * wide_ortho
    new_second = mlp_out * decay_keep - MUON_RATE * tall_scale * tall_ortho
    clipped = clip * grad_vec
    moment_one = BETA_FIRST * adam_first + (1.0 - BETA_FIRST) * clipped
    moment_two = BETA_SECOND * adam_second + (1.0 - BETA_SECOND) * clipped * clipped
    first_hat = moment_one / (1.0 - BETA_FIRST**OPT_STEP)
    second_hat = moment_two / (1.0 - BETA_SECOND**OPT_STEP)
    new_vec = vec_params - ADAM_RATE * first_hat / (jnp.sqrt(second_hat) + ADAM_EPS)
    return (
        out_patches,
        out_regions,
        d_patches,
        d_regions,
        new_attn,
        attn_mom_new,
        new_first,
        first_mom_new,
        new_second,
        second_mom_new,
        new_vec,
        moment_one,
        moment_two,
        grad_norm,
    )


def solution(mesh):
    placed = (
        P("opt", "dp", None, None, None),
        P("opt", None, "dp", None),
        P("opt", None, None),
        P("opt", None, None),
        P(None, "opt"),
        P("opt", None),
        P(),
        P("opt", None, "dp", None, None),
        P("opt", None, "dp", None),
        P("opt", None, None),
        P(None, "opt"),
        P("opt", None),
        P(),
        P(),
    )
    return jax.shard_map(
        per_device,
        mesh=mesh,
        in_specs=placed,
        out_specs=(
            P("opt", None, "dp", None, None),
            P("opt", None, "dp", None),
            P("opt", "dp", None, None, None),
            P("opt", None, "dp", None),
            P("opt", None, None),
            P("opt", None, None),
            P(None, "opt"),
            P(None, "opt"),
            P("opt", None),
            P("opt", None),
            P(),
            P(),
            P(),
            P(),
        ),
        check_vma=False,
    )
```

profile of v0, /device:TPU:0, one launch (start us, length us, event | category | flops | bytes accessed | tf_op | source)
XLA Modules:
  0.0 1162.0 jit_solution(2106583071585952819)
XLA Ops:
  13.6 21.9 %all-gather.5.cloned.1.call-done = bf16[4,512,512]{2,1,0:T(8,128)(2,1)} async-done(((bf16[1,512,512]{2,1,0:T(8,128)(2,1)}), bf16[4,512,512]{2,1,0:T(8,128)(2,1)}) %all-gather.5.cloned.1.call-update) | async-done | bytes 2097168 | tf_op jit(solution)/shard_map/all_gather | solution.py:227
  38.8 5.6 copy.128
  44.5 5.6 all-to-all-start
  59.0 69.2 %all-gather.7.cloned.1.call-done = bf16[512,1024]{1,0:T(8,128)(2,1)} async-done(((bf16[64,1024]{1,0:T(8,128)(2,1)}), bf16[512,1024]{1,0:T(8,128)(2,1)}) %all-gather.7.cloned.1.call-update) | async-done | bytes 1048592 | tf_op jit(solution)/shard_map/all_gather | solution.py:261
  137.4 6.4 all-to-all-done
  151.1 5.0 convolution_convert_fusion.1
  156.1 9.1 copy.167
  165.2 4.6 add_convert_fusion.4
  169.9 9.0 copy.165
  178.9 4.7 add_convert_fusion.3
  183.6 9.0 copy.166
  192.6 21.5 %fusion.194 = (f32[64,16,50]{2,1,0:T(8,128)S(1)}, f32[64,16,50,50]{2,3,1,0:T(8,128)}) fusion(bf16[64,50,16,32]{1,3,2,0:T(8,128)(2,1)} %bitcast.386, bf16[64,50,16,32]{1,3,2,0:T(8,128)(2,1)} %bitcast.389), kind=kOutput, calls=%fused_computation.333 | convolution fusion | flops 171520048 | bytes 16998400 | tf_op jit(solution)/shard_map/sub | solution.py:109
  214.1 17.5 %fusion.16 = bf16[64,16,32,50]{3,2,1,0:T(8,128)(2,1)} fusion(bf16[64,50,16,32]{1,3,2,0:T(8,128)(2,1)} %bitcast.398, f32[64,16,50,50]{2,3,1,0:T(8,128)} %get-tuple-element.129, f32[64,16,50]{2,1,0:T(8,128)S(1)} %get-tuple-element.128), kind=kOutput, calls=%fused_computation.39 | convolution fusion | flops 170598400 | bytes 16998400 | tf_op jit(solution)/shard_map/...hqk,...khd->...qhd/dot_general | solution.py:113
  231.6 8.5 copy.137
  240.1 5.2 fusion.195
  250.2 67.1 %multiply_convert_fusion.1 = (bf16[64,50,2048]{2,0,1:T(8,128)(2,1)}, f32[64,50,2048]{2,0,1:T(8,128)}, f32[64,50,2048]{2,0,1:T(8,128)}) fusion(f32[2048]{0:T(1024)S(1)} %bitcast.454, bf16[512,2048]{1,0:T(8,128)(2,1)} %all-gather.9.cloned.1.call-done, f32[64,50,512]{2,0,1:T(8,128)} %copy-done.4, f32[512]{0:T(512)S(1)} %bitcast.457, f32[512]{0:T(512)S(1)} %bitcast.445, ...), kind=kOutput, calls=%fused_computation.9 | convolution fusion | flops 7151616000 | bytes 74224640 | tf_op jit(solution)/shard_map/dot_general | solution.py:46
  317.3 27.8 %convert_reduce_fusion = (f32[2048]{0:T(1024)}, bf16[64,50,2048]{2,0,1:T(8,128)(2,1)}) fusion(f32[64,50,2048]{2,0,1:T(8,128)} %get-tuple-element.107, bf16[2048,512]{1,0:T(8,128)(2,1)} %all-gather.11.cloned.1.call-done, bf16[64,49,512]{2,0,1:T(8,128)(2,1)} %bitcast.392, bf16[64,1,512]{2,0,1:T(8,128)(2,1)S(1)} %bitcast.416, ...), kind=kOutput, calls=%fused_computation.7 | convolution fusion | flops 6823933952 | bytes 70926336 | tf_op jit(solution)/shard_map/dot_general | solution.py:55
  345.1 12.8 %multiply_reduce_fusion.2 = (f32[512]{0:T(512)}, f32[64,50]{0,1:T(8,128)S(1)}, f32[512]{0:T(512)}, f32[64,50,512]{2,0,1:T(8,128)S(1)}) fusion(f32[64,50,512]{2,0,1:T(8,128)S(1)} %copy-done.5, f32[64,50]{0,1:T(8,128)S(1)} %fusion.170, f32[64,50]{0,1:T(8,128)S(1)} %broadcast_multiply_fusion, f32[512]{0:T(512)S(1)} %bitcast.446, ...), kind=kOutput, calls=%fused_computation.43 | convolution fusion | flops 6723989504 | bytes 28356096 | tf_op jit(solution)/shard_map/dot_general | solution.py:55
  368.3 6.9 copy.169
  375.2 22.8 %convert_reduce_fusion.1 = (f32[16,32]{1,0:T(8,128)}, bf16[64,16,32,50]{3,2,1,0:T(8,128)(2,1)}) fusion(bf16[64,50,16,32]{1,3,2,0:T(8,128)(2,1)} %bitcast.401, f32[64,16,50,50]{2,3,1,0:T(8,128)} %get-tuple-element.129, f32[64,16,50]{2,1,0:T(8,128)} %copy-done.39), kind=kOutput, calls=%fused_computation.25 | convolution fusion | flops 173874688 | bytes 17000448 | tf_op jit(solution)/shard_map/...hqk,...qhd->...khd/dot_general | solution.py:147
  398.0 24.6 %multiply_reduce_fusion = (f32[64,16,50]{2,1,0:T(8,128)S(1)}, f32[64,16,50,50]{2,3,1,0:T(8,128)}) fusion(f32[64,16,50,50]{2,3,1,0:T(8,128)} %get-tuple-element.129, f32[64,16,50]{2,1,0:T(8,128)S(1)} %copy-done.40, bf16[64,50,16,32]{1,3,2,0:T(8,128)(2,1)} %bitcast.402, bf16[64,50,16,32]{1,3,2,0:T(8,128)(2,1)} %bitcast.399), kind=kOutput, calls=%fused_computation.4 | convolution fusion | flops 171468800 | bytes 27443200 | tf_op jit(solution)/shard_map/...qhd,...khd->...hqk/dot_general | solution.py:123
  422.6 26.1 %multiply_convert_fusion = bf16[64,16,50,50]{2,3,1,0:T(8,128)(2,1)} fusion(f32[64,16,50,50]{2,3,1,0:T(8,128)} %get-tuple-element.135, f32[64,16,50]{2,1,0:T(8,128)S(1)} %get-tuple-element.134, f32[64,16,50,50]{2,3,1,0:T(8,128)} %get-tuple-element.129, f32[64,16,50]{2,1,0:T(8,128)S(1)} %copy-done.40), kind=kLoop, calls=%fused_computation.3 | loop fusion | flops 10240000 | bytes 26009600 | tf_op jit(solution)/shard_map/convert_element_type | solution.py:130
  448.6 14.2 %multiply_convert_fusion.2 = bf16[64,16,32,50]{3,2,1,0:T(8,128)(2,1)} fusion(bf16[64,50,16,32]{1,3,2,0:T(8,128)(2,1)} %bitcast.387, bf16[64,16,50,50]{2,3,1,0:T(8,128)(2,1)} %multiply_convert_fusion), kind=kOutput, calls=%fused_computation.27 | convolution fusion | flops 167116800 | bytes 11673600 | tf_op jit(solution)/shard_map/...hqk,...qhd->...khd/dot_general | solution.py:141
  462.9 12.0 %convert_reduce_fusion.2 = (f32[16,32]{1,0:T(8,128)S(1)}, bf16[64,16,32,50]{3,2,1,0:T(8,128)(2,1)}) fusion(bf16[64,50,16,32]{1,3,2,0:T(8,128)(2,1)} %bitcast.390, bf16[64,16,50,50]{2,3,1,0:T(8,128)(2,1)} %multiply_convert_fusion), kind=kOutput, calls=%fused_computation.26 | convolution fusion | flops 170393088 | bytes 11675648 | tf_op jit(solution)/shard_map/...hqk,...khd->...qhd/dot_general | solution.py:131
  474.8 9.8 copy.150
  484.6 8.9 copy.144
  493.5 10.6 copy.147
  504.1 5.7 fusion.106
  509.9 5.9 fusion.103
  515.8 8.2 fusion.185
  540.3 12.4 %bitcast_convert_fusion = bf16[2048,512]{1,0:T(8,128)(2,1)} fusion(bf16[64,50,2048]{2,0,1:T(8,128)(2,1)} %get-tuple-element.106, bf16[64,49,512]{2,0,1:T(8,128)(2,1)} %bitcast.393, bf16[64,1,512]{2,0,1:T(8,128)(2,1)S(1)} %bitcast.419), kind=kOutput, calls=%fused_computation.58 | convolution fusion | flops 6713573376 | bytes 18481152 | tf_op jit(solution)/shard_map/dot_general | solution.py:66
  552.9 5.0 convolution_bitcast_fusion.5
  560.9 14.0 %bitcast_convert_fusion.1 = bf16[512,2048]{1,0:T(8,128)(2,1)} fusion(bf16[64,50,2048]{2,0,1:T(8,128)(2,1)} %get-tuple-element.147, f32[64,50,512]{2,0,1:T(8,128)S(1)} %bitcast.385, f32[512]{0:T(512)S(1)} %bitcast.458, f32[512]{0:T(512)S(1)} %bitcast.448, f32[64,50]{0,1:T(8,128)S(1)} %copy-done.62, f32[64,50]{0,1:T(8,128)S(1)} %copy-done.52), kind=kOutput, calls=%fused_computation.59 | convolution fusion | flops 6720126976 | bytes 21787648 | tf_op jit(solution)/shard_map/dot_general | solution.py:66
  580.2 4.5 all-to-all-start.1
  593.1 9.3 fusion.35
  605.7 12.4 %reduce-scatter.13.cloned.1.call-done = f32[64,1024]{1,0:T(8,128)} async-done(((f32[512,1024]{1,0:T(8,128)}), f32[64,1024]{1,0:T(8,128)}) %reduce-scatter.13.cloned.1.call-update) | async-done | bytes 262160
  626.5 13.6 %add_convert_fusion.1 = bf16[64,50,512]{2,0,1:T(8,128)(2,1)S(1)} fusion(f32[64,50,512]{2,0,1:T(8,128)} %copy-done.4, f32[512]{0:T(512)S(1)} %bitcast.456, bf16[64,50,2048]{2,0,1:T(8,128)(2,1)} %get-tuple-element.106, bf16[2048,512]{1,0:T(8,128)(2,1)} %all-gather.11.cloned.1.call-done), kind=kOutput, calls=%fused_computation.49 | convolution fusion | flops 6715801600 | bytes 25036800 | tf_op jit(solution)/shard_map/dot_general | solution.py:46
  646.6 20.2 %reduce-scatter.11.cloned.1.call-done = bf16[512,512]{1,0:T(8,128)(2,1)} async-done(((bf16[2048,512]{1,0:T(8,128)(2,1)}), bf16[512,512]{1,0:T(8,128)(2,1)}) %reduce-scatter.11.cloned.1.call-update) | async-done | bytes 524304 | tf_op jit(solution)/shard_map/reduce_scatter | solution.py:359
  666.8 34.1 %reduce-scatter.9.cloned.1.call-done = bf16[512,512]{1,0:T(8,128)(2,1)} async-done(((bf16[512,2048]{1,0:T(8,128)(2,1)}), bf16[512,512]{1,0:T(8,128)(2,1)}) %reduce-scatter.9.cloned.1.call-update) | async-done | bytes 524304 | tf_op jit(solution)/shard_map/reduce_scatter | solution.py:356
  705.0 29.9 %reduce-scatter.7.cloned.1.call-done = bf16[1,512,512]{2,1,0:T(8,128)(2,1)} async-done(((bf16[4,512,512]{2,1,0:T(8,128)(2,1)}), bf16[1,512,512]{2,1,0:T(8,128)(2,1)}) %reduce-scatter.7.cloned.1.call-update) | async-done | bytes 524304 | tf_op jit(solution)/shard_map/reduce_scatter | solution.py:353
  734.9 129.4 %all-reduce.23 = (f32[1,512,512]{2,1,0:T(8,128)S(1)}, f32[512,512]{1,0:T(8,128)S(1)}, f32[512,512]{1,0:T(8,128)S(1)}, f32[12,512]{1,0:T(8,128)S(1)}) all-reduce(bf16[1,512,512]{2,1,0:T(8,128)(2,1)} %reduce-scatter.7.cloned.1.call-done, ...), channel_id=1, replica_groups=mesh['dp'=8,'opt'=4] {'dp'}, use_global_device_ids=true, to_apply=%region_20.21 | all-reduce | flops 792576 | bytes 4767744 | tf_op jit(solution)/shard_map/psum | solution.py:363
  868.9 11.2 all-reduce.1
  911.7 29.9 %all-reduce.22.cloned.1.call-done = (bf16[512,512]{1,0:T(8,128)(2,1)}, bf16[512,512]{1,0:T(8,128)(2,1)}) async-done(((bf16[512,512]{1,0:T(8,128)(2,1)}, bf16[512,512]{1,0:T(8,128)(2,1)}), (bf16[512,512]{1,0:T(8,128)(2,1)}, bf16[512,512]{1,0:T(8,128)(2,1)})) %all-reduce.22.cloned.1.call-update) | async-done | bytes 1048592 | tf_op jit(solution)/shard_map/psum | solution.py:382
  968.8 29.2 %all-reduce.20.cloned.1.call-done = (bf16[512,512]{1,0:T(8,128)(2,1)}, bf16[512,512]{1,0:T(8,128)(2,1)}) async-done(((bf16[512,512]{1,0:T(8,128)(2,1)}, bf16[512,512]{1,0:T(8,128)(2,1)}), (bf16[512,512]{1,0:T(8,128)(2,1)}, bf16[512,512]{1,0:T(8,128)(2,1)})) %all-reduce.20.cloned.1.call-update) | async-done | bytes 1048592 | tf_op jit(solution)/shard_map/psum | solution.py:382
  1018.3 29.5 %all-reduce.18.cloned.1.call-done = (bf16[512,512]{1,0:T(8,128)(2,1)}, bf16[512,512]{1,0:T(8,128)(2,1)}) async-done(((bf16[512,512]{1,0:T(8,128)(2,1)}, bf16[512,512]{1,0:T(8,128)(2,1)}), (bf16[512,512]{1,0:T(8,128)(2,1)}, bf16[512,512]{1,0:T(8,128)(2,1)})) %all-reduce.18.cloned.1.call-update) | async-done | bytes 1048592 | tf_op jit(solution)/shard_map/psum | solution.py:382
  1065.8 30.2 %all-reduce.16.cloned.1.call-done = (bf16[512,512]{1,0:T(8,128)(2,1)}, bf16[512,512]{1,0:T(8,128)(2,1)}) async-done(((bf16[512,512]{1,0:T(8,128)(2,1)}, bf16[512,512]{1,0:T(8,128)(2,1)}), (bf16[512,512]{1,0:T(8,128)(2,1)}, bf16[512,512]{1,0:T(8,128)(2,1)})) %all-reduce.16.cloned.1.call-update) | async-done | bytes 1048592 | tf_op jit(solution)/shard_map/psum | solution.py:382
  1108.3 5.3 fusion.62
  1113.6 30.7 %all-reduce.14.cloned.1.call-done = (bf16[512,512]{1,0:T(8,128)(2,1)}, bf16[512,512]{1,0:T(8,128)(2,1)}) async-done(((bf16[512,512]{1,0:T(8,128)(2,1)}, bf16[512,512]{1,0:T(8,128)(2,1)}), (bf16[512,512]{1,0:T(8,128)(2,1)}, bf16[512,512]{1,0:T(8,128)(2,1)})) %all-reduce.14.cloned.1.call-update) | async-done | bytes 1048592 | tf_op jit(solution)/shard_map/psum | solution.py:382
  (363 shorter events, 222.3 us)
Async XLA Ops:
  7.2 28.3 %all-gather.5.cloned.1.call-start = ((), (), s32[]{:S(2)}) async-start(), calls=%async_computation.6 | async-start | bytes 2621440 | tf_op jit(solution)/shard_map/all_gather | solution.py:227
  9.3 118.9 %all-gather.7.cloned.1.call-start = ((), (), s32[]{:S(2)}) async-start(), calls=%async_computation.7 | async-start | bytes 1179648 | tf_op jit(solution)/shard_map/all_gather | solution.py:261
  10.3 48.2 %copy-start.64 = (f32[8,8]{1,0:T(8,128)}, f32[8,8]{1,0:T(8,128)S(1)}, u32[]{:S(2)}) copy-start(f32[8,8]{1,0:T(8,128)S(1)} %broadcast_multiply_fusion.2) | copy-start | bytes 772
  11.9 46.6 %copy-start.70 = (f32[8,8]{1,0:T(8,128)}, f32[8,8]{1,0:T(8,128)S(1)}, u32[]{:S(2)}) copy-start(f32[8,8]{1,0:T(8,128)S(1)} %get-tuple-element.123) | copy-start | bytes 772
  13.5 136.1 %copy-start.59 = (f32[1,512]{1,0:T(1,128)}, f32[1,512]{1,0:T(1,128)S(1)}, u32[]{:S(2)}) copy-start(f32[1,512]{1,0:T(1,128)S(1)} %get-tuple-element.120) | copy-start | bytes 6148
  13.6 136.1 %copy-start.66 = (f32[1,512]{1,0:T(1,128)}, f32[1,512]{1,0:T(1,128)S(1)}, u32[]{:S(2)}) copy-start(f32[1,512]{1,0:T(1,128)S(1)} %get-tuple-element.119) | copy-start | bytes 6148
  13.6 236.6 %copy-start.82 = (f32[1,512]{1,0:T(1,128)}, f32[1,512]{1,0:T(1,128)S(1)}, u32[]{:S(2)}) copy-start(f32[1,512]{1,0:T(1,128)S(1)} %get-tuple-element.115) | copy-start | bytes 6148
  13.6 344.3 %copy-start.76 = (f32[1,512]{1,0:T(1,128)}, f32[1,512]{1,0:T(1,128)S(1)}, u32[]{:S(2)}) copy-start(f32[1,512]{1,0:T(1,128)S(1)} %get-tuple-element.114) | copy-start | bytes 6148
  44.5 99.2 %all-to-all-start = ((bf16[1,1,64,49,512]{4,3,1,0,2:T(8,128)(2,1)}), bf16[1,1,64,49,512]{4,3,1,0,2:T(8,128)(2,1)}, u32[]{:S(2)}, u32[]{:S(2)}) async-start(bf16[1,1,64,49,512]{4,3,1,0,2:T(8,128)(2,1)} %copy.128), calls=%async_computation | async-start | bytes 7340032 | tf_op jit(solution)/shard_map/all_to_all | solution.py:245
  50.1 200.0 %all-gather.9.cloned.1.call-start = ((), (), s32[]{:S(2)}) async-start(), calls=%async_computation.8 | async-start | bytes 2621440 | tf_op jit(solution)/shard_map/all_gather | solution.py:228
  51.1 266.2 %all-gather.11.cloned.1.call-start = ((), (), s32[]{:S(2)}) async-start(), calls=%async_computation.9 | async-start | bytes 2621440 | tf_op jit(solution)/shard_map/all_gather | solution.py:229
  53.2 564.9 %reduce-scatter.13.cloned.1.call-start = ((), (), s32[]{:S(2)}) async-start(), calls=%async_computation.13 | async-start | bytes 2359296
  58.9 78.1 %copy-start.43 = (bf16[64,512]{0,1:T(8,128)(2,1)}, bf16[64,512]{0,1:T(8,128)(2,1)S(1)}, u32[]{:S(2)}) copy-start(bf16[64,512]{0,1:T(8,128)(2,1)S(1)} %copy.126) | copy-start | bytes 196612
  131.5 15.3 %copy-start.34 = (bf16[512,512]{0,1:T(8,128)(2,1)}, bf16[512,512]{0,1:T(8,128)(2,1)S(1)}, u32[]{:S(2)}) copy-start(bf16[512,512]{0,1:T(8,128)(2,1)S(1)} %copy.127) | copy-start | bytes 1572868
  137.3 102.8 %copy-start.21 = (f32[64,1,512]{2,0,1:T(8,128)}, f32[64,1,512]{2,0,1:T(8,128)S(1)}, u32[]{:S(2)}) copy-start(f32[64,1,512]{2,0,1:T(8,128)S(1)} %fusion.75) | copy-start | bytes 393220
  151.1 27.8 %copy-start.1 = (bf16[64,50,512]{2,0,1:T(8,128)(2,1)}, bf16[64,50,512]{2,0,1:T(8,128)(2,1)S(1)}, u32[]{:S(2)}) copy-start(bf16[64,50,512]{2,0,1:T(8,128)(2,1)S(1)} %add_convert_fusion.5) | copy-start | bytes 9830404
  214.1 17.5 %copy-start.39 = (f32[64,16,50]{2,1,0:T(8,128)}, f32[64,16,50]{2,1,0:T(8,128)S(1)}, u32[]{:S(2)}) copy-start(f32[64,16,50]{2,1,0:T(8,128)S(1)} %get-tuple-element.128) | copy-start | bytes 614404
  245.4 112.5 %copy-start.51 = (f32[64,50]{0,1:T(8,128)}, f32[64,50]{0,1:T(8,128)S(1)}, u32[]{:S(2)}) copy-start(f32[64,50]{0,1:T(8,128)S(1)} %broadcast_multiply_fusion) | copy-start | bytes 38404
  250.1 107.8 %copy-start.61 = (f32[64,50]{0,1:T(8,128)}, f32[64,50]{0,1:T(8,128)S(1)}, u32[]{:S(2)}) copy-start(f32[64,50]{0,1:T(8,128)S(1)} %fusion.170) | copy-start | bytes 38404
  250.1 67.1 %copy-start.49 = (bf16[1,8,8,512]{3,2,1,0:T(8,128)(2,1)S(1)}, bf16[1,8,8,512]{3,2,1,0:T(8,128)(2,1)}, u32[]{:S(2)}) copy-start(bf16[1,8,8,512]{3,2,1,0:T(8,128)(2,1)} %param.22) | copy-start | bytes 196612
  317.2 27.8 %copy-start.5 = (f32[64,50,512]{2,0,1:T(8,128)S(1)}, f32[64,50,512]{2,0,1:T(8,128)}, u32[]{:S(2)}) copy-start(f32[64,50,512]{2,0,1:T(8,128)} %copy-done.4) | copy-start | bytes 19660804
  345.1 12.8 %copy-start.58 = (f32[64,50]{0,1:T(8,128)S(1)}, f32[64,50]{0,1:T(8,128)}, u32[]{:S(2)}) copy-start(f32[64,50]{0,1:T(8,128)} %copy-done.57) | copy-start | bytes 38404
  375.2 22.8 %copy-start.40 = (f32[64,16,50]{2,1,0:T(8,128)S(1)}, f32[64,16,50]{2,1,0:T(8,128)}, u32[]{:S(2)}) copy-start(f32[64,16,50]{2,1,0:T(8,128)} %copy-done.39) | copy-start | bytes 614404
  493.5 16.3 %copy-start.6 = (bf16[64,50,512]{2,0,1:T(8,128)(2,1)}, bf16[64,50,512]{2,0,1:T(8,128)(2,1)S(1)}, u32[]{:S(2)}) copy-start(bf16[64,50,512]{2,0,1:T(8,128)(2,1)S(1)} %copy.144) | copy-start | bytes 9830404
  504.1 11.7 %slice-start = ((s8[6422528]{0:T(1024)(128)(4,1)}), s8[4194304]{0:T(1024)(128)(4,1)S(1)}, s32[]{:S(2)}) async-start(s8[6422528]{0:T(1024)(128)(4,1)} %bitcast.380), calls=%async_computation.19 | async-start | bytes 8388608
  509.9 17.9 %slice-start.2 = ((s8[6553600]{0:T(1024)(128)(4,1)}), s8[4194304]{0:T(1024)(128)(4,1)S(1)}, s32[]{:S(2)}) async-start(s8[6553600]{0:T(1024)(128)(4,1)} %bitcast.382), calls=%async_computation.21 | async-start | bytes 8388608
  515.8 11.9 %slice-start.3 = ((s8[6553600]{0:T(1024)(128)(4,1)}), s8[2359296]{0:T(1024)(128)(4,1)S(1)}, s32[]{:S(2)}) async-start(s8[6553600]{0:T(1024)(128)(4,1)} %bitcast.382), calls=%async_computation.22 | async-start | bytes 4718592
  540.1 126.7 %reduce-scatter.11.cloned.1.call-start = ((), (), s32[]{:S(2)}) async-start(), calls=%async_computation.12 | async-start | bytes 2621440 | tf_op jit(solution)/shard_map/reduce_scatter | solution.py:359
  540.3 12.6 %copy-start.2 = (bf16[64,50,512]{2,0,1:T(8,128)(2,1)S(1)}, bf16[64,50,512]{2,0,1:T(8,128)(2,1)}, u32[]{:S(2)}) copy-start(bf16[64,50,512]{2,0,1:T(8,128)(2,1)} %copy-done.1) | copy-start | bytes 9830404
  552.7 148.3 %reduce-scatter.9.cloned.1.call-start = ((), (), s32[]{:S(2)}) async-start(), calls=%async_computation.11 | async-start | bytes 2621440 | tf_op jit(solution)/shard_map/reduce_scatter | solution.py:356
  580.2 120.7 %all-to-all-start.1 = ((bf16[1,8,8,49,512]{4,2,3,0,1:T(8,128)(2,1)}), bf16[1,8,8,49,512]{4,2,3,0,1:T(8,128)(2,1)}, u32[]{:S(2)}, u32[]{:S(2)}) async-start(bf16[1,8,8,49,512]{4,2,3,0,1:T(8,128)(2,1)} %copy.151), calls=%async_computation.1 | async-start | bytes 6422528 | tf_op jit(solution)/shard_map/all_to_all | solution.py:317
  584.7 150.2 %reduce-scatter.7.cloned.1.call-start = ((), (), s32[]{:S(2)}) async-start(), calls=%async_computation.10 | async-start | bytes 2621440 | tf_op jit(solution)/shard_map/reduce_scatter | solution.py:353
  593.1 11.4 copy-start.24
  593.1 26.1 %copy-start.16 = (bf16[4,512,512]{2,1,0:T(8,128)(2,1)S(1)}, bf16[4,512,512]{2,1,0:T(8,128)(2,1)}, u32[]{:S(2)}) copy-start(bf16[4,512,512]{2,1,0:T(8,128)(2,1)} %all-gather.5.cloned.1.call-done) | copy-start | bytes 6291460
  602.4 20.7 %copy-start.29 = (f32[512,512]{1,0:T(8,128)S(1)}, f32[512,512]{1,0:T(8,128)}, u32[]{:S(2)}) copy-start(f32[512,512]{1,0:T(8,128)} %convolution_bitcast_fusion.6) | copy-start | bytes 3145732
  605.7 20.7 %copy-start.80 = (f32[2048]{0:T(1024)S(1)}, f32[2048]{0:T(1024)}, u32[]{:S(2)}) copy-start(f32[2048]{0:T(1024)} %get-tuple-element.146) | copy-start | bytes 24580
  605.7 20.7 %copy-start.81 = (f32[1,512]{1,0:T(1,128)S(1)}, f32[1,512]{1,0:T(1,128)}, u32[]{:S(2)}) copy-start(f32[1,512]{1,0:T(1,128)} %get-tuple-element.121) | copy-start | bytes 6148
  626.4 315.2 %all-reduce.22.cloned.1.call-start = ((), (), s32[]{:S(2)}) async-start(), calls=%async_computation.18 | async-start | bytes 2097152 | tf_op jit(solution)/shard_map/psum | solution.py:382
  864.3 20.8 %copy-start.25 = (f32[512,512]{1,0:T(8,128)}, f32[512,512]{1,0:T(8,128)S(1)}, u32[]{:S(2)}) copy-start(f32[512,512]{1,0:T(8,128)S(1)} %get-tuple-element.83) | copy-start | bytes 3145732
  888.2 61.7 %copy-start.12 = (f32[512,512]{1,0:T(8,128)}, f32[512,512]{1,0:T(8,128)S(1)}, u32[]{:S(2)}) copy-start(f32[512,512]{1,0:T(8,128)S(1)} %get-tuple-element.149) | copy-start | bytes 3145732
  888.2 68.3 %copy-start.11 = (f32[512,512]{1,0:T(8,128)}, f32[512,512]{1,0:T(8,128)S(1)}, u32[]{:S(2)}) copy-start(f32[512,512]{1,0:T(8,128)S(1)} %get-tuple-element.148) | copy-start | bytes 3145732
  906.8 39.6 %copy-start.17 = (f32[1,512,512]{2,1,0:T(8,128)}, f32[1,512,512]{2,1,0:T(8,128)S(1)}, u32[]{:S(2)}) copy-start(f32[1,512,512]{2,1,0:T(8,128)S(1)} %fusion.57) | copy-start | bytes 3145732
  906.9 91.2 %all-reduce.20.cloned.1.call-start = ((), (), s32[]{:S(2)}) async-start(), calls=%async_computation.17 | async-start | bytes 2097152 | tf_op jit(solution)/shard_map/psum | solution.py:382
  958.6 43.3 %copy-start.13 = (f32[512,512]{1,0:T(8,128)}, f32[512,512]{1,0:T(8,128)S(1)}, u32[]{:S(2)}) copy-start(f32[512,512]{1,0:T(8,128)S(1)} %convolution_add_fusion.4) | copy-start | bytes 3145732
  961.3 86.6 %all-reduce.18.cloned.1.call-start = ((), (), s32[]{:S(2)}) async-start(), calls=%async_computation.16 | async-start | bytes 2097152 | tf_op jit(solution)/shard_map/psum | solution.py:382
  1011.1 85.0 %all-reduce.16.cloned.1.call-start = ((), (), s32[]{:S(2)}) async-start(), calls=%async_computation.15 | async-start | bytes 2097152 | tf_op jit(solution)/shard_map/psum | solution.py:382
  1059.3 85.0 %all-reduce.14.cloned.1.call-start = ((), (), s32[]{:S(2)}) async-start(), calls=%async_computation.14 | async-start | bytes 2097152 | tf_op jit(solution)/shard_map/psum | solution.py:382
  1104.9 41.3 %copy-start.27 = (f32[512,512]{1,0:T(8,128)S(1)}, f32[512,512]{1,0:T(8,128)}, u32[]{:S(2)}) copy-start(f32[512,512]{1,0:T(8,128)} %param.18) | copy-start | bytes 3145732
  (62 other events, 332.1 us)
Sparse Core Ops, SparseCore 0:
  10.1 25.2 all-gather.4
  39.0 89.1 all-gather.6
  130.3 21.1 all-gather.8
  153.5 22.5 all-gather.10
  540.2 77.8 reduce-scatter.12
  620.5 46.2 reduce-scatter.10
  669.5 31.3 reduce-scatter.8
  703.5 31.4 reduce-scatter.6
  907.0 34.5 all-reduce.21
  961.4 36.6 all-reduce.19
  1011.2 36.6 all-reduce.17
  1059.5 36.5 all-reduce.15
  1107.7 36.5 all-reduce.13
where the time goes:
time: 1170 us; the launch traced here: 1160 us
  matrix products  454 us (39%)
  waiting for transfers between devices  344 us (29%)
  blocking collectives  141 us (12%)
  local copies, waits for them, and re-layouts  117 us (10%)
  other arithmetic  72.8 us (6%)
  between operations  22.4 us (2%)
  starting transfers between devices  11.8 us (1%)
    psum x5, waiting for transfers between devices, sum_grams(): lax.psum(wide_gram.astype(jnp.bfloat16), 'opt').astype(jnp.float32)  150 us
    psum x1, blocking collectives, per_device(): lax.psum((own_attn, own_first, own_second, grad_vec), 'dp')  129 us
    dot_general x10, matrix products, project(): lax.dot_general(low_rows, low_weight, (((low_rows.ndim - 1,), (0,)), ((),...  103 us
    all_gather x1, waiting for transfers between devices, per_device(): lax.all_gather(jnp.concatenate([reg_keys, reg_values], axis=-1), 'dp', ax...  69.2 us
    dot_general x10, matrix products, back_project(): lax.dot_general(low_grads, low_weight, (((low_grads.ndim - 1,), (1,)), ((...  68.9 us
    dot_general x30, matrix products, high_dot(): return jnp.dot(left, right, precision=lax.Precision.HIGHEST)  68.2 us
    dot_general x10, matrix products, weight_grad(): lax.dot_general(flat_rows, flat_grads, (((0,), (0,)), ((), ())), preferre...  52.9 us
    reduce_scatter x1, waiting for transfers between devices, per_device(): lax.psum_scatter(d_w_first.astype(jnp.bfloat16), 'opt', scatter_dimension...  34.1 us
  transfers between devices with their start and end apart: 15, of which 12 were waited for; matrix products, arithmetic and copies ran while one was open for 27% of the time, Pallas kernels for 0%

commit v1 on v0

v1 whole, which is shorter than its diff:
```python
from functools import partial

import jax
import jax.numpy as jnp
from jax import lax
from jax.experimental import pallas as pl
from jax.experimental.pallas import tpu as pltpu
from jax.sharding import PartitionSpec as P

BF = jnp.bfloat16
F32 = jnp.float32

D = 512
HEADS = 16
HEAD_DIM = 32
FF = 2048
PATCH = 49
LIVE = 50
ROWS = 56
GROUP = 128
STACK = 4 * ROWS
OPT_STEP = 10
OPT = 4

SCALE = HEAD_DIM ** (-0.5)
NORM_EPS = 1e-05
MASKED = -1e30
NS_FIRST = 3.4445
NS_SECOND = -4.775
NS_THIRD = 2.0315
MUON_RATE = 0.5
MUON_MOMENTUM = 0.5
MUON_DECAY = 0.01
ADAM_RATE = 0.5
BETA_FIRST = 0.9
BETA_SECOND = 0.95
ADAM_EPS = 1e-08
CLIP_LIMIT = 1.0
DECAY_KEEP = 1.0 - MUON_RATE * MUON_DECAY
VMEM = 60 * 2**20

ERF_P = 0.3275911 * 0.5**0.5
ERF = tuple(0.5 * c for c in (0.254829592, -0.284496736, 1.421413741, -1.453152027, 1.061405429))
INV_SQRT_2PI = 0.3989422804014327
LOG2E = 1.4426950408889634


def nn(a, b):
    return lax.dot_general(a, b, (((1,), (0,)), ((), ())), preferred_element_type=F32)


def nt(a, b):
    return lax.dot_general(a, b, (((1,), (1,)), ((), ())), preferred_element_type=F32)


def tn(a, b):
    return lax.dot_general(a, b, (((0,), (0,)), ((), ())), preferred_element_type=F32)


def full(shape):
    return pl.BlockSpec(shape, lambda i: (0,) * len(shape))


def block(shape):
    return pl.BlockSpec(shape, lambda i: (i,) + (0,) * (len(shape) - 1))


def norm_parts(x):
    centre = x - jnp.mean(x, axis=-1, keepdims=True)
    scale = lax.rsqrt(jnp.mean(centre * centre, axis=-1, keepdims=True) + NORM_EPS)
    return centre * scale, scale


def norm_back(grad, xhat, scale, gain):
    inner = grad * gain
    first = jnp.mean(inner, axis=-1, keepdims=True)
    second = jnp.mean(inner * xhat, axis=-1, keepdims=True)
    return scale * (inner - first - xhat * second)


def head_masks():
    lane = lax.broadcasted_iota(jnp.int32, (1, GROUP), 1) // HEAD_DIM
    return [lane == h for h in range(4)]


def spread(rows, masks):
    return jnp.concatenate([jnp.where(m, rows, 0.0) for m in masks], axis=0).astype(BF)


def collect(stacked, masks, rows):
    out = stacked[:rows]
    for h in range(1, 4):
        out = jnp.where(masks[h], stacked[h * rows : (h + 1) * rows], out)
    return out


def fill_rows(held, patches, regions):
    count = held.shape[0]
    held[:, 0:PATCH, :] = patches.astype(F32)
    held[:, PATCH:LIVE, :] = regions.astype(F32)
    held[:, LIVE:ROWS, :] = jnp.zeros((count, ROWS - LIVE, D), F32)


def fold(x):
    return jnp.sum(x.reshape(x.shape[0] // 8, 8, x.shape[1]), axis=0)


def gelu_parts(a):
    bell = jnp.exp2(a * a * (-0.5 * LOG2E))
    t = 1.0 / (1.0 + ERF_P * jnp.abs(a))
    tail = ((((ERF[4] * t + ERF[3]) * t + ERF[2]) * t + ERF[1]) * t + ERF[0]) * t * bell
    share = jnp.where(a < 0, tail, 1.0 - tail)
    return a * share, share + a * bell * INV_SQRT_2PI


def attn_fwd_kernel(count, batch, p_ref, r_ref, wq_ref, wk_ref, wv_ref, wo_ref, vec_ref,
                    x1_ref, q_ref, k_ref, v_ref, o_ref, pt_ref, held):
    total = count * ROWS
    fill_rows(held, p_ref[...], r_ref[...])
    x = held[...].reshape(total, D)
    vec = vec_ref[...]
    xhat, _ = norm_parts(x)
    xn = (xhat * vec[0:1] + vec[1:2]).astype(BF)
    shape = (count, ROWS, D)
    q_ref[...] = (nn(xn, wq_ref[...]) + vec[4:5]).reshape(shape).astype(BF)
    k_ref[...] = nn(xn, wk_ref[...]).reshape(shape).astype(BF)
    v_ref[...] = (nn(xn, wv_ref[...]) + vec[5:6]).reshape(shape).astype(BF)
    masks = head_masks()
    live = lax.broadcasted_iota(jnp.int32, (ROWS, 1), 0) < LIVE

    def body(step, carry):
        units = [(step * batch + w, g) for w in range(batch) for g in range(4)]
        scores, probs = [], []
        for w, g in units:
            lanes = slice(GROUP * g, GROUP * (g + 1))
            scores.append(nt(k_ref[w, :, lanes], spread(q_ref[w, :, lanes].astype(F32), masks)))
        for (w, g), s in zip(units, scores):
            s = jnp.where(live, s, MASKED)
            e = jnp.exp((s - jnp.max(s, axis=0, keepdims=True)) * SCALE)
            p = (e * (1.0 / jnp.sum(e, axis=0, keepdims=True))).astype(BF)
            pt_ref[w, g] = p
            probs.append(p)
        for (w, g), p in zip(units, probs):
            lanes = slice(GROUP * g, GROUP * (g + 1))
            o_ref[w, :, lanes] = collect(tn(p, v_ref[w, :, lanes]), masks, ROWS).astype(BF)
        return carry

    lax.fori_loop(0, count // batch, body, 0)
    mixed = o_ref[...].astype(F32).reshape(total, D).astype(BF)
    x1_ref[...] = (x + nn(mixed, wo_ref[...]) + vec[6:7]).reshape(shape)


def attn_fwd(patches, region_rows, weights, vec, count=8, batch=4):
    windows = patches.shape[0]
    rows = lambda dtype: jax.ShapeDtypeStruct((windows, ROWS, D), dtype)
    return pl.pallas_call(
        partial(attn_fwd_kernel, count, batch),
        grid=(windows // count,),
        in_specs=[block((count, PATCH, D)), block((count, 1, D))] + [full((D, D))] * 4 + [full(vec.shape)],
        out_specs=[block((count, ROWS, D))] * 5 + [block((count, 4, ROWS, STACK))],
        out_shape=[rows(F32), rows(BF), rows(BF), rows(BF), rows(BF),
                   jax.ShapeDtypeStruct((windows, 4, ROWS, STACK), BF)],
        scratch_shapes=[pltpu.VMEM((count, ROWS, D), F32)],
        compiler_params=pltpu.CompilerParams(vmem_limit_bytes=VMEM),
        cost_estimate=pl.CostEstimate(flops=3 * 10**10, bytes_accessed=3 * 10**7, transcendentals=0),
        name="window_attention_forward",
    )(patches, region_rows, *weights, vec)


def mlp_kernel(count, steps, cols, x1_ref, pc_ref, rc_ref, w1a, w1b, w1c, w1d, w2a, w2b, w2c, w2d,
               vec_ref, b1_ref, op_ref, or_ref, dx1_ref, dw1_ref, dw2_ref, dv_ref, db1_ref,
               held, acc1, acc2):
    total = count * ROWS
    step = pl.program_id(0)

    @pl.when(step == 0)
    def _():
        for ref in (acc1, acc2, dv_ref, db1_ref):
            ref[...] = jnp.zeros_like(ref)

    vec = vec_ref[...]
    gain = vec[2:3]
    x1 = x1_ref[...].reshape(total, D)
    xhat, scale = norm_parts(x1)
    h = (xhat * gain + vec[3:4]).astype(BF)
    fill_rows(held, pc_ref[...].reshape(count, PATCH, D), rc_ref[...].reshape(count, 1, D))
    dy = held[...].reshape(total, D)
    dm = dy.astype(BF)
    ht = h.T
    dmt = dm.T
    w1s, w2s = (w1a, w1b, w1c, w1d), (w2a, w2b, w2c, w2d)
    y = x1 + vec[7:8]
    dh = jnp.zeros((total, D), F32)
    parts = [(j, slice(c, c + cols)) for j in range(4) for c in range(0, D, cols)]

    def activate(j, s):
        u, slope = gelu_parts(nn(h, w1s[j][:, s]) + b1_ref[j : j + 1, s])
        da = slope * nt(dm, w2s[j][s, :])
        db1_ref[j, :, s] += fold(da)
        return u.astype(BF), da.astype(BF)

    def apply(j, s, u, da):
        acc1[j, :, s] += nn(ht, da)
        acc2[j, :, s] += nn(dmt, u)
        return nn(u, w2s[j][s, :]), nt(da, w1s[j][:, s])

    held_pair = activate(*parts[0])
    for n in range(1, len(parts) + 1):
        later = activate(*parts[n]) if n < len(parts) else None
        up, down = apply(*parts[n - 1], *held_pair)
        y, dh = y + up, dh + down
        held_pair = later
    y = y.reshape(count, ROWS, D)
    op_ref[...] = y[:, :PATCH].astype(BF).reshape(op_ref.shape)
    or_ref[...] = y[:, PATCH:LIVE].astype(BF).reshape(or_ref.shape)
    dx1_ref[...] = (dy + norm_back(dh, xhat, scale, gain)).reshape(dx1_ref.shape)
    dv_ref[0] += fold(dh * xhat)
    dv_ref[1] += fold(dh)
    dv_ref[2] += fold(dy)

    @pl.when(step == steps - 1)
    def _():
        dw1_ref[...] = acc1[...].astype(BF)
        dw2_ref[...] = acc2[...].astype(BF)


def mlp(x1, chunk, patch_cot, region_cot, first, second, vec, bias_first, count=8, cols=256):
    sources, _, per, _, _ = x1.shape
    many = count // per
    steps = sources // many
    some = lambda rows: pl.BlockSpec((many, per, rows, D), lambda i: (i, 0, 0, 0))
    array = jax.ShapeDtypeStruct
    return pl.pallas_call(
        partial(mlp_kernel, count, steps, cols),
        grid=(steps,),
        in_specs=[pl.BlockSpec((many, 1, per, ROWS, D), lambda i: (i, chunk, 0, 0, 0)), some(PATCH), some(1)]
        + [full((D, D))] * 8 + [full(vec.shape), full((4, D))],
        out_specs=[some(PATCH), some(1), some(ROWS), full((4, D, D)), full((4, D, D)), full((3, 8, D)), full((4, 8, D))],
        out_shape=[array((sources, per, PATCH, D), BF), array((sources, per, 1, D), BF),
                   array((sources, per, ROWS, D), F32), array((4, D, D), BF), array((4, D, D), BF),
                   array((3, 8, D), F32), array((4, 8, D), F32)],
        scratch_shapes=[pltpu.VMEM((count, ROWS, D), F32), pltpu.VMEM((4, D, D), F32), pltpu.VMEM((4, D, D), F32)],
        compiler_params=pltpu.CompilerParams(vmem_limit_bytes=VMEM),
        cost_estimate=pl.CostEstimate(flops=4 * 10**10, bytes_accessed=3 * 10**7, transcendentals=0),
        name="mlp_forward_backward",
    )(x1, patch_cot, region_cot, *first, *second, vec, bias_first)


def attn_bwd_kernel(count, batch, chunks, *refs):
    p_ref, r_ref = refs[:2]
    dx1_refs = refs[2 : 2 + chunks]
    (q_ref, k_ref, v_ref, o_ref, pt_ref, wq_ref, wk_ref, wv_ref, wo_ref, vec_ref,
     dp_ref, dr_ref, dw_ref, dv_ref, held, dq_held, dk_held, dvv_held, do_held) = refs[2 + chunks :]
    total = count * ROWS
    shape = (count, ROWS, D)

    @pl.when(pl.program_id(0) == 0)
    def _():
        dw_ref[...] = jnp.zeros_like(dw_ref)
        dv_ref[...] = jnp.zeros_like(dv_ref)

    vec = vec_ref[...]
    gain = vec[0:1]
    dx1 = jnp.concatenate([ref[...] for ref in dx1_refs], axis=1).reshape(total, D)
    gb = dx1.astype(BF)
    do_held[...] = nt(gb, wo_ref[...]).astype(BF).astype(F32).reshape(shape)
    masks = head_masks()

    def body(step, carry):
        units = [(step * batch + w, g) for w in range(batch) for g in range(4)]
        grads, scores = [], []
        for w, g in units:
            lanes = slice(GROUP * g, GROUP * (g + 1))
            do_wide = spread(do_held[w, :, lanes], masks)
            dvv_held[w, :, lanes] = nn(pt_ref[w, g], do_wide)
            grads.append(nt(v_ref[w, :, lanes], do_wide))
        for (w, g), grad in zip(units, grads):
            p = pt_ref[w, g].astype(F32)
            both = p * grad
            scores.append((both - p * jnp.sum(both, axis=0, keepdims=True)).astype(BF))
        for (w, g), ds in zip(units, scores):
            lanes = slice(GROUP * g, GROUP * (g + 1))
            dk_held[w, :, lanes] = nn(ds, spread(q_ref[w, :, lanes].astype(F32), masks)) * SCALE
            dq_held[w, :, lanes] = collect(tn(ds, k_ref[w, :, lanes]), masks, ROWS) * SCALE
        return carry

    lax.fori_loop(0, count // batch, body, 0)
    fill_rows(held, p_ref[...], r_ref[...])
    xhat, scale = norm_parts(held[...].reshape(total, D))
    xn = (xhat * gain + vec[1:2]).astype(BF)
    dq_wide = dq_held[...].reshape(total, D)
    dv_wide = dvv_held[...].reshape(total, D)
    dq = dq_wide.astype(BF)
    dk = dk_held[...].reshape(total, D).astype(BF)
    dv = dv_wide.astype(BF)
    dn = nt(dq, wq_ref[...]) + nt(dk, wk_ref[...]) + nt(dv, wv_ref[...])
    dx = (dx1 + norm_back(dn, xhat, scale, gain)).reshape(shape)
    dp_ref[...] = dx[:, :PATCH].astype(BF)
    dr_ref[...] = dx[:, PATCH:LIVE]
    xt = xn.T
    dw_ref[0] += nn(xt, dq)
    dw_ref[1] += nn(xt, dk)
    dw_ref[2] += nn(xt, dv)
    mixed = o_ref[...].astype(F32).reshape(total, D).astype(BF)
    dw_ref[3] += nn(mixed.T, gb)
    dv_ref[0] += fold(dn * xhat)
    dv_ref[1] += fold(dn)
    dv_ref[2] += fold(dq_wide)
    dv_ref[3] += fold(dv_wide)
    dv_ref[4] += fold(dx1)


def attn_bwd(patches, region_rows, dx1_parts, saved, weights, vec, count=8, batch=4):
    windows = patches.shape[0]
    per = dx1_parts[0].shape[1]
    chunks = len(dx1_parts)
    many = count // (per * chunks)
    array = jax.ShapeDtypeStruct
    return pl.pallas_call(
        partial(attn_bwd_kernel, count, batch, chunks),
        grid=(windows // count,),
        in_specs=[block((count, PATCH, D)), block((count, 1, D))] + [block((many, per, ROWS, D))] * chunks
        + [block((count, ROWS, D))] * 4 + [block((count, 4, ROWS, STACK))] + [full((D, D))] * 4 + [full(vec.shape)],
        out_specs=[block((count, PATCH, D)), block((count, 1, D)), full((4, D, D)), full((5, 8, D))],
        out_shape=[array((windows, PATCH, D), BF), array((windows, 1, D), F32),
                   array((4, D, D), F32), array((5, 8, D), F32)],
        scratch_shapes=[pltpu.VMEM((count, ROWS, D), F32)] * 5,
        compiler_params=pltpu.CompilerParams(vmem_limit_bytes=VMEM),
        cost_estimate=pl.CostEstimate(flops=4 * 10**10, bytes_accessed=5 * 10**7, transcendentals=0),
        name="window_attention_backward",
    )(patches, region_rows, *dx1_parts, *saved, *weights, vec)


def halves(a):
    high = a.astype(BF)
    return high, (a - high.astype(F32)).astype(BF)


def product(a, b, passes, dot=nn):
    if passes == 1:
        return dot(a.astype(BF), b.astype(BF))
    (ah, al), (bh, bl) = halves(a), halves(b)
    return dot(ah, bh) + (dot(ah, bl) + dot(al, bh))


DIRECT_STEPS = (1, 1, 1, -1, -1)
GRAM_STEPS = (3, 3, 3, 3, -1)
NEAR_ZERO = NS_FIRST + NS_SECOND + NS_THIRD
NEAR_ONE = NS_SECOND + 2.0 * NS_THIRD


def identity():
    rows = lax.broadcasted_iota(jnp.int32, (D, D), 0)
    return rows == lax.broadcasted_iota(jnp.int32, (D, D), 1)


def polynomial(gram, eye, step):
    if step > 0:
        return NS_FIRST, NS_SECOND * gram + NS_THIRD * product(gram, gram, step)
    rest = gram - jnp.where(eye, 1.0, 0.0)
    return NEAR_ZERO, NEAR_ONE * rest + NS_THIRD * product(rest, rest, -step)


def moments_kernel(clip_ref, g1_ref, g2_ref, m1_ref, m2_ref, n1_ref, n2_ref, gram1_ref, gram2_ref):
    clip = clip_ref[0, 0]
    first = MUON_MOMENTUM * m1_ref[...] + clip * g1_ref[...].astype(F32)
    n1_ref[...] = first
    gram1_ref[...] = product(first, first, 3, nt)
    second = MUON_MOMENTUM * m2_ref[...] + clip * g2_ref[...].astype(F32).T
    n2_ref[...] = second
    gram2_ref[...] = product(second, second, 3, tn)


def square_kernel(clip_ref, g_ref, m_ref, w_ref, n_ref, new_ref):
    moment = MUON_MOMENTUM * m_ref[...] + clip_ref[0, 0] * g_ref[...].astype(F32)
    n_ref[...] = moment
    z = moment * (1.0 / (jnp.sqrt(jnp.sum(moment * moment)) + 1e-07))
    eye = identity()
    for step in DIRECT_STEPS:
        scale, poly = polynomial(product(z, z, abs(step), nt), eye, step)
        z = scale * z + product(poly, z, abs(step))
    new_ref[...] = w_ref[...] * DECAY_KEEP - MUON_RATE * z


def gram_steps(gram):
    eye = identity()
    factor = 1.0 / (jnp.sqrt(jnp.sum(jnp.where(eye, gram, 0.0))) + 1e-07)
    gram = gram * (factor * factor)
    steps = None
    for n, step in enumerate(GRAM_STEPS):
        scale, poly = polynomial(gram, eye, step)
        if steps is None:
            steps = jnp.where(eye, scale, 0.0) + poly
        else:
            steps = scale * steps + product(poly, steps, abs(step))
        if n < len(GRAM_STEPS) - 1:
            half = scale * gram + product(poly, gram, step)
            gram = scale * half + product(poly, half, step)
    return steps * factor


def sharded_kernel(gram1_ref, gram2_ref, n1_ref, n2_ref, w1_ref, w2_ref, new1_ref, new2_ref):
    z = product(gram_steps(gram1_ref[...]), n1_ref[...], 3)
    new1_ref[...] = w1_ref[...] * DECAY_KEEP - MUON_RATE * z
    z = product(n2_ref[...], gram_steps(gram2_ref[...]), 3)
    new2_ref[...] = w2_ref[...] * DECAY_KEEP - (MUON_RATE * max(1.0, FF / D) ** 0.5) * z


def whole_call(kernel, outs, name, *args):
    in_specs = [pl.BlockSpec(memory_space=pltpu.VMEM) for _ in args]
    if args[0].shape == (1, 1):
        in_specs[0] = pl.BlockSpec(memory_space=pltpu.SMEM)
    return pl.pallas_call(
        kernel,
        in_specs=in_specs,
        out_specs=[pl.BlockSpec(memory_space=pltpu.VMEM) for _ in outs],
        out_shape=[jax.ShapeDtypeStruct((D, D), dtype) for dtype in outs],
        compiler_params=pltpu.CompilerParams(vmem_limit_bytes=VMEM),
        cost_estimate=pl.CostEstimate(flops=10**10, bytes_accessed=10**7, transcendentals=0),
        name=name,
    )(*args)


def pair(values, bit):
    return lax.ppermute(values, "opt", [(i, i ^ bit) for i in range(OPT)])


def pieces_of_owners(own):
    mate = pair(own, 1)
    across = pair(own, 2)
    return [own, mate, across, pair(across, 1)]


def sum_at_owner(pieces):
    near = pair(jnp.stack([pieces[1], pieces[3]]), 1).astype(F32)
    far = (pieces[2].astype(F32) + near[1]).astype(BF)
    return pieces[0].astype(F32) + near[0] + pair(far, 2).astype(F32)


def share(x):
    copies = jnp.broadcast_to(x[None], (lax.axis_size("dp"),) + x.shape)
    return lax.all_to_all(copies, "dp", 0, 0, tiled=True)


def sum_over_dp(x):
    parts = x.reshape((lax.axis_size("dp"), -1) + x.shape[1:])
    parts = lax.all_to_all(parts, "dp", 0, 0, tiled=True)
    return share(jnp.sum(parts.astype(F32), axis=0).astype(BF)).reshape(x.shape)


def split_heads(x):
    return x.reshape(x.shape[0], HEADS, HEAD_DIM)


def regional_forward(queries, keys, values, same_image):
    scores = jnp.einsum("qhd,khd->hqk", split_heads(queries), split_heads(keys), preferred_element_type=F32)
    scores = jnp.where(same_image[None], scores * SCALE, MASKED)
    peak = jnp.max(scores, axis=-1, keepdims=True)
    raised = jnp.exp(scores - peak)
    sums = jnp.sum(raised, axis=-1, keepdims=True)
    low = (raised / sums).astype(BF)
    mixed = jnp.einsum("hqk,khd->qhd", low, split_heads(values), preferred_element_type=F32)
    return mixed.reshape(queries.shape), (peak + jnp.log(sums))[:, :, 0]


def regional_terms(queries, keys, values, grad_mixed, same_image, level, delta):
    scores = jnp.einsum("qhd,khd->hqk", split_heads(queries), split_heads(keys), preferred_element_type=F32)
    probs = jnp.where(same_image[None], jnp.exp(scores * SCALE - level[:, :, None]), 0.0)
    grads = jnp.einsum("qhd,khd->hqk", split_heads(grad_mixed), split_heads(values), preferred_element_type=F32)
    return probs.astype(BF), (probs * (grads - delta[:, :, None])).astype(BF)


def regional_backward(tokens, start, columns, same_rows, same_columns, weights, grads, level, delta):
    queries, keys, values = tokens
    grad_mixed = nt(grads, weights[3]).astype(BF)
    own = partial(columns, start=start)
    _, scores = regional_terms(own(queries), keys, values, own(grad_mixed), same_columns.T,
                               own(level.T).T, own(delta.T).T)
    dq = jnp.einsum("hqk,khd->qhd", scores, split_heads(keys), preferred_element_type=F32)
    probs, scores = regional_terms(queries, own(keys), own(values), grad_mixed, same_columns, level, delta)
    dk = jnp.einsum("hqk,qhd->khd", scores, split_heads(queries), preferred_element_type=F32)
    dv = jnp.einsum("hqk,qhd->khd", probs, split_heads(grad_mixed), preferred_element_type=F32)
    flat = lambda x: x.reshape(-1, D)
    return flat(dq) * SCALE, flat(dk) * SCALE, flat(dv)


def per_device(patches, regions, image_ids, attn_w, mlp_in, mlp_out, vec_params, patch_cot, region_cot,
               attn_mom, mlp_in_mom, mlp_out_mom, adam_first, adam_second):
    dp_size = lax.axis_size("dp")
    dp_index = lax.axis_index("dp")
    opt_index = lax.axis_index("opt")
    _, grid_rows, cols, _, _ = patch_cot.shape
    grid_cols = patches.shape[2]
    tokens = grid_rows * grid_cols
    chunks = 2 if cols % 2 == 0 else 1
    per = cols // chunks
    vec = vec_params
    order = opt_index ^ jnp.arange(OPT)

    attn_pieces = jnp.stack(pieces_of_owners(attn_w[0].astype(BF)))
    weights = [lax.dynamic_index_in_dim(attn_pieces, opt_index ^ j, 0, keepdims=False) for j in range(OPT)]
    canvas = share(regions[0]).transpose(1, 0, 2, 3).reshape(tokens, D)
    first = pieces_of_owners(mlp_in.astype(BF))
    second = pieces_of_owners(mlp_out.astype(BF))
    bias_first = jnp.take(vec[8:], order, axis=0)
    cots = []
    for c in range(chunks):
        part = slice(c * per, (c + 1) * per)
        moved = lax.all_to_all(patch_cot[0, :, part], "dp", 0, 0, tiled=True)
        moved_regions = lax.all_to_all(region_cot[0, :, part, None], "dp", 0, 0, tiled=True)
        cots.append((moved, moved_regions))

    def columns(x, start):
        wide = x.reshape((grid_rows, grid_cols) + x.shape[1:])
        return lax.dynamic_slice_in_dim(wide, start, cols, 1).reshape((grid_rows * cols,) + x.shape[1:])

    band = lambda x: lax.dynamic_slice_in_dim(x, dp_index * grid_cols, grid_cols, 0)
    start = dp_index * cols
    ids = image_ids[0].reshape(tokens)
    same_rows = band(ids)[:, None] == ids[None, :]
    same_columns = ids[:, None] == columns(ids, start)[None, :]
    canvas_hat, _ = norm_parts(canvas.astype(F32))
    canvas_low = (canvas_hat * vec[0] + vec[1]).astype(BF)
    reg_q = (nn(canvas_low, weights[0]) + vec[4]).astype(BF)
    reg_k = nn(canvas_low, weights[1]).astype(BF)
    reg_v = (nn(canvas_low, weights[2]) + vec[5]).astype(BF)
    reg_mixed, reg_level = regional_forward(band(reg_q), reg_k, reg_v, same_rows)
    reg_low = reg_mixed.astype(BF)
    region_rows = band(canvas).astype(F32) + nn(reg_low, weights[3]) + vec[6]
    region_rows = region_rows[:, None, :]
    level_all = share(reg_level.T).reshape(tokens, HEADS).T

    windows = patches.reshape(grid_cols, PATCH, D)
    x1, *saved = attn_fwd(windows, region_rows, weights, vec)
    x1 = x1.reshape(dp_size, chunks, per, ROWS, D)
    outs = [mlp(x1, c, *cots[c], first, second, vec, bias_first) for c in range(chunks)]
    moved = [lax.all_to_all(o[0], "dp", 0, 0, tiled=True) for o in outs]
    out_patches = jnp.concatenate(moved, axis=1)[None]
    moved = [lax.all_to_all(o[1], "dp", 0, 0, tiled=True) for o in outs]
    out_regions = jnp.concatenate(moved, axis=1)[None, :, :, 0]
    d_patches, d_region, d_attn, d_vec_attn = attn_bwd(windows, region_rows, [o[2] for o in outs], saved, weights, vec)
    d_patches = d_patches.reshape(patches.shape)

    add = lambda n, j: sum(o[n][j].astype(F32) for o in outs).astype(BF) if chunks > 1 else outs[0][n][j]
    own_first = sum_at_owner([add(3, j) for j in range(OPT)])
    own_second = sum_at_owner([add(4, j) for j in range(OPT)])
    own_mlp = sum_over_dp(jnp.concatenate([own_first, own_second], axis=1).astype(BF))

    grad_low = d_region[:, 0].astype(BF)
    mixed_grad = nt(grad_low, weights[3]).astype(BF).astype(F32)
    delta = jnp.sum(split_heads(mixed_grad * reg_mixed), axis=-1)
    grads_all = share(grad_low).reshape(tokens, D)
    delta_all = share(delta).reshape(tokens, HEADS).T
    dq, dk, dv = regional_backward((reg_q, reg_k, reg_v), start, columns, same_rows, same_columns,
                                   weights, grads_all, level_all, delta_all)
    dq_low, dk_low, dv_low = dq.astype(BF), dk.astype(BF), dv.astype(BF)
    d_normed = nt(dq_low, weights[0]) + nt(dk_low, weights[1]) + nt(dv_low, weights[2])
    own_hat, own_scale = norm_parts(columns(canvas, start).astype(F32))
    d_regions = columns(grads_all, start).astype(F32) + norm_back(d_normed, own_hat, own_scale, vec[0])
    d_regions = d_regions.reshape(regions.shape)
    own_low = columns(canvas_low, start)

    grad_attn = jnp.stack([
        (d_attn[0] + tn(own_low, dq_low)).astype(BF),
        (d_attn[1] + tn(own_low, dk_low)).astype(BF),
        (d_attn[2] + tn(own_low, dv_low)).astype(BF),
        (d_attn[3] + tn(reg_low, grad_low)).astype(BF),
    ])
    pieces = [lax.dynamic_index_in_dim(grad_attn, opt_index ^ j, 0, keepdims=False) for j in range(OPT)]
    own_attn = sum_over_dp(sum_at_owner(pieces).astype(BF))

    d_vec_attn = jnp.sum(d_vec_attn, axis=1)
    d_vec_mlp = sum(jnp.sum(o[5], axis=1) for o in outs)
    d_bias_first = jnp.take(sum(jnp.sum(o[6], axis=1) for o in outs), order, axis=0)
    sums = lambda x: jnp.sum(x, axis=0)
    grad_vec = jnp.concatenate([
        jnp.stack([
            d_vec_attn[0] + sums(d_normed * own_hat),
            d_vec_attn[1] + sums(d_normed),
            d_vec_mlp[0],
            d_vec_mlp[1],
            d_vec_attn[2] + sums(dq),
            d_vec_attn[3] + sums(dv),
            d_vec_attn[4] + sums(d_region[:, 0]),
            d_vec_mlp[2],
        ]),
        d_bias_first,
    ])
    grad_vec = grad_vec + pair(grad_vec, 1)
    grad_vec = grad_vec + pair(grad_vec, 2)
    grad_vec = jnp.sum(share(grad_vec), axis=0)

    squares = lambda x: jnp.sum(x.astype(F32) ** 2)
    total = jnp.full((8, 128), squares(own_attn) + squares(own_mlp))
    total = total + pair(total, 1)
    total = total + pair(total, 2)
    grad_norm = jnp.sqrt(total[0, 0] + squares(grad_vec))
    clip = jnp.minimum(1.0, CLIP_LIMIT / (grad_norm + 1e-06))
    clip_cell = clip.reshape(1, 1)
    first_mom, second_mom, gram_first, gram_second = whole_call(
        moments_kernel, [F32, F32, F32, F32], "mlp_moments", clip_cell,
        own_mlp[:, :D], own_mlp[:, D:], mlp_in_mom, mlp_out_mom)
    grams = jnp.stack([gram_first, gram_second])
    grams = grams + pair(grams, 1)
    grams = grams + pair(grams, 2)
    attn_mom_new, new_attn = whole_call(
        square_kernel, [F32, F32], "attention_update", clip_cell, own_attn, attn_mom[0], attn_w[0])
    new_first, new_second = whole_call(
        sharded_kernel, [F32, F32], "mlp_update", grams[0], grams[1], first_mom, second_mom, mlp_in, mlp_out)
    clipped = clip * grad_vec
    moment_one = BETA_FIRST * adam_first + (1.0 - BETA_FIRST) * clipped
    moment_two = BETA_SECOND * adam_second + (1.0 - BETA_SECOND) * clipped * clipped
    first_hat = moment_one / (1.0 - BETA_FIRST**OPT_STEP)
    second_hat = moment_two / (1.0 - BETA_SECOND**OPT_STEP)
    new_vec = vec_params - ADAM_RATE * first_hat / (jnp.sqrt(second_hat) + ADAM_EPS)
    return (out_patches, out_regions, d_patches, d_regions, new_attn[None], attn_mom_new[None], new_first, first_mom,
            new_second, second_mom, new_vec, moment_one, moment_two, grad_norm)


def solution(mesh):
    canvas = P("opt", None, "dp", None)
    wide = P("opt", None, "dp", None, None)
    bands = P("opt", "dp", None, None, None)
    square, right, down = P("opt", None, None), P(None, "opt"), P("opt", None)
    return jax.shard_map(
        per_device,
        mesh=mesh,
        in_specs=(bands, canvas, square, square, right, down, P(), wide, canvas, square, right, down, P(), P()),
        out_specs=(wide, canvas, bands, canvas, square, square, right, right, down, down, P(), P(), P(), P()),
        check_vma=False,
    )
```

time: 1170 us -> 633 us (0.54)
  matrix products: 454 us -> 30.6 us
  Pallas kernels: 0 us -> 210 us
  waiting for transfers between devices: 344 us -> 159 us
  blocking collectives: 141 us -> 0 us
  starting transfers between devices: 11.8 us -> 94.3 us
  local copies, waits for them, and re-layouts: 117 us -> 61.1 us
  between operations: 22.4 us -> 6.04 us
  other arithmetic: 72.8 us -> 61 us
    dot_general x85 -> x20, matrix products: 430 us -> 30.6 us  [the longest x4 8.35 us: tn(): lax.dot_general(a, b, (((0,), (0,)), ((), ())), preferred_element_type=F32)]
    pallas_call x0 -> x7, Pallas kernels: none -> 210 us  [the longest x2 81.3 us: mlp(): pl.pallas_call(partial(mlp_kernel, count, steps, cols), grid=(steps,), in...]
    psum x5 -> x0, waiting for transfers between devices: 150 us -> none  [sum_grams(): lax.psum(wide_gram.astype(jnp.bfloat16), 'opt').astype(jnp.float32)]
    psum x2 -> x0, blocking collectives: 141 us -> none  [the longest x1 129 us: per_device(): lax.psum((own_attn, own_first, own_second, grad_vec), 'dp')]
    all_to_all x2 -> x17, waiting for transfers between devices: 6.37 us -> 126 us  [the longest x7 47 us: share(): return lax.all_to_all(copies, 'dp', 0, 0, tiled=True)]
    all_gather x4 -> x0, waiting for transfers between devices: 91.2 us -> none  [the longest x1 69.2 us: per_device(): lax.all_gather(jnp.concatenate([reg_keys, reg_values], axis=-1), 'dp', ax...]
    reduce_scatter x3 -> x0, waiting for transfers between devices: 84.3 us -> none  [the longest x1 34.1 us: per_device(): lax.psum_scatter(d_w_first.astype(jnp.bfloat16), 'opt', scatter_dimension...]
    all_to_all x2 -> x17, starting transfers between devices: 10.1 us -> 82.3 us  [the longest x7 33.9 us: share(): return lax.all_to_all(copies, 'dp', 0, 0, tiled=True)]
  transfers between devices with their start and end apart: 15 -> 38, of which waited for: 12 -> 21; matrix products, arithmetic and copies ran while one was open for 27% -> 22% of each run, Pallas kernels for 0% -> 7%
where the time goes in v1:
time: 633 us; the launch traced here: 622 us
  Pallas kernels  210 us (33%)
  waiting for transfers between devices  159 us (25%)
  starting transfers between devices  94.3 us (15%)
  local copies, waits for them, and re-layouts  61.1 us (10%)
  other arithmetic  61 us (10%)
  matrix products  30.6 us (5%)
    pallas_call x2, Pallas kernels, mlp(): pl.pallas_call(partial(mlp_kernel, count, steps, cols), grid=(steps,), in...  81.3 us
    pallas_call x1, Pallas kernels, attn_bwd(): pl.pallas_call(partial(attn_bwd_kernel, count, batch, chunks), grid=(wind...  50 us
    all_to_all x7, waiting for transfers between devices, share(): return lax.all_to_all(copies, 'dp', 0, 0, tiled=True)  47 us
    pallas_call x3, Pallas kernels, whole_call(): pl.pallas_call(kernel, in_specs=in_specs, out_specs=[pl.BlockSpec(memory_...  46.9 us
    all_to_all x2, waiting for transfers between devices, per_device(): moved = [lax.all_to_all(o[0], 'dp', 0, 0, tiled=True) for o in outs]  43 us
    all_to_all x7, starting transfers between devices, share(): return lax.all_to_all(copies, 'dp', 0, 0, tiled=True)  33.9 us
    ppermute x21, waiting for transfers between devices, pair(): return lax.ppermute(values, 'opt', [(i, i ^ bit) for i in range(OPT)])  32.9 us
    pallas_call x1, Pallas kernels, attn_fwd(): pl.pallas_call(partial(attn_fwd_kernel, count, batch), grid=(windows // c...  31.6 us
  transfers between devices with their start and end apart: 38, of which 21 were waited for; matrix products, arithmetic and copies ran while one was open for 22% of the time, Pallas kernels for 7%

profile of v1, /device:TPU:0, one launch (start us, length us, event | category | flops | bytes accessed | tf_op | source)
XLA Modules:
  0.0 622.2 jit_solution(3292281036392774458)
XLA Ops:
  2.4 7.3 %all-to-all-start = ((bf16[8,8,8,512]{3,2,1,0:T(8,128)(2,1)}), bf16[8,8,8,512]{3,2,1,0:T(8,128)(2,1)S(1)}, u32[]{:S(2)}, u32[]{:S(2)}) async-start(bf16[8,8,8,512]{3,2,1,0:T(8,128)(2,1)} %broadcast_in_dim.68), calls=%async_computation | async-start | bytes 1048576 | tf_op jit(solution)/shard_map/all_to_all | solution.py:442
  13.8 9.5 %collective-permute-done.1 = bf16[512,512]{1,0:T(8,128)(2,1)S(1)} collective-permute-done((bf16[512,512]{1,0:T(8,128)(2,1)S(1)}, bf16[512,512]{1,0:T(8,128)(2,1)S(1)}, u32[]{:S(2)}, u32[]{:S(2)}) %collective-permute-start.1) | collective-permute-done | bytes 524320 | tf_op jit(solution)/shard_map/ppermute | solution.py:425
  24.2 4.8 all-to-all-start.5
  37.5 6.0 all-to-all-start.2
  44.2 6.0 all-to-all-done.2
  50.2 3.3 all-to-all-start.10
  53.5 5.8 slice_bitcast_fusion.1
  60.1 5.1 all-to-all-start.4
  70.6 5.5 copy.223
  79.4 3.0 collective-permute-done.4.w1c
  82.5 10.8 %collective-permute-done.7.w2c = bf16[512,512]{1,0:T(8,128)(2,1)} collective-permute-done((bf16[512,512]{1,0:T(8,128)(2,1)}, bf16[512,512]{1,0:T(8,128)(2,1)}, u32[]{:S(2)}, u32[]{:S(2)}) %collective-permute-start.7) | collective-permute-done | bytes 524320 | tf_op jit(solution)/shard_map/ppermute | solution.py:425
  104.5 6.3 %all-to-all-start.1 = ((bf16[8,4,49,512]{3,1,2,0:T(4,128)(2,1)}), bf16[8,4,49,512]{3,1,2,0:T(4,128)(2,1)S(1)}, u32[]{:S(2)}, u32[]{:S(2)}) async-start(bf16[8,4,49,512]{3,1,2,0:T(4,128)(2,1)} %get-tuple-element.174), calls=%async_computation.1 | async-start | bytes 3211264 | tf_op jit(solution)/shard_map/all_to_all | solution.py:509
  110.8 31.6 %window_attention_forward.1 = (f32[64,56,512]{2,1,0:T(8,128)}, bf16[64,56,512]{2,1,0:T(8,128)(2,1)}, bf16[64,56,512]{2,1,0:T(8,128)(2,1)}, bf16[64,56,512]{2,1,0...) custom-call(bf16[64,49,512]{2,1,0:T(8,128)(2,1)} %bitcast.239, ...), custom_call_target="tpu_custom_call" | custom-call | flops 30000001024 | bytes 30000000 | tf_op jit(solution)/shard_map/window_attention_forward/pallas_call | solution.py:156
  147.0 3.0 copy.175.pc_ref
  151.7 35.7 %mlp_forward_backward.3 = (bf16[8,4,49,512]{3,2,1,0:T(8,128)(2,1)}, bf16[8,4,1,512]{3,2,1,0:T(2,128)(2,1)}, f32[8,4,56,512]{3,2,1,0:T(8,128)}, bf16[4,512,512]{2...) custom-call(f32[8,2,4,56,512]{4,3,2,1,0:T(8,128)} %bitcast.309, ...), custom_call_target="tpu_custom_call" | custom-call | flops 40000000000 | bytes 30000000 | tf_op jit(solution)/shard_map/mlp_forward_backward/pallas_call | solution.py:233
  187.4 45.6 %mlp_forward_backward.2 = (bf16[8,4,49,512]{3,2,1,0:T(8,128)(2,1)}, bf16[8,4,1,512]{3,2,1,0:T(2,128)(2,1)}, f32[8,4,56,512]{3,2,1,0:T(8,128)}, bf16[4,512,512]{2...) custom-call(f32[8,2,4,56,512]{4,3,2,1,0:T(8,128)} %bitcast.310, ...), custom_call_target="tpu_custom_call" | custom-call | flops 40000000000 | bytes 30000000 | tf_op jit(solution)/shard_map/mlp_forward_backward/pallas_call | solution.py:233
  233.0 50.0 %window_attention_backward.1 = (bf16[64,49,512]{2,1,0:T(8,128)(2,1)}, f32[64,1,512]{2,1,0:T(1,128)}, f32[4,512,512]{2,1,0:T(8,128)}, f32[5,8,512]{2,1,0:T(8,128)}) custom-call(bf16[64,49,512]{2,1,0:T(8,128)(2,1)} %bitcast.240, f32[64,1,512]{2,1,0:T(1,128)} %broadcast_in_dim.119.r_ref.refs_1_, f32[8,4,56,512]{3,2,1,0:T(8,128)} %get-tuple-element.52.refs_2_, ...), custom_call_target="tpu_custom_call" | custom-call | flops 40000000000 | bytes 50000000 | tf_op jit(solution)/shard_map/window_attention_backward/pallas_call | solution.py:319
  286.0 6.0 all-to-all-start.11
  293.3 5.4 all-to-all-done.11
  299.6 4.7 all-to-all-start.9
  335.0 2.9 fusion.88
  348.6 6.0 all-to-all-start.8
  361.3 4.9 all-to-all-start.7
  373.6 5.5 all-to-all-start.16
  384.3 3.0 all-to-all-done.16
  387.3 3.6 all-to-all-start.12
  392.9 3.0 collective-permute-done.12
  398.6 4.2 all-to-all-done.12
  402.8 3.7 all-to-all-start.14
  406.6 24.7 %all-to-all-done.14 = bf16[8,64,1024]{2,1,0:T(8,128)(2,1)S(1)} async-done(((bf16[8,64,1024]{2,1,0:T(8,128)(2,1)}), bf16[8,64,1024]{2,1,0:T(8,128)(2,1)S(1)}, u32[]{:S(2)}, u32[]{:S(2)}) %all-to-all-start.14) | async-done | bytes 1048608 | tf_op jit(solution)/shard_map/all_to_all | solution.py:447
  432.1 3.5 all-to-all-start.13
  435.7 14.4 %all-to-all-done.13 = bf16[8,64,512]{2,1,0:T(8,128)(2,1)S(1)} async-done(((bf16[8,64,512]{2,1,0:T(8,128)(2,1)}), bf16[8,64,512]{2,1,0:T(8,128)(2,1)S(1)}, u32[]{:S(2)}, u32[]{:S(2)}) %all-to-all-start.13) | async-done | bytes 524320 | tf_op jit(solution)/shard_map/all_to_all | solution.py:442
  451.3 3.6 all-to-all-start.15
  454.9 3.5 copy.177
  458.4 22.5 %all-to-all-done.15 = bf16[8,64,1024]{2,1,0:T(8,128)(2,1)S(1)} async-done(((bf16[8,64,1024]{2,1,0:T(8,128)(2,1)}), bf16[8,64,1024]{2,1,0:T(8,128)(2,1)S(1)}, u32[]{:S(2)}, u32[]{:S(2)}) %all-to-all-start.15) | async-done | bytes 1048608 | tf_op jit(solution)/shard_map/all_to_all | solution.py:442
  480.9 3.8 all-to-all-start.6
  494.8 4.7 mlp_moments.1
  499.5 3.2 pad_maximum_fusion.2
  504.7 17.9 %all-to-all-done.6 = bf16[8,4,49,512]{3,1,2,0:T(4,128)(2,1)S(1)} async-done(((bf16[8,4,49,512]{3,1,2,0:T(4,128)(2,1)}), bf16[8,4,49,512]{3,1,2,0:T(4,128)(2,1)S(1)}, u32[]{:S(2)}, u32[]{:S(2)}) %all-to-all-start.6) | async-done | bytes 1605664 | tf_op jit(solution)/shard_map/all_to_all | solution.py:537
  522.6 4.3 all-to-all-start.3
  526.9 5.0 copy.197
  531.9 3.5 fusion.83
  539.1 25.1 %all-to-all-done.3 = bf16[8,4,49,512]{3,1,2,0:T(4,128)(2,1)} async-done(((bf16[8,4,49,512]{3,1,2,0:T(4,128)(2,1)}), bf16[8,4,49,512]{3,1,2,0:T(4,128)(2,1)}, u32[]{:S(2)}, u32[]{:S(2)}) %all-to-all-start.3) | async-done | bytes 1605664 | tf_op jit(solution)/shard_map/all_to_all | solution.py:537
  564.2 5.1 maximum_bitcast_fusion
  570.0 8.3 %attention_update.1 = (f32[512,512]{1,0:T(8,128)}, f32[512,512]{1,0:T(8,128)}) custom-call(f32[1,1]{1,0:T(1,128)} %bitcast.83.clip_ref, bf16[512,512]{1,0:T(8,128)(2,1)} %bitcast.248, f32[512,512]{1,0:T(8,128)} %bitcast.308, f32[512,512]{1,0:T(8,128)} %bitcast.266), custom_call_target="tpu_custom_call" | custom-call | flops 10000000000 | bytes 10000000 | tf_op jit(solution)/shard_map/attention_update/pallas_call | solution.py:413
  578.3 3.9 collective-permute-done.20
  582.3 3.0 fusion.128
  586.7 33.9 %mlp_update.1 = (f32[512,512]{1,0:T(8,128)}, f32[512,512]{1,0:T(8,128)}) custom-call(f32[512,512]{1,0:T(8,128)} %get-tuple-element.177.gram1_ref, f32[512,512]{1,0:T(8,128)} %get-tuple-element.176.gram2_ref, f32[512,512]{1,0:T(8,128)} %get-tuple-element.156.n1_ref, f32[512,512]{1,0:T(8,128)} %get-tuple-element.158.n2_ref, f32[512,512]{1,0:T(8,128)} %w1_ref.1, ...), custom_call_target="tpu_custom_call" | custom-call | flops 10000000000 | bytes 10000000 | tf_op jit(solution)/shard_map/mlp_update/pallas_call | solution.py:413
  (336 shorter events, 130.1 us)
Async XLA Ops:
  2.4 21.7 %all-to-all-start = ((bf16[8,8,8,512]{3,2,1,0:T(8,128)(2,1)}), bf16[8,8,8,512]{3,2,1,0:T(8,128)(2,1)S(1)}, u32[]{:S(2)}, u32[]{:S(2)}) async-start(bf16[8,8,8,512]{3,2,1,0:T(8,128)(2,1)} %broadcast_in_dim.68), calls=%async_computation | async-start | bytes 1048576 | tf_op jit(solution)/shard_map/all_to_all | solution.py:442
  9.8 13.4 %collective-permute-start.1 = (bf16[512,512]{1,0:T(8,128)(2,1)S(1)}, bf16[512,512]{1,0:T(8,128)(2,1)S(1)}, u32[]{:S(2)}, u32[]{:S(2)}) collective-permute-start(bf16[512,512]{1,0:T(8,128)(2,1)S(1)} %get-tuple-element.187), channel_id=1, source_target_pairs={{0,2},{1,3},{2,0},{3,1},{4,6},{5,7},{6,4},{7,5},{8,10},{9,11},{10,... | collective-permute-start | bytes 1572872 | tf_op jit(solution)/shard_map/ppermute | solution.py:425
  11.4 18.4 %collective-permute-start = (bf16[512,512]{1,0:T(8,128)(2,1)S(1)}, bf16[512,512]{1,0:T(8,128)(2,1)S(1)}, u32[]{:S(2)}, u32[]{:S(2)}) collective-permute-start(bf16[512,512]{1,0:T(8,128)(2,1)S(1)} %get-tuple-element.187), channel_id=1, source_target_pairs={{0,1},{1,0},{2,3},{3,2},{4,5},{5,4},{6,7},{7,6},{8,9},{9,8},{10,11... | collective-permute-start | bytes 1572872 | tf_op jit(solution)/shard_map/ppermute | solution.py:425
  23.2 6.5 %collective-permute-start.2 = (bf16[512,512]{1,0:T(8,128)(2,1)S(1)}, bf16[512,512]{1,0:T(8,128)(2,1)}, u32[]{:S(2)}, u32[]{:S(2)}) collective-permute-start(bf16[512,512]{1,0:T(8,128)(2,1)S(1)} %collective-permute-done.1), channel_id=1, source_target_pairs={{0,1},{1,0},{2,3},{3,2},{4,5},{5,4},{6,7},{7,6},{8,9},{9,8},{10,11... | collective-permute-start | bytes 1572872 | tf_op jit(solution)/shard_map/ppermute | solution.py:425
  24.2 13.3 %all-to-all-start.5 = ((bf16[8,4,1,512]{3,1,2,0:T(4,128)(2,1)}), bf16[8,4,1,512]{3,1,2,0:T(4,128)(2,1)S(1)}, u32[]{:S(2)}, u32[]{:S(2)}) async-start(bf16[8,4,1,512]{3,1,2,0:T(4,128)(2,1)} %copy.174), calls=%async_computation.5 | async-start | bytes 65536 | tf_op jit(solution)/shard_map/all_to_all | solution.py:510
  32.2 70.4 %copy-start.4 = (bf16[512,512]{1,0:T(8,128)(2,1)}, bf16[512,512]{1,0:T(8,128)(2,1)S(1)}, u32[]{:S(2)}) copy-start(bf16[512,512]{1,0:T(8,128)(2,1)S(1)} %get-tuple-element.180.wo_ref.refs_12_) | copy-start | bytes 1572868
  37.5 12.7 %all-to-all-start.2 = ((bf16[8,4,1,512]{3,1,2,0:T(4,128)(2,1)}), bf16[8,4,1,512]{3,1,2,0:T(4,128)(2,1)S(1)}, u32[]{:S(2)}, u32[]{:S(2)}) async-start(bf16[8,4,1,512]{3,1,2,0:T(4,128)(2,1)} %copy.169), calls=%async_computation.2 | async-start | bytes 65536 | tf_op jit(solution)/shard_map/all_to_all | solution.py:510
  50.2 10.0 %all-to-all-start.10 = ((f32[8,1,1024]{2,1,0:T(1,128)}), f32[8,1,1024]{2,1,0:T(1,128)S(1)}, u32[]{:S(2)}, u32[]{:S(2)}) async-start(f32[8,1,1024]{2,1,0:T(1,128)} %reshape.512), calls=%async_computation.10 | async-start | bytes 65536 | tf_op jit(solution)/shard_map/all_to_all | solution.py:442
  60.1 44.4 %all-to-all-start.4 = ((bf16[8,4,49,512]{3,1,2,0:T(4,128)(2,1)}), bf16[8,4,49,512]{3,1,2,0:T(4,128)(2,1)}, u32[]{:S(2)}, u32[]{:S(2)}) async-start(bf16[8,4,49,512]{3,1,2,0:T(4,128)(2,1)} %get-tuple-element.175), calls=%async_computation.4 | async-start | bytes 3211264 | tf_op jit(solution)/shard_map/all_to_all | solution.py:509
  67.4 84.2 %collective-permute-start.3 = (bf16[512,512]{1,0:T(8,128)(2,1)}, bf16[512,512]{1,0:T(8,128)(2,1)}, u32[]{:S(2)}, u32[]{:S(2)}) collective-permute-start(bf16[512,512]{1,0:T(8,128)(2,1)} %convert_element_type.325.w1a), channel_id=1, source_target_pairs={{0,1},{1,0},{2,3},{3,2},{4,5},{5,4},{6,7},{7,6},{8,9},{9,8},{10,11... | collective-permute-start | bytes 1572872 | tf_op jit(solution)/shard_map/ppermute | solution.py:425
  67.4 15.0 %collective-permute-start.4 = (bf16[512,512]{1,0:T(8,128)(2,1)}, bf16[512,512]{1,0:T(8,128)(2,1)}, u32[]{:S(2)}, u32[]{:S(2)}) collective-permute-start(bf16[512,512]{1,0:T(8,128)(2,1)} %convert_element_type.325.w1a), channel_id=1, source_target_pairs={{0,2},{1,3},{2,0},{3,1},{4,6},{5,7},{6,4},{7,5},{8,10},{9,11},{10,... | collective-permute-start | bytes 1572872 | tf_op jit(solution)/shard_map/ppermute | solution.py:425
  69.8 81.8 %collective-permute-start.6 = (bf16[512,512]{1,0:T(8,128)(2,1)}, bf16[512,512]{1,0:T(8,128)(2,1)}, u32[]{:S(2)}, u32[]{:S(2)}) collective-permute-start(bf16[512,512]{1,0:T(8,128)(2,1)} %convert_element_type.326.w2a), channel_id=1, source_target_pairs={{0,1},{1,0},{2,3},{3,2},{4,5},{5,4},{6,7},{7,6},{8,9},{9,8},{10,11... | collective-permute-start | bytes 1572872 | tf_op jit(solution)/shard_map/ppermute | solution.py:425
  70.1 23.3 %collective-permute-start.7 = (bf16[512,512]{1,0:T(8,128)(2,1)}, bf16[512,512]{1,0:T(8,128)(2,1)}, u32[]{:S(2)}, u32[]{:S(2)}) collective-permute-start(bf16[512,512]{1,0:T(8,128)(2,1)} %convert_element_type.326.w2a), channel_id=1, source_target_pairs={{0,2},{1,3},{2,0},{3,1},{4,6},{5,7},{6,4},{7,5},{8,10},{9,11},{10,... | collective-permute-start | bytes 1572872 | tf_op jit(solution)/shard_map/ppermute | solution.py:425
  76.1 23.9 %copy-start.60 = (s32[1024]{0:T(1024)}, s32[1024]{0:T(1024)S(1)}, u32[]{:S(2)}) copy-start(s32[1024]{0:T(1024)S(1)} %pad_clamp_fusion) | copy-start | bytes 12292
  82.5 69.2 %collective-permute-start.5 = (bf16[512,512]{1,0:T(8,128)(2,1)}, bf16[512,512]{1,0:T(8,128)(2,1)}, u32[]{:S(2)}, u32[]{:S(2)}) collective-permute-start(bf16[512,512]{1,0:T(8,128)(2,1)} %collective-permute-done.4.w1c), channel_id=1, source_target_pairs={{0,1},{1,0},{2,3},{3,2},{4,5},{5,4},{6,7},{7,6},{8,9},{9,8},{10,11... | collective-permute-start | bytes 1572872 | tf_op jit(solution)/shard_map/ppermute | solution.py:425
  93.3 58.3 %collective-permute-start.8 = (bf16[512,512]{1,0:T(8,128)(2,1)}, bf16[512,512]{1,0:T(8,128)(2,1)}, u32[]{:S(2)}, u32[]{:S(2)}) collective-permute-start(bf16[512,512]{1,0:T(8,128)(2,1)} %collective-permute-done.7.w2c), channel_id=1, source_target_pairs={{0,1},{1,0},{2,3},{3,2},{4,5},{5,4},{6,7},{7,6},{8,9},{9,8},{10,11... | collective-permute-start | bytes 1572872 | tf_op jit(solution)/shard_map/ppermute | solution.py:425
  104.5 45.5 %all-to-all-start.1 = ((bf16[8,4,49,512]{3,1,2,0:T(4,128)(2,1)}), bf16[8,4,49,512]{3,1,2,0:T(4,128)(2,1)S(1)}, u32[]{:S(2)}, u32[]{:S(2)}) async-start(bf16[8,4,49,512]{3,1,2,0:T(4,128)(2,1)} %get-tuple-element.174), calls=%async_computation.1 | async-start | bytes 3211264 | tf_op jit(solution)/shard_map/all_to_all | solution.py:509
  110.8 31.6 %copy-start.26 = (bf16[512,512]{1,0:T(8,128)(2,1)S(1)}, bf16[512,512]{1,0:T(8,128)(2,1)}, u32[]{:S(2)}) copy-start(bf16[512,512]{1,0:T(8,128)(2,1)} %copy-done.25) | copy-start | bytes 1572868
  110.8 33.1 %copy-start.33 = (f32[16,32,64]{2,1,0:T(8,128)S(1)}, f32[16,32,64]{2,1,0:T(8,128)}, u32[]{:S(2)}) copy-start(f32[16,32,64]{2,1,0:T(8,128)} %get-tuple-element.213) | copy-start | bytes 393220
  142.6 149.3 %copy-start.12 = (bf16[512,512]{0,1:T(8,128)(2,1)}, bf16[512,512]{0,1:T(8,128)(2,1)S(1)}, u32[]{:S(2)}) copy-start(bf16[512,512]{0,1:T(8,128)(2,1)S(1)} %copy.190) | copy-start | bytes 1572868
  233.0 51.8 %copy-start.5 = (bf16[512,512]{1,0:T(8,128)(2,1)S(1)}, bf16[512,512]{1,0:T(8,128)(2,1)}, u32[]{:S(2)}) copy-start(bf16[512,512]{1,0:T(8,128)(2,1)} %copy-done.4) | copy-start | bytes 1572868
  286.0 12.8 %all-to-all-start.11 = ((f32[8,1,1024]{2,1,0:T(1,128)}), f32[8,1,1024]{2,1,0:T(1,128)}, u32[]{:S(2)}, u32[]{:S(2)}) async-start(f32[8,1,1024]{2,1,0:T(1,128)} %reshape.514), calls=%async_computation.11 | async-start | bytes 65536 | tf_op jit(solution)/shard_map/all_to_all | solution.py:442
  299.6 20.9 %all-to-all-start.9 = ((bf16[8,64,512]{2,1,0:T(8,128)(2,1)}), bf16[8,64,512]{2,1,0:T(8,128)(2,1)}, u32[]{:S(2)}, u32[]{:S(2)}) async-start(bf16[8,64,512]{2,1,0:T(8,128)(2,1)} %broadcast_in_dim.121), calls=%async_computation.9 | async-start | bytes 1048576 | tf_op jit(solution)/shard_map/all_to_all | solution.py:442
  309.7 45.5 %collective-permute-start.13 = (bf16[2,512,512]{2,1,0:T(8,128)(2,1)}, bf16[2,512,512]{2,1,0:T(8,128)(2,1)}, u32[]{:S(2)}, u32[]{:S(2)}) collective-permute-start(bf16[2,512,512]{2,1,0:T(8,128)(2,1)} %pad_maximum_fusion.5), channel_id=1, source_target_pairs={{0,1},{1,0},{2,3},{3,2},{4,5},{5,4},{6,7},{7,6},{8,9},{9,8},{10,11... | collective-permute-start | bytes 3145736 | tf_op jit(solution)/shard_map/ppermute | solution.py:425
  312.4 57.1 %collective-permute-start.11 = (bf16[2,512,512]{2,1,0:T(8,128)(2,1)}, bf16[2,512,512]{2,1,0:T(8,128)(2,1)}, u32[]{:S(2)}, u32[]{:S(2)}) collective-permute-start(bf16[2,512,512]{2,1,0:T(8,128)(2,1)} %pad_maximum_fusion.4), channel_id=1, source_target_pairs={{0,1},{1,0},{2,3},{3,2},{4,5},{5,4},{6,7},{7,6},{8,9},{9,8},{10,11... | collective-permute-start | bytes 3145736 | tf_op jit(solution)/shard_map/ppermute | solution.py:425
  341.6 16.5 %collective-permute-start.9 = (bf16[2,512,512]{2,1,0:T(8,128)(2,1)}, bf16[2,512,512]{2,1,0:T(8,128)(2,1)S(1)}, u32[]{:S(2)}, u32[]{:S(2)}) collective-permute-start(bf16[2,512,512]{2,1,0:T(8,128)(2,1)} %pad_maximum_fusion.3), channel_id=1, source_target_pairs={{0,1},{1,0},{2,3},{3,2},{4,5},{5,4},{6,7},{7,6},{8,9},{9,8},{10,11... | collective-permute-start | bytes 3145736 | tf_op jit(solution)/shard_map/ppermute | solution.py:425
  345.1 1.4 collective-permute-start.17
  346.5 8.8 %collective-permute-start.18 = (f32[12,512]{1,0:T(8,128)S(1)}, f32[12,512]{1,0:T(8,128)S(1)}, u32[]{:S(2)}, u32[]{:S(2)}) collective-permute-start(f32[12,512]{1,0:T(8,128)S(1)} %add.334), channel_id=1, source_target_pairs={{0,2},{1,3},{2,0},{3,1},{4,6},{5,7},{6,4},{7,5},{8,10},{9,11},{10,... | collective-permute-start | bytes 73736 | tf_op jit(solution)/shard_map/ppermute | solution.py:425
  348.6 12.7 %all-to-all-start.8 = ((bf16[8,4,1,512]{3,1,2,0:T(4,128)(2,1)}), bf16[8,4,1,512]{3,1,2,0:T(4,128)(2,1)S(1)}, u32[]{:S(2)}, u32[]{:S(2)}) async-start(bf16[8,4,1,512]{3,1,2,0:T(4,128)(2,1)} %copy.179), calls=%async_computation.8 | async-start | bytes 65536 | tf_op jit(solution)/shard_map/all_to_all | solution.py:539
  359.6 22.5 %collective-permute-start.10 = (bf16[512,512]{1,0:T(8,128)(2,1)S(1)}, bf16[512,512]{1,0:T(8,128)(2,1)}, u32[]{:S(2)}, u32[]{:S(2)}) collective-permute-start(bf16[512,512]{1,0:T(8,128)(2,1)S(1)} %fusion.47), channel_id=1, source_target_pairs={{0,2},{1,3},{2,0},{3,1},{4,6},{5,7},{6,4},{7,5},{8,10},{9,11},{10,... | collective-permute-start | bytes 1572872 | tf_op jit(solution)/shard_map/ppermute | solution.py:425
  361.3 11.6 %all-to-all-start.7 = ((bf16[8,4,1,512]{3,1,2,0:T(4,128)(2,1)}), bf16[8,4,1,512]{3,1,2,0:T(4,128)(2,1)S(1)}, u32[]{:S(2)}, u32[]{:S(2)}) async-start(bf16[8,4,1,512]{3,1,2,0:T(4,128)(2,1)} %copy.178), calls=%async_computation.7 | async-start | bytes 65536 | tf_op jit(solution)/shard_map/all_to_all | solution.py:539
  367.9 23.0 %collective-permute-start.14 = (bf16[512,512]{1,0:T(8,128)(2,1)S(1)}, bf16[512,512]{1,0:T(8,128)(2,1)}, u32[]{:S(2)}, u32[]{:S(2)}) collective-permute-start(bf16[512,512]{1,0:T(8,128)(2,1)S(1)} %fusion.49), channel_id=1, source_target_pairs={{0,2},{1,3},{2,0},{3,1},{4,6},{5,7},{6,4},{7,5},{8,10},{9,11},{10,... | collective-permute-start | bytes 1572872 | tf_op jit(solution)/shard_map/ppermute | solution.py:425
  373.6 13.7 %all-to-all-start.16 = ((f32[8,12,512]{2,1,0:T(8,128)}), f32[8,12,512]{2,1,0:T(8,128)S(1)}, u32[]{:S(2)}, u32[]{:S(2)}) async-start(f32[8,12,512]{2,1,0:T(8,128)} %broadcast_in_dim.131), calls=%async_computation.16 | async-start | bytes 524288 | tf_op jit(solution)/shard_map/all_to_all | solution.py:442
  381.6 14.3 %collective-permute-start.12 = (bf16[512,512]{1,0:T(8,128)(2,1)}, bf16[512,512]{1,0:T(8,128)(2,1)}, u32[]{:S(2)}, u32[]{:S(2)}) collective-permute-start(bf16[512,512]{1,0:T(8,128)(2,1)} %fusion.48), channel_id=1, source_target_pairs={{0,2},{1,3},{2,0},{3,1},{4,6},{5,7},{6,4},{7,5},{8,10},{9,11},{10,... | collective-permute-start | bytes 1572872 | tf_op jit(solution)/shard_map/ppermute | solution.py:425
  387.3 15.5 %all-to-all-start.12 = ((bf16[8,64,512]{2,1,0:T(8,128)(2,1)}), bf16[8,64,512]{2,1,0:T(8,128)(2,1)S(1)}, u32[]{:S(2)}, u32[]{:S(2)}) async-start(bf16[8,64,512]{2,1,0:T(8,128)(2,1)} %bitcast.72), calls=%async_computation.12 | async-start | bytes 1048576 | tf_op jit(solution)/shard_map/all_to_all | solution.py:447
  402.8 28.4 %all-to-all-start.14 = ((bf16[8,64,1024]{2,1,0:T(8,128)(2,1)}), bf16[8,64,1024]{2,1,0:T(8,128)(2,1)S(1)}, u32[]{:S(2)}, u32[]{:S(2)}) async-start(bf16[8,64,1024]{2,1,0:T(8,128)(2,1)} %pad_maximum_fusion.6), calls=%async_computation.14 | async-start | bytes 2097152 | tf_op jit(solution)/shard_map/all_to_all | solution.py:447
  432.1 18.1 %all-to-all-start.13 = ((bf16[8,64,512]{2,1,0:T(8,128)(2,1)}), bf16[8,64,512]{2,1,0:T(8,128)(2,1)S(1)}, u32[]{:S(2)}, u32[]{:S(2)}) async-start(bf16[8,64,512]{2,1,0:T(8,128)(2,1)} %broadcast_in_dim.128), calls=%async_computation.13 | async-start | bytes 1048576 | tf_op jit(solution)/shard_map/all_to_all | solution.py:442
  450.1 34.6 %copy-start.15 = (bf16[8,64,512]{2,1,0:T(8,128)(2,1)}, bf16[8,64,512]{2,1,0:T(8,128)(2,1)S(1)}, u32[]{:S(2)}) copy-start(bf16[8,64,512]{2,1,0:T(8,128)(2,1)S(1)} %all-to-all-done.13) | copy-start | bytes 1572868
  451.3 29.6 %all-to-all-start.15 = ((bf16[8,64,1024]{2,1,0:T(8,128)(2,1)}), bf16[8,64,1024]{2,1,0:T(8,128)(2,1)S(1)}, u32[]{:S(2)}, u32[]{:S(2)}) async-start(bf16[8,64,1024]{2,1,0:T(8,128)(2,1)} %broadcast_in_dim.129), calls=%async_computation.15 | async-start | bytes 2097152 | tf_op jit(solution)/shard_map/all_to_all | solution.py:442
  480.9 41.7 %all-to-all-start.6 = ((bf16[8,4,49,512]{3,1,2,0:T(4,128)(2,1)}), bf16[8,4,49,512]{3,1,2,0:T(4,128)(2,1)S(1)}, u32[]{:S(2)}, u32[]{:S(2)}) async-start(bf16[8,4,49,512]{3,1,2,0:T(4,128)(2,1)} %copy.177), calls=%async_computation.6 | async-start | bytes 3211264 | tf_op jit(solution)/shard_map/all_to_all | solution.py:537
  488.1 1.2 collective-permute-start.15
  489.3 3.6 collective-permute-start.16
  502.7 29.2 %collective-permute-start.19 = (f32[2,512,512]{2,1,0:T(8,128)}, f32[2,512,512]{2,1,0:T(8,128)}, u32[]{:S(2)}, u32[]{:S(2)}) collective-permute-start(f32[2,512,512]{2,1,0:T(8,128)} %pad_maximum_fusion.2), channel_id=1, source_target_pairs={{0,1},{1,0},{2,3},{3,2},{4,5},{5,4},{6,7},{7,6},{8,9},{9,8},{10,11... | collective-permute-start | bytes 6291464 | tf_op jit(solution)/shard_map/ppermute | solution.py:425
  522.6 41.6 %all-to-all-start.3 = ((bf16[8,4,49,512]{3,1,2,0:T(4,128)(2,1)}), bf16[8,4,49,512]{3,1,2,0:T(4,128)(2,1)}, u32[]{:S(2)}, u32[]{:S(2)}) async-start(bf16[8,4,49,512]{3,1,2,0:T(4,128)(2,1)} %copy.172), calls=%async_computation.3 | async-start | bytes 3211264 | tf_op jit(solution)/shard_map/all_to_all | solution.py:537
  535.3 46.9 %collective-permute-start.20 = (f32[2,512,512]{2,1,0:T(8,128)}, f32[2,512,512]{2,1,0:T(8,128)}, u32[]{:S(2)}, u32[]{:S(2)}) collective-permute-start(f32[2,512,512]{2,1,0:T(8,128)} %fusion.83), channel_id=1, source_target_pairs={{0,2},{1,3},{2,0},{3,1},{4,6},{5,7},{6,4},{7,5},{8,10},{9,11},{10,... | collective-permute-start | bytes 6291464 | tf_op jit(solution)/shard_map/ppermute | solution.py:425
  539.1 30.3 %copy-start.28 = (f32[12,512]{1,0:T(8,128)S(1)}, f32[12,512]{1,0:T(8,128)}, u32[]{:S(2)}) copy-start(f32[12,512]{1,0:T(8,128)} %refs_13_.1) | copy-start | bytes 73732
  539.1 30.3 %copy-start.52 = (f32[12,512]{1,0:T(8,128)S(1)}, f32[12,512]{1,0:T(8,128)}, u32[]{:S(2)}) copy-start(f32[12,512]{1,0:T(8,128)} %param.28) | copy-start | bytes 73732
  539.1 30.3 %copy-start.53 = (f32[12,512]{1,0:T(8,128)S(1)}, f32[12,512]{1,0:T(8,128)}, u32[]{:S(2)}) copy-start(f32[12,512]{1,0:T(8,128)} %param.29) | copy-start | bytes 73732
  (58 other events, 290.6 us)

commit v2 on v1

v2 whole, which is shorter than its diff:
```python
from functools import partial

import jax
import jax.numpy as jnp
from jax import lax
from jax.experimental import pallas as pl
from jax.experimental.pallas import tpu as pltpu
from jax.sharding import PartitionSpec as P

BF = jnp.bfloat16
F32 = jnp.float32

D = 512
HEADS = 16
HEAD_DIM = 32
FF = 2048
PATCH = 49
LIVE = 50
ROWS = 56
GROUP = 128
STACK = 4 * ROWS
OPT_STEP = 10
OPT = 4

SCALE = HEAD_DIM ** (-0.5)
NORM_EPS = 1e-05
MASKED = -1e30
NS_FIRST = 3.4445
NS_SECOND = -4.775
NS_THIRD = 2.0315
MUON_RATE = 0.5
MUON_MOMENTUM = 0.5
MUON_DECAY = 0.01
ADAM_RATE = 0.5
BETA_FIRST = 0.9
BETA_SECOND = 0.95
ADAM_EPS = 1e-08
CLIP_LIMIT = 1.0
DECAY_KEEP = 1.0 - MUON_RATE * MUON_DECAY
VMEM = 60 * 2**20

ERF_P = 0.3275911 * 0.5**0.5
ERF = tuple(0.5 * c for c in (0.254829592, -0.284496736, 1.421413741, -1.453152027, 1.061405429))
INV_SQRT_2PI = 0.3989422804014327
LOG2E = 1.4426950408889634


def nn(a, b):
    return lax.dot_general(a, b, (((1,), (0,)), ((), ())), preferred_element_type=F32)


def nt(a, b):
    return lax.dot_general(a, b, (((1,), (1,)), ((), ())), preferred_element_type=F32)


def tn(a, b):
    return lax.dot_general(a, b, (((0,), (0,)), ((), ())), preferred_element_type=F32)


def full(shape):
    return pl.BlockSpec(shape, lambda i: (0,) * len(shape))


def block(shape):
    return pl.BlockSpec(shape, lambda i: (i,) + (0,) * (len(shape) - 1))


def norm_parts(x):
    centre = x - jnp.mean(x, axis=-1, keepdims=True)
    scale = lax.rsqrt(jnp.mean(centre * centre, axis=-1, keepdims=True) + NORM_EPS)
    return centre * scale, scale


def norm_back(grad, xhat, scale, gain):
    inner = grad * gain
    first = jnp.mean(inner, axis=-1, keepdims=True)
    second = jnp.mean(inner * xhat, axis=-1, keepdims=True)
    return scale * (inner - first - xhat * second)


def head_masks():
    lane = lax.broadcasted_iota(jnp.int32, (1, GROUP), 1) // HEAD_DIM
    return [lane == h for h in range(4)]


def spread(rows, masks):
    return jnp.concatenate([jnp.where(m, rows, 0.0) for m in masks], axis=0).astype(BF)


def collect(stacked, masks, rows):
    out = stacked[:rows]
    for h in range(1, 4):
        out = jnp.where(masks[h], stacked[h * rows : (h + 1) * rows], out)
    return out


def lane_groups(x):
    return [x[:, GROUP * g : GROUP * (g + 1)] for g in range(4)]


def hold(ref, total, x):
    for g, part in enumerate(lane_groups(x)):
        ref[g, :total] = part


def held_rows(ref, total):
    return jnp.concatenate([ref[g, :total] for g in range(4)], axis=1)


def fold(x):
    return jnp.sum(x.reshape(x.shape[0] // 8, 8, x.shape[1]), axis=0)


def gelu_parts(a):
    bell = jnp.exp2(a * a * (-0.5 * LOG2E))
    t = 1.0 / (1.0 + ERF_P * jnp.abs(a))
    tail = ((((ERF[4] * t + ERF[3]) * t + ERF[2]) * t + ERF[1]) * t + ERF[0]) * t * bell
    share = jnp.where(a < 0, tail, 1.0 - tail)
    return a * share, share + a * bell * INV_SQRT_2PI


def attn_fwd_kernel(count, batch, p_ref, r_ref, wq_ref, wk_ref, wv_ref, wo_ref, vec_ref,
                    x1_ref, q_ref, k_ref, v_ref, o_ref, pt_ref, q_held, k_held, v_held, o_held):
    total = count * LIVE

    @pl.when(pl.program_id(0) == 0)
    def _():
        for ref in (q_held, k_held, v_held):
            ref[:, total:] = jnp.zeros((4, count * (ROWS - LIVE), GROUP), F32)

    x = jnp.concatenate([p_ref[...].astype(F32), r_ref[...][None]], axis=0).reshape(total, D)
    vec = vec_ref[...]
    xhat, _ = norm_parts(x)
    xn = (xhat * vec[0:1] + vec[1:2]).astype(BF)
    hold(q_held, total, nn(xn, wq_ref[...]) + vec[4:5])
    hold(k_held, total, nn(xn, wk_ref[...]))
    hold(v_held, total, nn(xn, wv_ref[...]) + vec[5:6])
    masks = head_masks()
    live = lax.broadcasted_iota(jnp.int32, (ROWS, 1), 0) < LIVE

    def body(step, carry):
        units = [(step * batch + w, g) for w in range(batch) for g in range(4)]
        scores, probs = [], []
        for w, g in units:
            lanes = slice(GROUP * g, GROUP * (g + 1))
            rows = pl.ds(w, ROWS, stride=count)
            q = q_held[g, rows, :]
            q_ref[w, :, lanes] = q.astype(BF)
            k = k_held[g, rows, :].astype(BF)
            k_ref[w, :, lanes] = k
            scores.append(nt(k, spread(q, masks)))
        for (w, g), s in zip(units, scores):
            s = jnp.where(live, s, MASKED)
            e = jnp.exp((s - jnp.max(s, axis=0, keepdims=True)) * SCALE)
            p = (e * (1.0 / jnp.sum(e, axis=0, keepdims=True))).astype(BF)
            pt_ref[w, g] = p
            probs.append(p)
        for (w, g), p in zip(units, probs):
            lanes = slice(GROUP * g, GROUP * (g + 1))
            rows = pl.ds(w, ROWS, stride=count)
            v = v_held[g, rows, :].astype(BF)
            v_ref[w, :, lanes] = v
            o_held[g, rows, :] = collect(tn(p, v), masks, ROWS)
        return carry

    lax.fori_loop(0, count // batch, body, 0)
    mixed = held_rows(o_held, total).astype(BF)
    o_ref[...] = mixed.reshape(LIVE, count, D)
    x1_ref[...] = (x + nn(mixed, wo_ref[...]) + vec[6:7]).reshape(LIVE, count, D)


def middle(rows, count):
    return pl.BlockSpec((rows, count, D), lambda i: (0, i, 0))


def attn_fwd(patches, region_rows, weights, vec, count=16, batch=4):
    windows = patches.shape[1]
    array = jax.ShapeDtypeStruct
    return pl.pallas_call(
        partial(attn_fwd_kernel, count, batch),
        grid=(windows // count,),
        in_specs=[middle(PATCH, count), block((count, D))] + [full((D, D))] * 4 + [full(vec.shape)],
        out_specs=[middle(LIVE, count)] + [block((count, ROWS, D))] * 3
        + [middle(LIVE, count), block((count, 4, ROWS, STACK))],
        out_shape=[array((LIVE, windows, D), F32)] + [array((windows, ROWS, D), BF)] * 3
        + [array((LIVE, windows, D), BF), array((windows, 4, ROWS, STACK), BF)],
        scratch_shapes=[pltpu.VMEM((4, count * ROWS, GROUP), F32)] * 4,
        compiler_params=pltpu.CompilerParams(vmem_limit_bytes=VMEM),
        cost_estimate=pl.CostEstimate(flops=3 * 10**10, bytes_accessed=3 * 10**7, transcendentals=0),
        name="window_attention_forward",
    )(patches, region_rows, *weights, vec)


def mlp_kernel(many, sources, cols, steps, lanes, x1_ref, pc_ref, w1a, w1b, w1c, w1d, w2a, w2b, w2c, w2d,
               vec_ref, b1_ref, op_ref, dx1_ref, dw1_ref, dw2_ref, dv_ref, db1_ref, acc1, acc2):
    total = many * sources * cols
    step = pl.program_id(0)

    @pl.when(step == 0)
    def _():
        for ref in (acc1, acc2, dv_ref, db1_ref):
            ref[...] = jnp.zeros_like(ref)

    vec = vec_ref[...]
    gain = vec[2:3]
    x1 = x1_ref[...].reshape(total, D)
    xhat, scale = norm_parts(x1)
    h = (xhat * gain + vec[3:4]).astype(BF)
    for s in range(sources):
        dx1_ref[:, s * cols : (s + 1) * cols] = pc_ref[s].astype(F32)
    dy = dx1_ref[...].reshape(total, D)
    dm = dy.astype(BF)
    ht = h.T
    dmt = dm.T
    w1s, w2s = (w1a, w1b, w1c, w1d), (w2a, w2b, w2c, w2d)
    y = x1 + vec[7:8]
    dh = jnp.zeros((total, D), F32)
    parts = [(j, slice(c, c + lanes)) for j in range(4) for c in range(0, D, lanes)]

    def activate(j, s):
        u, slope = gelu_parts(nn(h, w1s[j][:, s]) + b1_ref[j : j + 1, s])
        da = slope * nt(dm, w2s[j][s, :])
        db1_ref[j, :, s] += fold(da)
        return u.astype(BF), da.astype(BF)

    def apply(j, s, u, da):
        acc1[j, :, s] += nn(ht, da)
        acc2[j, :, s] += nn(dmt, u)
        return nn(u, w2s[j][s, :]), nt(da, w1s[j][:, s])

    held_pair = activate(*parts[0])
    for n in range(1, len(parts) + 1):
        later = activate(*parts[n]) if n < len(parts) else None
        up, down = apply(*parts[n - 1], *held_pair)
        y, dh = y + up, dh + down
        held_pair = later
    y = y.reshape(many, sources * cols, D)
    for s in range(sources):
        op_ref[s] = y[:, s * cols : (s + 1) * cols].astype(BF)
    dy = dx1_ref[...].reshape(total, D)
    dx1_ref[...] = (dy + norm_back(dh, xhat, scale, gain)).reshape(dx1_ref.shape)
    dv_ref[0] += fold(dh * xhat)
    dv_ref[1] += fold(dh)
    dv_ref[2] += fold(dy)

    @pl.when(step == steps - 1)
    def _():
        dw1_ref[...] = acc1[...].astype(BF)
        dw2_ref[...] = acc2[...].astype(BF)


def mlp(x1, first_position, cot, first, second, vec, bias_first, many=10, lanes=256):
    sources, positions, cols, _ = cot.shape
    windows = x1.shape[1]
    steps = positions // many
    skip = first_position // many
    some = pl.BlockSpec((sources, many, cols, D), lambda i: (0, i, 0, 0))
    array = jax.ShapeDtypeStruct
    return pl.pallas_call(
        partial(mlp_kernel, many, sources, cols, steps, lanes),
        grid=(steps,),
        in_specs=[pl.BlockSpec((many, windows, D), lambda i: (i + skip, 0, 0)), some]
        + [full((D, D))] * 8 + [full(vec.shape), full((4, D))],
        out_specs=[some, block((many, windows, D)), full((4, D, D)), full((4, D, D)), full((3, 8, D)), full((4, 8, D))],
        out_shape=[array(cot.shape, BF), array((positions, windows, D), F32), array((4, D, D), BF),
                   array((4, D, D), BF), array((3, 8, D), F32), array((4, 8, D), F32)],
        scratch_shapes=[pltpu.VMEM((4, D, D), F32), pltpu.VMEM((4, D, D), F32)],
        compiler_params=pltpu.CompilerParams(vmem_limit_bytes=VMEM),
        cost_estimate=pl.CostEstimate(flops=4 * 10**10, bytes_accessed=3 * 10**7, transcendentals=0),
        name="mlp_forward_backward",
    )(x1, cot, *first, *second, vec, bias_first)


def attn_bwd_kernel(count, batch, chunks, *refs):
    p_ref, r_ref = refs[:2]
    dx1_refs = refs[2 : 2 + chunks]
    (q_ref, k_ref, v_ref, o_ref, pt_ref, wq_ref, wk_ref, wv_ref, wo_ref, vec_ref,
     dp_ref, dr_ref, dw_ref, dv_ref, dq_held, dk_held, dvv_held, do_held) = refs[2 + chunks :]
    total = count * LIVE

    @pl.when(pl.program_id(0) == 0)
    def _():
        dw_ref[...] = jnp.zeros_like(dw_ref)
        dv_ref[...] = jnp.zeros_like(dv_ref)
        do_held[:, total:] = jnp.zeros((4, count * (ROWS - LIVE), GROUP), F32)

    vec = vec_ref[...]
    gain = vec[0:1]
    dx1 = jnp.concatenate([ref[...] for ref in dx1_refs], axis=0).reshape(total, D)
    gb = dx1.astype(BF)
    hold(do_held, total, nt(gb, wo_ref[...]))
    masks = head_masks()

    def body(step, carry):
        units = [(step * batch + w, g) for w in range(batch) for g in range(4)]
        grads, scores = [], []
        for w, g in units:
            lanes = slice(GROUP * g, GROUP * (g + 1))
            rows = pl.ds(w, ROWS, stride=count)
            do_wide = spread(do_held[g, rows, :], masks)
            dvv_held[g, rows, :] = nn(pt_ref[w, g], do_wide)
            grads.append(nt(v_ref[w, :, lanes], do_wide))
        for (w, g), grad in zip(units, grads):
            p = pt_ref[w, g].astype(F32)
            both = p * grad
            scores.append((both - p * jnp.sum(both, axis=0, keepdims=True)).astype(BF))
        for (w, g), ds in zip(units, scores):
            lanes = slice(GROUP * g, GROUP * (g + 1))
            rows = pl.ds(w, ROWS, stride=count)
            dk_held[g, rows, :] = nn(ds, spread(q_ref[w, :, lanes].astype(F32), masks)) * SCALE
            dq_held[g, rows, :] = collect(tn(ds, k_ref[w, :, lanes]), masks, ROWS) * SCALE
        return carry

    lax.fori_loop(0, count // batch, body, 0)
    x = jnp.concatenate([p_ref[...].astype(F32), r_ref[...][None]], axis=0).reshape(total, D)
    xhat, scale = norm_parts(x)
    xn = (xhat * gain + vec[1:2]).astype(BF)
    dq_wide = held_rows(dq_held, total)
    dv_wide = held_rows(dvv_held, total)
    dq = dq_wide.astype(BF)
    dk = held_rows(dk_held, total).astype(BF)
    dv = dv_wide.astype(BF)
    dn = nt(dq, wq_ref[...]) + nt(dk, wk_ref[...]) + nt(dv, wv_ref[...])
    dx = (dx1 + norm_back(dn, xhat, scale, gain)).reshape(LIVE, count, D)
    dp_ref[...] = dx[:PATCH].astype(BF)
    dr_ref[...] = dx[PATCH]
    xt = xn.T
    dw_ref[0] += nn(xt, dq)
    dw_ref[1] += nn(xt, dk)
    dw_ref[2] += nn(xt, dv)
    dw_ref[3] += nn(o_ref[...].reshape(total, D).T, gb)
    dv_ref[0] += fold(dn * xhat)
    dv_ref[1] += fold(dn)
    dv_ref[2] += fold(dq_wide)
    dv_ref[3] += fold(dv_wide)
    dv_ref[4] += fold(dx1)


def attn_bwd(patches, region_rows, dx1_parts, saved, weights, vec, count=16, batch=4):
    windows = patches.shape[1]
    array = jax.ShapeDtypeStruct
    return pl.pallas_call(
        partial(attn_bwd_kernel, count, batch, len(dx1_parts)),
        grid=(windows // count,),
        in_specs=[middle(PATCH, count), block((count, D))] + [middle(part.shape[0], count) for part in dx1_parts]
        + [block((count, ROWS, D))] * 3 + [middle(LIVE, count), block((count, 4, ROWS, STACK))]
        + [full((D, D))] * 4 + [full(vec.shape)],
        out_specs=[middle(PATCH, count), block((count, D)), full((4, D, D)), full((5, 8, D))],
        out_shape=[array((PATCH, windows, D), BF), array((windows, D), F32),
                   array((4, D, D), F32), array((5, 8, D), F32)],
        scratch_shapes=[pltpu.VMEM((4, count * ROWS, GROUP), F32)] * 4,
        compiler_params=pltpu.CompilerParams(vmem_limit_bytes=VMEM),
        cost_estimate=pl.CostEstimate(flops=4 * 10**10, bytes_accessed=5 * 10**7, transcendentals=0),
        name="window_attention_backward",
    )(patches, region_rows, *dx1_parts, *saved, *weights, vec)


def regional_fwd_kernel(canvas_ref, band_ref, ids_ref, band_ids_ref, wq_ref, wk_ref, wv_ref, wo_ref, vec_ref,
                        r1_ref, mixed_ref, level_ref, q_ref, k_ref, v_ref):
    vec = vec_ref[...]
    xhat, _ = norm_parts(canvas_ref[...].astype(F32))
    low = (xhat * vec[0:1] + vec[1:2]).astype(BF)
    q_ref[...] = (nn(low, wq_ref[...]) + vec[4:5]).astype(BF)
    k_ref[...] = nn(low, wk_ref[...]).astype(BF)
    v_ref[...] = (nn(low, wv_ref[...]) + vec[5:6]).astype(BF)
    band = band_ref[...].astype(F32)
    rows = band.shape[0]
    xhat, _ = norm_parts(band)
    q = nn((xhat * vec[0:1] + vec[1:2]).astype(BF), wq_ref[...]) + vec[4:5]
    masks = head_masks()
    same = ids_ref[...] == band_ids_ref[...]
    scores, probs = [], []
    for g in range(4):
        lanes = slice(GROUP * g, GROUP * (g + 1))
        scores.append(nt(k_ref[:, lanes], spread(q[:, lanes], masks)))
    for g, s in enumerate(scores):
        s = jnp.where(same, s, MASKED)
        peak = jnp.max(s, axis=0, keepdims=True)
        e = jnp.exp((s - peak) * SCALE)
        sums = jnp.sum(e, axis=0, keepdims=True)
        level_ref[g : g + 1] = peak * SCALE + jnp.log(sums)
        probs.append((e * (1.0 / sums)).astype(BF))
    for g, p in enumerate(probs):
        lanes = slice(GROUP * g, GROUP * (g + 1))
        mixed_ref[:, lanes] = collect(tn(p, v_ref[:, lanes]), masks, rows)
    r1_ref[...] = band + nn(mixed_ref[...].astype(BF), wo_ref[...]) + vec[6:7]


def in_vmem(kernel, outs, name, *args):
    return pl.pallas_call(
        kernel,
        in_specs=[pl.BlockSpec(memory_space=pltpu.VMEM) for _ in args],
        out_specs=[pl.BlockSpec(memory_space=pltpu.VMEM) for _ in outs],
        out_shape=[jax.ShapeDtypeStruct(*out) for out in outs],
        compiler_params=pltpu.CompilerParams(vmem_limit_bytes=VMEM),
        cost_estimate=pl.CostEstimate(flops=10**10, bytes_accessed=10**7, transcendentals=0),
        name=name,
    )(*args)


def payload_kernel(dr_ref, mixed_ref, level_ref, wo_ref, grad_ref, extra_ref):
    low = dr_ref[...].astype(BF)
    grad_ref[...] = low
    both = nt(low, wo_ref[...]).astype(BF).astype(F32) * mixed_ref[...]
    head = lax.broadcasted_iota(jnp.int32, (D, GROUP), 0) // HEAD_DIM
    lane = lax.broadcasted_iota(jnp.int32, (D, GROUP), 1)
    pick = ((head == lane) | (head + HEADS == lane)).astype(BF)
    high, low_part = halves(both)
    rest = (both - high.astype(F32) - low_part.astype(F32)).astype(BF)
    delta = nn(high, pick) + (nn(low_part, pick) + nn(rest, pick))
    top = delta.astype(BF).astype(F32)
    lane = lax.broadcasted_iota(jnp.int32, (1, GROUP), 1)
    extra = jnp.where(lane < HEADS, top, jnp.where(lane < 2 * HEADS, delta - top, level_ref[...]))
    extra_ref[...] = extra.astype(BF)


def regional_bwd_kernel(own_rows, q_ref, k_ref, v_ref, grads_ref, qo_ref, ko_ref, vo_ref, own_ref, ids_ref, ids_row_ref,
                        ids_own_ref, ids_own_row_ref, level_ref, delta_ref, level_own_ref, delta_own_ref,
                        grads_own_ref, mixed_ref, band_grad_ref, dw_ref, wq_ref, wk_ref, wv_ref, wo_ref, vec_ref,
                        dr_ref, gw_ref, gv_ref):
    vec = vec_ref[...]
    masks = head_masks()
    do = nt(grads_ref[...], wo_ref[...]).astype(BF).astype(F32)
    do_own = nt(grads_own_ref[...], wo_ref[...]).astype(BF).astype(F32)
    same_own = ids_ref[...] == ids_own_row_ref[...]
    same = ids_own_ref[...] == ids_row_ref[...]
    lanes = [slice(GROUP * g, GROUP * (g + 1)) for g in range(4)]
    first, second = [], []
    dqs, dks, dvs = [], [], []
    for g in range(4):
        q_wide = spread(qo_ref[:, lanes[g]].astype(F32), masks)
        do_wide = spread(do_own[:, lanes[g]], masks)
        first.append((nt(k_ref[:, lanes[g]], q_wide), nt(v_ref[:, lanes[g]], do_wide)))
        q_wide = spread(q_ref[:, lanes[g]].astype(F32), masks)
        do_wide = spread(do[:, lanes[g]], masks)
        second.append((nt(ko_ref[:, lanes[g]], q_wide), nt(vo_ref[:, lanes[g]], do_wide), q_wide, do_wide))
    for g in range(4):
        s, dp = first[g]
        p = jnp.where(same_own, jnp.exp(s * SCALE - level_own_ref[g : g + 1]), 0.0)
        ds = (p * (dp - delta_own_ref[g : g + 1])).astype(BF)
        dqs.append(collect(tn(ds, k_ref[:, lanes[g]]), masks, own_rows) * SCALE)
        s, dp, q_wide, do_wide = second[g]
        p = jnp.where(same, jnp.exp(s * SCALE - level_ref[g : g + 1]), 0.0)
        ds = (p * (dp - delta_ref[g : g + 1])).astype(BF)
        dvs.append(nn(p.astype(BF), do_wide))
        dks.append(nn(ds, q_wide) * SCALE)
    xhat, scale = norm_parts(own_ref[...].astype(F32))
    low = (xhat * vec[0:1] + vec[1:2]).astype(BF)
    dq_wide, dk_wide, dv_wide = (jnp.concatenate(x, axis=1) for x in (dqs, dks, dvs))
    dq, dk, dv = dq_wide.astype(BF), dk_wide.astype(BF), dv_wide.astype(BF)
    dn = nt(dq, wq_ref[...]) + nt(dk, wk_ref[...]) + nt(dv, wv_ref[...])
    dr_ref[...] = grads_own_ref[...].astype(F32) + norm_back(dn, xhat, scale, vec[0:1])
    gw_ref[0] = (dw_ref[0] + tn(low, dq)).astype(BF)
    gw_ref[1] = (dw_ref[1] + tn(low, dk)).astype(BF)
    gw_ref[2] = (dw_ref[2] + tn(low, dv)).astype(BF)
    gw_ref[3] = (dw_ref[3] + tn(mixed_ref[...].astype(BF), band_grad_ref[...])).astype(BF)
    gv_ref[0] = fold(dn * xhat)
    gv_ref[1] = fold(dn)
    gv_ref[2] = fold(dq_wide)
    gv_ref[3] = fold(dv_wide)
    gv_ref[4] = fold(band_grad_ref[...].astype(F32))


def halves(a):
    high = a.astype(BF)
    return high, (a - high.astype(F32)).astype(BF)


def product(a, b, passes, dot=nn):
    if passes == 1:
        return dot(a.astype(BF), b.astype(BF))
    (ah, al), (bh, bl) = halves(a), halves(b)
    return dot(ah, bh) + (dot(ah, bl) + dot(al, bh))


DIRECT_STEPS = (1, 1, 1, -1, -1)
GRAM_STEPS = (3, 3, 3, 3, -1)
NEAR_ZERO = NS_FIRST + NS_SECOND + NS_THIRD
NEAR_ONE = NS_SECOND + 2.0 * NS_THIRD


def identity():
    rows = lax.broadcasted_iota(jnp.int32, (D, D), 0)
    return rows == lax.broadcasted_iota(jnp.int32, (D, D), 1)


def polynomial(gram, eye, step):
    if step > 0:
        return NS_FIRST, NS_SECOND * gram + NS_THIRD * product(gram, gram, step)
    rest = gram - jnp.where(eye, 1.0, 0.0)
    return NEAR_ZERO, NEAR_ONE * rest + NS_THIRD * product(rest, rest, -step)


def moments_kernel(clip_ref, g1_ref, g2_ref, m1_ref, m2_ref, n1_ref, n2_ref, gram1_ref, gram2_ref):
    clip = clip_ref[0, 0]
    first = MUON_MOMENTUM * m1_ref[...] + clip * g1_ref[...].astype(F32)
    n1_ref[...] = first
    gram1_ref[...] = product(first, first, 3, nt)
    second = MUON_MOMENTUM * m2_ref[...] + clip * g2_ref[...].astype(F32).T
    n2_ref[...] = second
    gram2_ref[...] = product(second, second, 3, tn)


def square_kernel(clip_ref, g_ref, m_ref, w_ref, n_ref, new_ref):
    moment = MUON_MOMENTUM * m_ref[...] + clip_ref[0, 0] * g_ref[...].astype(F32)
    n_ref[...] = moment
    z = moment * (1.0 / (jnp.sqrt(jnp.sum(moment * moment)) + 1e-07))
    eye = identity()
    for step in DIRECT_STEPS:
        scale, poly = polynomial(product(z, z, abs(step), nt), eye, step)
        z = scale * z + product(poly, z, abs(step))
    new_ref[...] = w_ref[...] * DECAY_KEEP - MUON_RATE * z


def gram_steps(gram):
    eye = identity()
    factor = 1.0 / (jnp.sqrt(jnp.sum(jnp.where(eye, gram, 0.0))) + 1e-07)
    gram = gram * (factor * factor)
    steps = None
    for n, step in enumerate(GRAM_STEPS):
        scale, poly = polynomial(gram, eye, step)
        if steps is None:
            steps = jnp.where(eye, scale, 0.0) + poly
        else:
            steps = scale * steps + product(poly, steps, abs(step))
        if n < len(GRAM_STEPS) - 1:
            half = scale * gram + product(poly, gram, step)
            gram = scale * half + product(poly, half, step)
    return steps * factor


def sharded_kernel(gram1_ref, gram2_ref, n1_ref, n2_ref, w1_ref, w2_ref, new1_ref, new2_ref):
    z = product(gram_steps(gram1_ref[...]), n1_ref[...], 3)
    new1_ref[...] = w1_ref[...] * DECAY_KEEP - MUON_RATE * z
    z = product(n2_ref[...], gram_steps(gram2_ref[...]), 3)
    new2_ref[...] = w2_ref[...] * DECAY_KEEP - (MUON_RATE * max(1.0, FF / D) ** 0.5) * z


def whole_call(kernel, outs, name, *args):
    in_specs = [pl.BlockSpec(memory_space=pltpu.VMEM) for _ in args]
    if args[0].shape == (1, 1):
        in_specs[0] = pl.BlockSpec(memory_space=pltpu.SMEM)
    return pl.pallas_call(
        kernel,
        in_specs=in_specs,
        out_specs=[pl.BlockSpec(memory_space=pltpu.VMEM) for _ in outs],
        out_shape=[jax.ShapeDtypeStruct((D, D), dtype) for dtype in outs],
        compiler_params=pltpu.CompilerParams(vmem_limit_bytes=VMEM),
        cost_estimate=pl.CostEstimate(flops=10**10, bytes_accessed=10**7, transcendentals=0),
        name=name,
    )(*args)


def pair(values, bit):
    return lax.ppermute(values, "opt", [(i, i ^ bit) for i in range(OPT)])


def pieces_of_owners(own):
    mate = pair(own, 1)
    across = pair(own, 2)
    return [own, mate, across, pair(across, 1)]


def sum_at_owner(pieces):
    near = pair(jnp.stack([pieces[1], pieces[3]]), 1).astype(F32)
    far = (pieces[2].astype(F32) + near[1]).astype(BF)
    return pieces[0].astype(F32) + near[0] + pair(far, 2).astype(F32)


def share(x):
    copies = jnp.broadcast_to(x[None], (lax.axis_size("dp"),) + x.shape)
    return lax.all_to_all(copies, "dp", 0, 0, tiled=True)


def sum_over_dp(x):
    parts = x.reshape((lax.axis_size("dp"), -1) + x.shape[1:])
    parts = lax.all_to_all(parts, "dp", 0, 0, tiled=True)
    return share(jnp.sum(parts.astype(F32), axis=0).astype(BF)).reshape(x.shape)


def split_heads(x):
    return x.reshape(x.shape[0], HEADS, HEAD_DIM)


def regional_forward(canvas, band, same, weights, vec):
    low = lambda x: (norm_parts(x.astype(F32))[0] * vec[0] + vec[1]).astype(BF)
    normed = low(canvas)
    queries = (nn(normed, weights[0]) + vec[4]).astype(BF)
    keys = nn(normed, weights[1]).astype(BF)
    values = (nn(normed, weights[2]) + vec[5]).astype(BF)
    own = (nn(low(band), weights[0]) + vec[4]).astype(BF)
    scores = jnp.einsum("qhd,khd->hqk", split_heads(own), split_heads(keys), preferred_element_type=F32)
    scores = jnp.where(same[None], scores * SCALE, MASKED)
    peak = jnp.max(scores, axis=-1, keepdims=True)
    raised = jnp.exp(scores - peak)
    sums = jnp.sum(raised, axis=-1, keepdims=True)
    probs = (raised / sums).astype(BF)
    mixed = jnp.einsum("hqk,khd->qhd", probs, split_heads(values), preferred_element_type=F32).reshape(own.shape)
    region_rows = band.astype(F32) + nn(mixed.astype(BF), weights[3]) + vec[6]
    return region_rows, mixed, (peak + jnp.log(sums))[:, :, 0], queries, keys, values


def regional_terms(queries, keys, values, grad_mixed, same, level, delta):
    scores = jnp.einsum("qhd,khd->hqk", split_heads(queries), split_heads(keys), preferred_element_type=F32)
    probs = jnp.where(same[None], jnp.exp(scores * SCALE - level[:, :, None]), 0.0)
    grads = jnp.einsum("qhd,khd->hqk", split_heads(grad_mixed), split_heads(values), preferred_element_type=F32)
    return probs.astype(BF), (probs * (grads - delta[:, :, None])).astype(BF)


def regional_backward(queries, keys, values, grads, own, rows, same, level, delta, weights, vec, mixed, band_grad, dw):
    grad_mixed = nt(grads, weights[3]).astype(BF)
    level_own, delta_own = own(level.T).T, own(delta.T).T
    _, scores = regional_terms(own(queries), keys, values, own(grad_mixed), same.T, level_own, delta_own)
    dq = jnp.einsum("hqk,khd->qhd", scores, split_heads(keys), preferred_element_type=F32)
    probs, scores = regional_terms(queries, own(keys), own(values), grad_mixed, same, level, delta)
    dk = jnp.einsum("hqk,qhd->khd", scores, split_heads(queries), preferred_element_type=F32)
    dv = jnp.einsum("hqk,qhd->khd", probs, split_heads(grad_mixed), preferred_element_type=F32)
    flat = lambda x: x.reshape(-1, D)
    dq, dk, dv = flat(dq) * SCALE, flat(dk) * SCALE, flat(dv)
    lows = [x.astype(BF) for x in (dq, dk, dv)]
    dn = sum(nt(x, w) for x, w in zip(lows, weights))
    xhat, scale = norm_parts(rows.astype(F32))
    low = (xhat * vec[0] + vec[1]).astype(BF)
    d_regions = own(grads).astype(F32) + norm_back(dn, xhat, scale, vec[0])
    matrices = [dw[j] + tn(low, x) for j, x in enumerate(lows)] + [dw[3] + tn(mixed.astype(BF), band_grad)]
    vectors = [fold(x) for x in (dn * xhat, dn, dq, dv, band_grad.astype(F32))]
    return d_regions, jnp.stack(matrices).astype(BF), jnp.stack(vectors)


def per_device(patches, regions, image_ids, attn_w, mlp_in, mlp_out, vec_params, patch_cot, region_cot,
               attn_mom, mlp_in_mom, mlp_out_mom, adam_first, adam_second):
    dp_size = lax.axis_size("dp")
    dp_index = lax.axis_index("dp")
    opt_index = lax.axis_index("opt")
    _, grid_rows, cols, _, _ = patch_cot.shape
    grid_cols = patches.shape[2]
    tokens = grid_rows * grid_cols
    own_count = grid_rows * cols
    one_kernel = tokens <= 1024
    vec = vec_params
    order = opt_index ^ jnp.arange(OPT)
    move = lambda x: lax.all_to_all(x, "dp", 0, 0, tiled=True)

    attn_pieces = jnp.stack(pieces_of_owners(attn_w[0].astype(BF)))
    weights = [lax.dynamic_index_in_dim(attn_pieces, opt_index ^ j, 0, keepdims=False) for j in range(OPT)]
    canvas_blocks = share(regions[0])
    canvas = canvas_blocks.reshape(tokens, D)
    by_position = patch_cot[0].transpose(0, 2, 1, 3)
    split = 20
    last = jnp.concatenate([by_position[:, split:], region_cot[0][:, None]], axis=1)
    cots = [move(by_position[:, :split]), move(last)]
    first = pieces_of_owners(mlp_in.astype(BF))
    second = pieces_of_owners(mlp_out.astype(BF))
    bias_first = jnp.take(vec[8:], order, axis=0)

    band_of = lambda x: lax.dynamic_slice_in_dim(x, dp_index, 1, 1).reshape((grid_cols,) + x.shape[3:])
    own_of = lambda x: lax.dynamic_slice_in_dim(x, dp_index * own_count, own_count, 0)
    ids_blocks = image_ids[0].reshape(grid_rows, dp_size, cols).transpose(1, 0, 2)
    ids = ids_blocks.reshape(tokens)
    band_ids, own_ids = band_of(ids_blocks), own_of(ids)
    band = band_of(canvas_blocks)
    if one_kernel:
        repeat = lambda x: jnp.tile(x, 4)[None]
        region_rows, mixed, level, reg_q, reg_k, reg_v = in_vmem(
            regional_fwd_kernel,
            [((grid_cols, D), F32), ((grid_cols, D), F32), ((4, 4 * grid_cols), F32)] + [((tokens, D), BF)] * 3,
            "regional_attention_forward", canvas, band, ids[:, None], repeat(band_ids), *weights, vec)
        level = level.reshape(HEADS, grid_cols)
    else:
        region_rows, mixed, level, reg_q, reg_k, reg_v = regional_forward(
            canvas, band, band_ids[:, None] == ids[None, :], weights, vec)
    level = level.T
    level_high = level.astype(BF).astype(F32)
    level_mid = (level - level_high).astype(BF).astype(F32)
    level_parts = jnp.concatenate([level_high, level_mid, level - level_high - level_mid], axis=1)
    level_parts = jnp.pad(level_parts, ((0, 0), (2 * HEADS, GROUP - 5 * HEADS)))

    windows = patches[0, 0].transpose(1, 0, 2)
    x1, *saved = attn_fwd(windows, region_rows, weights, vec)
    outs = [mlp(x1, start, cot, first, second, vec, bias_first) for start, cot in zip((0, split), cots)]
    moved = [move(o[0]) for o in outs]
    out_patches = jnp.concatenate([moved[0], moved[1][:, : PATCH - split]], axis=1).transpose(0, 2, 1, 3)[None]
    out_regions = moved[1][None, :, PATCH - split]
    d_patches, d_region, d_attn, d_vec_attn = attn_bwd(windows, region_rows, [o[1] for o in outs], saved, weights, vec)
    d_patches = d_patches.transpose(1, 0, 2)[None, None]

    add = lambda n, j: (outs[0][n][j].astype(F32) + outs[1][n][j].astype(F32)).astype(BF)
    own_first = sum_at_owner([add(2, j) for j in range(OPT)])
    own_second = sum_at_owner([add(3, j) for j in range(OPT)])
    own_mlp = sum_over_dp(jnp.concatenate([own_first, own_second], axis=1).astype(BF))

    band_grad, extra = in_vmem(payload_kernel, [((grid_cols, D), BF), ((grid_cols, GROUP), BF)],
                               "regional_payload", d_region, mixed, level_parts, weights[3])
    payload = share(jnp.concatenate([band_grad, extra], axis=1)).reshape(grid_rows, dp_size, cols, D + GROUP)
    payload = payload.transpose(1, 0, 2, 3).reshape(tokens, D + GROUP)
    grads = payload[:, :D]
    extra = payload[:, D:].astype(F32)
    part = lambda n: extra[:, n * HEADS : (n + 1) * HEADS]
    delta = (part(0) + part(1)).T
    level = (part(2) + part(3) + part(4)).T
    if one_kernel:
        wide = lambda x: x.reshape(4, -1)
        own_columns = lambda x: wide(lax.dynamic_slice_in_dim(x, dp_index * own_count, own_count, 1))
        d_regions, grad_attn, d_vec_reg = in_vmem(
            partial(regional_bwd_kernel, own_count),
            [((own_count, D), F32), ((4, D, D), BF), ((5, 8, D), F32)],
            "regional_attention_backward", reg_q, reg_k, reg_v, grads, own_of(reg_q), own_of(reg_k), own_of(reg_v),
            own_of(canvas), ids[:, None], repeat(ids), own_ids[:, None], repeat(own_ids), wide(level), wide(delta),
            own_columns(level), own_columns(delta), own_of(grads), mixed, band_grad, d_attn, *weights, vec)
    else:
        d_regions, grad_attn, d_vec_reg = regional_backward(
            reg_q, reg_k, reg_v, grads, own_of, own_of(canvas), ids[:, None] == own_ids[None, :], level, delta,
            weights, vec, mixed, band_grad, d_attn)
    d_regions = d_regions.reshape(regions.shape)

    pieces = [lax.dynamic_index_in_dim(grad_attn, opt_index ^ j, 0, keepdims=False) for j in range(OPT)]
    own_attn = sum_over_dp(sum_at_owner(pieces).astype(BF))

    d_vec_attn = jnp.sum(d_vec_attn + d_vec_reg, axis=1)
    d_vec_mlp = jnp.sum(outs[0][4] + outs[1][4], axis=1)
    d_bias_first = jnp.take(jnp.sum(outs[0][5] + outs[1][5], axis=1), order, axis=0)
    grad_vec = jnp.concatenate([d_vec_attn[:2], d_vec_mlp[:2], d_vec_attn[2:], d_vec_mlp[2:], d_bias_first])
    grad_vec = grad_vec + pair(grad_vec, 1)
    grad_vec = grad_vec + pair(grad_vec, 2)
    grad_vec = jnp.sum(share(grad_vec), axis=0)

    squares = lambda x: jnp.sum(x.astype(F32) ** 2)
    total = jnp.full((8, 128), squares(own_attn) + squares(own_mlp))
    total = total + pair(total, 1)
    total = total + pair(total, 2)
    grad_norm = jnp.sqrt(total[0, 0] + squares(grad_vec))
    clip = jnp.minimum(1.0, CLIP_LIMIT / (grad_norm + 1e-06))
    clip_cell = clip.reshape(1, 1)
    first_mom, second_mom, gram_first, gram_second = whole_call(
        moments_kernel, [F32, F32, F32, F32], "mlp_moments", clip_cell,
        own_mlp[:, :D], own_mlp[:, D:], mlp_in_mom, mlp_out_mom)
    grams = jnp.stack([gram_first, gram_second])
    grams = grams + pair(grams, 1)
    grams = grams + pair(grams, 2)
    attn_mom_new, new_attn = whole_call(
        square_kernel, [F32, F32], "attention_update", clip_cell, own_attn, attn_mom[0], attn_w[0])
    new_first, new_second = whole_call(
        sharded_kernel, [F32, F32], "mlp_update", grams[0], grams[1], first_mom, second_mom, mlp_in, mlp_out)
    clipped = clip * grad_vec
    moment_one = BETA_FIRST * adam_first + (1.0 - BETA_FIRST) * clipped
    moment_two = BETA_SECOND * adam_second + (1.0 - BETA_SECOND) * clipped * clipped
    first_hat = moment_one / (1.0 - BETA_FIRST**OPT_STEP)
    second_hat = moment_two / (1.0 - BETA_SECOND**OPT_STEP)
    new_vec = vec_params - ADAM_RATE * first_hat / (jnp.sqrt(second_hat) + ADAM_EPS)
    return (out_patches, out_regions, d_patches, d_regions, new_attn[None], attn_mom_new[None], new_first, first_mom,
            new_second, second_mom, new_vec, moment_one, moment_two, grad_norm)


def solution(mesh):
    canvas = P("opt", None, "dp", None)
    wide = P("opt", None, "dp", None, None)
    bands = P("opt", "dp", None, None, None)
    square, right, down = P("opt", None, None), P(None, "opt"), P("opt", None)
    return jax.shard_map(
        per_device,
        mesh=mesh,
        in_specs=(bands, canvas, square, square, right, down, P(), wide, canvas, square, right, down, P(), P()),
        out_specs=(wide, canvas, bands, canvas, square, square, right, right, down, down, P(), P(), P(), P()),
        check_vma=False,
    )
```

time: 633 us -> 552 us (0.87)
  starting transfers between devices: 94.3 us -> 56.5 us
  matrix products: 30.6 us -> 0 us
  blocking collectives: 0 us -> 29.3 us
  local copies, waits for them, and re-layouts: 61.1 us -> 36.2 us
  other arithmetic: 61 us -> 47.9 us
  Pallas kernels: 210 us -> 218 us
  waiting for transfers between devices: 159 us -> 151 us
    dot_general x20 -> x0, matrix products: 30.6 us -> none  [the longest x4 8.35 us: tn(): lax.dot_general(a, b, (((0,), (0,)), ((), ())), preferred_element_type=F32)]
    all_to_all x0 -> x1, blocking collectives: none -> 29.3 us  [share(): return lax.all_to_all(copies, 'dp', 0, 0, tiled=True)]
    all_to_all x7 -> x4, waiting for transfers between devices: 47 us -> 25.7 us  [share(): return lax.all_to_all(copies, 'dp', 0, 0, tiled=True)]
    all_to_all x8 -> x4, starting transfers between devices: 41.2 us -> 20.9 us  [per_device(): move = lambda x: lax.all_to_all(x, 'dp', 0, 0, tiled=True)]
    all_to_all x8 -> x4, waiting for transfers between devices: 50.6 us -> 68.5 us  [per_device(): move = lambda x: lax.all_to_all(x, 'dp', 0, 0, tiled=True)]
    all_to_all x7 -> x4, starting transfers between devices: 33.9 us -> 16.7 us  [share(): return lax.all_to_all(copies, 'dp', 0, 0, tiled=True)]
    unnamed x143 -> x64, local copies, waits for them, and re-layouts: 14.5 us -> 3.91 us
    pallas_call x4 -> x0, local copies, waits for them, and re-layouts: 6.74 us -> none  [mlp(): pl.pallas_call(partial(mlp_kernel, count, steps, cols), grid=(steps,), in...]
  transfers between devices with their start and end apart: 38 -> 31, of which waited for: 21 -> 16; matrix products, arithmetic and copies ran while one was open for 22% -> 13% of each run, Pallas kernels for 7% -> 17%
where the time goes in v2:
time: 552 us; the launch traced here: 544 us
  Pallas kernels  218 us (39%)
  waiting for transfers between devices  151 us (27%)
  starting transfers between devices  56.5 us (10%)
  other arithmetic  47.9 us (9%)
  local copies, waits for them, and re-layouts  36.2 us (7%)
  blocking collectives  29.3 us (5%)
    all_to_all x4, waiting for transfers between devices, per_device(): move = lambda x: lax.all_to_all(x, 'dp', 0, 0, tiled=True)  68.5 us
    pallas_call x2, Pallas kernels, mlp(): pl.pallas_call(partial(mlp_kernel, many, sources, cols, steps, lanes), gr...  66.4 us
    pallas_call x1, Pallas kernels, attn_bwd(): pl.pallas_call(partial(attn_bwd_kernel, count, batch, len(dx1_parts)), gr...  52.6 us
    pallas_call x3, Pallas kernels, whole_call(): pl.pallas_call(kernel, in_specs=in_specs, out_specs=[pl.BlockSpec(memory_...  46.8 us
    pallas_call x1, Pallas kernels, attn_fwd(): pl.pallas_call(partial(attn_fwd_kernel, count, batch), grid=(windows // c...  35.1 us
    ppermute x21, waiting for transfers between devices, pair(): return lax.ppermute(values, 'opt', [(i, i ^ bit) for i in range(OPT)])  31.1 us
    all_to_all x1, blocking collectives, share(): return lax.all_to_all(copies, 'dp', 0, 0, tiled=True)  29.3 us
    all_to_all x4, waiting for transfers between devices, share(): return lax.all_to_all(copies, 'dp', 0, 0, tiled=True)  25.7 us
  transfers between devices with their start and end apart: 31, of which 16 were waited for; matrix products, arithmetic and copies ran while one was open for 13% of the time, Pallas kernels for 17%

profile of v2, /device:TPU:0, one launch (start us, length us, event | category | flops | bytes accessed | tf_op | source)
XLA Modules:
  0.0 543.6 jit_solution(10858748979124626119)
XLA Ops:
  0.7 2.6 fusion.24
  3.2 3.0 collective-permute-start.1
  7.0 5.9 %all-to-all-start = ((bf16[8,8,8,512]{3,2,1,0:T(8,128)(2,1)}), bf16[8,8,8,512]{3,2,1,0:T(8,128)(2,1)}, u32[]{:S(2)}, u32[]{:S(2)}) async-start(bf16[8,8,8,512]{3,2,1,0:T(8,128)(2,1)} %broadcast_in_dim.59), calls=%async_computation | async-start | bytes 1048576 | tf_op jit(solution)/shard_map/all_to_all | solution.py:572
  17.1 2.2 collective-permute-done.1
  19.3 1.7 slice.177
  21.0 2.5 slice.176
  27.8 6.3 %all-to-all-start.1 = ((bf16[8,20,8,512]{3,2,1,0:T(8,128)(2,1)}), bf16[8,20,8,512]{3,2,1,0:T(8,128)(2,1)S(1)}, u32[]{:S(2)}, u32[]{:S(2)}) async-start(bf16[8,20,8,512]{3,2,1,0:T(8,128)(2,1)} %slice.176), calls=%async_computation.1 | async-start | bytes 2621440 | tf_op jit(solution)/shard_map/all_to_all | solution.py:642
  36.2 4.7 collective-permute-done.7.w2c
  43.7 5.2 regional_attention_forward.1
  49.7 35.1 %window_attention_forward.1 = (f32[50,64,512]{2,1,0:T(8,128)}, bf16[64,56,512]{2,1,0:T(8,128)(2,1)}, bf16[64,56,512]{2,1,0:T(8,128)(2,1)}, bf16[64,56,512]{2,1,0...) custom-call(bf16[49,64,512]{2,1,0:T(8,128)(2,1)} %bitcast.132, ...), custom_call_target="tpu_custom_call" | custom-call | flops 30000001024 | bytes 30000000 | tf_op jit(solution)/shard_map/window_attention_forward/pallas_call | solution.py:179
  86.6 6.2 %all-to-all-start.3 = ((bf16[8,30,8,512]{3,2,1,0:T(8,128)(2,1)}), bf16[8,30,8,512]{3,2,1,0:T(8,128)(2,1)S(1)}, u32[]{:S(2)}, u32[]{:S(2)}) async-start(bf16[8,30,8,512]{3,2,1,0:T(8,128)(2,1)} %pad_maximum_fusion.2), calls=%async_computation.3 | async-start | bytes 3932160 | tf_op jit(solution)/shard_map/all_to_all | solution.py:642
  93.7 27.6 %mlp_forward_backward.2 = (bf16[8,20,8,512]{3,2,1,0:T(8,128)(2,1)}, f32[20,64,512]{2,1,0:T(8,128)}, bf16[4,512,512]{2,1,0:T(8,128)(2,1)}, bf16[4,512,512]{2,1,0:...) custom-call(f32[50,64,512]{2,1,0:T(8,128)} %get-tuple-element.57.x1_ref, bf16[8,20,8,512]{3,2,1,0:T(8,128)(2,1)} %copy-done.9, ...), custom_call_target="tpu_custom_call" | custom-call | flops 40000000000 | bytes 30000000 | tf_op jit(solution)/shard_map/mlp_forward_backward/pallas_call | solution.py:259
  121.4 17.6 %all-to-all-done.3.pc_ref = bf16[8,30,8,512]{3,2,1,0:T(8,128)(2,1)S(1)} async-done(((bf16[8,30,8,512]{3,2,1,0:T(8,128)(2,1)}), bf16[8,30,8,512]{3,2,1,0:T(8,128)(2,1)S(1)}, u32[]{:S(2)}, u32[]{:S(2)}) %all-to-all-start.3) | async-done | bytes 1966112 | tf_op jit(solution)/shard_map/all_to_all | solution.py:642
  140.2 38.8 %mlp_forward_backward.3 = (bf16[8,30,8,512]{3,2,1,0:T(8,128)(2,1)}, f32[30,64,512]{2,1,0:T(8,128)}, bf16[4,512,512]{2,1,0:T(8,128)(2,1)}, bf16[4,512,512]{2,1,0:...) custom-call(f32[50,64,512]{2,1,0:T(8,128)} %get-tuple-element.57.x1_ref, bf16[8,30,8,512]{3,2,1,0:T(8,128)(2,1)} %copy-done.8, ...), custom_call_target="tpu_custom_call" | custom-call | flops 40000000000 | bytes 30000000 | tf_op jit(solution)/shard_map/mlp_forward_backward/pallas_call | solution.py:259
  179.0 52.6 %window_attention_backward.1 = (bf16[49,64,512]{2,1,0:T(8,128)(2,1)}, f32[64,512]{1,0:T(8,128)}, f32[4,512,512]{2,1,0:T(8,128)}, f32[5,8,512]{2,1,0:T(8,128)}) custom-call(bf16[49,64,512]{2,1,0:T(8,128)(2,1)} %bitcast.133, f32[64,512]{1,0:T(8,128)} %get-tuple-element.56.r_ref.refs_1_, f32[20,64,512]{2,1,0:T(8,128)} %get-tuple-element.60.refs_2_, ...), custom_call_target="tpu_custom_call" | custom-call | flops 40000000000 | bytes 50000000 | tf_op jit(solution)/shard_map/window_attention_backward/pallas_call | solution.py:342
  231.6 2.3 regional_payload.1
  235.8 3.6 all-to-all-start.5
  247.2 9.7 %all-to-all-done.5 = bf16[8,64,640]{2,1,0:T(8,128)(2,1)S(1)} async-done(((bf16[8,64,640]{2,1,0:T(8,128)(2,1)}), bf16[8,64,640]{2,1,0:T(8,128)(2,1)S(1)}, u32[]{:S(2)}, u32[]{:S(2)}) %all-to-all-start.5) | async-done | bytes 655392 | tf_op jit(solution)/shard_map/all_to_all | solution.py:572
  261.9 9.4 %regional_attention_backward.1 = (f32[64,512]{1,0:T(8,128)}, bf16[4,512,512]{2,1,0:T(8,128)(2,1)}, f32[5,8,512]{2,1,0:T(8,128)}) custom-call(bf16[512,512]{1,0:T(8,128)(2,1)} %get-tuple-element.68.q_ref, bf16[512,512]{1,0:T(8,128)(2,1)} %get-tuple-element.69.k_ref, bf16[512,512]{1,0:T(8,128)(2,1)} %get-tuple-element.70.v_ref, bf16[512,512]{1,0:T(8,128)(2,1)} %copy-done.13, ...), custom_call_target="tpu_custom_call" | custom-call | flops 10000000000 | bytes 10000000 | tf_op jit(solution)/shard_map/regional_attention_backward/pallas_call | solution.py:390
  281.1 2.0 fusion.12
  283.6 2.2 fusion.13
  289.7 3.6 all-to-all-start.10
  293.4 1.7 fusion.14
  295.7 2.5 collective-permute-done.10
  298.2 2.2 fusion.11
  302.0 3.7 all-to-all-start.6
  305.7 3.8 collective-permute-done.12
  309.4 2.0 fusion.7
  311.4 8.4 %collective-permute-done.14 = bf16[512,512]{1,0:T(8,128)(2,1)} collective-permute-done((bf16[512,512]{1,0:T(8,128)(2,1)S(1)}, bf16[512,512]{1,0:T(8,128)(2,1)}, u32[]{:S(2)}, u32[]{:S(2)}) %collective-permute-start.14) | collective-permute-done | bytes 524320 | tf_op jit(solution)/shard_map/ppermute | solution.py:555
  322.6 3.6 all-to-all-start.8
  326.3 25.4 %all-to-all-done.8 = bf16[8,64,1024]{2,1,0:T(8,128)(2,1)S(1)} async-done(((bf16[8,64,1024]{2,1,0:T(8,128)(2,1)}), bf16[8,64,1024]{2,1,0:T(8,128)(2,1)S(1)}, u32[]{:S(2)}, u32[]{:S(2)}) %all-to-all-start.8) | async-done | bytes 1048608 | tf_op jit(solution)/shard_map/all_to_all | solution.py:577
  352.5 3.5 all-to-all-start.7
  356.2 14.4 %all-to-all-done.7 = bf16[8,64,512]{2,1,0:T(8,128)(2,1)S(1)} async-done(((bf16[8,64,512]{2,1,0:T(8,128)(2,1)}), bf16[8,64,512]{2,1,0:T(8,128)(2,1)S(1)}, u32[]{:S(2)}, u32[]{:S(2)}) %all-to-all-start.7) | async-done | bytes 524320 | tf_op jit(solution)/shard_map/all_to_all | solution.py:572
  370.7 29.3 %all_to_all.55 = bf16[8,64,1024]{2,1,0:T(8,128)(2,1)S(1)} all-to-all(bf16[8,64,1024]{2,1,0:T(8,128)(2,1)S(1)} %broadcast_in_dim.65), channel_id=1, replica_groups=mesh['dp'=8,'opt'=4] {'dp'}, dimensions={0} | all-to-all | bytes 2097152 | tf_op jit(solution)/shard_map/all_to_all | solution.py:572
  400.0 4.3 all-to-all-start.4
  410.5 2.1 collective-permute-done.16
  414.5 4.7 mlp_moments.1
  419.2 3.0 pad_maximum_fusion.1
  422.2 26.6 %all-to-all-done.4 = bf16[8,30,8,512]{3,2,1,0:T(8,128)(2,1)} async-done(((bf16[8,30,8,512]{3,2,1,0:T(8,128)(2,1)}), bf16[8,30,8,512]{3,2,1,0:T(8,128)(2,1)}, u32[]{:S(2)}, u32[]{:S(2)}) %all-to-all-start.4) | async-done | bytes 1966112 | tf_op jit(solution)/shard_map/all_to_all | solution.py:642
  448.9 4.0 all-to-all-start.2
  452.9 3.4 fusion.21
  456.9 2.9 slice.178
  459.8 24.3 %all-to-all-done.2 = bf16[8,20,8,512]{3,2,1,0:T(8,128)(2,1)S(1)} async-done(((bf16[8,20,8,512]{3,2,1,0:T(8,128)(2,1)}), bf16[8,20,8,512]{3,2,1,0:T(8,128)(2,1)S(1)}, u32[]{:S(2)}, u32[]{:S(2)}) %all-to-all-start.2) | async-done | bytes 1310752 | tf_op jit(solution)/shard_map/all_to_all | solution.py:642
  484.1 3.5 maximum_bitcast_fusion
  489.7 8.3 %attention_update.1 = (f32[512,512]{1,0:T(8,128)}, f32[512,512]{1,0:T(8,128)}) custom-call(f32[1,1]{1,0:T(1,128)} %bitcast.44.clip_ref, bf16[512,512]{1,0:T(8,128)(2,1)} %bitcast.120, f32[512,512]{1,0:T(8,128)} %bitcast.134, f32[512,512]{1,0:T(8,128)} %bitcast.125), custom_call_target="tpu_custom_call" | custom-call | flops 10000000000 | bytes 10000000 | tf_op jit(solution)/shard_map/attention_update/pallas_call | solution.py:543
  498.0 5.9 %collective-permute-done.20 = f32[2,512,512]{2,1,0:T(8,128)} collective-permute-done((f32[2,512,512]{2,1,0:T(8,128)}, f32[2,512,512]{2,1,0:T(8,128)}, u32[]{:S(2)}, u32[]{:S(2)}) %collective-permute-start.20) | collective-permute-done | bytes 2097184 | tf_op jit(solution)/shard_map/ppermute | solution.py:555
  503.9 3.0 fusion.25
  508.4 33.8 %mlp_update.1 = (f32[512,512]{1,0:T(8,128)}, f32[512,512]{1,0:T(8,128)}) custom-call(f32[512,512]{1,0:T(8,128)} %get-tuple-element.105.gram1_ref, f32[512,512]{1,0:T(8,128)} %get-tuple-element.104.gram2_ref, f32[512,512]{1,0:T(8,128)} %get-tuple-element.49.n1_ref, f32[512,512]{1,0:T(8,128)} %get-tuple-element.51.n2_ref, f32[512,512]{1,0:T(8,128)} %w1_ref.1, ...), custom_call_target="tpu_custom_call" | custom-call | flops 10000000000 | bytes 10000000 | tf_op jit(solution)/shard_map/mlp_update/pallas_call | solution.py:543
  (192 shorter events, 63.0 us)
Async XLA Ops:
  0.6 5.6 %copy-start.19 = (bf16[1,8,8,512]{3,2,1,0:T(8,128)(2,1)S(1)}, bf16[1,8,8,512]{3,2,1,0:T(8,128)(2,1)}, u32[]{:S(2)}) copy-start(bf16[1,8,8,512]{3,2,1,0:T(8,128)(2,1)} %param.17) | copy-start | bytes 196612
  0.7 12.3 %copy-start.10 = (f32[512,512]{1,0:T(8,128)S(1)}, f32[512,512]{1,0:T(8,128)}, u32[]{:S(2)}) copy-start(f32[512,512]{1,0:T(8,128)} %w1_ref.1) | copy-start | bytes 3145732
  3.2 11.4 %copy-start.11 = (f32[512,512]{1,0:T(8,128)S(1)}, f32[512,512]{1,0:T(8,128)}, u32[]{:S(2)}) copy-start(f32[512,512]{1,0:T(8,128)} %w2_ref.1) | copy-start | bytes 3145732
  3.2 16.0 %collective-permute-start.1 = (bf16[512,512]{1,0:T(8,128)(2,1)}, bf16[512,512]{1,0:T(8,128)(2,1)}, u32[]{:S(2)}, u32[]{:S(2)}) collective-permute-start(bf16[512,512]{1,0:T(8,128)(2,1)} %get-tuple-element.115), channel_id=1, source_target_pairs={{0,2},{1,3},{2,0},{3,1},{4,6},{5,7},{6,4},{7,5},{8,10},{9,11},{10,... | collective-permute-start | bytes 1572872 | tf_op jit(solution)/shard_map/ppermute | solution.py:555
  7.0 9.9 %copy-start.27 = (s32[1,8,64]{2,1,0:T(8,128)S(1)}, s32[1,8,64]{2,1,0:T(8,128)}, u32[]{:S(2)}) copy-start(s32[1,8,64]{2,1,0:T(8,128)} %param.18) | copy-start | bytes 6148
  7.0 20.8 %all-to-all-start = ((bf16[8,8,8,512]{3,2,1,0:T(8,128)(2,1)}), bf16[8,8,8,512]{3,2,1,0:T(8,128)(2,1)}, u32[]{:S(2)}, u32[]{:S(2)}) async-start(bf16[8,8,8,512]{3,2,1,0:T(8,128)(2,1)} %broadcast_in_dim.59), calls=%async_computation | async-start | bytes 1048576 | tf_op jit(solution)/shard_map/all_to_all | solution.py:572
  13.0 22.7 %collective-permute-start = (bf16[512,512]{1,0:T(8,128)(2,1)}, bf16[512,512]{1,0:T(8,128)(2,1)}, u32[]{:S(2)}, u32[]{:S(2)}) collective-permute-start(bf16[512,512]{1,0:T(8,128)(2,1)} %get-tuple-element.115), channel_id=1, source_target_pairs={{0,1},{1,0},{2,3},{3,2},{4,5},{5,4},{6,7},{7,6},{8,9},{9,8},{10,11... | collective-permute-start | bytes 1572872 | tf_op jit(solution)/shard_map/ppermute | solution.py:555
  13.9 22.0 %collective-permute-start.4 = (bf16[512,512]{1,0:T(8,128)(2,1)}, bf16[512,512]{1,0:T(8,128)(2,1)}, u32[]{:S(2)}, u32[]{:S(2)}) collective-permute-start(bf16[512,512]{1,0:T(8,128)(2,1)} %convert_element_type.206.w1a), channel_id=1, source_target_pairs={{0,2},{1,3},{2,0},{3,1},{4,6},{5,7},{6,4},{7,5},{8,10},{9,11},{10,... | collective-permute-start | bytes 1572872 | tf_op jit(solution)/shard_map/ppermute | solution.py:555
  14.4 78.5 %collective-permute-start.3 = (bf16[512,512]{1,0:T(8,128)(2,1)}, bf16[512,512]{1,0:T(8,128)(2,1)}, u32[]{:S(2)}, u32[]{:S(2)}) collective-permute-start(bf16[512,512]{1,0:T(8,128)(2,1)} %convert_element_type.206.w1a), channel_id=1, source_target_pairs={{0,1},{1,0},{2,3},{3,2},{4,5},{5,4},{6,7},{7,6},{8,9},{9,8},{10,11... | collective-permute-start | bytes 1572872 | tf_op jit(solution)/shard_map/ppermute | solution.py:555
  15.4 25.5 %collective-permute-start.7 = (bf16[512,512]{1,0:T(8,128)(2,1)}, bf16[512,512]{1,0:T(8,128)(2,1)}, u32[]{:S(2)}, u32[]{:S(2)}) collective-permute-start(bf16[512,512]{1,0:T(8,128)(2,1)} %convert_element_type.207.w2a), channel_id=1, source_target_pairs={{0,2},{1,3},{2,0},{3,1},{4,6},{5,7},{6,4},{7,5},{8,10},{9,11},{10,... | collective-permute-start | bytes 1572872 | tf_op jit(solution)/shard_map/ppermute | solution.py:555
  17.1 8.1 %copy-start.26 = (s32[1024]{0:T(1024)}, s32[1024]{0:T(1024)S(1)}, u32[]{:S(2)}) copy-start(s32[1024]{0:T(1024)S(1)} %pad_clamp_fusion) | copy-start | bytes 12292
  19.3 21.6 %collective-permute-start.2 = (bf16[512,512]{1,0:T(8,128)(2,1)}, bf16[512,512]{1,0:T(8,128)(2,1)S(1)}, u32[]{:S(2)}, u32[]{:S(2)}) collective-permute-start(bf16[512,512]{1,0:T(8,128)(2,1)} %collective-permute-done.1), channel_id=1, source_target_pairs={{0,1},{1,0},{2,3},{3,2},{4,5},{5,4},{6,7},{7,6},{8,9},{9,8},{10,11... | collective-permute-start | bytes 1572872 | tf_op jit(solution)/shard_map/ppermute | solution.py:555
  19.3 7.9 %copy-start.28 = (pred[4]{0:T(512)(128)(4,1)}, pred[4]{0:T(512)(128)(4,1)S(1)}, u32[]{:S(2)}) copy-start(pred[4]{0:T(512)(128)(4,1)S(1)} %compare_and_fusion) | copy-start | bytes 16
  19.3 5.0 copy-start.14
  27.8 57.8 %all-to-all-start.1 = ((bf16[8,20,8,512]{3,2,1,0:T(8,128)(2,1)}), bf16[8,20,8,512]{3,2,1,0:T(8,128)(2,1)S(1)}, u32[]{:S(2)}, u32[]{:S(2)}) async-start(bf16[8,20,8,512]{3,2,1,0:T(8,128)(2,1)} %slice.176), calls=%async_computation.1 | async-start | bytes 2621440 | tf_op jit(solution)/shard_map/all_to_all | solution.py:642
  35.6 57.3 %collective-permute-start.6 = (bf16[512,512]{1,0:T(8,128)(2,1)}, bf16[512,512]{1,0:T(8,128)(2,1)S(1)}, u32[]{:S(2)}, u32[]{:S(2)}) collective-permute-start(bf16[512,512]{1,0:T(8,128)(2,1)} %convert_element_type.207.w2a), channel_id=1, source_target_pairs={{0,1},{1,0},{2,3},{3,2},{4,5},{5,4},{6,7},{7,6},{8,9},{9,8},{10,11... | collective-permute-start | bytes 1572872 | tf_op jit(solution)/shard_map/ppermute | solution.py:555
  35.9 57.1 %collective-permute-start.5 = (bf16[512,512]{1,0:T(8,128)(2,1)}, bf16[512,512]{1,0:T(8,128)(2,1)}, u32[]{:S(2)}, u32[]{:S(2)}) collective-permute-start(bf16[512,512]{1,0:T(8,128)(2,1)} %collective-permute-done.4.w1c), channel_id=1, source_target_pairs={{0,1},{1,0},{2,3},{3,2},{4,5},{5,4},{6,7},{7,6},{8,9},{9,8},{10,11... | collective-permute-start | bytes 1572872 | tf_op jit(solution)/shard_map/ppermute | solution.py:555
  40.9 52.0 %collective-permute-start.8 = (bf16[512,512]{1,0:T(8,128)(2,1)}, bf16[512,512]{1,0:T(8,128)(2,1)}, u32[]{:S(2)}, u32[]{:S(2)}) collective-permute-start(bf16[512,512]{1,0:T(8,128)(2,1)} %collective-permute-done.7.w2c), channel_id=1, source_target_pairs={{0,1},{1,0},{2,3},{3,2},{4,5},{5,4},{6,7},{7,6},{8,9},{9,8},{10,11... | collective-permute-start | bytes 1572872 | tf_op jit(solution)/shard_map/ppermute | solution.py:555
  86.6 52.3 %all-to-all-start.3 = ((bf16[8,30,8,512]{3,2,1,0:T(8,128)(2,1)}), bf16[8,30,8,512]{3,2,1,0:T(8,128)(2,1)S(1)}, u32[]{:S(2)}, u32[]{:S(2)}) async-start(bf16[8,30,8,512]{3,2,1,0:T(8,128)(2,1)} %pad_maximum_fusion.2), calls=%async_computation.3 | async-start | bytes 3932160 | tf_op jit(solution)/shard_map/all_to_all | solution.py:642
  233.9 5.6 %copy-start.15 = (s32[8,8,8]{2,0,1:T(8,128)S(1)}, s32[8,8,8]{2,0,1:T(8,128)}, u32[]{:S(2)}) copy-start(s32[8,8,8]{2,0,1:T(8,128)} %copy-done.14) | copy-start | bytes 6148
  233.9 10.7 %copy-start.5 = (bf16[4,512,512]{2,1,0:T(8,128)(2,1)S(1)}, bf16[4,512,512]{2,1,0:T(8,128)(2,1)}, u32[]{:S(2)}) copy-start(bf16[4,512,512]{2,1,0:T(8,128)(2,1)} %get-tuple-element.79) | copy-start | bytes 6291460
  235.8 21.1 %all-to-all-start.5 = ((bf16[8,64,640]{2,1,0:T(8,128)(2,1)}), bf16[8,64,640]{2,1,0:T(8,128)(2,1)S(1)}, u32[]{:S(2)}, u32[]{:S(2)}) async-start(bf16[8,64,640]{2,1,0:T(8,128)(2,1)} %broadcast_in_dim.62), calls=%async_computation.5 | async-start | bytes 1310720 | tf_op jit(solution)/shard_map/all_to_all | solution.py:572
  247.2 29.7 %collective-permute-start.11 = (bf16[2,512,512]{2,1,0:T(8,128)(2,1)}, bf16[2,512,512]{2,1,0:T(8,128)(2,1)S(1)}, u32[]{:S(2)}, u32[]{:S(2)}) collective-permute-start(bf16[2,512,512]{2,1,0:T(8,128)(2,1)} %pad_maximum_fusion.4), channel_id=1, source_target_pairs={{0,1},{1,0},{2,3},{3,2},{4,5},{5,4},{6,7},{7,6},{8,9},{9,8},{10,11... | collective-permute-start | bytes 3145736 | tf_op jit(solution)/shard_map/ppermute | solution.py:555
  273.8 5.8 %collective-permute-start.9 = (bf16[2,512,512]{2,1,0:T(8,128)(2,1)}, bf16[2,512,512]{2,1,0:T(8,128)(2,1)}, u32[]{:S(2)}, u32[]{:S(2)}) collective-permute-start(bf16[2,512,512]{2,1,0:T(8,128)(2,1)} %pad_maximum_fusion.3), channel_id=1, source_target_pairs={{0,1},{1,0},{2,3},{3,2},{4,5},{5,4},{6,7},{7,6},{8,9},{9,8},{10,11... | collective-permute-start | bytes 3145736 | tf_op jit(solution)/shard_map/ppermute | solution.py:555
  275.3 12.1 %collective-permute-start.13 = (bf16[2,512,512]{2,1,0:T(8,128)(2,1)}, bf16[2,512,512]{2,1,0:T(8,128)(2,1)S(1)}, u32[]{:S(2)}, u32[]{:S(2)}) collective-permute-start(bf16[2,512,512]{2,1,0:T(8,128)(2,1)} %pad_maximum_fusion.5), channel_id=1, source_target_pairs={{0,1},{1,0},{2,3},{3,2},{4,5},{5,4},{6,7},{7,6},{8,9},{9,8},{10,11... | collective-permute-start | bytes 3145736 | tf_op jit(solution)/shard_map/ppermute | solution.py:555
  276.7 1.3 collective-permute-start.17
  277.1 6.5 %copy-start.2 = (f32[2,512,512]{2,1,0:T(8,128)}, f32[2,512,512]{2,1,0:T(8,128)S(1)}, u32[]{:S(2)}) copy-start(f32[2,512,512]{2,1,0:T(8,128)S(1)} %convert_element_type.232) | copy-start | bytes 6291460
  278.1 10.9 %collective-permute-start.18 = (f32[12,512]{1,0:T(8,128)S(1)}, f32[12,512]{1,0:T(8,128)S(1)}, u32[]{:S(2)}, u32[]{:S(2)}) collective-permute-start(f32[12,512]{1,0:T(8,128)S(1)} %add.189), channel_id=1, source_target_pairs={{0,2},{1,3},{2,0},{3,1},{4,6},{5,7},{6,4},{7,5},{8,10},{9,11},{10,... | collective-permute-start | bytes 73736 | tf_op jit(solution)/shard_map/ppermute | solution.py:555
  283.1 15.1 %collective-permute-start.10 = (bf16[512,512]{1,0:T(8,128)(2,1)}, bf16[512,512]{1,0:T(8,128)(2,1)}, u32[]{:S(2)}, u32[]{:S(2)}) collective-permute-start(bf16[512,512]{1,0:T(8,128)(2,1)} %fusion.12), channel_id=1, source_target_pairs={{0,2},{1,3},{2,0},{3,1},{4,6},{5,7},{6,4},{7,5},{8,10},{9,11},{10,... | collective-permute-start | bytes 1572872 | tf_op jit(solution)/shard_map/ppermute | solution.py:555
  285.8 23.6 %collective-permute-start.12 = (bf16[512,512]{1,0:T(8,128)(2,1)}, bf16[512,512]{1,0:T(8,128)(2,1)}, u32[]{:S(2)}, u32[]{:S(2)}) collective-permute-start(bf16[512,512]{1,0:T(8,128)(2,1)} %fusion.13), channel_id=1, source_target_pairs={{0,2},{1,3},{2,0},{3,1},{4,6},{5,7},{6,4},{7,5},{8,10},{9,11},{10,... | collective-permute-start | bytes 1572872 | tf_op jit(solution)/shard_map/ppermute | solution.py:555
  289.7 12.2 %all-to-all-start.10 = ((f32[8,12,512]{2,1,0:T(8,128)}), f32[8,12,512]{2,1,0:T(8,128)S(1)}, u32[]{:S(2)}, u32[]{:S(2)}) async-start(f32[8,12,512]{2,1,0:T(8,128)} %broadcast_in_dim.67), calls=%async_computation.10 | async-start | bytes 524288 | tf_op jit(solution)/shard_map/all_to_all | solution.py:572
  295.1 24.7 %collective-permute-start.14 = (bf16[512,512]{1,0:T(8,128)(2,1)S(1)}, bf16[512,512]{1,0:T(8,128)(2,1)}, u32[]{:S(2)}, u32[]{:S(2)}) collective-permute-start(bf16[512,512]{1,0:T(8,128)(2,1)S(1)} %fusion.14), channel_id=1, source_target_pairs={{0,2},{1,3},{2,0},{3,1},{4,6},{5,7},{6,4},{7,5},{8,10},{9,11},{10,... | collective-permute-start | bytes 1572872 | tf_op jit(solution)/shard_map/ppermute | solution.py:555
  302.0 17.8 %copy-start.3 = (f32[2,512,512]{2,1,0:T(8,128)S(1)}, f32[2,512,512]{2,1,0:T(8,128)}, u32[]{:S(2)}) copy-start(f32[2,512,512]{2,1,0:T(8,128)} %convert_element_type.251) | copy-start | bytes 6291460
  302.0 20.6 %all-to-all-start.6 = ((bf16[8,64,512]{2,1,0:T(8,128)(2,1)}), bf16[8,64,512]{2,1,0:T(8,128)(2,1)S(1)}, u32[]{:S(2)}, u32[]{:S(2)}) async-start(bf16[8,64,512]{2,1,0:T(8,128)(2,1)} %bitcast.36), calls=%async_computation.6 | async-start | bytes 1048576 | tf_op jit(solution)/shard_map/all_to_all | solution.py:577
  322.6 29.1 %all-to-all-start.8 = ((bf16[8,64,1024]{2,1,0:T(8,128)(2,1)}), bf16[8,64,1024]{2,1,0:T(8,128)(2,1)S(1)}, u32[]{:S(2)}, u32[]{:S(2)}) async-start(bf16[8,64,1024]{2,1,0:T(8,128)(2,1)} %pad_maximum_fusion.6), calls=%async_computation.8 | async-start | bytes 2097152 | tf_op jit(solution)/shard_map/all_to_all | solution.py:577
  352.5 18.1 %all-to-all-start.7 = ((bf16[8,64,512]{2,1,0:T(8,128)(2,1)}), bf16[8,64,512]{2,1,0:T(8,128)(2,1)S(1)}, u32[]{:S(2)}, u32[]{:S(2)}) async-start(bf16[8,64,512]{2,1,0:T(8,128)(2,1)} %broadcast_in_dim.64), calls=%async_computation.7 | async-start | bytes 1048576 | tf_op jit(solution)/shard_map/all_to_all | solution.py:572
  370.6 33.8 %copy-start.7 = (bf16[8,64,512]{2,1,0:T(8,128)(2,1)}, bf16[8,64,512]{2,1,0:T(8,128)(2,1)S(1)}, u32[]{:S(2)}) copy-start(bf16[8,64,512]{2,1,0:T(8,128)(2,1)S(1)} %all-to-all-done.7) | copy-start | bytes 1572868
  400.0 48.8 %all-to-all-start.4 = ((bf16[8,30,8,512]{3,2,1,0:T(8,128)(2,1)}), bf16[8,30,8,512]{3,2,1,0:T(8,128)(2,1)}, u32[]{:S(2)}, u32[]{:S(2)}) async-start(bf16[8,30,8,512]{3,2,1,0:T(8,128)(2,1)} %get-tuple-element.59), calls=%async_computation.4 | async-start | bytes 3932160 | tf_op jit(solution)/shard_map/all_to_all | solution.py:642
  407.7 1.2 collective-permute-start.15
  409.0 3.6 collective-permute-start.16
  422.2 30.7 %copy-start = (f32[512,512]{1,0:T(8,128)S(1)}, f32[512,512]{1,0:T(8,128)}, u32[]{:S(2)}) copy-start(f32[512,512]{1,0:T(8,128)} %get-tuple-element.91) | copy-start | bytes 3145732
  422.2 30.7 %copy-start.1 = (f32[512,512]{1,0:T(8,128)S(1)}, f32[512,512]{1,0:T(8,128)}, u32[]{:S(2)}) copy-start(f32[512,512]{1,0:T(8,128)} %get-tuple-element.92) | copy-start | bytes 3145732
  422.2 30.7 %collective-permute-start.19 = (f32[2,512,512]{2,1,0:T(8,128)}, f32[2,512,512]{2,1,0:T(8,128)}, u32[]{:S(2)}, u32[]{:S(2)}) collective-permute-start(f32[2,512,512]{2,1,0:T(8,128)} %pad_maximum_fusion.1), channel_id=1, source_target_pairs={{0,1},{1,0},{2,3},{3,2},{4,5},{5,4},{6,7},{7,6},{8,9},{9,8},{10,11... | collective-permute-start | bytes 6291464 | tf_op jit(solution)/shard_map/ppermute | solution.py:555
  448.9 35.2 %all-to-all-start.2 = ((bf16[8,20,8,512]{3,2,1,0:T(8,128)(2,1)}), bf16[8,20,8,512]{3,2,1,0:T(8,128)(2,1)S(1)}, u32[]{:S(2)}, u32[]{:S(2)}) async-start(bf16[8,20,8,512]{3,2,1,0:T(8,128)(2,1)} %get-tuple-element.58), calls=%async_computation.2 | async-start | bytes 2621440 | tf_op jit(solution)/shard_map/all_to_all | solution.py:642
  456.3 47.6 %collective-permute-start.20 = (f32[2,512,512]{2,1,0:T(8,128)}, f32[2,512,512]{2,1,0:T(8,128)}, u32[]{:S(2)}, u32[]{:S(2)}) collective-permute-start(f32[2,512,512]{2,1,0:T(8,128)} %fusion.21), channel_id=1, source_target_pairs={{0,2},{1,3},{2,0},{3,1},{4,6},{5,7},{6,4},{7,5},{8,10},{9,11},{10,... | collective-permute-start | bytes 6291464 | tf_op jit(solution)/shard_map/ppermute | solution.py:555
  459.7 29.3 %copy-start.12 = (f32[12,512]{1,0:T(8,128)S(1)}, f32[12,512]{1,0:T(8,128)}, u32[]{:S(2)}) copy-start(f32[12,512]{1,0:T(8,128)} %vec_ref.9) | copy-start | bytes 73732
  459.7 29.3 %copy-start.24 = (f32[12,512]{1,0:T(8,128)S(1)}, f32[12,512]{1,0:T(8,128)}, u32[]{:S(2)}) copy-start(f32[12,512]{1,0:T(8,128)} %param.28) | copy-start | bytes 73732
  459.7 29.3 %copy-start.25 = (f32[12,512]{1,0:T(8,128)S(1)}, f32[12,512]{1,0:T(8,128)}, u32[]{:S(2)}) copy-start(f32[12,512]{1,0:T(8,128)} %param.29) | copy-start | bytes 73732
  (15 other events, 37.7 us)

commit v3 on v2

--- a/solution.py
+++ b/solution.py
@@ -38,6 +38,7 @@
 CLIP_LIMIT = 1.0
 DECAY_KEEP = 1.0 - MUON_RATE * MUON_DECAY
 VMEM = 60 * 2**20
+BRIEF = pl.CostEstimate(flops=10**6, bytes_accessed=10**5, transcendentals=0)
 
 ERF_P = 0.3275911 * 0.5**0.5
 ERF = tuple(0.5 * c for c in (0.254829592, -0.284496736, 1.421413741, -1.453152027, 1.061405429))
@@ -186,7 +187,7 @@
         + [array((LIVE, windows, D), BF), array((windows, 4, ROWS, STACK), BF)],
         scratch_shapes=[pltpu.VMEM((4, count * ROWS, GROUP), F32)] * 4,
         compiler_params=pltpu.CompilerParams(vmem_limit_bytes=VMEM),
-        cost_estimate=pl.CostEstimate(flops=3 * 10**10, bytes_accessed=3 * 10**7, transcendentals=0),
+        cost_estimate=BRIEF,
         name="window_attention_forward",
     )(patches, region_rows, *weights, vec)
 
@@ -266,16 +267,16 @@
                    array((4, D, D), BF), array((3, 8, D), F32), array((4, 8, D), F32)],
         scratch_shapes=[pltpu.VMEM((4, D, D), F32), pltpu.VMEM((4, D, D), F32)],
         compiler_params=pltpu.CompilerParams(vmem_limit_bytes=VMEM),
-        cost_estimate=pl.CostEstimate(flops=4 * 10**10, bytes_accessed=3 * 10**7, transcendentals=0),
+        cost_estimate=BRIEF,
         name="mlp_forward_backward",
     )(x1, cot, *first, *second, vec, bias_first)
 
 
 def attn_bwd_kernel(count, batch, chunks, *refs):
-    p_ref, r_ref = refs[:2]
-    dx1_refs = refs[2 : 2 + chunks]
+    p_ref, r_ref, _ = refs[:3]
+    dx1_refs = refs[3 : 3 + chunks]
     (q_ref, k_ref, v_ref, o_ref, pt_ref, wq_ref, wk_ref, wv_ref, wo_ref, vec_ref,
-     dp_ref, dr_ref, dw_ref, dv_ref, dq_held, dk_held, dvv_held, do_held) = refs[2 + chunks :]
+     dp_ref, dr_ref, dw_ref, dv_ref, dq_held, dk_held, dvv_held, do_held) = refs[3 + chunks :]
     total = count * LIVE
 
     @pl.when(pl.program_id(0) == 0)
@@ -336,13 +337,14 @@
     dv_ref[4] += fold(dx1)
 
 
-def attn_bwd(patches, region_rows, dx1_parts, saved, weights, vec, count=16, batch=4):
+def attn_bwd(patches, region_rows, dx1_parts, saved, weights, vec, after, count=16, batch=4):
     windows = patches.shape[1]
     array = jax.ShapeDtypeStruct
     return pl.pallas_call(
         partial(attn_bwd_kernel, count, batch, len(dx1_parts)),
         grid=(windows // count,),
-        in_specs=[middle(PATCH, count), block((count, D))] + [middle(part.shape[0], count) for part in dx1_parts]
+        in_specs=[middle(PATCH, count), block((count, D)), pl.BlockSpec(memory_space=pl.ANY)]
+        + [middle(part.shape[0], count) for part in dx1_parts]
         + [block((count, ROWS, D))] * 3 + [middle(LIVE, count), block((count, 4, ROWS, STACK))]
         + [full((D, D))] * 4 + [full(vec.shape)],
         out_specs=[middle(PATCH, count), block((count, D)), full((4, D, D)), full((5, 8, D))],
@@ -350,9 +352,9 @@
                    array((4, D, D), F32), array((5, 8, D), F32)],
         scratch_shapes=[pltpu.VMEM((4, count * ROWS, GROUP), F32)] * 4,
         compiler_params=pltpu.CompilerParams(vmem_limit_bytes=VMEM),
-        cost_estimate=pl.CostEstimate(flops=4 * 10**10, bytes_accessed=5 * 10**7, transcendentals=0),
+        cost_estimate=BRIEF,
         name="window_attention_backward",
-    )(patches, region_rows, *dx1_parts, *saved, *weights, vec)
+    )(patches, region_rows, after, *dx1_parts, *saved, *weights, vec)
 
 
 def regional_fwd_kernel(canvas_ref, band_ref, ids_ref, band_ids_ref, wq_ref, wk_ref, wv_ref, wo_ref, vec_ref,
@@ -386,16 +388,19 @@
     r1_ref[...] = band + nn(mixed_ref[...].astype(BF), wo_ref[...]) + vec[6:7]
 
 
-def in_vmem(kernel, outs, name, *args):
+def in_vmem(kernel, outs, name, *args, after=()):
+    spaces = [pltpu.SMEM if arg.shape == (1, 1) else pltpu.VMEM for arg in args]
+    count = len(args)
     return pl.pallas_call(
-        kernel,
-        in_specs=[pl.BlockSpec(memory_space=pltpu.VMEM) for _ in args],
+        lambda *refs: kernel(*refs[:count], *refs[count + len(after) :]),
+        in_specs=[pl.BlockSpec(memory_space=space) for space in spaces]
+        + [pl.BlockSpec(memory_space=pl.ANY) for _ in after],
         out_specs=[pl.BlockSpec(memory_space=pltpu.VMEM) for _ in outs],
         out_shape=[jax.ShapeDtypeStruct(*out) for out in outs],
         compiler_params=pltpu.CompilerParams(vmem_limit_bytes=VMEM),
-        cost_estimate=pl.CostEstimate(flops=10**10, bytes_accessed=10**7, transcendentals=0),
+        cost_estimate=BRIEF,
         name=name,
-    )(*args)
+    )(*args, *after)
 
 
 def payload_kernel(dr_ref, mixed_ref, level_ref, wo_ref, grad_ref, extra_ref):
@@ -410,7 +415,13 @@
     delta = nn(high, pick) + (nn(low_part, pick) + nn(rest, pick))
     top = delta.astype(BF).astype(F32)
     lane = lax.broadcasted_iota(jnp.int32, (1, GROUP), 1)
-    extra = jnp.where(lane < HEADS, top, jnp.where(lane < 2 * HEADS, delta - top, level_ref[...]))
+    level = level_ref[...]
+    level_top = level.astype(BF).astype(F32)
+    level_rest = level - level_top
+    level_mid = level_rest.astype(BF).astype(F32)
+    extra = level_rest - level_mid
+    for place, term in ((4, level_mid), (3, level_top), (2, delta - top), (1, top)):
+        extra = jnp.where(lane < place * HEADS, term, extra)
     extra_ref[...] = extra.astype(BF)
 
 
@@ -466,15 +477,26 @@
     return high, (a - high.astype(F32)).astype(BF)
 
 
-def product(a, b, passes, dot=nn):
-    if passes == 1:
-        return dot(a.astype(BF), b.astype(BF))
-    (ah, al), (bh, bl) = halves(a), halves(b)
-    return dot(ah, bh) + (dot(ah, bl) + dot(al, bh))
+def terms(a, passes):
+    return (a.astype(BF),) if passes == 1 else halves(a)
+
+
+def product(a, b, dot=nn):
+    if len(a) == 1:
+        return dot(a[0], b[0])
+    return dot(a[0], b[0]) + (dot(a[0], b[1]) + dot(a[1], b[0]))
+
+
+def symmetric(a, b, dot=nn):
+    half = D // 2
+    right = (lambda x: x[half:]) if dot is nt else (lambda x: x[:, half:])
+    top = product([x[:half] for x in a], b, dot)
+    corner = product([x[half:] for x in a], [right(x) for x in b], dot)
+    return jnp.concatenate([top, jnp.concatenate([top[:, half:].T, corner], axis=1)], axis=0)
 
 
 DIRECT_STEPS = (1, 1, 1, -1, -1)
-GRAM_STEPS = (3, 3, 3, 3, -1)
+GRAM_STEPS = (1, 1, 3, 3, 3)
 NEAR_ZERO = NS_FIRST + NS_SECOND + NS_THIRD
 NEAR_ONE = NS_SECOND + 2.0 * NS_THIRD
 
@@ -486,69 +508,95 @@
 
 def polynomial(gram, eye, step):
     if step > 0:
-        return NS_FIRST, NS_SECOND * gram + NS_THIRD * product(gram, gram, step)
+        parts = terms(gram, step)
+        return NS_FIRST, NS_SECOND * gram + NS_THIRD * symmetric(parts, parts)
     rest = gram - jnp.where(eye, 1.0, 0.0)
-    return NEAR_ZERO, NEAR_ONE * rest + NS_THIRD * product(rest, rest, -step)
-
-
-def moments_kernel(clip_ref, g1_ref, g2_ref, m1_ref, m2_ref, n1_ref, n2_ref, gram1_ref, gram2_ref):
-    clip = clip_ref[0, 0]
-    first = MUON_MOMENTUM * m1_ref[...] + clip * g1_ref[...].astype(F32)
-    n1_ref[...] = first
-    gram1_ref[...] = product(first, first, 3, nt)
-    second = MUON_MOMENTUM * m2_ref[...] + clip * g2_ref[...].astype(F32).T
-    n2_ref[...] = second
-    gram2_ref[...] = product(second, second, 3, tn)
-
-
-def square_kernel(clip_ref, g_ref, m_ref, w_ref, n_ref, new_ref):
-    moment = MUON_MOMENTUM * m_ref[...] + clip_ref[0, 0] * g_ref[...].astype(F32)
-    n_ref[...] = moment
+    parts = terms(rest, -step)
+    return NEAR_ZERO, NEAR_ONE * rest + NS_THIRD * symmetric(parts, parts)
+
+
+def direct_steps(moment, eye):
     z = moment * (1.0 / (jnp.sqrt(jnp.sum(moment * moment)) + 1e-07))
-    eye = identity()
     for step in DIRECT_STEPS:
-        scale, poly = polynomial(product(z, z, abs(step), nt), eye, step)
-        z = scale * z + product(poly, z, abs(step))
-    new_ref[...] = w_ref[...] * DECAY_KEEP - MUON_RATE * z
-
-
-def gram_steps(gram):
-    eye = identity()
+        parts = terms(z, abs(step))
+        gram = symmetric(parts, parts, nt)
+        yield
+        scale, poly = polynomial(gram, eye, step)
+        yield
+        z = scale * z + product(terms(poly, abs(step)), parts)
+        yield
+    return z
+
+
+def gram_steps(gram, eye):
     factor = 1.0 / (jnp.sqrt(jnp.sum(jnp.where(eye, gram, 0.0))) + 1e-07)
     gram = gram * (factor * factor)
     steps = None
-    for n, step in enumerate(GRAM_STEPS):
-        scale, poly = polynomial(gram, eye, step)
+    for n, passes in enumerate(GRAM_STEPS):
+        scale, poly = polynomial(gram, eye, passes)
+        yield
+        parts = terms(poly, passes)
         if steps is None:
             steps = jnp.where(eye, scale, 0.0) + poly
         else:
-            steps = scale * steps + product(poly, steps, abs(step))
+            steps = scale * steps + symmetric(parts, terms(steps, passes))
+            yield
         if n < len(GRAM_STEPS) - 1:
-            half = scale * gram + product(poly, gram, step)
-            gram = scale * half + product(poly, half, step)
+            half = scale * gram + symmetric(parts, terms(gram, passes))
+            yield
+            gram = scale * half + symmetric(parts, terms(half, passes))
+            yield
     return steps * factor
 
 
-def sharded_kernel(gram1_ref, gram2_ref, n1_ref, n2_ref, w1_ref, w2_ref, new1_ref, new2_ref):
-    z = product(gram_steps(gram1_ref[...]), n1_ref[...], 3)
+def in_turns(*chains):
+    results = [None] * len(chains)
+    running = list(enumerate(chains))
+    while running:
+        still = []
+        for n, chain in running:
+            try:
+                next(chain)
+                still.append((n, chain))
+            except StopIteration as stop:
+                results[n] = stop.value
+        running = still
+    return results
+
+
+def grams_kernel(*refs):
+    for n in range(2):
+        old, mixed, new = (jnp.zeros((D, D), F32) for _ in range(3))
+        cross = jnp.zeros((D, D), F32)
+        for j in range(4):
+            high, low = halves(refs[4 * n + j][...])
+            if n == 1:
+                high, low = high.T, low.T
+            g = refs[8 + j][:, n * D : (n + 1) * D]
+            old = old + nt(high, high)
+            cross = cross + nt(high, low)
+            mixed = mixed + (nt(high, g) + nt(low, g))
+            new = new + nt(g, g)
+        for k, x in enumerate((old + (cross + cross.T), mixed + mixed.T, new)):
+            refs[12 + 3 * n + k][...] = x
+
+
+def update_kernel(clip_ref, ga_ref, ma_ref, wa_ref, g_ref, m1_ref, m2_ref, w1_ref, w2_ref,
+                  old1, mixed1, new1, old2, mixed2, new2, na_ref, newa_ref, n1_ref, new1_ref, n2_ref, new2_ref):
+    clip = clip_ref[0, 0]
+    eye = identity()
+    na_ref[...] = MUON_MOMENTUM * ma_ref[...] + clip * ga_ref[...].astype(F32)
+    n1_ref[...] = MUON_MOMENTUM * m1_ref[...] + clip * g_ref[:, :D].astype(F32)
+    n2_ref[...] = MUON_MOMENTUM * m2_ref[...] + clip * g_ref[:, D:].astype(F32).T
+    a, b, c = MUON_MOMENTUM * MUON_MOMENTUM, MUON_MOMENTUM * clip, clip * clip
+    gram1 = a * old1[...] + b * mixed1[...] + c * new1[...]
+    gram2 = a * old2[...] + b * mixed2[...] + c * new2[...]
+    steps1, steps2, z = in_turns(gram_steps(gram1, eye), gram_steps(gram2, eye), direct_steps(na_ref[...], eye))
+    newa_ref[...] = wa_ref[...] * DECAY_KEEP - MUON_RATE * z
+    z = product(halves(steps1), halves(n1_ref[...]))
     new1_ref[...] = w1_ref[...] * DECAY_KEEP - MUON_RATE * z
-    z = product(n2_ref[...], gram_steps(gram2_ref[...]), 3)
+    z = product(halves(n2_ref[...]), halves(steps2))
     new2_ref[...] = w2_ref[...] * DECAY_KEEP - (MUON_RATE * max(1.0, FF / D) ** 0.5) * z
-
-
-def whole_call(kernel, outs, name, *args):
-    in_specs = [pl.BlockSpec(memory_space=pltpu.VMEM) for _ in args]
-    if args[0].shape == (1, 1):
-        in_specs[0] = pl.BlockSpec(memory_space=pltpu.SMEM)
-    return pl.pallas_call(
-        kernel,
-        in_specs=in_specs,
-        out_specs=[pl.BlockSpec(memory_space=pltpu.VMEM) for _ in outs],
-        out_shape=[jax.ShapeDtypeStruct((D, D), dtype) for dtype in outs],
-        compiler_params=pltpu.CompilerParams(vmem_limit_bytes=VMEM),
-        cost_estimate=pl.CostEstimate(flops=10**10, bytes_accessed=10**7, transcendentals=0),
-        name=name,
-    )(*args)
 
 
 def pair(values, bit):
@@ -572,10 +620,34 @@
     return lax.all_to_all(copies, "dp", 0, 0, tiled=True)
 
 
+def swap(x, bit):
+    return lax.ppermute(x, "dp", [(i, i ^ bit) for i in range(lax.axis_size("dp"))])
+
+
+def bits():
+    return [1 << n for n in range(lax.axis_size("dp").bit_length() - 1)]
+
+
 def sum_over_dp(x):
-    parts = x.reshape((lax.axis_size("dp"), -1) + x.shape[1:])
-    parts = lax.all_to_all(parts, "dp", 0, 0, tiled=True)
-    return share(jnp.sum(parts.astype(F32), axis=0).astype(BF)).reshape(x.shape)
+    index = lax.axis_index("dp")
+    for bit in bits():
+        half = x.shape[0] // 2
+        side = (index // bit) % 2
+        give = lax.dynamic_slice_in_dim(x, (1 - side) * half, half, 0)
+        keep = lax.dynamic_slice_in_dim(x, side * half, half, 0)
+        x = keep + swap(give.astype(BF), bit).astype(F32)
+    x = x.astype(BF)
+    for bit in reversed(bits()):
+        other = swap(x, bit)
+        side = (index // bit) % 2
+        x = jnp.where(side == 0, jnp.concatenate([x, other]), jnp.concatenate([other, x]))
+    return x
+
+
+def sum_small_over_dp(x):
+    for bit in bits():
+        x = x + swap(x, bit)
+    return x
 
 
 def split_heads(x):
@@ -669,11 +741,7 @@
     else:
         region_rows, mixed, level, reg_q, reg_k, reg_v = regional_forward(
             canvas, band, band_ids[:, None] == ids[None, :], weights, vec)
-    level = level.T
-    level_high = level.astype(BF).astype(F32)
-    level_mid = (level - level_high).astype(BF).astype(F32)
-    level_parts = jnp.concatenate([level_high, level_mid, level - level_high - level_mid], axis=1)
-    level_parts = jnp.pad(level_parts, ((0, 0), (2 * HEADS, GROUP - 5 * HEADS)))
+    level_wide = jnp.tile(level.T, (1, GROUP // HEADS))
 
     windows = patches[0, 0].transpose(1, 0, 2)
     x1, *saved = attn_fwd(windows, region_rows, weights, vec)
@@ -681,16 +749,20 @@
     moved = [move(o[0]) for o in outs]
     out_patches = jnp.concatenate([moved[0], moved[1][:, : PATCH - split]], axis=1).transpose(0, 2, 1, 3)[None]
     out_regions = moved[1][None, :, PATCH - split]
-    d_patches, d_region, d_attn, d_vec_attn = attn_bwd(windows, region_rows, [o[1] for o in outs], saved, weights, vec)
+    d_patches, d_region, d_attn, d_vec_attn = attn_bwd(windows, region_rows, [o[1] for o in outs],
+                                                     saved, weights, vec, moved[0])
     d_patches = d_patches.transpose(1, 0, 2)[None, None]
 
     add = lambda n, j: (outs[0][n][j].astype(F32) + outs[1][n][j].astype(F32)).astype(BF)
     own_first = sum_at_owner([add(2, j) for j in range(OPT)])
     own_second = sum_at_owner([add(3, j) for j in range(OPT)])
-    own_mlp = sum_over_dp(jnp.concatenate([own_first, own_second], axis=1).astype(BF))
+    own_mlp = sum_over_dp(jnp.concatenate([own_first, own_second], axis=1))
+    grams = in_vmem(grams_kernel, [((D, D), F32)] * 6, "mlp_grams", *pieces_of_owners(mlp_in_mom),
+                    *pieces_of_owners(mlp_out_mom), *pieces_of_owners(own_mlp))
 
     band_grad, extra = in_vmem(payload_kernel, [((grid_cols, D), BF), ((grid_cols, GROUP), BF)],
-                               "regional_payload", d_region, mixed, level_parts, weights[3])
+                               "regional_payload", d_region, mixed, level_wide, weights[3],
+                               after=(own_first, own_second, moved[1]))
     payload = share(jnp.concatenate([band_grad, extra], axis=1)).reshape(grid_rows, dp_size, cols, D + GROUP)
     payload = payload.transpose(1, 0, 2, 3).reshape(tokens, D + GROUP)
     grads = payload[:, :D]
@@ -714,7 +786,7 @@
     d_regions = d_regions.reshape(regions.shape)
 
     pieces = [lax.dynamic_index_in_dim(grad_attn, opt_index ^ j, 0, keepdims=False) for j in range(OPT)]
-    own_attn = sum_over_dp(sum_at_owner(pieces).astype(BF))
+    own_attn = sum_over_dp(sum_at_owner(pieces))
 
     d_vec_attn = jnp.sum(d_vec_attn + d_vec_reg, axis=1)
     d_vec_mlp = jnp.sum(outs[0][4] + outs[1][4], axis=1)
@@ -722,7 +794,7 @@
     grad_vec = jnp.concatenate([d_vec_attn[:2], d_vec_mlp[:2], d_vec_attn[2:], d_vec_mlp[2:], d_bias_first])
     grad_vec = grad_vec + pair(grad_vec, 1)
     grad_vec = grad_vec + pair(grad_vec, 2)
-    grad_vec = jnp.sum(share(grad_vec), axis=0)
+    grad_vec = sum_small_over_dp(grad_vec)
 
     squares = lambda x: jnp.sum(x.astype(F32) ** 2)
     total = jnp.full((8, 128), squares(own_attn) + squares(own_mlp))
@@ -730,17 +802,9 @@
     total = total + pair(total, 2)
     grad_norm = jnp.sqrt(total[0, 0] + squares(grad_vec))
     clip = jnp.minimum(1.0, CLIP_LIMIT / (grad_norm + 1e-06))
-    clip_cell = clip.reshape(1, 1)
-    first_mom, second_mom, gram_first, gram_second = whole_call(
-        moments_kernel, [F32, F32, F32, F32], "mlp_moments", clip_cell,
-        own_mlp[:, :D], own_mlp[:, D:], mlp_in_mom, mlp_out_mom)
-    grams = jnp.stack([gram_first, gram_second])
-    grams = grams + pair(grams, 1)
-    grams = grams + pair(grams, 2)
-    attn_mom_new, new_attn = whole_call(
-        square_kernel, [F32, F32], "attention_update", clip_cell, own_attn, attn_mom[0], attn_w[0])
-    new_first, new_second = whole_call(
-        sharded_kernel, [F32, F32], "mlp_update", grams[0], grams[1], first_mom, second_mom, mlp_in, mlp_out)
+    attn_mom_new, new_attn, first_mom, new_first, second_mom, new_second = in_vmem(
+        update_kernel, [((D, D), F32)] * 6, "matrix_updates", clip.reshape(1, 1), own_attn, attn_mom[0], attn_w[0],
+        own_mlp, mlp_in_mom, mlp_out_mom, mlp_in, mlp_out, *grams)
     clipped = clip * grad_vec
     moment_one = BETA_FIRST * adam_first + (1.0 - BETA_FIRST) * clipped
     moment_two = BETA_SECOND * adam_second + (1.0 - BETA_SECOND) * clipped * clipped

time: 552 us -> 527 us (0.955)
  blocking collectives: 29.3 us -> 0 us
  starting transfers between devices: 56.5 us -> 67.5 us
  waiting for transfers between devices: 151 us -> 162 us
  other arithmetic: 47.9 us -> 37.4 us
  local copies, waits for them, and re-layouts: 36.2 us -> 30.6 us
    ppermute x0 -> x15, waiting for transfers between devices: none -> 51.3 us  [swap(): lax.ppermute(x, 'dp', [(i, i ^ bit) for i in range(lax.axis_size('dp'))])]
    all_to_all x4, waiting for transfers between devices: 68.5 us -> 28.4 us  [per_device(): move = lambda x: lax.all_to_all(x, 'dp', 0, 0, tiled=True)]
    ppermute x21 -> x28, waiting for transfers between devices: 31.1 us -> 61.1 us  [pair(): return lax.ppermute(values, 'opt', [(i, i ^ bit) for i in range(OPT)])]
    all_to_all x1 -> x0, blocking collectives: 29.3 us -> none  [share(): return lax.all_to_all(copies, 'dp', 0, 0, tiled=True)]
    all_to_all x2 -> x0, waiting for transfers between devices: 25.4 us -> none  [sum_over_dp(): parts = lax.all_to_all(parts, 'dp', 0, 0, tiled=True)]
    ppermute x0 -> x15, starting transfers between devices: none -> 18.7 us  [swap(): lax.ppermute(x, 'dp', [(i, i ^ bit) for i in range(lax.axis_size('dp'))])]
    all_to_all x2 -> x0, starting transfers between devices: 7.35 us -> none  [sum_over_dp(): parts = lax.all_to_all(parts, 'dp', 0, 0, tiled=True)]
    another operation x3 -> x0, other arithmetic: 6.62 us -> none
  transfers between devices with their start and end apart: 31 -> 49, of which waited for: 16 -> 23; matrix products, arithmetic and copies ran while one was open for 13% -> 11% of each run, Pallas kernels for 17% -> 36%
where the time goes in v3:
time: 527 us; the launch traced here: 520 us
  Pallas kernels  218 us (41%)
  waiting for transfers between devices  162 us (31%)
  starting transfers between devices  67.5 us (13%)
  other arithmetic  37.4 us (7%)
  local copies, waits for them, and re-layouts  30.6 us (6%)
  between operations  5.53 us (1%)
    pallas_call x2, Pallas kernels, mlp(): pl.pallas_call(partial(mlp_kernel, many, sources, cols, steps, lanes), gr...  66.4 us
    pallas_call x5, Pallas kernels, in_vmem(): pl.pallas_call(lambda *refs: kernel(*refs[:count], *refs[count + len(afte...  63.7 us
    ppermute x28, waiting for transfers between devices, pair(): return lax.ppermute(values, 'opt', [(i, i ^ bit) for i in range(OPT)])  61.1 us
    pallas_call x1, Pallas kernels, attn_bwd(): pl.pallas_call(partial(attn_bwd_kernel, count, batch, len(dx1_parts)), gr...  52.4 us
    ppermute x15, waiting for transfers between devices, swap(): lax.ppermute(x, 'dp', [(i, i ^ bit) for i in range(lax.axis_size('dp'))])  51.3 us
    pallas_call x1, Pallas kernels, attn_fwd(): pl.pallas_call(partial(attn_fwd_kernel, count, batch), grid=(windows // c...  35.2 us
    all_to_all x4, waiting for transfers between devices, per_device(): move = lambda x: lax.all_to_all(x, 'dp', 0, 0, tiled=True)  28.4 us
    all_to_all x2, waiting for transfers between devices, share(): return lax.all_to_all(copies, 'dp', 0, 0, tiled=True)  20.7 us
  transfers between devices with their start and end apart: 49, of which 23 were waited for; matrix products, arithmetic and copies ran while one was open for 11% of the time, Pallas kernels for 36%

profile of v3, /device:TPU:0, one launch (start us, length us, event | category | flops | bytes accessed | tf_op | source)
XLA Modules:
  0.0 520.2 jit_solution(7225835486417895439)
XLA Ops:
  2.3 7.3 %all-to-all-start = ((bf16[8,8,8,512]{3,2,1,0:T(8,128)(2,1)}), bf16[8,8,8,512]{3,2,1,0:T(8,128)(2,1)S(1)}, u32[]{:S(2)}, u32[]{:S(2)}) async-start(bf16[8,8,8,512]{3,2,1,0:T(8,128)(2,1)} %broadcast_in_dim.41), calls=%async_computation | async-start | bytes 1048576 | tf_op jit(solution)/shard_map/all_to_all | solution.py:620
  9.6 2.5 slice.160
  12.0 12.0 %all-to-all-done = bf16[8,8,8,512]{3,2,1,0:T(8,128)(2,1)S(1)} async-done(((bf16[8,8,8,512]{3,2,1,0:T(8,128)(2,1)}), bf16[8,8,8,512]{3,2,1,0:T(8,128)(2,1)S(1)}, u32[]{:S(2)}, u32[]{:S(2)}) %all-to-all-start) | async-done | bytes 524320 | tf_op jit(solution)/shard_map/all_to_all | solution.py:620
  24.9 3.6 all-to-all-start.1
  31.6 28.4 %all-to-all-done.1.pc_ref = bf16[8,20,8,512]{3,2,1,0:T(8,128)(2,1)S(1)} async-done(((bf16[8,20,8,512]{3,2,1,0:T(8,128)(2,1)}), bf16[8,20,8,512]{3,2,1,0:T(8,128)(2,1)S(1)}, u32[]{:S(2)}, u32[]{:S(2)}) %all-to-all-start.1) | async-done | bytes 1310752 | tf_op jit(solution)/shard_map/all_to_all | solution.py:714
  60.1 4.3 all-to-all-start.3
  70.2 10.3 %collective-permute-done.1 = bf16[512,512]{1,0:T(8,128)(2,1)S(1)} collective-permute-done((bf16[512,512]{1,0:T(8,128)(2,1)}, bf16[512,512]{1,0:T(8,128)(2,1)S(1)}, u32[]{:S(2)}, u32[]{:S(2)}) %collective-permute-start.1) | collective-permute-done | bytes 524320 | tf_op jit(solution)/shard_map/ppermute | solution.py:603
  81.8 10.1 %collective-permute-done.4.w1c = bf16[512,512]{1,0:T(8,128)(2,1)} collective-permute-done((bf16[512,512]{1,0:T(8,128)(2,1)S(1)}, bf16[512,512]{1,0:T(8,128)(2,1)}, u32[]{:S(2)}, u32[]{:S(2)}) %collective-permute-start.4) | collective-permute-done | bytes 524320 | tf_op jit(solution)/shard_map/ppermute | solution.py:603
  91.9 9.2 %collective-permute-done.7.w2c = bf16[512,512]{1,0:T(8,128)(2,1)} collective-permute-done((bf16[512,512]{1,0:T(8,128)(2,1)S(1)}, bf16[512,512]{1,0:T(8,128)(2,1)}, u32[]{:S(2)}, u32[]{:S(2)}) %collective-permute-start.7) | collective-permute-done | bytes 524320 | tf_op jit(solution)/shard_map/ppermute | solution.py:603
  105.0 1.8 pad_maximum_fusion
  108.1 5.2 regional_attention_forward.1
  113.3 35.2 %window_attention_forward.1 = (f32[50,64,512]{2,1,0:T(8,128)}, bf16[64,56,512]{2,1,0:T(8,128)(2,1)}, bf16[64,56,512]{2,1,0:T(8,128)(2,1)}, bf16[64,56,512]{2,1,0...) custom-call(bf16[49,64,512]{2,1,0:T(8,128)(2,1)} %bitcast.78, ...), custom_call_target="tpu_custom_call" | custom-call | flops 1000000 | bytes 100000 | tf_op jit(solution)/shard_map/window_attention_forward/pallas_call | solution.py:180
  148.5 28.0 %mlp_forward_backward.2 = (bf16[8,20,8,512]{3,2,1,0:T(8,128)(2,1)}, f32[20,64,512]{2,1,0:T(8,128)}, bf16[4,512,512]{2,1,0:T(8,128)(2,1)}, bf16[4,512,512]{2,1,0:...) custom-call(f32[50,64,512]{2,1,0:T(8,128)} %get-tuple-element.61.x1_ref, bf16[8,20,8,512]{3,2,1,0:T(8,128)(2,1)} %copy-done.9, ...), custom_call_target="tpu_custom_call" | custom-call | flops 1000000 | bytes 100000 | tf_op jit(solution)/shard_map/mlp_forward_backward/pallas_call | solution.py:260
  176.6 6.3 %all-to-all-start.2 = ((bf16[8,20,8,512]{3,2,1,0:T(8,128)(2,1)}), bf16[8,20,8,512]{3,2,1,0:T(8,128)(2,1)S(1)}, u32[]{:S(2)}, u32[]{:S(2)}) async-start(bf16[8,20,8,512]{3,2,1,0:T(8,128)(2,1)} %get-tuple-element.62), calls=%async_computation.2 | async-start | bytes 2621440 | tf_op jit(solution)/shard_map/all_to_all | solution.py:714
  182.8 38.4 %mlp_forward_backward.3 = (bf16[8,30,8,512]{3,2,1,0:T(8,128)(2,1)}, f32[30,64,512]{2,1,0:T(8,128)}, bf16[4,512,512]{2,1,0:T(8,128)(2,1)}, bf16[4,512,512]{2,1,0:...) custom-call(f32[50,64,512]{2,1,0:T(8,128)} %get-tuple-element.61.x1_ref, ...), custom_call_target="tpu_custom_call" | custom-call | flops 1000000 | bytes 100000 | tf_op jit(solution)/shard_map/mlp_forward_backward/pallas_call | solution.py:260
  221.2 6.2 %all-to-all-start.4 = ((bf16[8,30,8,512]{3,2,1,0:T(8,128)(2,1)}), bf16[8,30,8,512]{3,2,1,0:T(8,128)(2,1)S(1)}, u32[]{:S(2)}, u32[]{:S(2)}) async-start(bf16[8,30,8,512]{3,2,1,0:T(8,128)(2,1)} %get-tuple-element.63), calls=%async_computation.4 | async-start | bytes 3932160 | tf_op jit(solution)/shard_map/all_to_all | solution.py:714
  227.5 2.0 add_convert_fusion.2
  232.6 3.0 fusion.14
  240.1 52.4 %window_attention_backward.1 = (bf16[49,64,512]{2,1,0:T(8,128)(2,1)}, f32[64,512]{1,0:T(8,128)}, f32[4,512,512]{2,1,0:T(8,128)}, f32[5,8,512]{2,1,0:T(8,128)}) custom-call(bf16[49,64,512]{2,1,0:T(8,128)(2,1)} %bitcast.79, f32[64,512]{1,0:T(8,128)} %get-tuple-element.60.r_ref.refs_1_, bf16[8,20,8,512]{3,2,1,0:T(8,128)(2,1)} %copy-done.4, ...), custom_call_target="tpu_custom_call" | custom-call | flops 1000000 | bytes 100000 | tf_op jit(solution)/shard_map/window_attention_backward/pallas_call | solution.py:343
  292.6 2.9 fusion.9.refs_5_
  295.5 2.5 fusion.12.refs_4_
  299.2 2.3 regional_payload.1
  303.4 6.2 %all-to-all-start.5 = ((bf16[8,64,640]{2,1,0:T(8,128)(2,1)}), bf16[8,64,640]{2,1,0:T(8,128)(2,1)S(1)}, u32[]{:S(2)}, u32[]{:S(2)}) async-start(bf16[8,64,640]{2,1,0:T(8,128)(2,1)} %broadcast_in_dim.44), calls=%async_computation.5 | async-start | bytes 1310720 | tf_op jit(solution)/shard_map/all_to_all | solution.py:620
  315.7 2.0 collective-permute-start.21
  317.7 8.7 %all-to-all-done.5 = bf16[8,64,640]{2,1,0:T(8,128)(2,1)S(1)} async-done(((bf16[8,64,640]{2,1,0:T(8,128)(2,1)}), bf16[8,64,640]{2,1,0:T(8,128)(2,1)S(1)}, u32[]{:S(2)}, u32[]{:S(2)}) %all-to-all-start.5) | async-done | bytes 655392 | tf_op jit(solution)/shard_map/all_to_all | solution.py:620
  330.6 9.4 %regional_attention_backward.1 = (f32[64,512]{1,0:T(8,128)}, bf16[4,512,512]{2,1,0:T(8,128)(2,1)}, f32[5,8,512]{2,1,0:T(8,128)}) custom-call(bf16[512,512]{1,0:T(8,128)(2,1)} %get-tuple-element.72.refs_0_, bf16[512,512]{1,0:T(8,128)(2,1)} %get-tuple-element.73.refs_1_, bf16[512,512]{1,0:T(8,128)(2,1)} %get-tuple-element.74.refs_2_, ...), custom_call_target="tpu_custom_call" | custom-call | flops 1000000 | bytes 100000 | tf_op jit(solution)/shard_map/regional_attention_backward/pallas_call | solution.py:394
  344.2 8.0 %collective-permute-done.22 = bf16[128,1024]{1,0:T(8,128)(2,1)S(1)} collective-permute-done((bf16[128,1024]{1,0:T(8,128)(2,1)S(1)}, bf16[128,1024]{1,0:T(8,128)(2,1)S(1)}, u32[]{:S(2)}, u32[]{:S(2)}) %collective-permute-start.22) | collective-permute-done | bytes 262176 | tf_op jit(solution)/shard_map/ppermute | solution.py:624
  354.7 2.1 fusion.15
  358.3 3.0 collective-permute-done.23
  365.1 4.9 collective-permute-done.24
  370.1 1.8 collective-permute-done.14
  374.9 3.4 collective-permute-done.25
  378.5 1.8 collective-permute-start.26
  380.6 11.1 %collective-permute-done.26 = bf16[256,1024]{1,0:T(8,128)(2,1)S(1)} collective-permute-done((bf16[256,1024]{1,0:T(8,128)(2,1)S(1)}, bf16[256,1024]{1,0:T(8,128)(2,1)S(1)}, u32[]{:S(2)}, u32[]{:S(2)}) %collective-permute-start.26) | collective-permute-done | bytes 524320 | tf_op jit(solution)/shard_map/ppermute | solution.py:624
  392.9 2.2 multiply_reduce_fusion
  398.3 2.3 collective-permute-start.17
  400.7 2.8 collective-permute-done.17
  404.8 2.3 collective-permute-start.18
  407.1 4.1 collective-permute-done.18
  411.8 26.9 %collective-permute-done.30 = f32[12,512]{1,0:T(8,128)S(1)} collective-permute-done((f32[12,512]{1,0:T(8,128)S(1)}, f32[12,512]{1,0:T(8,128)S(1)}, u32[]{:S(2)}, u32[]{:S(2)}) %collective-permute-start.30) | collective-permute-done | bytes 24608 | tf_op jit(solution)/shard_map/ppermute | solution.py:603
  440.6 3.1 collective-permute-done.19
  445.2 2.6 collective-permute-done.31
  451.3 2.9 collective-permute-done.20
  458.1 3.5 maximum_bitcast_fusion
  461.6 2.1 collective-permute-start.33
  463.7 3.5 collective-permute-done.33
  469.4 17.4 %mlp_grams.1 = (f32[512,512]{1,0:T(8,128)}, f32[512,512]{1,0:T(8,128)}, f32[512,512]{1,0:T(8,128)}, f32[512,512]{1,0:T(8,128)}, f32[512,512]{1,0:T(8,128)}, /*index=5*/f32[512,512]{1,0:T(8,128)}) custom-call(f32[512,512]{1,0:T(8,128)} %refs_5_.1, f32[512,512]{1,0:T(8,128)} %collective-permute-done.34.refs_1_, f32[512,512]{1,0:T(8,128)} %collective-permute-done.35.refs_2_, ...), custom_call_target="tpu_custom_call" | custom-call | flops 1000000 | bytes 100000 | tf_op jit(solution)/shard_map/mlp_grams/pallas_call | solution.py:394
  489.4 29.5 %matrix_updates.1 = (f32[512,512]{1,0:T(8,128)}, f32[512,512]{1,0:T(8,128)}, f32[512,512]{1,0:T(8,128)}, f32[512,512]{1,0:T(8,128)}, f32[512,512]{1,0:T(8,128)}, /*index=5*/f32[512,512]{1,0:T(8,128)}) custom-call(f32[1,1]{1,0:T(1,128)} %bitcast.42.refs_0_, bf16[512,512]{1,0:T(8,128)(2,1)} %get-tuple-element.113.refs_1_, f32[512,512]{1,0:T(8,128)} %bitcast.90, ...), custom_call_target="tpu_custom_call" | custom-call | flops 1000000 | bytes 100000 | tf_op jit(solution)/shard_map/matrix_updates/pallas_call | solution.py:394
  (240 shorter events, 73.2 us)
Async XLA Ops:
  2.3 21.7 %all-to-all-start = ((bf16[8,8,8,512]{3,2,1,0:T(8,128)(2,1)}), bf16[8,8,8,512]{3,2,1,0:T(8,128)(2,1)S(1)}, u32[]{:S(2)}, u32[]{:S(2)}) async-start(bf16[8,8,8,512]{3,2,1,0:T(8,128)(2,1)} %broadcast_in_dim.41), calls=%async_computation | async-start | bytes 1048576 | tf_op jit(solution)/shard_map/all_to_all | solution.py:620
  24.9 35.2 %all-to-all-start.1 = ((bf16[8,20,8,512]{3,2,1,0:T(8,128)(2,1)}), bf16[8,20,8,512]{3,2,1,0:T(8,128)(2,1)S(1)}, u32[]{:S(2)}, u32[]{:S(2)}) async-start(bf16[8,20,8,512]{3,2,1,0:T(8,128)(2,1)} %slice.160), calls=%async_computation.1 | async-start | bytes 2621440 | tf_op jit(solution)/shard_map/all_to_all | solution.py:714
  60.1 116.5 %all-to-all-start.3 = ((bf16[8,30,8,512]{3,2,1,0:T(8,128)(2,1)}), bf16[8,30,8,512]{3,2,1,0:T(8,128)(2,1)}, u32[]{:S(2)}, u32[]{:S(2)}) async-start(bf16[8,30,8,512]{3,2,1,0:T(8,128)(2,1)} %pad_maximum_fusion.1), calls=%async_computation.3 | async-start | bytes 3932160 | tf_op jit(solution)/shard_map/all_to_all | solution.py:714
  65.5 15.1 %collective-permute-start.1 = (bf16[512,512]{1,0:T(8,128)(2,1)}, bf16[512,512]{1,0:T(8,128)(2,1)S(1)}, u32[]{:S(2)}, u32[]{:S(2)}) collective-permute-start(bf16[512,512]{1,0:T(8,128)(2,1)} %get-tuple-element.125), channel_id=1, source_target_pairs={{0,2},{1,3},{2,0},{3,1},{4,6},{5,7},{6,4},{7,5},{8,10},{9,11},{10,... | collective-permute-start | bytes 1572872 | tf_op jit(solution)/shard_map/ppermute | solution.py:603
  67.0 14.3 %collective-permute-start = (bf16[512,512]{1,0:T(8,128)(2,1)}, bf16[512,512]{1,0:T(8,128)(2,1)S(1)}, u32[]{:S(2)}, u32[]{:S(2)}) collective-permute-start(bf16[512,512]{1,0:T(8,128)(2,1)} %get-tuple-element.125), channel_id=1, source_target_pairs={{0,1},{1,0},{2,3},{3,2},{4,5},{5,4},{6,7},{7,6},{8,9},{9,8},{10,11... | collective-permute-start | bytes 1572872 | tf_op jit(solution)/shard_map/ppermute | solution.py:603
  67.1 24.8 %collective-permute-start.4 = (bf16[512,512]{1,0:T(8,128)(2,1)S(1)}, bf16[512,512]{1,0:T(8,128)(2,1)}, u32[]{:S(2)}, u32[]{:S(2)}) collective-permute-start(bf16[512,512]{1,0:T(8,128)(2,1)S(1)} %convert_element_type.223.w1a), channel_id=1, source_target_pairs={{0,2},{1,3},{2,0},{3,1},{4,6},{5,7},{6,4},{7,5},{8,10},{9,11},{10,... | collective-permute-start | bytes 1572872 | tf_op jit(solution)/shard_map/ppermute | solution.py:603
  67.7 80.8 %collective-permute-start.3 = (bf16[512,512]{1,0:T(8,128)(2,1)S(1)}, bf16[512,512]{1,0:T(8,128)(2,1)}, u32[]{:S(2)}, u32[]{:S(2)}) collective-permute-start(bf16[512,512]{1,0:T(8,128)(2,1)S(1)} %convert_element_type.223.w1a), channel_id=1, source_target_pairs={{0,1},{1,0},{2,3},{3,2},{4,5},{5,4},{6,7},{7,6},{8,9},{9,8},{10,11... | collective-permute-start | bytes 1572872 | tf_op jit(solution)/shard_map/ppermute | solution.py:603
  68.0 33.2 %collective-permute-start.7 = (bf16[512,512]{1,0:T(8,128)(2,1)S(1)}, bf16[512,512]{1,0:T(8,128)(2,1)}, u32[]{:S(2)}, u32[]{:S(2)}) collective-permute-start(bf16[512,512]{1,0:T(8,128)(2,1)S(1)} %convert_element_type.224.w2a), channel_id=1, source_target_pairs={{0,2},{1,3},{2,0},{3,1},{4,6},{5,7},{6,4},{7,5},{8,10},{9,11},{10,... | collective-permute-start | bytes 1572872 | tf_op jit(solution)/shard_map/ppermute | solution.py:603
  80.6 23.6 %collective-permute-start.2 = (bf16[512,512]{1,0:T(8,128)(2,1)S(1)}, bf16[512,512]{1,0:T(8,128)(2,1)S(1)}, u32[]{:S(2)}, u32[]{:S(2)}) collective-permute-start(bf16[512,512]{1,0:T(8,128)(2,1)S(1)} %collective-permute-done.1), channel_id=1, source_target_pairs={{0,1},{1,0},{2,3},{3,2},{4,5},{5,4},{6,7},{7,6},{8,9},{9,8},{10,11... | collective-permute-start | bytes 1572872 | tf_op jit(solution)/shard_map/ppermute | solution.py:603
  81.3 67.2 %collective-permute-start.6 = (bf16[512,512]{1,0:T(8,128)(2,1)S(1)}, bf16[512,512]{1,0:T(8,128)(2,1)}, u32[]{:S(2)}, u32[]{:S(2)}) collective-permute-start(bf16[512,512]{1,0:T(8,128)(2,1)S(1)} %convert_element_type.224.w2a), channel_id=1, source_target_pairs={{0,1},{1,0},{2,3},{3,2},{4,5},{5,4},{6,7},{7,6},{8,9},{9,8},{10,11... | collective-permute-start | bytes 1572872 | tf_op jit(solution)/shard_map/ppermute | solution.py:603
  91.9 56.6 %collective-permute-start.5 = (bf16[512,512]{1,0:T(8,128)(2,1)}, bf16[512,512]{1,0:T(8,128)(2,1)}, u32[]{:S(2)}, u32[]{:S(2)}) collective-permute-start(bf16[512,512]{1,0:T(8,128)(2,1)} %collective-permute-done.4.w1c), channel_id=1, source_target_pairs={{0,1},{1,0},{2,3},{3,2},{4,5},{5,4},{6,7},{7,6},{8,9},{9,8},{10,11... | collective-permute-start | bytes 1572872 | tf_op jit(solution)/shard_map/ppermute | solution.py:603
  101.1 47.4 %collective-permute-start.8 = (bf16[512,512]{1,0:T(8,128)(2,1)}, bf16[512,512]{1,0:T(8,128)(2,1)}, u32[]{:S(2)}, u32[]{:S(2)}) collective-permute-start(bf16[512,512]{1,0:T(8,128)(2,1)} %collective-permute-done.7.w2c), channel_id=1, source_target_pairs={{0,1},{1,0},{2,3},{3,2},{4,5},{5,4},{6,7},{7,6},{8,9},{9,8},{10,11... | collective-permute-start | bytes 1572872 | tf_op jit(solution)/shard_map/ppermute | solution.py:603
  176.6 44.7 %all-to-all-start.2 = ((bf16[8,20,8,512]{3,2,1,0:T(8,128)(2,1)}), bf16[8,20,8,512]{3,2,1,0:T(8,128)(2,1)S(1)}, u32[]{:S(2)}, u32[]{:S(2)}) async-start(bf16[8,20,8,512]{3,2,1,0:T(8,128)(2,1)} %get-tuple-element.62), calls=%async_computation.2 | async-start | bytes 2621440 | tf_op jit(solution)/shard_map/all_to_all | solution.py:714
  221.2 76.7 %all-to-all-start.4 = ((bf16[8,30,8,512]{3,2,1,0:T(8,128)(2,1)}), bf16[8,30,8,512]{3,2,1,0:T(8,128)(2,1)S(1)}, u32[]{:S(2)}, u32[]{:S(2)}) async-start(bf16[8,30,8,512]{3,2,1,0:T(8,128)(2,1)} %get-tuple-element.63), calls=%async_computation.4 | async-start | bytes 3932160 | tf_op jit(solution)/shard_map/all_to_all | solution.py:714
  229.6 2.7 collective-permute-start.11
  230.7 6.3 %collective-permute-start.9 = (bf16[2,512,512]{2,1,0:T(8,128)(2,1)S(1)}, bf16[2,512,512]{2,1,0:T(8,128)(2,1)S(1)}, u32[]{:S(2)}, u32[]{:S(2)}) collective-permute-start(bf16[2,512,512]{2,1,0:T(8,128)(2,1)S(1)} %pad_maximum_fusion.2), channel_id=1, source_target_pairs={{0,1},{1,0},{2,3},{3,2},{4,5},{5,4},{6,7},{7,6},{8,9},{9,8},{10,11... | collective-permute-start | bytes 3145736 | tf_op jit(solution)/shard_map/ppermute | solution.py:603
  235.5 57.0 %collective-permute-start.12 = (bf16[512,512]{1,0:T(8,128)(2,1)}, bf16[512,512]{1,0:T(8,128)(2,1)S(1)}, u32[]{:S(2)}, u32[]{:S(2)}) collective-permute-start(bf16[512,512]{1,0:T(8,128)(2,1)} %fusion.14), channel_id=1, source_target_pairs={{0,2},{1,3},{2,0},{3,1},{4,6},{5,7},{6,4},{7,5},{8,10},{9,11},{10,... | collective-permute-start | bytes 1572872 | tf_op jit(solution)/shard_map/ppermute | solution.py:603
  238.8 56.6 %collective-permute-start.10 = (bf16[512,512]{1,0:T(8,128)(2,1)}, bf16[512,512]{1,0:T(8,128)(2,1)S(1)}, u32[]{:S(2)}, u32[]{:S(2)}) collective-permute-start(bf16[512,512]{1,0:T(8,128)(2,1)} %fusion.13), channel_id=1, source_target_pairs={{0,2},{1,3},{2,0},{3,1},{4,6},{5,7},{6,4},{7,5},{8,10},{9,11},{10,... | collective-permute-start | bytes 1572872 | tf_op jit(solution)/shard_map/ppermute | solution.py:603
  303.4 23.0 %all-to-all-start.5 = ((bf16[8,64,640]{2,1,0:T(8,128)(2,1)}), bf16[8,64,640]{2,1,0:T(8,128)(2,1)S(1)}, u32[]{:S(2)}, u32[]{:S(2)}) async-start(bf16[8,64,640]{2,1,0:T(8,128)(2,1)} %broadcast_in_dim.44), calls=%async_computation.5 | async-start | bytes 1310720 | tf_op jit(solution)/shard_map/all_to_all | solution.py:620
  315.7 26.6 %collective-permute-start.21 = (bf16[256,1024]{1,0:T(8,128)(2,1)}, bf16[256,1024]{1,0:T(8,128)(2,1)}, u32[]{:S(2)}, u32[]{:S(2)}) collective-permute-start(bf16[256,1024]{1,0:T(8,128)(2,1)} %fusion.1), channel_id=1, source_target_pairs={{0,4},{4,0},{8,12},{12,8},{16,20},{20,16},{24,28},{28,24},{1,5},{5... | collective-permute-start | bytes 1572872 | tf_op jit(solution)/shard_map/ppermute | solution.py:624
  342.3 10.9 %collective-permute-start.13 = (bf16[2,512,512]{2,1,0:T(8,128)(2,1)}, bf16[2,512,512]{2,1,0:T(8,128)(2,1)}, u32[]{:S(2)}, u32[]{:S(2)}) collective-permute-start(bf16[2,512,512]{2,1,0:T(8,128)(2,1)} %pad_maximum_fusion.4), channel_id=1, source_target_pairs={{0,1},{1,0},{2,3},{3,2},{4,5},{5,4},{6,7},{7,6},{8,9},{9,8},{10,11... | collective-permute-start | bytes 3145736 | tf_op jit(solution)/shard_map/ppermute | solution.py:603
  343.5 8.8 %collective-permute-start.22 = (bf16[128,1024]{1,0:T(8,128)(2,1)S(1)}, bf16[128,1024]{1,0:T(8,128)(2,1)S(1)}, u32[]{:S(2)}, u32[]{:S(2)}) collective-permute-start(bf16[128,1024]{1,0:T(8,128)(2,1)S(1)} %dynamic-slice_convert_fusion), channel_id=1, source_target_pairs={{0,8},{4,12},{8,0},{12,4},{16,24},{20,28},{24,16},{28,20},{1,9},{5... | collective-permute-start | bytes 786440 | tf_op jit(solution)/shard_map/ppermute | solution.py:624
  352.4 8.9 %collective-permute-start.23 = (bf16[64,1024]{1,0:T(8,128)(2,1)S(1)}, bf16[64,1024]{1,0:T(8,128)(2,1)S(1)}, u32[]{:S(2)}, u32[]{:S(2)}) collective-permute-start(bf16[64,1024]{1,0:T(8,128)(2,1)S(1)} %dynamic-slice_convert_fusion.2), channel_id=1, source_target_pairs={{0,16},{4,20},{8,24},{12,28},{16,0},{20,4},{24,8},{28,12},{1,17},{... | collective-permute-start | bytes 393224 | tf_op jit(solution)/shard_map/ppermute | solution.py:624
  356.8 15.1 %collective-permute-start.14 = (bf16[512,512]{1,0:T(8,128)(2,1)}, bf16[512,512]{1,0:T(8,128)(2,1)}, u32[]{:S(2)}, u32[]{:S(2)}) collective-permute-start(bf16[512,512]{1,0:T(8,128)(2,1)} %fusion.15), channel_id=1, source_target_pairs={{0,2},{1,3},{2,0},{3,1},{4,6},{5,7},{6,4},{7,5},{8,10},{9,11},{10,... | collective-permute-start | bytes 1572872 | tf_op jit(solution)/shard_map/ppermute | solution.py:603
  362.3 7.7 %collective-permute-start.24 = (bf16[64,1024]{1,0:T(8,128)(2,1)S(1)}, bf16[64,1024]{1,0:T(8,128)(2,1)S(1)}, u32[]{:S(2)}, u32[]{:S(2)}) collective-permute-start(bf16[64,1024]{1,0:T(8,128)(2,1)S(1)} %add_convert_fusion.8), channel_id=1, source_target_pairs={{0,16},{4,20},{8,24},{12,28},{16,0},{20,4},{24,8},{28,12},{1,17},{... | collective-permute-start | bytes 393224 | tf_op jit(solution)/shard_map/ppermute | solution.py:624
  362.4 35.9 %collective-permute-start.35 = (f32[512,512]{1,0:T(8,128)S(1)}, f32[512,512]{1,0:T(8,128)}, u32[]{:S(2)}, u32[]{:S(2)}) collective-permute-start(f32[512,512]{1,0:T(8,128)S(1)} %copy-done.12), channel_id=1, source_target_pairs={{0,2},{1,3},{2,0},{3,1},{4,6},{5,7},{6,4},{7,5},{8,10},{9,11},{10,... | collective-permute-start | bytes 3145736 | tf_op jit(solution)/shard_map/ppermute | solution.py:603
  363.9 75.6 %collective-permute-start.34 = (f32[512,512]{1,0:T(8,128)S(1)}, f32[512,512]{1,0:T(8,128)}, u32[]{:S(2)}, u32[]{:S(2)}) collective-permute-start(f32[512,512]{1,0:T(8,128)S(1)} %copy-done.12), channel_id=1, source_target_pairs={{0,1},{1,0},{2,3},{3,2},{4,5},{5,4},{6,7},{7,6},{8,9},{9,8},{10,11... | collective-permute-start | bytes 3145736 | tf_op jit(solution)/shard_map/ppermute | solution.py:603
  364.0 75.5 %collective-permute-start.38 = (f32[512,512]{1,0:T(8,128)}, f32[512,512]{1,0:T(8,128)}, u32[]{:S(2)}, u32[]{:S(2)}) collective-permute-start(f32[512,512]{1,0:T(8,128)} %refs_6_.1), channel_id=1, source_target_pairs={{0,2},{1,3},{2,0},{3,1},{4,6},{5,7},{6,4},{7,5},{8,10},{9,11},{10,... | collective-permute-start | bytes 3145736 | tf_op jit(solution)/shard_map/ppermute | solution.py:603
  370.1 8.3 %collective-permute-start.25 = (bf16[128,1024]{1,0:T(8,128)(2,1)S(1)}, bf16[128,1024]{1,0:T(8,128)(2,1)S(1)}, u32[]{:S(2)}, u32[]{:S(2)}) collective-permute-start(bf16[128,1024]{1,0:T(8,128)(2,1)S(1)} %maximum_select_fusion.4), channel_id=1, source_target_pairs={{0,8},{4,12},{8,0},{12,4},{16,24},{20,28},{24,16},{28,20},{1,9},{5... | collective-permute-start | bytes 786440 | tf_op jit(solution)/shard_map/ppermute | solution.py:624
  373.4 7.0 %collective-permute-start.15 = (bf16[256,512]{1,0:T(8,128)(2,1)S(1)}, bf16[256,512]{1,0:T(8,128)(2,1)S(1)}, u32[]{:S(2)}, u32[]{:S(2)}) collective-permute-start(bf16[256,512]{1,0:T(8,128)(2,1)S(1)} %dynamic-slice_convert_fusion.1), channel_id=1, source_target_pairs={{0,4},{4,0},{8,12},{12,8},{16,20},{20,16},{24,28},{28,24},{1,5},{5... | collective-permute-start | bytes 786440 | tf_op jit(solution)/shard_map/ppermute | solution.py:624
  378.5 13.2 %collective-permute-start.26 = (bf16[256,1024]{1,0:T(8,128)(2,1)S(1)}, bf16[256,1024]{1,0:T(8,128)(2,1)S(1)}, u32[]{:S(2)}, u32[]{:S(2)}) collective-permute-start(bf16[256,1024]{1,0:T(8,128)(2,1)S(1)} %maximum_select_fusion.2), channel_id=1, source_target_pairs={{0,4},{4,0},{8,12},{12,8},{16,20},{20,16},{24,28},{28,24},{1,5},{5... | collective-permute-start | bytes 1572872 | tf_op jit(solution)/shard_map/ppermute | solution.py:624
  380.4 59.7 %collective-permute-start.37 = (f32[512,512]{1,0:T(8,128)}, f32[512,512]{1,0:T(8,128)}, u32[]{:S(2)}, u32[]{:S(2)}) collective-permute-start(f32[512,512]{1,0:T(8,128)} %refs_6_.1), channel_id=1, source_target_pairs={{0,1},{1,0},{2,3},{3,2},{4,5},{5,4},{6,7},{7,6},{8,9},{9,8},{10,11... | collective-permute-start | bytes 3145736 | tf_op jit(solution)/shard_map/ppermute | solution.py:603
  391.7 5.0 collective-permute-start.16
  396.6 43.5 %collective-permute-start.41 = (bf16[512,1024]{1,0:T(8,128)(2,1)}, bf16[512,1024]{1,0:T(8,128)(2,1)}, u32[]{:S(2)}, u32[]{:S(2)}) collective-permute-start(bf16[512,1024]{1,0:T(8,128)(2,1)} %get-tuple-element.111.refs_8_.refs_4_), channel_id=1, source_target_pairs={{0,2},{1,3},{2,0},{3,1},{4,6},{5,7},{6,4},{7,5},{8,10},{9,11},{10,... | collective-permute-start | bytes 3145736 | tf_op jit(solution)/shard_map/ppermute | solution.py:603
  398.3 5.2 %collective-permute-start.17 = (bf16[64,512]{1,0:T(8,128)(2,1)S(1)}, bf16[64,512]{1,0:T(8,128)(2,1)S(1)}, u32[]{:S(2)}, u32[]{:S(2)}) collective-permute-start(bf16[64,512]{1,0:T(8,128)(2,1)S(1)} %dynamic-slice_convert_fusion.4), channel_id=1, source_target_pairs={{0,16},{4,20},{8,24},{12,28},{16,0},{20,4},{24,8},{28,12},{1,17},{... | collective-permute-start | bytes 196616 | tf_op jit(solution)/shard_map/ppermute | solution.py:624
  404.8 6.5 %collective-permute-start.18 = (bf16[64,512]{1,0:T(8,128)(2,1)S(1)}, bf16[64,512]{1,0:T(8,128)(2,1)S(1)}, u32[]{:S(2)}, u32[]{:S(2)}) collective-permute-start(bf16[64,512]{1,0:T(8,128)(2,1)S(1)} %add_convert_fusion.9), channel_id=1, source_target_pairs={{0,16},{4,20},{8,24},{12,28},{16,0},{20,4},{24,8},{28,12},{1,17},{... | collective-permute-start | bytes 196616 | tf_op jit(solution)/shard_map/ppermute | solution.py:624
  411.2 27.4 %collective-permute-start.30 = (f32[12,512]{1,0:T(8,128)S(1)}, f32[12,512]{1,0:T(8,128)S(1)}, u32[]{:S(2)}, u32[]{:S(2)}) collective-permute-start(f32[12,512]{1,0:T(8,128)S(1)} %add.269), channel_id=1, source_target_pairs={{0,2},{1,3},{2,0},{3,1},{4,6},{5,7},{6,4},{7,5},{8,10},{9,11},{10,... | collective-permute-start | bytes 73736 | tf_op jit(solution)/shard_map/ppermute | solution.py:603
  438.7 5.0 collective-permute-start.19
  439.5 29.9 %collective-permute-start.36 = (f32[512,512]{1,0:T(8,128)}, f32[512,512]{1,0:T(8,128)}, u32[]{:S(2)}, u32[]{:S(2)}) collective-permute-start(f32[512,512]{1,0:T(8,128)} %collective-permute-done.35.refs_2_), channel_id=1, source_target_pairs={{0,1},{1,0},{2,3},{3,2},{4,5},{5,4},{6,7},{7,6},{8,9},{9,8},{10,11... | collective-permute-start | bytes 3145736 | tf_op jit(solution)/shard_map/ppermute | solution.py:603
  439.5 29.8 %collective-permute-start.39 = (f32[512,512]{1,0:T(8,128)}, f32[512,512]{1,0:T(8,128)}, u32[]{:S(2)}, u32[]{:S(2)}) collective-permute-start(f32[512,512]{1,0:T(8,128)} %collective-permute-done.38.refs_6_), channel_id=1, source_target_pairs={{0,1},{1,0},{2,3},{3,2},{4,5},{5,4},{6,7},{7,6},{8,9},{9,8},{10,11... | collective-permute-start | bytes 3145736 | tf_op jit(solution)/shard_map/ppermute | solution.py:603
  440.0 29.3 %collective-permute-start.40 = (bf16[512,1024]{1,0:T(8,128)(2,1)}, bf16[512,1024]{1,0:T(8,128)(2,1)}, u32[]{:S(2)}, u32[]{:S(2)}) collective-permute-start(bf16[512,1024]{1,0:T(8,128)(2,1)} %get-tuple-element.111.refs_8_.refs_4_), channel_id=1, source_target_pairs={{0,1},{1,0},{2,3},{3,2},{4,5},{5,4},{6,7},{7,6},{8,9},{9,8},{10,11... | collective-permute-start | bytes 3145736 | tf_op jit(solution)/shard_map/ppermute | solution.py:603
  440.1 29.2 %collective-permute-start.42 = (bf16[512,1024]{1,0:T(8,128)(2,1)}, bf16[512,1024]{1,0:T(8,128)(2,1)}, u32[]{:S(2)}, u32[]{:S(2)}) collective-permute-start(bf16[512,1024]{1,0:T(8,128)(2,1)} %collective-permute-done.41.refs_10_), channel_id=1, source_target_pairs={{0,1},{1,0},{2,3},{3,2},{4,5},{5,4},{6,7},{7,6},{8,9},{9,8},{10,11... | collective-permute-start | bytes 3145736 | tf_op jit(solution)/shard_map/ppermute | solution.py:603
  443.6 4.2 collective-permute-start.31
  447.8 6.4 %collective-permute-start.20 = (bf16[256,512]{1,0:T(8,128)(2,1)S(1)}, bf16[256,512]{1,0:T(8,128)(2,1)S(1)}, u32[]{:S(2)}, u32[]{:S(2)}) collective-permute-start(bf16[256,512]{1,0:T(8,128)(2,1)S(1)} %maximum_select_fusion.3), channel_id=1, source_target_pairs={{0,4},{4,0},{8,12},{12,8},{16,20},{20,16},{24,28},{28,24},{1,5},{5... | collective-permute-start | bytes 786440 | tf_op jit(solution)/shard_map/ppermute | solution.py:624
  454.2 3.9 collective-permute-start.32
  458.1 3.5 collective-permute-start.27
  461.6 5.6 %collective-permute-start.33 = (f32[12,512]{1,0:T(8,128)S(1)}, f32[12,512]{1,0:T(8,128)S(1)}, u32[]{:S(2)}, u32[]{:S(2)}) collective-permute-start(f32[12,512]{1,0:T(8,128)S(1)} %add.272), channel_id=1, source_target_pairs={{0,16},{4,20},{8,24},{12,28},{16,0},{20,4},{24,8},{28,12},{1,17},{... | collective-permute-start | bytes 73736 | tf_op jit(solution)/shard_map/ppermute | solution.py:624
  467.2 19.6 %collective-permute-start.28 = (f32[8,128]{1,0:T(8,128)S(1)}, f32[8,128]{1,0:T(8,128)S(1)}, u32[]{:S(2)}, u32[]{:S(2)}) collective-permute-start(f32[8,128]{1,0:T(8,128)S(1)} %broadcast_add_fusion), channel_id=1, source_target_pairs={{0,2},{1,3},{2,0},{3,1},{4,6},{5,7},{6,4},{7,5},{8,10},{9,11},{10,... | collective-permute-start | bytes 12296 | tf_op jit(solution)/shard_map/ppermute | solution.py:603
  (38 other events, 519.0 us)

commit v4 on v3

--- a/solution.py
+++ b/solution.py
@@ -120,7 +120,7 @@
     return a * share, share + a * bell * INV_SQRT_2PI
 
 
-def attn_fwd_kernel(count, batch, p_ref, r_ref, wq_ref, wk_ref, wv_ref, wo_ref, vec_ref,
+def attn_fwd_kernel(count, batch, p_ref, r_ref, wq_ref, wk_ref, wv_ref, wo_ref, vec_ref, _,
                     x1_ref, q_ref, k_ref, v_ref, o_ref, pt_ref, q_held, k_held, v_held, o_held):
     total = count * LIVE
 
@@ -170,17 +170,18 @@
     x1_ref[...] = (x + nn(mixed, wo_ref[...]) + vec[6:7]).reshape(LIVE, count, D)
 
 
-def middle(rows, count):
-    return pl.BlockSpec((rows, count, D), lambda i: (0, i, 0))
-
-
-def attn_fwd(patches, region_rows, weights, vec, count=16, batch=4):
-    windows = patches.shape[1]
+def middle(rows, count, skip=0):
+    return pl.BlockSpec((rows, count, D), lambda i: (0, i + skip, 0))
+
+
+def attn_fwd(patches, region_rows, weights, vec, start, windows, after, count=16, batch=4):
+    skip = start // count
     array = jax.ShapeDtypeStruct
     return pl.pallas_call(
         partial(attn_fwd_kernel, count, batch),
         grid=(windows // count,),
-        in_specs=[middle(PATCH, count), block((count, D))] + [full((D, D))] * 4 + [full(vec.shape)],
+        in_specs=[middle(PATCH, count, skip), pl.BlockSpec((count, D), lambda i: (i + skip, 0))]
+        + [full((D, D))] * 4 + [full(vec.shape), pl.BlockSpec(memory_space=pl.ANY)],
         out_specs=[middle(LIVE, count)] + [block((count, ROWS, D))] * 3
         + [middle(LIVE, count), block((count, 4, ROWS, STACK))],
         out_shape=[array((LIVE, windows, D), F32)] + [array((windows, ROWS, D), BF)] * 3
@@ -189,11 +190,13 @@
         compiler_params=pltpu.CompilerParams(vmem_limit_bytes=VMEM),
         cost_estimate=BRIEF,
         name="window_attention_forward",
-    )(patches, region_rows, *weights, vec)
-
-
-def mlp_kernel(many, sources, cols, steps, lanes, x1_ref, pc_ref, w1a, w1b, w1c, w1d, w2a, w2b, w2c, w2d,
-               vec_ref, b1_ref, op_ref, dx1_ref, dw1_ref, dw2_ref, dv_ref, db1_ref, acc1, acc2):
+    )(patches, region_rows, *weights, vec, after)
+
+
+def mlp_kernel(many, sources, cols, steps, lanes, last, *refs):
+    x1a_ref, x1b_ref, pc_ref, *w_refs, vec_ref, b1_ref = refs[:9]
+    prev_refs = refs[9 : 11 if last else 9]
+    op_ref, dx1_ref, dwa_ref, dwb_ref, dv_ref, db1_ref, acc1, acc2 = refs[9 + len(prev_refs) :]
     total = many * sources * cols
     step = pl.program_id(0)
 
@@ -204,7 +207,7 @@
 
     vec = vec_ref[...]
     gain = vec[2:3]
-    x1 = x1_ref[...].reshape(total, D)
+    x1 = jnp.concatenate([x1a_ref[...], x1b_ref[...]], axis=1).reshape(total, D)
     xhat, scale = norm_parts(x1)
     h = (xhat * gain + vec[3:4]).astype(BF)
     for s in range(sources):
@@ -213,21 +216,20 @@
     dm = dy.astype(BF)
     ht = h.T
     dmt = dm.T
-    w1s, w2s = (w1a, w1b, w1c, w1d), (w2a, w2b, w2c, w2d)
     y = x1 + vec[7:8]
     dh = jnp.zeros((total, D), F32)
     parts = [(j, slice(c, c + lanes)) for j in range(4) for c in range(0, D, lanes)]
 
     def activate(j, s):
-        u, slope = gelu_parts(nn(h, w1s[j][:, s]) + b1_ref[j : j + 1, s])
-        da = slope * nt(dm, w2s[j][s, :])
+        u, slope = gelu_parts(nn(h, w_refs[j][0, :, s]) + b1_ref[j : j + 1, s])
+        da = slope * nt(dm, w_refs[j][1, s, :])
         db1_ref[j, :, s] += fold(da)
         return u.astype(BF), da.astype(BF)
 
     def apply(j, s, u, da):
         acc1[j, :, s] += nn(ht, da)
         acc2[j, :, s] += nn(dmt, u)
-        return nn(u, w2s[j][s, :]), nt(da, w1s[j][:, s])
+        return nn(u, w_refs[j][1, s, :]), nt(da, w_refs[j][0, :, s])
 
     held_pair = activate(*parts[0])
     for n in range(1, len(parts) + 1):
@@ -246,43 +248,50 @@
 
     @pl.when(step == steps - 1)
     def _():
-        dw1_ref[...] = acc1[...].astype(BF)
-        dw2_ref[...] = acc2[...].astype(BF)
-
-
-def mlp(x1, first_position, cot, first, second, vec, bias_first, many=10, lanes=256):
+        for refs_out, first in ((dwa_ref, 0), (dwb_ref, 1)):
+            for n, acc in enumerate((acc1, acc2)):
+                for m in range(2):
+                    piece = acc[first + 2 * m]
+                    for prev in prev_refs[first : first + 1]:
+                        piece = piece + prev[2 * n + m].astype(F32)
+                    refs_out[2 * n + m] = piece.astype(BF)
+
+
+def mlp(x1_parts, first_position, cot, weights, vec, bias_first, prev=(), many=10, lanes=256):
     sources, positions, cols, _ = cot.shape
-    windows = x1.shape[1]
+    windows = sources * cols
     steps = positions // many
     skip = first_position // many
     some = pl.BlockSpec((sources, many, cols, D), lambda i: (0, i, 0, 0))
     array = jax.ShapeDtypeStruct
+    matrices = full((4, D, D))
     return pl.pallas_call(
-        partial(mlp_kernel, many, sources, cols, steps, lanes),
+        partial(mlp_kernel, many, sources, cols, steps, lanes, len(prev) > 0),
         grid=(steps,),
-        in_specs=[pl.BlockSpec((many, windows, D), lambda i: (i + skip, 0, 0)), some]
-        + [full((D, D))] * 8 + [full(vec.shape), full((4, D))],
-        out_specs=[some, block((many, windows, D)), full((4, D, D)), full((4, D, D)), full((3, 8, D)), full((4, 8, D))],
+        in_specs=[pl.BlockSpec((many, part.shape[1], D), lambda i: (i + skip, 0, 0)) for part in x1_parts] + [some]
+        + [full((2, D, D))] * 4 + [full(vec.shape), full((4, D))] + [matrices] * len(prev),
+        out_specs=[some, block((many, windows, D)), matrices, matrices, full((3, 8, D)), full((4, 8, D))],
         out_shape=[array(cot.shape, BF), array((positions, windows, D), F32), array((4, D, D), BF),
                    array((4, D, D), BF), array((3, 8, D), F32), array((4, 8, D), F32)],
         scratch_shapes=[pltpu.VMEM((4, D, D), F32), pltpu.VMEM((4, D, D), F32)],
         compiler_params=pltpu.CompilerParams(vmem_limit_bytes=VMEM),
         cost_estimate=BRIEF,
         name="mlp_forward_backward",
-    )(x1, cot, *first, *second, vec, bias_first)
-
-
-def attn_bwd_kernel(count, batch, chunks, *refs):
+    )(*x1_parts, cot, *weights, vec, bias_first, *prev)
+
+
+def attn_bwd_kernel(count, batch, chunks, more, *refs):
     p_ref, r_ref, _ = refs[:3]
     dx1_refs = refs[3 : 3 + chunks]
-    (q_ref, k_ref, v_ref, o_ref, pt_ref, wq_ref, wk_ref, wv_ref, wo_ref, vec_ref,
-     dp_ref, dr_ref, dw_ref, dv_ref, dq_held, dk_held, dvv_held, do_held) = refs[3 + chunks :]
+    q_ref, k_ref, v_ref, o_ref, pt_ref, wq_ref, wk_ref, wv_ref, wo_ref, vec_ref = refs[3 + chunks : 13 + chunks]
+    prev_refs = refs[13 + chunks : 17 + chunks] if more else ()
+    dp_ref, dr_ref, dw_ref, dv_ref, dq_held, dk_held, dvv_held, do_held = refs[13 + chunks + len(prev_refs) :]
     total = count * LIVE
 
     @pl.when(pl.program_id(0) == 0)
     def _():
-        dw_ref[...] = jnp.zeros_like(dw_ref)
-        dv_ref[...] = jnp.zeros_like(dv_ref)
+        dw_ref[...] = prev_refs[2][...] if more else jnp.zeros_like(dw_ref)
+        dv_ref[...] = prev_refs[3][...] if more else jnp.zeros_like(dv_ref)
         do_held[:, total:] = jnp.zeros((4, count * (ROWS - LIVE), GROUP), F32)
 
     vec = vec_ref[...]
@@ -337,24 +346,29 @@
     dv_ref[4] += fold(dx1)
 
 
-def attn_bwd(patches, region_rows, dx1_parts, saved, weights, vec, after, count=16, batch=4):
-    windows = patches.shape[1]
+def attn_bwd(patches, region_rows, dx1_parts, saved, weights, vec, start, windows, after, prev=(), count=16, batch=4):
+    skip = start // count
     array = jax.ShapeDtypeStruct
+    sums = [full((4, D, D)), full((5, 8, D))]
+    anywhere = pl.BlockSpec(memory_space=pl.ANY)
+    rows = pl.BlockSpec((count, D), lambda i: (i + skip, 0))
+    before = 13 + len(dx1_parts)
     return pl.pallas_call(
-        partial(attn_bwd_kernel, count, batch, len(dx1_parts)),
+        partial(attn_bwd_kernel, count, batch, len(dx1_parts), len(prev) > 0),
         grid=(windows // count,),
-        in_specs=[middle(PATCH, count), block((count, D)), pl.BlockSpec(memory_space=pl.ANY)]
-        + [middle(part.shape[0], count) for part in dx1_parts]
+        in_specs=[middle(PATCH, count, skip), rows, anywhere]
+        + [middle(part.shape[0], count, skip) for part in dx1_parts]
         + [block((count, ROWS, D))] * 3 + [middle(LIVE, count), block((count, 4, ROWS, STACK))]
-        + [full((D, D))] * 4 + [full(vec.shape)],
-        out_specs=[middle(PATCH, count), block((count, D)), full((4, D, D)), full((5, 8, D))],
-        out_shape=[array((PATCH, windows, D), BF), array((windows, D), F32),
+        + [full((D, D))] * 4 + [full(vec.shape)] + ([anywhere] * 2 + sums)[: len(prev)],
+        out_specs=[middle(PATCH, count, skip), rows] + sums,
+        out_shape=[array(patches.shape, BF), array(region_rows.shape, F32),
                    array((4, D, D), F32), array((5, 8, D), F32)],
         scratch_shapes=[pltpu.VMEM((4, count * ROWS, GROUP), F32)] * 4,
+        input_output_aliases={before: 0, before + 1: 1} if prev else {},
         compiler_params=pltpu.CompilerParams(vmem_limit_bytes=VMEM),
         cost_estimate=BRIEF,
         name="window_attention_backward",
-    )(patches, region_rows, after, *dx1_parts, *saved, *weights, vec)
+    )(patches, region_rows, after, *dx1_parts, *saved, *weights, vec, *prev)
 
 
 def regional_fwd_kernel(canvas_ref, band_ref, ids_ref, band_ids_ref, wq_ref, wk_ref, wv_ref, wo_ref, vec_ref,
@@ -388,7 +402,7 @@
     r1_ref[...] = band + nn(mixed_ref[...].astype(BF), wo_ref[...]) + vec[6:7]
 
 
-def in_vmem(kernel, outs, name, *args, after=()):
+def in_vmem(kernel, outs, name, *args, after=(), scratch=()):
     spaces = [pltpu.SMEM if arg.shape == (1, 1) else pltpu.VMEM for arg in args]
     count = len(args)
     return pl.pallas_call(
@@ -397,6 +411,7 @@
         + [pl.BlockSpec(memory_space=pl.ANY) for _ in after],
         out_specs=[pl.BlockSpec(memory_space=pltpu.VMEM) for _ in outs],
         out_shape=[jax.ShapeDtypeStruct(*out) for out in outs],
+        scratch_shapes=list(scratch),
         compiler_params=pltpu.CompilerParams(vmem_limit_bytes=VMEM),
         cost_estimate=BRIEF,
         name=name,
@@ -425,10 +440,10 @@
     extra_ref[...] = extra.astype(BF)
 
 
-def regional_bwd_kernel(own_rows, q_ref, k_ref, v_ref, grads_ref, qo_ref, ko_ref, vo_ref, own_ref, ids_ref, ids_row_ref,
+def regional_bwd_kernel(own_rows, owner_ref, q_ref, k_ref, v_ref, grads_ref, qo_ref, ko_ref, vo_ref, own_ref, ids_ref, ids_row_ref,
                         ids_own_ref, ids_own_row_ref, level_ref, delta_ref, level_own_ref, delta_own_ref,
                         grads_own_ref, mixed_ref, band_grad_ref, dw_ref, wq_ref, wk_ref, wv_ref, wo_ref, vec_ref,
-                        dr_ref, gw_ref, gv_ref):
+                        dr_ref, keep_ref, give_ref, gv_ref, sum_held):
     vec = vec_ref[...]
     masks = head_masks()
     do = nt(grads_ref[...], wo_ref[...]).astype(BF).astype(F32)
@@ -461,10 +476,14 @@
     dq, dk, dv = dq_wide.astype(BF), dk_wide.astype(BF), dv_wide.astype(BF)
     dn = nt(dq, wq_ref[...]) + nt(dk, wk_ref[...]) + nt(dv, wv_ref[...])
     dr_ref[...] = grads_own_ref[...].astype(F32) + norm_back(dn, xhat, scale, vec[0:1])
-    gw_ref[0] = (dw_ref[0] + tn(low, dq)).astype(BF)
-    gw_ref[1] = (dw_ref[1] + tn(low, dk)).astype(BF)
-    gw_ref[2] = (dw_ref[2] + tn(low, dv)).astype(BF)
-    gw_ref[3] = (dw_ref[3] + tn(mixed_ref[...].astype(BF), band_grad_ref[...])).astype(BF)
+    sum_held[0] = dw_ref[0] + tn(low, dq)
+    sum_held[1] = dw_ref[1] + tn(low, dk)
+    sum_held[2] = dw_ref[2] + tn(low, dv)
+    sum_held[3] = dw_ref[3] + tn(mixed_ref[...].astype(BF), band_grad_ref[...])
+    owner = owner_ref[0, 0]
+    for n in range(2):
+        keep_ref[n] = sum_held[owner ^ (2 * n)].astype(BF)
+        give_ref[n] = sum_held[owner ^ (2 * n + 1)].astype(BF)
     gv_ref[0] = fold(dn * xhat)
     gv_ref[1] = fold(dn)
     gv_ref[2] = fold(dq_wide)
@@ -569,16 +588,16 @@
         old, mixed, new = (jnp.zeros((D, D), F32) for _ in range(3))
         cross = jnp.zeros((D, D), F32)
         for j in range(4):
-            high, low = halves(refs[4 * n + j][...])
+            high, low = halves(refs[j][n])
             if n == 1:
                 high, low = high.T, low.T
-            g = refs[8 + j][:, n * D : (n + 1) * D]
+            g = refs[4 + j][:, n * D : (n + 1) * D]
             old = old + nt(high, high)
             cross = cross + nt(high, low)
             mixed = mixed + (nt(high, g) + nt(low, g))
             new = new + nt(g, g)
         for k, x in enumerate((old + (cross + cross.T), mixed + mixed.T, new)):
-            refs[12 + 3 * n + k][...] = x
+            refs[8 + 3 * n + k][...] = x
 
 
 def update_kernel(clip_ref, ga_ref, ma_ref, wa_ref, g_ref, m1_ref, m2_ref, w1_ref, w2_ref,
@@ -603,16 +622,24 @@
     return lax.ppermute(values, "opt", [(i, i ^ bit) for i in range(OPT)])
 
 
-def pieces_of_owners(own):
+def fence(x, *first):
+    here = pl.BlockSpec(memory_space=pl.ANY)
+    return pl.pallas_call(
+        lambda *refs: None,
+        in_specs=[here] * (1 + len(first)),
+        out_specs=here,
+        out_shape=jax.ShapeDtypeStruct(x.shape, x.dtype),
+        input_output_aliases={0: 0},
+        cost_estimate=BRIEF,
+        name="fence",
+    )(x, *first)
+
+
+def pieces_of_owners(own, before_relay=()):
     mate = pair(own, 1)
     across = pair(own, 2)
-    return [own, mate, across, pair(across, 1)]
-
-
-def sum_at_owner(pieces):
-    near = pair(jnp.stack([pieces[1], pieces[3]]), 1).astype(F32)
-    far = (pieces[2].astype(F32) + near[1]).astype(BF)
-    return pieces[0].astype(F32) + near[0] + pair(far, 2).astype(F32)
+    relay = fence(across, *before_relay) if before_relay else across
+    return [own, mate, relay, pair(relay, 1)]
 
 
 def share(x):
@@ -628,20 +655,17 @@
     return [1 << n for n in range(lax.axis_size("dp").bit_length() - 1)]
 
 
-def sum_over_dp(x):
-    index = lax.axis_index("dp")
-    for bit in bits():
-        half = x.shape[0] // 2
-        side = (index // bit) % 2
-        give = lax.dynamic_slice_in_dim(x, (1 - side) * half, half, 0)
-        keep = lax.dynamic_slice_in_dim(x, side * half, half, 0)
-        x = keep + swap(give.astype(BF), bit).astype(F32)
-    x = x.astype(BF)
-    for bit in reversed(bits()):
-        other = swap(x, bit)
-        side = (index // bit) % 2
-        x = jnp.where(side == 0, jnp.concatenate([x, other]), jnp.concatenate([other, x]))
-    return x
+def halving_step(x, bit):
+    half = x.shape[0] // 2
+    side = (lax.axis_index("dp") // bit) % 2
+    give = lax.dynamic_slice_in_dim(x, (1 - side) * half, half, 0).astype(BF)
+    return lax.dynamic_slice_in_dim(x, side * half, half, 0), give
+
+
+def doubling_step(x, bit):
+    other = swap(x, bit)
+    side = (lax.axis_index("dp") // bit) % 2
+    return jnp.where(side == 0, jnp.concatenate([x, other]), jnp.concatenate([other, x]))
 
 
 def sum_small_over_dp(x):
@@ -713,16 +737,16 @@
     order = opt_index ^ jnp.arange(OPT)
     move = lambda x: lax.all_to_all(x, "dp", 0, 0, tiled=True)
 
-    attn_pieces = jnp.stack(pieces_of_owners(attn_w[0].astype(BF)))
+    attn_pieces = pieces_of_owners(attn_w[0].astype(BF))
+    across = attn_pieces[2]
+    attn_pieces = jnp.stack(attn_pieces)
     weights = [lax.dynamic_index_in_dim(attn_pieces, opt_index ^ j, 0, keepdims=False) for j in range(OPT)]
     canvas_blocks = share(regions[0])
     canvas = canvas_blocks.reshape(tokens, D)
     by_position = patch_cot[0].transpose(0, 2, 1, 3)
     split = 20
     last = jnp.concatenate([by_position[:, split:], region_cot[0][:, None]], axis=1)
-    cots = [move(by_position[:, :split]), move(last)]
-    first = pieces_of_owners(mlp_in.astype(BF))
-    second = pieces_of_owners(mlp_out.astype(BF))
+    first_cot = move(fence(by_position[:, :split], canvas))
     bias_first = jnp.take(vec[8:], order, axis=0)
 
     band_of = lambda x: lax.dynamic_slice_in_dim(x, dp_index, 1, 1).reshape((grid_cols,) + x.shape[3:])
@@ -744,25 +768,40 @@
     level_wide = jnp.tile(level.T, (1, GROUP // HEADS))
 
     windows = patches[0, 0].transpose(1, 0, 2)
-    x1, *saved = attn_fwd(windows, region_rows, weights, vec)
-    outs = [mlp(x1, start, cot, first, second, vec, bias_first) for start, cot in zip((0, split), cots)]
-    moved = [move(o[0]) for o in outs]
-    out_patches = jnp.concatenate([moved[0], moved[1][:, : PATCH - split]], axis=1).transpose(0, 2, 1, 3)[None]
-    out_regions = moved[1][None, :, PATCH - split]
-    d_patches, d_region, d_attn, d_vec_attn = attn_bwd(windows, region_rows, [o[1] for o in outs],
-                                                     saved, weights, vec, moved[0])
+    some = grid_cols // 2
+    x1a, *saved_a = attn_fwd(windows, region_rows, weights, vec, 0, some, across)
+    own_mlp_w = fence(jnp.stack([mlp_in, mlp_out]).astype(BF), across)
+    mlp_w = pieces_of_owners(own_mlp_w, before_relay=(x1a,))
+    last_cot = move(fence(last, x1a))
+    x1b, *saved_b = attn_fwd(windows, region_rows, weights, vec, some, some, first_cot)
+    x1 = (x1a, x1b)
+    out_a = mlp(x1, 0, first_cot, mlp_w, vec, bias_first)
+    moms = pieces_of_owners(fence(jnp.stack([mlp_in_mom, mlp_out_mom]), x1b), before_relay=(out_a[1],))
+    moved_a = move(out_a[0])
+    out_b = mlp(x1, split, last_cot, mlp_w, vec, bias_first, prev=out_a[2:4])
+    moved_b = move(out_b[0])
+    out_patches = jnp.concatenate([moved_a, moved_b[:, : PATCH - split]], axis=1).transpose(0, 2, 1, 3)[None]
+    out_regions = moved_b[None, :, PATCH - split]
+
+    near = pair(out_b[3], 1).astype(F32) + out_b[2].astype(F32)
+    far = jnp.stack([near[1], near[3]]).astype(BF)
+    dx1 = (out_a[1], out_b[1])
+    early = attn_bwd(windows, region_rows, dx1, saved_a, weights, vec, 0, some, far)
+    far = pair(far, 2).astype(F32)
+    own_mlp = jnp.concatenate([near[0] + far[0], near[2] + far[1]], axis=1)
+    keep, give = halving_step(own_mlp, 1)
+    d_patches, d_region, d_attn, d_vec_attn = attn_bwd(
+        windows, region_rows, dx1, saved_b, weights, vec, some, some, give, prev=early)
     d_patches = d_patches.transpose(1, 0, 2)[None, None]
-
-    add = lambda n, j: (outs[0][n][j].astype(F32) + outs[1][n][j].astype(F32)).astype(BF)
-    own_first = sum_at_owner([add(2, j) for j in range(OPT)])
-    own_second = sum_at_owner([add(3, j) for j in range(OPT)])
-    own_mlp = sum_over_dp(jnp.concatenate([own_first, own_second], axis=1))
-    grams = in_vmem(grams_kernel, [((D, D), F32)] * 6, "mlp_grams", *pieces_of_owners(mlp_in_mom),
-                    *pieces_of_owners(mlp_out_mom), *pieces_of_owners(own_mlp))
+    gives = []
+    for bit in bits()[1:]:
+        keep, give = halving_step(keep + swap(give, bit // 2).astype(F32), bit)
+        gives.append(give)
+    piece_mlp = (keep + swap(give, bits()[-1]).astype(F32)).astype(BF)
 
     band_grad, extra = in_vmem(payload_kernel, [((grid_cols, D), BF), ((grid_cols, GROUP), BF)],
                                "regional_payload", d_region, mixed, level_wide, weights[3],
-                               after=(own_first, own_second, moved[1]))
+                               after=(gives[0], moved_b))
     payload = share(jnp.concatenate([band_grad, extra], axis=1)).reshape(grid_rows, dp_size, cols, D + GROUP)
     payload = payload.transpose(1, 0, 2, 3).reshape(tokens, D + GROUP)
     grads = payload[:, :D]
@@ -773,33 +812,46 @@
     if one_kernel:
         wide = lambda x: x.reshape(4, -1)
         own_columns = lambda x: wide(lax.dynamic_slice_in_dim(x, dp_index * own_count, own_count, 1))
-        d_regions, grad_attn, d_vec_reg = in_vmem(
+        matrices = ((2, D, D), BF)
+        d_regions, keep_attn, give_attn, d_vec_reg = in_vmem(
             partial(regional_bwd_kernel, own_count),
-            [((own_count, D), F32), ((4, D, D), BF), ((5, 8, D), F32)],
-            "regional_attention_backward", reg_q, reg_k, reg_v, grads, own_of(reg_q), own_of(reg_k), own_of(reg_v),
+            [((own_count, D), F32), matrices, matrices, ((5, 8, D), F32)],
+            "regional_attention_backward", opt_index.reshape(1, 1),
+            reg_q, reg_k, reg_v, grads, own_of(reg_q), own_of(reg_k), own_of(reg_v),
             own_of(canvas), ids[:, None], repeat(ids), own_ids[:, None], repeat(own_ids), wide(level), wide(delta),
-            own_columns(level), own_columns(delta), own_of(grads), mixed, band_grad, d_attn, *weights, vec)
+            own_columns(level), own_columns(delta), own_of(grads), mixed, band_grad, d_attn, *weights, vec,
+            after=tuple(gives[1:2]), scratch=[pltpu.VMEM((4, D, D), F32)])
     else:
         d_regions, grad_attn, d_vec_reg = regional_backward(
             reg_q, reg_k, reg_v, grads, own_of, own_of(canvas), ids[:, None] == own_ids[None, :], level, delta,
             weights, vec, mixed, band_grad, d_attn)
+        pick = lambda j: lax.dynamic_index_in_dim(grad_attn, opt_index ^ j, 0, keepdims=False)
+        keep_attn, give_attn = jnp.stack([pick(0), pick(2)]), jnp.stack([pick(1), pick(3)])
     d_regions = d_regions.reshape(regions.shape)
 
-    pieces = [lax.dynamic_index_in_dim(grad_attn, opt_index ^ j, 0, keepdims=False) for j in range(OPT)]
-    own_attn = sum_over_dp(sum_at_owner(pieces))
+    near = pair(give_attn, 1).astype(F32) + keep_attn.astype(F32)
+    piece_attn = near[0] + pair(near[1].astype(BF), 2).astype(F32)
+    piece_attn = move(piece_attn.astype(BF).reshape(dp_size, D // dp_size, D))
+    piece_attn = jnp.sum(piece_attn.astype(F32), axis=0).astype(BF)
+    own_attn = share(piece_attn).reshape(D, D)
+    own_mlp = piece_mlp
+    for bit in reversed(bits()):
+        own_mlp = doubling_step(own_mlp, bit)
+    grams = in_vmem(grams_kernel, [((D, D), F32)] * 6, "mlp_grams", *moms, *pieces_of_owners(own_mlp))
 
     d_vec_attn = jnp.sum(d_vec_attn + d_vec_reg, axis=1)
-    d_vec_mlp = jnp.sum(outs[0][4] + outs[1][4], axis=1)
-    d_bias_first = jnp.take(jnp.sum(outs[0][5] + outs[1][5], axis=1), order, axis=0)
+    d_vec_mlp = jnp.sum(out_a[4] + out_b[4], axis=1)
+    d_bias_first = jnp.take(jnp.sum(out_a[5] + out_b[5], axis=1), order, axis=0)
     grad_vec = jnp.concatenate([d_vec_attn[:2], d_vec_mlp[:2], d_vec_attn[2:], d_vec_mlp[2:], d_bias_first])
     grad_vec = grad_vec + pair(grad_vec, 1)
     grad_vec = grad_vec + pair(grad_vec, 2)
     grad_vec = sum_small_over_dp(grad_vec)
 
     squares = lambda x: jnp.sum(x.astype(F32) ** 2)
-    total = jnp.full((8, 128), squares(own_attn) + squares(own_mlp))
+    total = jnp.full((8, 128), squares(piece_attn) + squares(piece_mlp))
     total = total + pair(total, 1)
     total = total + pair(total, 2)
+    total = sum_small_over_dp(total)
     grad_norm = jnp.sqrt(total[0, 0] + squares(grad_vec))
     clip = jnp.minimum(1.0, CLIP_LIMIT / (grad_norm + 1e-06))
     attn_mom_new, new_attn, first_mom, new_first, second_mom, new_second = in_vmem(

time: 527 us -> 560 us (1.063)
  Pallas kernels: 218 us -> 232 us
  starting transfers between devices: 67.5 us -> 78.6 us
  local copies, waits for them, and re-layouts: 30.6 us -> 37.6 us
    ppermute x28 -> x20, waiting for transfers between devices: 61.1 us -> 93.3 us  [pair(): return lax.ppermute(values, 'opt', [(i, i ^ bit) for i in range(OPT)])]
    all_to_all x4 -> x5, waiting for transfers between devices: 28.4 us -> 0.01 us  [per_device(): move = lambda x: lax.all_to_all(x, 'dp', 0, 0, tiled=True)]
    pallas_call x3 -> x10, Pallas kernels: 119 us -> 128 us  [the longest x2 68.2 us: mlp(): pl.pallas_call(partial(mlp_kernel, many, sources, cols, steps, lanes, len...]
    convert_element_type x14 -> x4, other arithmetic: 13.6 us -> 4.61 us  [the longest x1 1.99 us: per_device(): piece_attn = move(piece_attn.astype(BF).reshape(dp_size, D // dp_size, D))]
    all_to_all x2 -> x3, waiting for transfers between devices: 20.7 us -> 12 us  [share(): return lax.all_to_all(copies, 'dp', 0, 0, tiled=True)]
    ppermute x15 -> x12, waiting for transfers between devices: 51.3 us -> 58.5 us  [swap(): lax.ppermute(x, 'dp', [(i, i ^ bit) for i in range(lax.axis_size('dp'))])]
    all_to_all x2 -> x3, starting transfers between devices: 13.4 us -> 18.3 us  [share(): return lax.all_to_all(copies, 'dp', 0, 0, tiled=True)]
    pallas_call x1 -> x2, Pallas kernels: 35.2 us -> 39.9 us  [attn_fwd(): pl.pallas_call(partial(attn_fwd_kernel, count, batch), grid=(windows // c...]
  transfers between devices with their start and end apart: 49 -> 40, of which waited for: 23 -> 17; matrix products, arithmetic and copies ran while one was open for 11% -> 10% of each run, Pallas kernels for 36% -> 27%
where the time goes in v4:
time: 560 us; the launch traced here: 551 us
  Pallas kernels  232 us (41%)
  waiting for transfers between devices  164 us (29%)
  starting transfers between devices  78.6 us (14%)
  local copies, waits for them, and re-layouts  37.6 us (7%)
  other arithmetic  33.5 us (6%)
    ppermute x20, waiting for transfers between devices, pair(): return lax.ppermute(values, 'opt', [(i, i ^ bit) for i in range(OPT)])  93.3 us
    pallas_call x2, Pallas kernels, mlp(): pl.pallas_call(partial(mlp_kernel, many, sources, cols, steps, lanes, len...  68.2 us
    pallas_call x5, Pallas kernels, in_vmem(): pl.pallas_call(lambda *refs: kernel(*refs[:count], *refs[count + len(afte...  63.5 us
    pallas_call x2, Pallas kernels, attn_bwd(): pl.pallas_call(partial(attn_bwd_kernel, count, batch, len(dx1_parts), len...  60.1 us
    ppermute x12, waiting for transfers between devices, swap(): lax.ppermute(x, 'dp', [(i, i ^ bit) for i in range(lax.axis_size('dp'))])  58.5 us
    pallas_call x2, Pallas kernels, attn_fwd(): pl.pallas_call(partial(attn_fwd_kernel, count, batch), grid=(windows // c...  39.9 us
    all_to_all x5, starting transfers between devices, per_device(): move = lambda x: lax.all_to_all(x, 'dp', 0, 0, tiled=True)  24.7 us
    ppermute x12, starting transfers between devices, swap(): lax.ppermute(x, 'dp', [(i, i ^ bit) for i in range(lax.axis_size('dp'))])  23.1 us
  transfers between devices with their start and end apart: 40, of which 17 were waited for; matrix products, arithmetic and copies ran while one was open for 10% of the time, Pallas kernels for 27%

profile of v4, /device:TPU:0, one launch (start us, length us, event | category | flops | bytes accessed | tf_op | source)
XLA Modules:
  0.0 550.7 jit_solution(9752182591335469062)
XLA Ops:
  2.3 7.3 %all-to-all-start = ((bf16[8,8,8,512]{3,2,1,0:T(8,128)(2,1)}), bf16[8,8,8,512]{3,2,1,0:T(8,128)(2,1)S(1)}, u32[]{:S(2)}, u32[]{:S(2)}) async-start(bf16[8,8,8,512]{3,2,1,0:T(8,128)(2,1)} %broadcast_in_dim.47), calls=%async_computation | async-start | bytes 1048576 | tf_op jit(solution)/shard_map/all_to_all | solution.py:647
  9.6 2.5 slice.107.refs_0_
  12.0 12.0 %all-to-all-done = bf16[8,8,8,512]{3,2,1,0:T(8,128)(2,1)S(1)} async-done(((bf16[8,8,8,512]{3,2,1,0:T(8,128)(2,1)}), bf16[8,8,8,512]{3,2,1,0:T(8,128)(2,1)S(1)}, u32[]{:S(2)}, u32[]{:S(2)}) %all-to-all-start) | async-done | bytes 524320 | tf_op jit(solution)/shard_map/all_to_all | solution.py:647
  24.9 3.8 all-to-all-start.1
  31.2 12.4 %collective-permute-done.1._.refs_1_ = bf16[512,512]{1,0:T(8,128)(2,1)} collective-permute-done((bf16[512,512]{1,0:T(8,128)(2,1)}, bf16[512,512]{1,0:T(8,128)(2,1)}, u32[]{:S(2)}, u32[]{:S(2)}) %collective-permute-start.1) | collective-permute-done | bytes 524320 | tf_op jit(solution)/shard_map/ppermute | solution.py:622
  43.6 1.7 slice.108
  52.9 5.2 regional_attention_forward.1
  58.1 19.9 %window_attention_forward.2 = (f32[50,32,512]{2,1,0:T(8,128)}, bf16[32,56,512]{2,1,0:T(8,128)(2,1)}, bf16[32,56,512]{2,1,0:T(8,128)(2,1)}, bf16[32,56,512]{2,1,0...) custom-call(bf16[49,64,512]{2,1,0:T(8,128)(2,1)} %bitcast.81, ...), custom_call_target="tpu_custom_call" | custom-call | flops 1000000 | bytes 100000 | tf_op jit(solution)/shard_map/window_attention_forward/pallas_call | solution.py:180
  78.0 5.7 %all-to-all-start.3 = ((bf16[8,30,8,512]{3,2,1,0:T(8,128)(2,1)}), bf16[8,30,8,512]{3,2,1,0:T(8,128)(2,1)S(1)}, u32[]{:S(2)}, u32[]{:S(2)}) async-start(bf16[8,30,8,512]{3,2,1,0:T(8,128)(2,1)} %fence.9), calls=%async_computation.3 | async-start | bytes 3932160 | tf_op jit(solution)/shard_map/all_to_all | solution.py:738
  88.0 24.0 %collective-permute-done.4.refs_0_ = bf16[2,512,512]{2,1,0:T(8,128)(2,1)S(1)} collective-permute-done((bf16[2,512,512]{2,1,0:T(8,128)(2,1)}, bf16[2,512,512]{2,1,0:T(8,128)(2,1)S(1)}, u32[]{:S(2)}, u32[]{:S(2)}) %collective-permute-start.4) | collective-permute-done | bytes 1048608 | tf_op jit(solution)/shard_map/ppermute | solution.py:622
  114.3 20.0 %window_attention_forward.3 = (f32[50,32,512]{2,1,0:T(8,128)}, bf16[32,56,512]{2,1,0:T(8,128)(2,1)}, bf16[32,56,512]{2,1,0:T(8,128)(2,1)}, bf16[32,56,512]{2,1,0...) custom-call(bf16[49,64,512]{2,1,0:T(8,128)(2,1)} %bitcast.82, ...), custom_call_target="tpu_custom_call" | custom-call | flops 1000000 | bytes 100000 | tf_op jit(solution)/shard_map/window_attention_forward/pallas_call | solution.py:180
  135.2 27.9 %mlp_forward_backward.2 = (bf16[8,20,8,512]{3,2,1,0:T(8,128)(2,1)}, f32[20,64,512]{2,1,0:T(8,128)}, bf16[4,512,512]{2,1,0:T(8,128)(2,1)}, bf16[4,512,512]{2,1,0:...) custom-call(f32[50,32,512]{2,1,0:T(8,128)} %get-tuple-element.72.refs_1_.refs_0_, ...), custom_call_target="tpu_custom_call" | custom-call | flops 1000000 | bytes 100000 | tf_op jit(solution)/shard_map/mlp_forward_backward/pallas_call | solution.py:268
  164.4 40.3 %mlp_forward_backward.3 = (bf16[8,30,8,512]{3,2,1,0:T(8,128)(2,1)}, f32[30,64,512]{2,1,0:T(8,128)}, bf16[4,512,512]{2,1,0:T(8,128)(2,1)}, bf16[4,512,512]{2,1,0:...) custom-call(f32[50,32,512]{2,1,0:T(8,128)} %get-tuple-element.72.refs_1_.refs_0_, ...), custom_call_target="tpu_custom_call" | custom-call | flops 1000000 | bytes 100000 | tf_op jit(solution)/shard_map/mlp_forward_backward/pallas_call | solution.py:268
  205.3 5.9 %all-to-all-start.4 = ((bf16[8,30,8,512]{3,2,1,0:T(8,128)(2,1)}), bf16[8,30,8,512]{3,2,1,0:T(8,128)(2,1)S(1)}, u32[]{:S(2)}, u32[]{:S(2)}) async-start(bf16[8,30,8,512]{3,2,1,0:T(8,128)(2,1)} %get-tuple-element.77), calls=%async_computation.4 | async-start | bytes 3932160 | tf_op jit(solution)/shard_map/all_to_all | solution.py:738
  211.2 5.0 convert_add_fusion
  217.9 23.4 %collective-permute-done.7 = bf16[2,512,512]{2,1,0:T(8,128)(2,1)} collective-permute-done((bf16[2,512,512]{2,1,0:T(8,128)(2,1)S(1)}, bf16[2,512,512]{2,1,0:T(8,128)(2,1)}, u32[]{:S(2)}, u32[]{:S(2)}) %collective-permute-start.7) | collective-permute-done | bytes 1048608 | tf_op jit(solution)/shard_map/ppermute | solution.py:622
  242.8 2.0 fusion.6
  245.9 1.8 collective-permute-start.8
  250.0 29.4 %window_attention_backward.2 = (bf16[49,64,512]{2,1,0:T(8,128)(2,1)}, f32[64,512]{1,0:T(8,128)}, f32[4,512,512]{2,1,0:T(8,128)}, f32[5,8,512]{2,1,0:T(8,128)}) custom-call(bf16[49,64,512]{2,1,0:T(8,128)(2,1)} %bitcast.83, f32[64,512]{1,0:T(8,128)} %get-tuple-element.71.r_ref.refs_1_, bf16[2,512,512]{2,1,0:T(8,128)(2,1)} %copy-done.8, ...), custom_call_target="tpu_custom_call" | custom-call | flops 1000000 | bytes 100000 | tf_op jit(solution)/shard_map/window_attention_backward/pallas_call | solution.py:356
  279.4 30.7 %window_attention_backward.3 = (bf16[49,64,512]{2,1,0:T(8,128)(2,1)}, f32[64,512]{1,0:T(8,128)}, f32[4,512,512]{2,1,0:T(8,128)}, f32[5,8,512]{2,1,0:T(8,128)}) custom-call(bf16[49,64,512]{2,1,0:T(8,128)(2,1)} %bitcast.84, f32[64,512]{1,0:T(8,128)} %get-tuple-element.71.r_ref.refs_1_, ...), custom_call_target="tpu_custom_call", output_to_operand_aliasing={{0}: (15, {}), {1}: (16, {})} | custom-call | flops 1000000 | bytes 100000 | tf_op jit(solution)/shard_map/window_attention_backward/pallas_call | solution.py:356
  314.4 2.3 regional_payload.1
  318.6 4.8 all-to-all-start.5
  325.7 2.0 collective-permute-start.9
  332.2 8.5 %collective-permute-done.9 = bf16[128,1024]{1,0:T(8,128)(2,1)S(1)} collective-permute-done((bf16[128,1024]{1,0:T(8,128)(2,1)S(1)}, bf16[128,1024]{1,0:T(8,128)(2,1)S(1)}, u32[]{:S(2)}, u32[]{:S(2)}) %collective-permute-start.9) | collective-permute-done | bytes 262176 | tf_op jit(solution)/shard_map/ppermute | solution.py:651
  345.5 9.5 %regional_attention_backward.1 = (f32[64,512]{1,0:T(8,128)}, bf16[2,512,512]{2,1,0:T(8,128)(2,1)}, bf16[2,512,512]{2,1,0:T(8,128)(2,1)}, f32[5,8,512]{2,1,0:T(8,128)}) custom-call(s32[1,1]{1,0:T(1,128)} %bitcast.28.refs_0_, bf16[512,512]{1,0:T(8,128)(2,1)} %get-tuple-element.97.refs_1_, bf16[512,512]{1,0:T(8,128)(2,1)} %get-tuple-element.98.refs_2_, ...), custom_call_target="tpu_custom_call" | custom-call | flops 1000000 | bytes 100000 | tf_op jit(solution)/shard_map/regional_attention_backward/pallas_call | solution.py:408
  355.1 2.9 collective-permute-done.10
  363.3 11.3 %collective-permute-done.11 = bf16[512,512]{1,0:T(8,128)(2,1)} collective-permute-done((bf16[512,512]{1,0:T(8,128)(2,1)S(1)}, bf16[512,512]{1,0:T(8,128)(2,1)}, u32[]{:S(2)}, u32[]{:S(2)}) %collective-permute-start.11) | collective-permute-done | bytes 524320 | tf_op jit(solution)/shard_map/ppermute | solution.py:622
  374.6 2.0 fusion.5
  376.6 4.2 all-to-all-start.6
  380.8 2.9 collective-permute-start.12
  383.7 15.9 %collective-permute-done.12 = bf16[64,1024]{1,0:T(8,128)(2,1)S(1)} collective-permute-done((bf16[64,1024]{1,0:T(8,128)(2,1)S(1)}, bf16[64,1024]{1,0:T(8,128)(2,1)S(1)}, u32[]{:S(2)}, u32[]{:S(2)}) %collective-permute-start.12) | collective-permute-done | bytes 131104 | tf_op jit(solution)/shard_map/ppermute | solution.py:651
  400.3 6.3 %collective-permute-done.23 = bf16[64,1024]{1,0:T(8,128)(2,1)S(1)} collective-permute-done((bf16[64,1024]{1,0:T(8,128)(2,1)S(1)}, bf16[64,1024]{1,0:T(8,128)(2,1)S(1)}, u32[]{:S(2)}, u32[]{:S(2)}) %collective-permute-start.23) | collective-permute-done | bytes 131104 | tf_op jit(solution)/shard_map/ppermute | solution.py:651
  407.5 5.1 all-to-all-start.2
  414.2 4.8 collective-permute-start.25
  418.9 21.6 %collective-permute-done.25 = bf16[256,1024]{1,0:T(8,128)(2,1)} collective-permute-done((bf16[256,1024]{1,0:T(8,128)(2,1)S(1)}, bf16[256,1024]{1,0:T(8,128)(2,1)}, u32[]{:S(2)}, u32[]{:S(2)}) %collective-permute-start.25) | collective-permute-done | bytes 524320 | tf_op jit(solution)/shard_map/ppermute | solution.py:651
  440.5 2.0 maximum_select_fusion.refs_4_
  451.1 15.9 %collective-permute-done.30.refs_6_ = bf16[512,1024]{1,0:T(8,128)(2,1)} collective-permute-done((bf16[512,1024]{1,0:T(8,128)(2,1)S(1)}, bf16[512,1024]{1,0:T(8,128)(2,1)}, u32[]{:S(2)}, u32[]{:S(2)}) %collective-permute-start.30) | collective-permute-done | bytes 1048608 | tf_op jit(solution)/shard_map/ppermute | solution.py:622
  469.1 2.1 collective-permute-done.14
  472.0 6.2 %all-to-all-start.7 = ((bf16[8,64,512]{2,1,0:T(8,128)(2,1)}), bf16[8,64,512]{2,1,0:T(8,128)(2,1)}, u32[]{:S(2)}, u32[]{:S(2)}) async-start(bf16[8,64,512]{2,1,0:T(8,128)(2,1)} %broadcast_in_dim.53), calls=%async_computation.7 | async-start | bytes 1048576 | tf_op jit(solution)/shard_map/all_to_all | solution.py:647
  478.3 2.1 collective-permute-start.15
  480.4 2.5 collective-permute-done.15
  482.8 2.6 collective-permute-start.21
  485.4 2.0 collective-permute-done.21
  487.4 1.9 collective-permute-start.16
  491.2 3.5 collective-permute-start.22
  494.7 3.3 maximum_bitcast_fusion
  500.1 17.0 %mlp_grams.1 = (f32[512,512]{1,0:T(8,128)}, f32[512,512]{1,0:T(8,128)}, f32[512,512]{1,0:T(8,128)}, f32[512,512]{1,0:T(8,128)}, f32[512,512]{1,0:T(8,128)}, /*index=5*/f32[512,512]{1,0:T(8,128)}) custom-call(f32[2,512,512]{2,1,0:T(8,128)} %fence.10.refs_0_, f32[2,512,512]{2,1,0:T(8,128)} %collective-permute-done.26.refs_1_, f32[2,512,512]{2,1,0:T(8,128)} %fence.11.refs_2_, ...), custom_call_target="tpu_custom_call" | custom-call | flops 1000000 | bytes 100000 | tf_op jit(solution)/shard_map/mlp_grams/pallas_call | solution.py:408
  519.7 29.6 %matrix_updates.1 = (f32[512,512]{1,0:T(8,128)}, f32[512,512]{1,0:T(8,128)}, f32[512,512]{1,0:T(8,128)}, f32[512,512]{1,0:T(8,128)}, f32[512,512]{1,0:T(8,128)}, /*index=5*/f32[512,512]{1,0:T(8,128)}) custom-call(f32[1,1]{1,0:T(1,128)} %bitcast.44.refs_0_, bf16[512,512]{1,0:T(8,128)(2,1)} %bitcast.45.refs_1_, f32[512,512]{1,0:T(8,128)} %bitcast.99, ...), custom_call_target="tpu_custom_call" | custom-call | flops 1000000 | bytes 100000 | tf_op jit(solution)/shard_map/matrix_updates/pallas_call | solution.py:408
  (228 shorter events, 70.0 us)
Async XLA Ops:
  2.3 21.7 %all-to-all-start = ((bf16[8,8,8,512]{3,2,1,0:T(8,128)(2,1)}), bf16[8,8,8,512]{3,2,1,0:T(8,128)(2,1)S(1)}, u32[]{:S(2)}, u32[]{:S(2)}) async-start(bf16[8,8,8,512]{3,2,1,0:T(8,128)(2,1)} %broadcast_in_dim.47), calls=%async_computation | async-start | bytes 1048576 | tf_op jit(solution)/shard_map/all_to_all | solution.py:647
  24.9 53.2 %all-to-all-start.1 = ((bf16[8,20,8,512]{3,2,1,0:T(8,128)(2,1)}), bf16[8,20,8,512]{3,2,1,0:T(8,128)(2,1)S(1)}, u32[]{:S(2)}, u32[]{:S(2)}) async-start(bf16[8,20,8,512]{3,2,1,0:T(8,128)(2,1)} %fence.6), calls=%async_computation.1 | async-start | bytes 2621440 | tf_op jit(solution)/shard_map/all_to_all | solution.py:738
  29.7 13.9 %collective-permute-start.1 = (bf16[512,512]{1,0:T(8,128)(2,1)}, bf16[512,512]{1,0:T(8,128)(2,1)}, u32[]{:S(2)}, u32[]{:S(2)}) collective-permute-start(bf16[512,512]{1,0:T(8,128)(2,1)} %get-tuple-element.145), channel_id=1, source_target_pairs={{0,2},{1,3},{2,0},{3,1},{4,6},{5,7},{6,4},{7,5},{8,10},{9,11},{10,... | collective-permute-start | bytes 1572872 | tf_op jit(solution)/shard_map/ppermute | solution.py:622
  31.2 18.7 %collective-permute-start = (bf16[512,512]{1,0:T(8,128)(2,1)}, bf16[512,512]{1,0:T(8,128)(2,1)}, u32[]{:S(2)}, u32[]{:S(2)}) collective-permute-start(bf16[512,512]{1,0:T(8,128)(2,1)} %get-tuple-element.145), channel_id=1, source_target_pairs={{0,1},{1,0},{2,3},{3,2},{4,5},{5,4},{6,7},{7,6},{8,9},{9,8},{10,11... | collective-permute-start | bytes 1572872 | tf_op jit(solution)/shard_map/ppermute | solution.py:622
  43.6 6.4 %collective-permute-start.2 = (bf16[512,512]{1,0:T(8,128)(2,1)}, bf16[512,512]{1,0:T(8,128)(2,1)}, u32[]{:S(2)}, u32[]{:S(2)}) collective-permute-start(bf16[512,512]{1,0:T(8,128)(2,1)} %collective-permute-done.1._.refs_1_), channel_id=1, source_target_pairs={{0,1},{1,0},{2,3},{3,2},{4,5},{5,4},{6,7},{7,6},{8,9},{9,8},{10,11... | collective-permute-start | bytes 1572872 | tf_op jit(solution)/shard_map/ppermute | solution.py:622
  78.0 85.1 %all-to-all-start.3 = ((bf16[8,30,8,512]{3,2,1,0:T(8,128)(2,1)}), bf16[8,30,8,512]{3,2,1,0:T(8,128)(2,1)S(1)}, u32[]{:S(2)}, u32[]{:S(2)}) async-start(bf16[8,30,8,512]{3,2,1,0:T(8,128)(2,1)} %fence.9), calls=%async_computation.3 | async-start | bytes 3932160 | tf_op jit(solution)/shard_map/all_to_all | solution.py:738
  86.5 26.5 %slice-start.1 = ((f32[12,512]{1,0:T(8,128)}), f32[4,512]{1,0:T(4,128)S(1)}, s32[]{:S(2)}) async-start(f32[12,512]{1,0:T(8,128)} %refs_25_.1), calls=%async_computation.9 | async-start | bytes 16384 | tf_op jit(solution)/shard_map/slice | solution.py:750
  86.5 25.5 %collective-permute-start.4 = (bf16[2,512,512]{2,1,0:T(8,128)(2,1)}, bf16[2,512,512]{2,1,0:T(8,128)(2,1)S(1)}, u32[]{:S(2)}, u32[]{:S(2)}) collective-permute-start(bf16[2,512,512]{2,1,0:T(8,128)(2,1)} %fence.7.refs_3_), channel_id=1, source_target_pairs={{0,2},{1,3},{2,0},{3,1},{4,6},{5,7},{6,4},{7,5},{8,10},{9,11},{10,... | collective-permute-start | bytes 3145736 | tf_op jit(solution)/shard_map/ppermute | solution.py:622
  88.0 46.2 %collective-permute-start.3 = (bf16[2,512,512]{2,1,0:T(8,128)(2,1)}, bf16[2,512,512]{2,1,0:T(8,128)(2,1)}, u32[]{:S(2)}, u32[]{:S(2)}) collective-permute-start(bf16[2,512,512]{2,1,0:T(8,128)(2,1)} %fence.7.refs_3_), channel_id=1, source_target_pairs={{0,1},{1,0},{2,3},{3,2},{4,5},{5,4},{6,7},{7,6},{8,9},{9,8},{10,11... | collective-permute-start | bytes 3145736 | tf_op jit(solution)/shard_map/ppermute | solution.py:622
  113.0 21.3 %collective-permute-start.5 = (bf16[2,512,512]{2,1,0:T(8,128)(2,1)}, bf16[2,512,512]{2,1,0:T(8,128)(2,1)S(1)}, u32[]{:S(2)}, u32[]{:S(2)}) collective-permute-start(bf16[2,512,512]{2,1,0:T(8,128)(2,1)} %fence.8.refs_5_), channel_id=1, source_target_pairs={{0,1},{1,0},{2,3},{3,2},{4,5},{5,4},{6,7},{7,6},{8,9},{9,8},{10,11... | collective-permute-start | bytes 3145736 | tf_op jit(solution)/shard_map/ppermute | solution.py:622
  113.6 20.7 %copy-start.36 = (pred[4]{0:T(512)(128)(4,1)}, pred[4]{0:T(512)(128)(4,1)S(1)}, u32[]{:S(2)}) copy-start(pred[4]{0:T(512)(128)(4,1)S(1)} %compare_and_fusion) | copy-start | bytes 16
  204.7 6.4 %collective-permute-start.6 = (bf16[4,512,512]{2,1,0:T(8,128)(2,1)}, bf16[4,512,512]{2,1,0:T(8,128)(2,1)}, u32[]{:S(2)}, u32[]{:S(2)}) collective-permute-start(bf16[4,512,512]{2,1,0:T(8,128)(2,1)} %get-tuple-element.78), channel_id=1, source_target_pairs={{0,1},{1,0},{2,3},{3,2},{4,5},{5,4},{6,7},{7,6},{8,9},{9,8},{10,11... | collective-permute-start | bytes 6291464 | tf_op jit(solution)/shard_map/ppermute | solution.py:622
  205.3 107.9 %all-to-all-start.4 = ((bf16[8,30,8,512]{3,2,1,0:T(8,128)(2,1)}), bf16[8,30,8,512]{3,2,1,0:T(8,128)(2,1)S(1)}, u32[]{:S(2)}, u32[]{:S(2)}) async-start(bf16[8,30,8,512]{3,2,1,0:T(8,128)(2,1)} %get-tuple-element.77), calls=%async_computation.4 | async-start | bytes 3932160 | tf_op jit(solution)/shard_map/all_to_all | solution.py:738
  216.3 26.5 %copy-start.8 = (bf16[2,512,512]{2,1,0:T(8,128)(2,1)}, bf16[2,512,512]{2,1,0:T(8,128)(2,1)S(1)}, u32[]{:S(2)}) copy-start(bf16[2,512,512]{2,1,0:T(8,128)(2,1)S(1)} %pad_maximum_fusion.4.refs_2_) | copy-start | bytes 3145732
  216.3 25.0 %collective-permute-start.7 = (bf16[2,512,512]{2,1,0:T(8,128)(2,1)S(1)}, bf16[2,512,512]{2,1,0:T(8,128)(2,1)}, u32[]{:S(2)}, u32[]{:S(2)}) collective-permute-start(bf16[2,512,512]{2,1,0:T(8,128)(2,1)S(1)} %pad_maximum_fusion.4.refs_2_), channel_id=1, source_target_pairs={{0,2},{1,3},{2,0},{3,1},{4,6},{5,7},{6,4},{7,5},{8,10},{9,11},{10,... | collective-permute-start | bytes 3145736 | tf_op jit(solution)/shard_map/ppermute | solution.py:622
  245.9 33.5 %copy-start.17 = (bf16[256,1024]{1,0:T(8,128)(2,1)}, bf16[256,1024]{1,0:T(8,128)(2,1)S(1)}, u32[]{:S(2)}) copy-start(bf16[256,1024]{1,0:T(8,128)(2,1)S(1)} %fusion.3.refs_2_) | copy-start | bytes 1572868
  245.9 64.2 %collective-permute-start.8 = (bf16[256,1024]{1,0:T(8,128)(2,1)S(1)}, bf16[256,1024]{1,0:T(8,128)(2,1)}, u32[]{:S(2)}, u32[]{:S(2)}) collective-permute-start(bf16[256,1024]{1,0:T(8,128)(2,1)S(1)} %fusion.3.refs_2_), channel_id=1, source_target_pairs={{0,4},{4,0},{8,12},{12,8},{16,20},{20,16},{24,28},{28,24},{1,5},{5... | collective-permute-start | bytes 1572872 | tf_op jit(solution)/shard_map/ppermute | solution.py:651
  316.8 23.9 %copy-start.14 = (f32[256,1024]{1,0:T(8,128)S(1)}, f32[256,1024]{1,0:T(8,128)}, u32[]{:S(2)}) copy-start(f32[256,1024]{1,0:T(8,128)} %copy-done.13) | copy-start | bytes 3145732
  318.6 22.8 %all-to-all-start.5 = ((bf16[8,64,640]{2,1,0:T(8,128)(2,1)}), bf16[8,64,640]{2,1,0:T(8,128)(2,1)S(1)}, u32[]{:S(2)}, u32[]{:S(2)}) async-start(bf16[8,64,640]{2,1,0:T(8,128)(2,1)} %broadcast_in_dim.50), calls=%async_computation.5 | async-start | bytes 1310720 | tf_op jit(solution)/shard_map/all_to_all | solution.py:647
  325.7 15.0 %collective-permute-start.9 = (bf16[128,1024]{1,0:T(8,128)(2,1)S(1)}, bf16[128,1024]{1,0:T(8,128)(2,1)S(1)}, u32[]{:S(2)}, u32[]{:S(2)}) collective-permute-start(bf16[128,1024]{1,0:T(8,128)(2,1)S(1)} %copy-done.21), channel_id=1, source_target_pairs={{0,8},{4,12},{8,0},{12,4},{16,24},{20,28},{24,16},{28,20},{1,9},{5... | collective-permute-start | bytes 786440 | tf_op jit(solution)/shard_map/ppermute | solution.py:651
  355.0 2.9 collective-permute-start.10
  359.7 14.9 %collective-permute-start.11 = (bf16[512,512]{1,0:T(8,128)(2,1)S(1)}, bf16[512,512]{1,0:T(8,128)(2,1)}, u32[]{:S(2)}, u32[]{:S(2)}) collective-permute-start(bf16[512,512]{1,0:T(8,128)(2,1)S(1)} %fusion.8), channel_id=1, source_target_pairs={{0,2},{1,3},{2,0},{3,1},{4,6},{5,7},{6,4},{7,5},{8,10},{9,11},{10,... | collective-permute-start | bytes 1572872 | tf_op jit(solution)/shard_map/ppermute | solution.py:622
  362.8 81.4 %collective-permute-start.27 = (f32[2,512,512]{2,1,0:T(8,128)}, f32[2,512,512]{2,1,0:T(8,128)}, u32[]{:S(2)}, u32[]{:S(2)}) collective-permute-start(f32[2,512,512]{2,1,0:T(8,128)} %fence.10.refs_0_), channel_id=1, source_target_pairs={{0,2},{1,3},{2,0},{3,1},{4,6},{5,7},{6,4},{7,5},{8,10},{9,11},{10,... | collective-permute-start | bytes 6291464 | tf_op jit(solution)/shard_map/ppermute | solution.py:622
  376.6 30.1 %all-to-all-start.6 = ((bf16[8,64,512]{2,1,0:T(8,128)(2,1)}), bf16[8,64,512]{2,1,0:T(8,128)(2,1)S(1)}, u32[]{:S(2)}, u32[]{:S(2)}) async-start(bf16[8,64,512]{2,1,0:T(8,128)(2,1)} %bitcast.42), calls=%async_computation.6 | async-start | bytes 1048576 | tf_op jit(solution)/shard_map/all_to_all | solution.py:738
  380.8 18.8 %collective-permute-start.12 = (bf16[64,1024]{1,0:T(8,128)(2,1)S(1)}, bf16[64,1024]{1,0:T(8,128)(2,1)S(1)}, u32[]{:S(2)}, u32[]{:S(2)}) collective-permute-start(bf16[64,1024]{1,0:T(8,128)(2,1)S(1)} %copy-done.22), channel_id=1, source_target_pairs={{0,16},{4,20},{8,24},{12,28},{16,0},{20,4},{24,8},{28,12},{1,17},{... | collective-permute-start | bytes 393224 | tf_op jit(solution)/shard_map/ppermute | solution.py:651
  400.3 6.3 %collective-permute-start.23 = (bf16[64,1024]{1,0:T(8,128)(2,1)S(1)}, bf16[64,1024]{1,0:T(8,128)(2,1)S(1)}, u32[]{:S(2)}, u32[]{:S(2)}) collective-permute-start(bf16[64,1024]{1,0:T(8,128)(2,1)S(1)} %get-tuple-element.133), channel_id=1, source_target_pairs={{0,16},{4,20},{8,24},{12,28},{16,0},{20,4},{24,8},{28,12},{1,17},{... | collective-permute-start | bytes 393224 | tf_op jit(solution)/shard_map/ppermute | solution.py:651
  406.6 7.4 %collective-permute-start.24 = (bf16[128,1024]{1,0:T(8,128)(2,1)S(1)}, bf16[128,1024]{1,0:T(8,128)(2,1)S(1)}, u32[]{:S(2)}, u32[]{:S(2)}) collective-permute-start(bf16[128,1024]{1,0:T(8,128)(2,1)S(1)} %maximum_select_fusion.2), channel_id=1, source_target_pairs={{0,8},{4,12},{8,0},{12,4},{16,24},{20,28},{24,16},{28,20},{1,9},{5... | collective-permute-start | bytes 786440 | tf_op jit(solution)/shard_map/ppermute | solution.py:651
  407.5 63.7 %all-to-all-start.2 = ((bf16[8,20,8,512]{3,2,1,0:T(8,128)(2,1)}), bf16[8,20,8,512]{3,2,1,0:T(8,128)(2,1)}, u32[]{:S(2)}, u32[]{:S(2)}) async-start(bf16[8,20,8,512]{3,2,1,0:T(8,128)(2,1)} %get-tuple-element.74), calls=%async_computation.2 | async-start | bytes 2621440 | tf_op jit(solution)/shard_map/all_to_all | solution.py:738
  412.6 31.6 %copy-start = (f32[2,512,512]{2,1,0:T(8,128)S(1)}, f32[2,512,512]{2,1,0:T(8,128)}, u32[]{:S(2)}) copy-start(f32[2,512,512]{2,1,0:T(8,128)} %fence.10.refs_0_) | copy-start | bytes 6291460
  414.2 26.4 %collective-permute-start.25 = (bf16[256,1024]{1,0:T(8,128)(2,1)S(1)}, bf16[256,1024]{1,0:T(8,128)(2,1)}, u32[]{:S(2)}, u32[]{:S(2)}) collective-permute-start(bf16[256,1024]{1,0:T(8,128)(2,1)S(1)} %maximum_select_fusion.1), channel_id=1, source_target_pairs={{0,4},{4,0},{8,12},{12,8},{16,20},{20,16},{24,28},{28,24},{1,5},{5... | collective-permute-start | bytes 1572872 | tf_op jit(solution)/shard_map/ppermute | solution.py:651
  442.6 24.5 %copy-start.3 = (bf16[512,1024]{1,0:T(8,128)(2,1)}, bf16[512,1024]{1,0:T(8,128)(2,1)S(1)}, u32[]{:S(2)}) copy-start(bf16[512,1024]{1,0:T(8,128)(2,1)S(1)} %maximum_select_fusion.refs_4_) | copy-start | bytes 3145732
  442.6 24.4 %collective-permute-start.30 = (bf16[512,1024]{1,0:T(8,128)(2,1)S(1)}, bf16[512,1024]{1,0:T(8,128)(2,1)}, u32[]{:S(2)}, u32[]{:S(2)}) collective-permute-start(bf16[512,1024]{1,0:T(8,128)(2,1)S(1)} %maximum_select_fusion.refs_4_), channel_id=1, source_target_pairs={{0,2},{1,3},{2,0},{3,1},{4,6},{5,7},{6,4},{7,5},{8,10},{9,11},{10,... | collective-permute-start | bytes 3145736 | tf_op jit(solution)/shard_map/ppermute | solution.py:622
  444.2 55.9 %collective-permute-start.26 = (f32[2,512,512]{2,1,0:T(8,128)S(1)}, f32[2,512,512]{2,1,0:T(8,128)}, u32[]{:S(2)}, u32[]{:S(2)}) collective-permute-start(f32[2,512,512]{2,1,0:T(8,128)S(1)} %copy-done), channel_id=1, source_target_pairs={{0,1},{1,0},{2,3},{3,2},{4,5},{5,4},{6,7},{7,6},{8,9},{9,8},{10,11... | collective-permute-start | bytes 6291464 | tf_op jit(solution)/shard_map/ppermute | solution.py:622
  444.2 55.9 %collective-permute-start.28 = (f32[2,512,512]{2,1,0:T(8,128)}, f32[2,512,512]{2,1,0:T(8,128)}, u32[]{:S(2)}, u32[]{:S(2)}) collective-permute-start(f32[2,512,512]{2,1,0:T(8,128)} %fence.11.refs_2_), channel_id=1, source_target_pairs={{0,1},{1,0},{2,3},{3,2},{4,5},{5,4},{6,7},{7,6},{8,9},{9,8},{10,11... | collective-permute-start | bytes 6291464 | tf_op jit(solution)/shard_map/ppermute | solution.py:622
  445.6 5.0 collective-permute-start.18
  448.8 18.2 %collective-permute-start.13 = (f32[8,128]{1,0:T(8,128)S(1)}, f32[8,128]{1,0:T(8,128)S(1)}, u32[]{:S(2)}, u32[]{:S(2)}) collective-permute-start(f32[8,128]{1,0:T(8,128)S(1)} %broadcast_in_dim.52), channel_id=1, source_target_pairs={{0,1},{1,0},{2,3},{3,2},{4,5},{5,4},{6,7},{7,6},{8,9},{9,8},{10,11... | collective-permute-start | bytes 12296 | tf_op jit(solution)/shard_map/ppermute | solution.py:622
  450.6 16.9 %collective-permute-start.19 = (f32[12,512]{1,0:T(8,128)S(1)}, f32[12,512]{1,0:T(8,128)S(1)}, u32[]{:S(2)}, u32[]{:S(2)}) collective-permute-start(f32[12,512]{1,0:T(8,128)S(1)} %add.200), channel_id=1, source_target_pairs={{0,2},{1,3},{2,0},{3,1},{4,6},{5,7},{6,4},{7,5},{8,10},{9,11},{10,... | collective-permute-start | bytes 73736 | tf_op jit(solution)/shard_map/ppermute | solution.py:622
  467.0 33.1 %collective-permute-start.29 = (bf16[512,1024]{1,0:T(8,128)(2,1)S(1)}, bf16[512,1024]{1,0:T(8,128)(2,1)}, u32[]{:S(2)}, u32[]{:S(2)}) collective-permute-start(bf16[512,1024]{1,0:T(8,128)(2,1)S(1)} %maximum_select_fusion.refs_4_), channel_id=1, source_target_pairs={{0,1},{1,0},{2,3},{3,2},{4,5},{5,4},{6,7},{7,6},{8,9},{9,8},{10,11... | collective-permute-start | bytes 3145736 | tf_op jit(solution)/shard_map/ppermute | solution.py:622
  467.1 33.1 %collective-permute-start.31 = (bf16[512,1024]{1,0:T(8,128)(2,1)}, bf16[512,1024]{1,0:T(8,128)(2,1)}, u32[]{:S(2)}, u32[]{:S(2)}) collective-permute-start(bf16[512,1024]{1,0:T(8,128)(2,1)} %collective-permute-done.30.refs_6_), channel_id=1, source_target_pairs={{0,1},{1,0},{2,3},{3,2},{4,5},{5,4},{6,7},{7,6},{8,9},{9,8},{10,11... | collective-permute-start | bytes 3145736 | tf_op jit(solution)/shard_map/ppermute | solution.py:622
  467.6 3.6 collective-permute-start.14
  471.2 7.1 %collective-permute-start.20 = (f32[12,512]{1,0:T(8,128)S(1)}, f32[12,512]{1,0:T(8,128)S(1)}, u32[]{:S(2)}, u32[]{:S(2)}) collective-permute-start(f32[12,512]{1,0:T(8,128)S(1)} %add.201), channel_id=1, source_target_pairs={{0,4},{4,0},{8,12},{12,8},{16,20},{20,16},{24,28},{28,24},{1,5},{5... | collective-permute-start | bytes 73736 | tf_op jit(solution)/shard_map/ppermute | solution.py:651
  472.0 47.7 %all-to-all-start.7 = ((bf16[8,64,512]{2,1,0:T(8,128)(2,1)}), bf16[8,64,512]{2,1,0:T(8,128)(2,1)}, u32[]{:S(2)}, u32[]{:S(2)}) async-start(bf16[8,64,512]{2,1,0:T(8,128)(2,1)} %broadcast_in_dim.53), calls=%async_computation.7 | async-start | bytes 1048576 | tf_op jit(solution)/shard_map/all_to_all | solution.py:647
  478.3 4.6 collective-permute-start.15
  482.8 4.6 collective-permute-start.21
  487.4 3.8 collective-permute-start.16
  491.2 6.8 %collective-permute-start.22 = (f32[12,512]{1,0:T(8,128)S(1)}, f32[12,512]{1,0:T(8,128)S(1)}, u32[]{:S(2)}, u32[]{:S(2)}) collective-permute-start(f32[12,512]{1,0:T(8,128)S(1)} %add.203), channel_id=1, source_target_pairs={{0,16},{4,20},{8,24},{12,28},{16,0},{20,4},{24,8},{28,12},{1,17},{... | collective-permute-start | bytes 73736 | tf_op jit(solution)/shard_map/ppermute | solution.py:651
  497.9 19.2 %collective-permute-start.17 = (f32[8,128]{1,0:T(8,128)S(1)}, f32[8,128]{1,0:T(8,128)S(1)}, u32[]{:S(2)}, u32[]{:S(2)}) collective-permute-start(f32[8,128]{1,0:T(8,128)S(1)} %add.195), channel_id=1, source_target_pairs={{0,16},{4,20},{8,24},{12,28},{16,0},{20,4},{24,8},{28,12},{1,17},{... | collective-permute-start | bytes 12296 | tf_op jit(solution)/shard_map/ppermute | solution.py:651
  500.1 19.0 %copy-start.33 = (f32[12,512]{1,0:T(8,128)S(1)}, f32[12,512]{1,0:T(8,128)}, u32[]{:S(2)}) copy-start(f32[12,512]{1,0:T(8,128)} %param.29) | copy-start | bytes 73732
  (32 other events, 172.5 us)

commit v5 on v4

--- a/solution.py
+++ b/solution.py
@@ -38,7 +38,10 @@
 CLIP_LIMIT = 1.0
 DECAY_KEEP = 1.0 - MUON_RATE * MUON_DECAY
 VMEM = 60 * 2**20
-BRIEF = pl.CostEstimate(flops=10**6, bytes_accessed=10**5, transcendentals=0)
+
+
+def cost(flops):
+    return pl.CostEstimate(flops=int(flops), bytes_accessed=10**5, transcendentals=0)
 
 ERF_P = 0.3275911 * 0.5**0.5
 ERF = tuple(0.5 * c for c in (0.254829592, -0.284496736, 1.421413741, -1.453152027, 1.061405429))
@@ -120,7 +123,7 @@
     return a * share, share + a * bell * INV_SQRT_2PI
 
 
-def attn_fwd_kernel(count, batch, p_ref, r_ref, wq_ref, wk_ref, wv_ref, wo_ref, vec_ref, _,
+def attn_fwd_kernel(count, batch, p_ref, r_ref, wq_ref, wk_ref, wv_ref, wo_ref, vec_ref,
                     x1_ref, q_ref, k_ref, v_ref, o_ref, pt_ref, q_held, k_held, v_held, o_held):
     total = count * LIVE
 
@@ -174,29 +177,32 @@
     return pl.BlockSpec((rows, count, D), lambda i: (0, i + skip, 0))
 
 
-def attn_fwd(patches, region_rows, weights, vec, start, windows, after, count=16, batch=4):
-    skip = start // count
+def attn_fwd(patches, region_rows, weights, vec, count=16, batch=4):
+    windows = patches.shape[1]
     array = jax.ShapeDtypeStruct
     return pl.pallas_call(
         partial(attn_fwd_kernel, count, batch),
         grid=(windows // count,),
-        in_specs=[middle(PATCH, count, skip), pl.BlockSpec((count, D), lambda i: (i + skip, 0))]
-        + [full((D, D))] * 4 + [full(vec.shape), pl.BlockSpec(memory_space=pl.ANY)],
+        in_specs=[middle(PATCH, count), block((count, D))] + [full((D, D))] * 4 + [full(vec.shape)],
         out_specs=[middle(LIVE, count)] + [block((count, ROWS, D))] * 3
         + [middle(LIVE, count), block((count, 4, ROWS, STACK))],
         out_shape=[array((LIVE, windows, D), F32)] + [array((windows, ROWS, D), BF)] * 3
         + [array((LIVE, windows, D), BF), array((windows, 4, ROWS, STACK), BF)],
         scratch_shapes=[pltpu.VMEM((4, count * ROWS, GROUP), F32)] * 4,
         compiler_params=pltpu.CompilerParams(vmem_limit_bytes=VMEM),
-        cost_estimate=BRIEF,
+        cost_estimate=cost(16e9),
         name="window_attention_forward",
-    )(patches, region_rows, *weights, vec, after)
+    )(patches, region_rows, *weights, vec)
 
 
 def mlp_kernel(many, sources, cols, steps, lanes, last, *refs):
-    x1a_ref, x1b_ref, pc_ref, *w_refs, vec_ref, b1_ref = refs[:9]
-    prev_refs = refs[9 : 11 if last else 9]
-    op_ref, dx1_ref, dwa_ref, dwb_ref, dv_ref, db1_ref, acc1, acc2 = refs[9 + len(prev_refs) :]
+    x1_ref, pc_ref, *w_refs, vec_ref, b1_ref = refs[:8]
+    if last:
+        prev_refs = refs[9:11]
+        op_ref, dx1_ref, dwa_ref, dwb_ref, dv_ref, db1_ref, acc1, acc2 = refs[11:]
+    else:
+        prev_refs = ()
+        early_ref, op_ref, dx1_ref, dwa_ref, dwb_ref, dv_ref, db1_ref, acc1, acc2 = refs[8:]
     total = many * sources * cols
     step = pl.program_id(0)
 
@@ -207,7 +213,7 @@
 
     vec = vec_ref[...]
     gain = vec[2:3]
-    x1 = jnp.concatenate([x1a_ref[...], x1b_ref[...]], axis=1).reshape(total, D)
+    x1 = x1_ref[...].reshape(total, D)
     xhat, scale = norm_parts(x1)
     h = (xhat * gain + vec[3:4]).astype(BF)
     for s in range(sources):
@@ -238,8 +244,16 @@
         y, dh = y + up, dh + down
         held_pair = later
     y = y.reshape(many, sources * cols, D)
-    for s in range(sources):
-        op_ref[s] = y[:, s * cols : (s + 1) * cols].astype(BF)
+
+    def put(ref):
+        for s in range(sources):
+            ref[s] = y[:, s * cols : (s + 1) * cols].astype(BF)
+
+    if last:
+        put(op_ref)
+    else:
+        pl.when(step < steps - 1)(lambda: put(early_ref))
+        pl.when(step == steps - 1)(lambda: put(op_ref))
     dy = dx1_ref[...].reshape(total, D)
     dx1_ref[...] = (dy + norm_back(dh, xhat, scale, gain)).reshape(dx1_ref.shape)
     dv_ref[0] += fold(dh * xhat)
@@ -253,35 +267,42 @@
                 for m in range(2):
                     piece = acc[first + 2 * m]
                     for prev in prev_refs[first : first + 1]:
-                        piece = piece + prev[2 * n + m].astype(F32)
-                    refs_out[2 * n + m] = piece.astype(BF)
-
-
-def mlp(x1_parts, first_position, cot, weights, vec, bias_first, prev=(), many=10, lanes=256):
+                        piece = piece + prev[2 * m + n].astype(F32)
+                    refs_out[2 * m + n] = piece.astype(BF)
+
+
+def mlp(x1, first_position, cot, weights, vec, bias_first, prev=(), many=10, lanes=256):
     sources, positions, cols, _ = cot.shape
     windows = sources * cols
     steps = positions // many
     skip = first_position // many
-    some = pl.BlockSpec((sources, many, cols, D), lambda i: (0, i, 0, 0))
+    some = lambda place: pl.BlockSpec((sources, many, cols, D), lambda i: (0, place(i), 0, 0))
     array = jax.ShapeDtypeStruct
     matrices = full((4, D, D))
+    rows = lambda count: array((sources, count, cols, D), BF)
+    late = (LIVE - positions if not prev else positions) + many
+    outs = [some(lambda i: i + 1)] if prev else [some(lambda i: jnp.minimum(i, steps - 2)), some(lambda i: 0)]
+    shapes = [rows(late)] if prev else [rows(positions - many), rows(late)]
     return pl.pallas_call(
         partial(mlp_kernel, many, sources, cols, steps, lanes, len(prev) > 0),
         grid=(steps,),
-        in_specs=[pl.BlockSpec((many, part.shape[1], D), lambda i: (i + skip, 0, 0)) for part in x1_parts] + [some]
-        + [full((2, D, D))] * 4 + [full(vec.shape), full((4, D))] + [matrices] * len(prev),
-        out_specs=[some, block((many, windows, D)), matrices, matrices, full((3, 8, D)), full((4, 8, D))],
-        out_shape=[array(cot.shape, BF), array((positions, windows, D), F32), array((4, D, D), BF),
-                   array((4, D, D), BF), array((3, 8, D), F32), array((4, 8, D), F32)],
+        in_specs=[pl.BlockSpec((many, windows, D), lambda i: (i + skip, 0, 0)), some(lambda i: i)]
+        + [full((2, D, D))] * 4 + [full(vec.shape), full((4, D))]
+        + ([pl.BlockSpec(memory_space=pl.ANY)] + [matrices] * 2 if prev else []),
+        out_specs=outs + [block((many, windows, D)), matrices, matrices, full((3, 8, D)), full((4, 8, D))],
+        out_shape=shapes + [array((positions, windows, D), F32), array((4, D, D), BF),
+                            array((4, D, D), BF), array((3, 8, D), F32), array((4, 8, D), F32)],
         scratch_shapes=[pltpu.VMEM((4, D, D), F32), pltpu.VMEM((4, D, D), F32)],
+        input_output_aliases={8: 0} if prev else {},
         compiler_params=pltpu.CompilerParams(vmem_limit_bytes=VMEM),
-        cost_estimate=BRIEF,
+        cost_estimate=cost(4e9 * steps),
         name="mlp_forward_backward",
-    )(*x1_parts, cot, *weights, vec, bias_first, *prev)
+    )(x1, cot, *weights, vec, bias_first, *prev)
 
 
 def attn_bwd_kernel(count, batch, chunks, more, *refs):
-    p_ref, r_ref, _ = refs[:3]
+    p_ref, r_ref = refs[:2]
+    refs = refs[:3] + refs[4:]
     dx1_refs = refs[3 : 3 + chunks]
     q_ref, k_ref, v_ref, o_ref, pt_ref, wq_ref, wk_ref, wv_ref, wo_ref, vec_ref = refs[3 + chunks : 13 + chunks]
     prev_refs = refs[13 + chunks : 17 + chunks] if more else ()
@@ -352,13 +373,14 @@
     sums = [full((4, D, D)), full((5, 8, D))]
     anywhere = pl.BlockSpec(memory_space=pl.ANY)
     rows = pl.BlockSpec((count, D), lambda i: (i + skip, 0))
-    before = 13 + len(dx1_parts)
+    before = 14 + len(dx1_parts)
     return pl.pallas_call(
         partial(attn_bwd_kernel, count, batch, len(dx1_parts), len(prev) > 0),
         grid=(windows // count,),
-        in_specs=[middle(PATCH, count, skip), rows, anywhere]
+        in_specs=[middle(PATCH, count, skip), rows, anywhere, anywhere]
         + [middle(part.shape[0], count, skip) for part in dx1_parts]
-        + [block((count, ROWS, D))] * 3 + [middle(LIVE, count), block((count, 4, ROWS, STACK))]
+        + [pl.BlockSpec((count, ROWS, D), lambda i: (i + skip, 0, 0))] * 3
+        + [middle(LIVE, count, skip), pl.BlockSpec((count, 4, ROWS, STACK), lambda i: (i + skip, 0, 0, 0))]
         + [full((D, D))] * 4 + [full(vec.shape)] + ([anywhere] * 2 + sums)[: len(prev)],
         out_specs=[middle(PATCH, count, skip), rows] + sums,
         out_shape=[array(patches.shape, BF), array(region_rows.shape, F32),
@@ -366,9 +388,9 @@
         scratch_shapes=[pltpu.VMEM((4, count * ROWS, GROUP), F32)] * 4,
         input_output_aliases={before: 0, before + 1: 1} if prev else {},
         compiler_params=pltpu.CompilerParams(vmem_limit_bytes=VMEM),
-        cost_estimate=BRIEF,
+        cost_estimate=cost(12e9),
         name="window_attention_backward",
-    )(patches, region_rows, after, *dx1_parts, *saved, *weights, vec, *prev)
+    )(patches, region_rows, *after, *dx1_parts, *saved, *weights, vec, *prev)
 
 
 def regional_fwd_kernel(canvas_ref, band_ref, ids_ref, band_ids_ref, wq_ref, wk_ref, wv_ref, wo_ref, vec_ref,
@@ -402,7 +424,7 @@
     r1_ref[...] = band + nn(mixed_ref[...].astype(BF), wo_ref[...]) + vec[6:7]
 
 
-def in_vmem(kernel, outs, name, *args, after=(), scratch=()):
+def in_vmem(kernel, outs, name, *args, after=(), scratch=(), flops=2e9):
     spaces = [pltpu.SMEM if arg.shape == (1, 1) else pltpu.VMEM for arg in args]
     count = len(args)
     return pl.pallas_call(
@@ -413,7 +435,7 @@
         out_shape=[jax.ShapeDtypeStruct(*out) for out in outs],
         scratch_shapes=list(scratch),
         compiler_params=pltpu.CompilerParams(vmem_limit_bytes=VMEM),
-        cost_estimate=BRIEF,
+        cost_estimate=cost(flops),
         name=name,
     )(*args, *after)
 
@@ -583,21 +605,33 @@
     return results
 
 
-def grams_kernel(*refs):
-    for n in range(2):
-        old, mixed, new = (jnp.zeros((D, D), F32) for _ in range(3))
-        cross = jnp.zeros((D, D), F32)
-        for j in range(4):
-            high, low = halves(refs[j][n])
+def old_grams_kernel(moms_ref, *out_refs):
+    for n, out_ref in enumerate(out_refs):
+        square, cross = jnp.zeros((D, D), F32), jnp.zeros((D, D), F32)
+        for j in range(OPT):
+            high, low = halves(moms_ref[j, n])
             if n == 1:
                 high, low = high.T, low.T
-            g = refs[4 + j][:, n * D : (n + 1) * D]
-            old = old + nt(high, high)
+            square = square + nt(high, high)
             cross = cross + nt(high, low)
+        out_ref[...] = square + (cross + cross.T)
+
+
+def grams_kernel(places, owner_ref, moms_ref, all_ref, mixed1_ref, new1_ref, mixed2_ref, new2_ref, own_ref):
+    half = len(places) // 2
+    for n, (mixed_ref, new_ref) in enumerate(((mixed1_ref, new1_ref), (mixed2_ref, new2_ref))):
+        mixed, new = jnp.zeros((D, D), F32), jnp.zeros((D, D), F32)
+        mine = places[n * half : (n + 1) * half]
+        for j in range(OPT):
+            high, low = halves(moms_ref[j, n])
+            if n == 1:
+                high, low = high.T, low.T
+            g = jnp.concatenate([all_ref[d, j] for d in mine], axis=0)
             mixed = mixed + (nt(high, g) + nt(low, g))
             new = new + nt(g, g)
-        for k, x in enumerate((old + (cross + cross.T), mixed + mixed.T, new)):
-            refs[8 + 3 * n + k][...] = x
+        mixed_ref[...] = mixed + mixed.T
+        new_ref[...] = new
+        own_ref[n] = jnp.concatenate([all_ref[d, owner_ref[0, 0]] for d in mine], axis=0)
 
 
 def update_kernel(clip_ref, ga_ref, ma_ref, wa_ref, g_ref, m1_ref, m2_ref, w1_ref, w2_ref,
@@ -605,8 +639,8 @@
     clip = clip_ref[0, 0]
     eye = identity()
     na_ref[...] = MUON_MOMENTUM * ma_ref[...] + clip * ga_ref[...].astype(F32)
-    n1_ref[...] = MUON_MOMENTUM * m1_ref[...] + clip * g_ref[:, :D].astype(F32)
-    n2_ref[...] = MUON_MOMENTUM * m2_ref[...] + clip * g_ref[:, D:].astype(F32).T
+    n1_ref[...] = MUON_MOMENTUM * m1_ref[...] + clip * g_ref[0].astype(F32)
+    n2_ref[...] = MUON_MOMENTUM * m2_ref[...] + clip * g_ref[1].astype(F32).T
     a, b, c = MUON_MOMENTUM * MUON_MOMENTUM, MUON_MOMENTUM * clip, clip * clip
     gram1 = a * old1[...] + b * mixed1[...] + c * new1[...]
     gram2 = a * old2[...] + b * mixed2[...] + c * new2[...]
@@ -630,16 +664,15 @@
         out_specs=here,
         out_shape=jax.ShapeDtypeStruct(x.shape, x.dtype),
         input_output_aliases={0: 0},
-        cost_estimate=BRIEF,
+        cost_estimate=cost(1e3),
         name="fence",
     )(x, *first)
 
 
-def pieces_of_owners(own, before_relay=()):
+def pieces_of_owners(own):
     mate = pair(own, 1)
     across = pair(own, 2)
-    relay = fence(across, *before_relay) if before_relay else across
-    return [own, mate, relay, pair(relay, 1)]
+    return [own, mate, across, pair(across, 1)]
 
 
 def share(x):
@@ -662,10 +695,9 @@
     return lax.dynamic_slice_in_dim(x, side * half, half, 0), give
 
 
-def doubling_step(x, bit):
-    other = swap(x, bit)
-    side = (lax.axis_index("dp") // bit) % 2
-    return jnp.where(side == 0, jnp.concatenate([x, other]), jnp.concatenate([other, x]))
+def order_of_halves(count):
+    width = count.bit_length() - 1
+    return [int(format(n, "b").zfill(width)[::-1], 2) if width else 0 for n in range(count)]
 
 
 def sum_small_over_dp(x):
@@ -737,14 +769,13 @@
     order = opt_index ^ jnp.arange(OPT)
     move = lambda x: lax.all_to_all(x, "dp", 0, 0, tiled=True)
 
-    attn_pieces = pieces_of_owners(attn_w[0].astype(BF))
-    across = attn_pieces[2]
-    attn_pieces = jnp.stack(attn_pieces)
+    attn_pieces = jnp.stack(pieces_of_owners(attn_w[0].astype(BF)))
+    mlp_w = pieces_of_owners(jnp.stack([mlp_in, mlp_out]).astype(BF))
     weights = [lax.dynamic_index_in_dim(attn_pieces, opt_index ^ j, 0, keepdims=False) for j in range(OPT)]
     canvas_blocks = share(regions[0])
     canvas = canvas_blocks.reshape(tokens, D)
     by_position = patch_cot[0].transpose(0, 2, 1, 3)
-    split = 20
+    split = 30
     last = jnp.concatenate([by_position[:, split:], region_cot[0][:, None]], axis=1)
     first_cot = move(fence(by_position[:, :split], canvas))
     bias_first = jnp.take(vec[8:], order, axis=0)
@@ -760,7 +791,8 @@
         region_rows, mixed, level, reg_q, reg_k, reg_v = in_vmem(
             regional_fwd_kernel,
             [((grid_cols, D), F32), ((grid_cols, D), F32), ((4, 4 * grid_cols), F32)] + [((tokens, D), BF)] * 3,
-            "regional_attention_forward", canvas, band, ids[:, None], repeat(band_ids), *weights, vec)
+            "regional_attention_forward", canvas, band, ids[:, None], repeat(band_ids), *weights, vec,
+            after=(mlp_w[2],))
         level = level.reshape(HEADS, grid_cols)
     else:
         region_rows, mixed, level, reg_q, reg_k, reg_v = regional_forward(
@@ -769,39 +801,37 @@
 
     windows = patches[0, 0].transpose(1, 0, 2)
     some = grid_cols // 2
-    x1a, *saved_a = attn_fwd(windows, region_rows, weights, vec, 0, some, across)
-    own_mlp_w = fence(jnp.stack([mlp_in, mlp_out]).astype(BF), across)
-    mlp_w = pieces_of_owners(own_mlp_w, before_relay=(x1a,))
-    last_cot = move(fence(last, x1a))
-    x1b, *saved_b = attn_fwd(windows, region_rows, weights, vec, some, some, first_cot)
-    x1 = (x1a, x1b)
-    out_a = mlp(x1, 0, first_cot, mlp_w, vec, bias_first)
-    moms = pieces_of_owners(fence(jnp.stack([mlp_in_mom, mlp_out_mom]), x1b), before_relay=(out_a[1],))
-    moved_a = move(out_a[0])
-    out_b = mlp(x1, split, last_cot, mlp_w, vec, bias_first, prev=out_a[2:4])
-    moved_b = move(out_b[0])
-    out_patches = jnp.concatenate([moved_a, moved_b[:, : PATCH - split]], axis=1).transpose(0, 2, 1, 3)[None]
-    out_regions = moved_b[None, :, PATCH - split]
-
-    near = pair(out_b[3], 1).astype(F32) + out_b[2].astype(F32)
-    far = jnp.stack([near[1], near[3]]).astype(BF)
-    dx1 = (out_a[1], out_b[1])
-    early = attn_bwd(windows, region_rows, dx1, saved_a, weights, vec, 0, some, far)
-    far = pair(far, 2).astype(F32)
-    own_mlp = jnp.concatenate([near[0] + far[0], near[2] + far[1]], axis=1)
-    keep, give = halving_step(own_mlp, 1)
+    x1, *saved = attn_fwd(windows, region_rows, weights, vec)
+    last_cot = move(fence(last, x1))
+    early_out, late_out, dx1_a, *grads_a = mlp(x1, 0, first_cot, mlp_w, vec, bias_first)
+    moved_a = move(early_out)
+    moms = lax.all_gather(fence(jnp.stack([mlp_in_mom, mlp_out_mom]), x1), "opt", axis=0)
+    late_out, dx1_b, *grads_b = mlp(x1, split, last_cot, mlp_w, vec, bias_first, prev=(late_out, *grads_a[:2]))
+    near = pair(fence(grads_b[1], moved_a), 1)
+    far = (near[2:].astype(F32) + grads_b[0][2:].astype(F32)).astype(BF)
+    moved_b = move(fence(late_out, far))
+    out_patches = jnp.concatenate([moved_a, moved_b[:, :-1]], axis=1).transpose(0, 2, 1, 3)[None]
+    out_regions = moved_b[None, :, -1]
+
+    dx1 = (dx1_a, dx1_b)
+    early = attn_bwd(windows, region_rows, dx1, saved, weights, vec, 0, some, (far, far))
+    own_mlp = near[:2].astype(F32) + grads_b[0][:2].astype(F32) + fence(pair(far, 2), early[3]).astype(F32)
+    keep, give = halving_step(own_mlp.reshape(2 * D, D), 1)
     d_patches, d_region, d_attn, d_vec_attn = attn_bwd(
-        windows, region_rows, dx1, saved_b, weights, vec, some, some, give, prev=early)
+        windows, region_rows, dx1, saved, weights, vec, some, some, (give, moms), prev=early)
     d_patches = d_patches.transpose(1, 0, 2)[None, None]
-    gives = []
-    for bit in bits()[1:]:
-        keep, give = halving_step(keep + swap(give, bit // 2).astype(F32), bit)
-        gives.append(give)
-    piece_mlp = (keep + swap(give, bits()[-1]).astype(F32)).astype(BF)
+    gives, owner = [], opt_index.reshape(1, 1)
+    old_grams = in_vmem(old_grams_kernel, [((D, D), F32)] * 2, "momentum_grams", moms, after=(d_vec_attn,),
+                         flops=4e9)
 
     band_grad, extra = in_vmem(payload_kernel, [((grid_cols, D), BF), ((grid_cols, GROUP), BF)],
                                "regional_payload", d_region, mixed, level_wide, weights[3],
-                               after=(gives[0], moved_b))
+                               after=(give, moved_b))
+    taken = fence(swap(give, 1), band_grad)
+    for bit in bits()[1:]:
+        keep, give = halving_step(keep + taken.astype(F32), bit)
+        gives.append(give)
+        taken = swap(give, bit)
     payload = share(jnp.concatenate([band_grad, extra], axis=1)).reshape(grid_rows, dp_size, cols, D + GROUP)
     payload = payload.transpose(1, 0, 2, 3).reshape(tokens, D + GROUP)
     grads = payload[:, :D]
@@ -816,11 +846,11 @@
         d_regions, keep_attn, give_attn, d_vec_reg = in_vmem(
             partial(regional_bwd_kernel, own_count),
             [((own_count, D), F32), matrices, matrices, ((5, 8, D), F32)],
-            "regional_attention_backward", opt_index.reshape(1, 1),
+            "regional_attention_backward", owner,
             reg_q, reg_k, reg_v, grads, own_of(reg_q), own_of(reg_k), own_of(reg_v),
             own_of(canvas), ids[:, None], repeat(ids), own_ids[:, None], repeat(own_ids), wide(level), wide(delta),
             own_columns(level), own_columns(delta), own_of(grads), mixed, band_grad, d_attn, *weights, vec,
-            after=tuple(gives[1:2]), scratch=[pltpu.VMEM((4, D, D), F32)])
+            after=tuple(gives[-1:]) + tuple(old_grams), scratch=[pltpu.VMEM((4, D, D), F32)], flops=4e9)
     else:
         d_regions, grad_attn, d_vec_reg = regional_backward(
             reg_q, reg_k, reg_v, grads, own_of, own_of(canvas), ids[:, None] == own_ids[None, :], level, delta,
@@ -829,19 +859,22 @@
         keep_attn, give_attn = jnp.stack([pick(0), pick(2)]), jnp.stack([pick(1), pick(3)])
     d_regions = d_regions.reshape(regions.shape)
 
-    near = pair(give_attn, 1).astype(F32) + keep_attn.astype(F32)
-    piece_attn = near[0] + pair(near[1].astype(BF), 2).astype(F32)
+    piece_mlp = (keep + fence(taken, give_attn).astype(F32)).astype(BF)
+
+    near = pair(give_attn, 1)
+    far = (near[1].astype(F32) + keep_attn[1].astype(F32)).astype(BF)
+    piece_attn = near[0].astype(F32) + keep_attn[0].astype(F32) + pair(far, 2).astype(F32)
     piece_attn = move(piece_attn.astype(BF).reshape(dp_size, D // dp_size, D))
     piece_attn = jnp.sum(piece_attn.astype(F32), axis=0).astype(BF)
     own_attn = share(piece_attn).reshape(D, D)
-    own_mlp = piece_mlp
-    for bit in reversed(bits()):
-        own_mlp = doubling_step(own_mlp, bit)
-    grams = in_vmem(grams_kernel, [((D, D), F32)] * 6, "mlp_grams", *moms, *pieces_of_owners(own_mlp))
+    all_mlp = lax.all_gather(piece_mlp, ("dp", "opt"), axis=0).reshape(dp_size, OPT, -1, D)
+    *grams, own_mlp = in_vmem(partial(grams_kernel, order_of_halves(dp_size)),
+                              [((D, D), F32)] * 4 + [((2, D, D), BF)], "mlp_grams", owner, moms, all_mlp, flops=4e9)
+    grams = [old_grams[0], *grams[:2], old_grams[1], *grams[2:]]
 
     d_vec_attn = jnp.sum(d_vec_attn + d_vec_reg, axis=1)
-    d_vec_mlp = jnp.sum(out_a[4] + out_b[4], axis=1)
-    d_bias_first = jnp.take(jnp.sum(out_a[5] + out_b[5], axis=1), order, axis=0)
+    d_vec_mlp = jnp.sum(grads_a[2] + grads_b[2], axis=1)
+    d_bias_first = jnp.take(jnp.sum(grads_a[3] + grads_b[3], axis=1), order, axis=0)
     grad_vec = jnp.concatenate([d_vec_attn[:2], d_vec_mlp[:2], d_vec_attn[2:], d_vec_mlp[2:], d_bias_first])
     grad_vec = grad_vec + pair(grad_vec, 1)
     grad_vec = grad_vec + pair(grad_vec, 2)
@@ -856,7 +889,7 @@
     clip = jnp.minimum(1.0, CLIP_LIMIT / (grad_norm + 1e-06))
     attn_mom_new, new_attn, first_mom, new_first, second_mom, new_second = in_vmem(
         update_kernel, [((D, D), F32)] * 6, "matrix_updates", clip.reshape(1, 1), own_attn, attn_mom[0], attn_w[0],
-        own_mlp, mlp_in_mom, mlp_out_mom, mlp_in, mlp_out, *grams)
+        own_mlp, mlp_in_mom, mlp_out_mom, mlp_in, mlp_out, *grams, flops=12e9)
     clipped = clip * grad_vec
     moment_one = BETA_FIRST * adam_first + (1.0 - BETA_FIRST) * clipped
     moment_two = BETA_SECOND * adam_second + (1.0 - BETA_SECOND) * clipped * clipped

time: 560 us -> 448 us (0.80)
  waiting for transfers between devices: 164 us -> 65.4 us
  starting transfers between devices: 78.6 us -> 63 us
  between operations: 5.49 us -> 18.8 us
  other arithmetic: 33.5 us -> 27.8 us
    ppermute x20 -> x14, waiting for transfers between devices: 93.3 us -> 33.6 us  [pair(): return lax.ppermute(values, 'opt', [(i, i ^ bit) for i in range(OPT)])]
    ppermute x12 -> x9, waiting for transfers between devices: 58.5 us -> 10.2 us  [swap(): lax.ppermute(x, 'dp', [(i, i ^ bit) for i in range(lax.axis_size('dp'))])]
    all_to_all x5, waiting for transfers between devices: 0.01 us -> 19.5 us  [per_device(): move = lambda x: lax.all_to_all(x, 'dp', 0, 0, tiled=True)]
    all_to_all x3, waiting for transfers between devices: 12 us -> 2.11 us  [share(): return lax.all_to_all(copies, 'dp', 0, 0, tiled=True)]
    ppermute x12 -> x9, starting transfers between devices: 23.1 us -> 16.1 us  [swap(): lax.ppermute(x, 'dp', [(i, i ^ bit) for i in range(lax.axis_size('dp'))])]
    add x5 -> x3, other arithmetic: 10.1 us -> 3.55 us  [the longest x1 2.28 us: per_device(): near[:2].astype(F32) + grads_b[0][:2].astype(F32)]
    ppermute x20 -> x14, starting transfers between devices: 12.6 us -> 7.22 us  [pair(): return lax.ppermute(values, 'opt', [(i, i ^ bit) for i in range(OPT)])]
    pallas_call x5 -> x6, Pallas kernels: 63.5 us -> 68.4 us  [in_vmem(): pl.pallas_call(lambda *refs: kernel(*refs[:count], *refs[count + len(afte...]
  transfers between devices with their start and end apart: 40 -> 33, of which waited for: 17 -> 17; matrix products, arithmetic and copies ran while one was open for 10% -> 11% of each run, Pallas kernels for 27% -> 46%
where the time goes in v5:
time: 448 us; the launch traced here: 441 us
  Pallas kernels  233 us (52%)
  waiting for transfers between devices  65.4 us (15%)
  starting transfers between devices  63 us (14%)
  local copies, waits for them, and re-layouts  32.9 us (7%)
  other arithmetic  27.8 us (6%)
  between operations  18.8 us (4%)
    pallas_call x2, Pallas kernels, mlp(): pl.pallas_call(partial(mlp_kernel, many, sources, cols, steps, lanes, len...  69.3 us
    pallas_call x6, Pallas kernels, in_vmem(): pl.pallas_call(lambda *refs: kernel(*refs[:count], *refs[count + len(afte...  68.4 us
    pallas_call x2, Pallas kernels, attn_bwd(): pl.pallas_call(partial(attn_bwd_kernel, count, batch, len(dx1_parts), len...  59.9 us
    pallas_call x1, Pallas kernels, attn_fwd(): pl.pallas_call(partial(attn_fwd_kernel, count, batch), grid=(windows // c...  35.2 us
    ppermute x14, waiting for transfers between devices, pair(): return lax.ppermute(values, 'opt', [(i, i ^ bit) for i in range(OPT)])  33.6 us
    all_to_all x5, starting transfers between devices, per_device(): move = lambda x: lax.all_to_all(x, 'dp', 0, 0, tiled=True)  24.2 us
    all_to_all x5, waiting for transfers between devices, per_device(): move = lambda x: lax.all_to_all(x, 'dp', 0, 0, tiled=True)  19.5 us
    ppermute x9, starting transfers between devices, swap(): lax.ppermute(x, 'dp', [(i, i ^ bit) for i in range(lax.axis_size('dp'))])  16.1 us
  transfers between devices with their start and end apart: 33, of which 17 were waited for; matrix products, arithmetic and copies ran while one was open for 11% of the time, Pallas kernels for 46%

profile of v5, /device:TPU:0, one launch (start us, length us, event | category | flops | bytes accessed | tf_op | source)
XLA Modules:
  0.0 440.7 jit_solution(5152093208817488954)
XLA Ops:
  7.2 2.7 fusion.4
  9.9 3.0 collective-permute-start.1
  13.7 5.8 %all-to-all-start = ((bf16[8,8,8,512]{3,2,1,0:T(8,128)(2,1)}), bf16[8,8,8,512]{3,2,1,0:T(8,128)(2,1)}, u32[]{:S(2)}, u32[]{:S(2)}) async-start(bf16[8,8,8,512]{3,2,1,0:T(8,128)(2,1)} %broadcast_in_dim.47), calls=%async_computation | async-start | bytes 1048576 | tf_op jit(solution)/shard_map/all_to_all | solution.py:680
  19.5 1.8 convert_bitcast_fusion
  22.9 2.6 collective-permute-done.1
  28.6 3.1 pad_maximum_fusion.1.refs_0_
  31.7 2.1 all-to-all-done
  33.8 4.3 all-to-all-start.1
  39.7 1.8 pad_maximum_fusion
  42.9 4.7 %collective-permute-done.3.refs_9_.refs_4_ = bf16[2,512,512]{2,1,0:T(8,128)(2,1)} collective-permute-done((bf16[2,512,512]{2,1,0:T(8,128)(2,1)}, bf16[2,512,512]{2,1,0:T(8,128)(2,1)}, u32[]{:S(2)}, u32[]{:S(2)}) %collective-permute-start.3) | collective-permute-done | bytes 1048608 | tf_op jit(solution)/shard_map/ppermute | solution.py:656
  47.5 5.2 %regional_attention_forward.1 = (f32[64,512]{1,0:T(8,128)}, f32[64,512]{1,0:T(8,128)}, f32[4,256]{1,0:T(4,128)}, bf16[512,512]{1,0:T(8,128)(2,1)}, bf16[512,512]{1,0:T(8,128)(2,1)}, /*index=5*/bf16[512,512]{1,0:T(8,128)(2,1)}) custom-call(bf16[512,512]{1,0:T(8,128)(2,1)} %bitcast.3.refs_0_.refs_1_, bf16[64,512]{1,0:T(8,128)(2,1)} %dynamic-slice_bitcast_fusion.4.refs_1_, ...), custom_call_target="tpu_custom_call" | custom-call | flops 2000000000 | bytes 100000 | tf_op jit(solution)/shard_map/regional_attention_forward/pallas_call | solution.py:430
  52.7 35.2 %window_attention_forward.1 = (f32[50,64,512]{2,1,0:T(8,128)}, bf16[64,56,512]{2,1,0:T(8,128)(2,1)}, bf16[64,56,512]{2,1,0:T(8,128)(2,1)}, bf16[64,56,512]{2,1,0...) custom-call(bf16[49,64,512]{2,1,0:T(8,128)(2,1)} %bitcast.83, ...), custom_call_target="tpu_custom_call" | custom-call | flops 16000000000 | bytes 100000 | tf_op jit(solution)/shard_map/window_attention_forward/pallas_call | solution.py:183
  89.9 6.2 %all-to-all-start.3 = ((bf16[8,20,8,512]{3,2,1,0:T(8,128)(2,1)}), bf16[8,20,8,512]{3,2,1,0:T(8,128)(2,1)S(1)}, u32[]{:S(2)}, u32[]{:S(2)}) async-start(bf16[8,20,8,512]{3,2,1,0:T(8,128)(2,1)} %fence.9), calls=%async_computation.3 | async-start | bytes 2621440 | tf_op jit(solution)/shard_map/all_to_all | solution.py:770
  97.8 1.9 collective-permute-done.4.refs_3_
  100.9 39.8 %mlp_forward_backward.2 = (bf16[8,20,8,512]{3,2,1,0:T(8,128)(2,1)}, bf16[8,30,8,512]{3,2,1,0:T(8,128)(2,1)}, f32[30,64,512]{2,1,0:T(8,128)}, bf16[4,512,512]{2,1...) custom-call(f32[50,64,512]{2,1,0:T(8,128)} %get-tuple-element.68.refs_0_.refs_1_, ...), custom_call_target="tpu_custom_call" | custom-call | flops 12000000000 | bytes 100000 | tf_op jit(solution)/shard_map/mlp_forward_backward/pallas_call | solution.py:286
  140.8 6.3 %all-to-all-start.2 = ((bf16[8,20,8,512]{3,2,1,0:T(8,128)(2,1)}), bf16[8,20,8,512]{3,2,1,0:T(8,128)(2,1)S(1)}, u32[]{:S(2)}, u32[]{:S(2)}) async-start(bf16[8,20,8,512]{3,2,1,0:T(8,128)(2,1)} %get-tuple-element.69), calls=%async_computation.2 | async-start | bytes 2621440 | tf_op jit(solution)/shard_map/all_to_all | solution.py:770
  147.1 29.5 %mlp_forward_backward.3 = (bf16[8,30,8,512]{3,2,1,0:T(8,128)(2,1)}, f32[20,64,512]{2,1,0:T(8,128)}, bf16[4,512,512]{2,1,0:T(8,128)(2,1)}, bf16[4,512,512]{2,1,0:...) custom-call(f32[50,64,512]{2,1,0:T(8,128)} %get-tuple-element.68.refs_0_.refs_1_, ...), custom_call_target="tpu_custom_call", output_to_operand_aliasing={{0}: (8, {})} | custom-call | flops 8000000000 | bytes 100000 | tf_op jit(solution)/shard_map/mlp_forward_backward/pallas_call | solution.py:286
  176.6 2.2 all-to-all-done.2.refs_1_
  179.9 4.4 collective-permute-done.6
  184.2 1.5 add_convert_fusion.refs_1_.refs_2_.refs_3_
  185.9 3.9 all-to-all-start.4
  197.2 1.5 collective-permute-start.7
  198.7 29.4 %window_attention_backward.2 = (bf16[49,64,512]{2,1,0:T(8,128)(2,1)}, f32[64,512]{1,0:T(8,128)}, f32[4,512,512]{2,1,0:T(8,128)}, f32[5,8,512]{2,1,0:T(8,128)}) custom-call(bf16[49,64,512]{2,1,0:T(8,128)(2,1)} %bitcast.84, f32[64,512]{1,0:T(8,128)} %get-tuple-element.67.r_ref.refs_1_, bf16[2,512,512]{2,1,0:T(8,128)(2,1)} %add_convert_fusion.refs_1_.refs_2_.refs_3_, ...), custom_call_target="tpu_custom_call" | custom-call | flops 12000000000 | bytes 100000 | tf_op jit(solution)/shard_map/window_attention_backward/pallas_call | solution.py:377
  228.1 2.3 convert_add_fusion
  231.7 2.1 collective-permute-start.8
  233.8 30.6 %window_attention_backward.3 = (bf16[49,64,512]{2,1,0:T(8,128)(2,1)}, f32[64,512]{1,0:T(8,128)}, f32[4,512,512]{2,1,0:T(8,128)}, f32[5,8,512]{2,1,0:T(8,128)}) custom-call(bf16[49,64,512]{2,1,0:T(8,128)(2,1)} %bitcast.85, f32[64,512]{1,0:T(8,128)} %get-tuple-element.67.r_ref.refs_1_, ...), custom_call_target="tpu_custom_call", output_to_operand_aliasing={{0}: (16, {}), {1}: (17, {})} | custom-call | flops 12000000000 | bytes 100000 | tf_op jit(solution)/shard_map/window_attention_backward/pallas_call | solution.py:377
  265.7 2.3 regional_payload.1
  269.9 4.7 %all-to-all-start.5 = ((bf16[8,64,640]{2,1,0:T(8,128)(2,1)}), bf16[8,64,640]{2,1,0:T(8,128)(2,1)}, u32[]{:S(2)}, u32[]{:S(2)}) async-start(bf16[8,64,640]{2,1,0:T(8,128)(2,1)} %broadcast_in_dim.50), calls=%async_computation.5 | async-start | bytes 1310720 | tf_op jit(solution)/shard_map/all_to_all | solution.py:680
  275.0 1.5 constant_dynamic-slice_fusion.4.refs_5_
  278.6 2.0 collective-permute-start.9
  280.6 9.1 %momentum_grams.1 = (f32[512,512]{1,0:T(8,128)}, f32[512,512]{1,0:T(8,128)}) custom-call(f32[4,2,512,512]{3,2,1,0:T(8,128)} %bitcast.79, f32[5,8,512]{2,1,0:T(8,128)} %get-tuple-element.97.refs_1_), custom_call_target="tpu_custom_call" | custom-call | flops 4000000000 | bytes 100000 | tf_op jit(solution)/shard_map/momentum_grams/pallas_call | solution.py:430
  289.7 3.0 collective-permute-done.9
  292.9 2.4 collective-permute-start.12
  300.4 9.4 %regional_attention_backward.1 = (f32[64,512]{1,0:T(8,128)}, bf16[2,512,512]{2,1,0:T(8,128)(2,1)}, bf16[2,512,512]{2,1,0:T(8,128)(2,1)}, f32[5,8,512]{2,1,0:T(8,128)}) custom-call(s32[1,1]{1,0:T(1,128)} %bitcast.30.refs_0_, bf16[512,512]{1,0:T(8,128)(2,1)} %get-tuple-element.88.refs_1_, bf16[512,512]{1,0:T(8,128)(2,1)} %get-tuple-element.89.refs_2_, ...), custom_call_target="tpu_custom_call" | custom-call | flops 4000000000 | bytes 100000 | tf_op jit(solution)/shard_map/regional_attention_backward/pallas_call | solution.py:430
  310.6 2.2 multiply_reduce_fusion
  312.9 2.9 collective-permute-done.10
  316.5 14.4 %collective-permute-done.11 = bf16[512,512]{1,0:T(8,128)(2,1)S(1)} collective-permute-done((bf16[512,512]{1,0:T(8,128)(2,1)S(1)}, bf16[512,512]{1,0:T(8,128)(2,1)S(1)}, u32[]{:S(2)}, u32[]{:S(2)}) %collective-permute-start.11) | collective-permute-done | bytes 524320 | tf_op jit(solution)/shard_map/ppermute | solution.py:656
  331.9 3.5 all-to-all-start.6
  338.0 17.2 %all-to-all-done.6 = bf16[8,64,512]{2,1,0:T(8,128)(2,1)S(1)} async-done(((bf16[8,64,512]{2,1,0:T(8,128)(2,1)}), bf16[8,64,512]{2,1,0:T(8,128)(2,1)S(1)}, u32[]{:S(2)}, u32[]{:S(2)}) %all-to-all-start.6) | async-done | bytes 524320 | tf_op jit(solution)/shard_map/all_to_all | solution.py:770
  357.4 1.5 collective-permute-start.20
  359.4 2.7 collective-permute-done.20
  368.3 4.5 %all-to-all-start.7 = ((bf16[8,64,512]{2,1,0:T(8,128)(2,1)}), bf16[8,64,512]{2,1,0:T(8,128)(2,1)S(1)}, u32[]{:S(2)}, u32[]{:S(2)}) async-start(bf16[8,64,512]{2,1,0:T(8,128)(2,1)} %broadcast_in_dim.53), calls=%async_computation.7 | async-start | bytes 1048576 | tf_op jit(solution)/shard_map/all_to_all | solution.py:680
  372.8 2.1 collective-permute-start.16
  374.9 3.6 maximum_bitcast_fusion
  378.5 2.7 collective-permute-done.16
  381.2 3.7 collective-permute-start.17
  389.3 12.8 %mlp_grams.1 = (f32[512,512]{1,0:T(8,128)}, f32[512,512]{1,0:T(8,128)}, f32[512,512]{1,0:T(8,128)}, f32[512,512]{1,0:T(8,128)}, bf16[2,512,512]{2,1,0:T(8,128)(2,1)}) custom-call(s32[1,1]{1,0:T(1,128)} %bitcast.30.refs_0_, f32[4,2,512,512]{3,2,1,0:T(8,128)} %bitcast.80, bf16[8,4,128,512]{3,2,1,0:T(8,128)(2,1)} %bitcast.104), custom_call_target="tpu_custom_call" | custom-call | flops 4000000000 | bytes 100000 | tf_op jit(solution)/shard_map/mlp_grams/pallas_call | solution.py:430
  402.9 29.6 %matrix_updates.1 = (f32[512,512]{1,0:T(8,128)}, f32[512,512]{1,0:T(8,128)}, f32[512,512]{1,0:T(8,128)}, f32[512,512]{1,0:T(8,128)}, f32[512,512]{1,0:T(8,128)}, /*index=5*/f32[512,512]{1,0:T(8,128)}) custom-call(f32[1,1]{1,0:T(1,128)} %bitcast.46.refs_0_, bf16[512,512]{1,0:T(8,128)(2,1)} %bitcast.96, f32[512,512]{1,0:T(8,128)} %bitcast.105, ...), custom_call_target="tpu_custom_call" | custom-call | flops 12000000000 | bytes 100000 | tf_op jit(solution)/shard_map/matrix_updates/pallas_call | solution.py:430
  (199 shorter events, 50.5 us)
Async XLA Ops:
  9.9 15.6 %collective-permute-start.1 = (bf16[512,512]{1,0:T(8,128)(2,1)}, bf16[512,512]{1,0:T(8,128)(2,1)}, u32[]{:S(2)}, u32[]{:S(2)}) collective-permute-start(bf16[512,512]{1,0:T(8,128)(2,1)} %get-tuple-element.131), channel_id=1, source_target_pairs={{0,2},{1,3},{2,0},{3,1},{4,6},{5,7},{6,4},{7,5},{8,10},{9,11},{10,... | collective-permute-start | bytes 1572872 | tf_op jit(solution)/shard_map/ppermute | solution.py:656
  13.7 20.2 %all-to-all-start = ((bf16[8,8,8,512]{3,2,1,0:T(8,128)(2,1)}), bf16[8,8,8,512]{3,2,1,0:T(8,128)(2,1)}, u32[]{:S(2)}, u32[]{:S(2)}) async-start(bf16[8,8,8,512]{3,2,1,0:T(8,128)(2,1)} %broadcast_in_dim.47), calls=%async_computation | async-start | bytes 1048576 | tf_op jit(solution)/shard_map/all_to_all | solution.py:680
  19.5 7.7 %copy-start.7 = (bf16[1,8,8,49,512]{4,2,3,1,0:T(8,128)(2,1)S(1)}, bf16[1,8,8,49,512]{4,2,3,1,0:T(8,128)(2,1)}, u32[]{:S(2)}) copy-start(bf16[1,8,8,49,512]{4,2,3,1,0:T(8,128)(2,1)} %param.23) | copy-start | bytes 9633796
  22.4 25.1 %collective-permute-start.3 = (bf16[2,512,512]{2,1,0:T(8,128)(2,1)}, bf16[2,512,512]{2,1,0:T(8,128)(2,1)}, u32[]{:S(2)}, u32[]{:S(2)}) collective-permute-start(bf16[2,512,512]{2,1,0:T(8,128)(2,1)} %pad_maximum_fusion.3.refs_2_), channel_id=1, source_target_pairs={{0,2},{1,3},{2,0},{3,1},{4,6},{5,7},{6,4},{7,5},{8,10},{9,11},{10,... | collective-permute-start | bytes 3145736 | tf_op jit(solution)/shard_map/ppermute | solution.py:656
  22.9 16.8 %collective-permute-start = (bf16[512,512]{1,0:T(8,128)(2,1)}, bf16[512,512]{1,0:T(8,128)(2,1)}, u32[]{:S(2)}, u32[]{:S(2)}) collective-permute-start(bf16[512,512]{1,0:T(8,128)(2,1)} %get-tuple-element.131), channel_id=1, source_target_pairs={{0,1},{1,0},{2,3},{3,2},{4,5},{5,4},{6,7},{7,6},{8,9},{9,8},{10,11... | collective-permute-start | bytes 1572872 | tf_op jit(solution)/shard_map/ppermute | solution.py:656
  25.5 14.2 %collective-permute-start.2 = (bf16[512,512]{1,0:T(8,128)(2,1)}, bf16[512,512]{1,0:T(8,128)(2,1)}, u32[]{:S(2)}, u32[]{:S(2)}) collective-permute-start(bf16[512,512]{1,0:T(8,128)(2,1)} %collective-permute-done.1), channel_id=1, source_target_pairs={{0,1},{1,0},{2,3},{3,2},{4,5},{5,4},{6,7},{7,6},{8,9},{9,8},{10,11... | collective-permute-start | bytes 1572872 | tf_op jit(solution)/shard_map/ppermute | solution.py:656
  33.8 56.1 %all-to-all-start.1 = ((bf16[8,30,8,512]{3,2,1,0:T(8,128)(2,1)}), bf16[8,30,8,512]{3,2,1,0:T(8,128)(2,1)}, u32[]{:S(2)}, u32[]{:S(2)}) async-start(bf16[8,30,8,512]{3,2,1,0:T(8,128)(2,1)} %fence.8), calls=%async_computation.1 | async-start | bytes 3932160 | tf_op jit(solution)/shard_map/all_to_all | solution.py:770
  38.2 195.6 %all-gather.5.cloned.1.call-start = ((), (), s32[]{:S(2)}) async-start(), calls=%async_computation.8 | async-start | bytes 10485760 | tf_op jit(solution)/shard_map/all_gather | solution.py:808
  89.9 50.9 %all-to-all-start.3 = ((bf16[8,20,8,512]{3,2,1,0:T(8,128)(2,1)}), bf16[8,20,8,512]{3,2,1,0:T(8,128)(2,1)S(1)}, u32[]{:S(2)}, u32[]{:S(2)}) async-start(bf16[8,20,8,512]{3,2,1,0:T(8,128)(2,1)} %fence.9), calls=%async_computation.3 | async-start | bytes 2621440 | tf_op jit(solution)/shard_map/all_to_all | solution.py:770
  96.1 3.6 collective-permute-start.4
  96.1 4.9 %collective-permute-start.5 = (bf16[2,512,512]{2,1,0:T(8,128)(2,1)}, bf16[2,512,512]{2,1,0:T(8,128)(2,1)}, u32[]{:S(2)}, u32[]{:S(2)}) collective-permute-start(bf16[2,512,512]{2,1,0:T(8,128)(2,1)} %collective-permute-done.3.refs_9_.refs_4_), channel_id=1, source_target_pairs={{0,1},{1,0},{2,3},{3,2},{4,5},{5,4},{6,7},{7,6},{8,9},{9,8},{10,11... | collective-permute-start | bytes 3145736 | tf_op jit(solution)/shard_map/ppermute | solution.py:656
  140.8 38.0 %all-to-all-start.2 = ((bf16[8,20,8,512]{3,2,1,0:T(8,128)(2,1)}), bf16[8,20,8,512]{3,2,1,0:T(8,128)(2,1)S(1)}, u32[]{:S(2)}, u32[]{:S(2)}) async-start(bf16[8,20,8,512]{3,2,1,0:T(8,128)(2,1)} %get-tuple-element.69), calls=%async_computation.2 | async-start | bytes 2621440 | tf_op jit(solution)/shard_map/all_to_all | solution.py:770
  179.9 4.4 collective-permute-start.6
  185.9 7.6 %copy-start.30 = (f32[4,256]{1,0:T(4,128)S(1)}, f32[4,256]{1,0:T(4,128)}, u32[]{:S(2)}) copy-start(f32[4,256]{1,0:T(4,128)} %get-tuple-element.93) | copy-start | bytes 12292
  185.9 11.3 %copy-start.6 = (bf16[2,512,512]{2,1,0:T(8,128)(2,1)S(1)}, bf16[2,512,512]{2,1,0:T(8,128)(2,1)}, u32[]{:S(2)}) copy-start(bf16[2,512,512]{2,1,0:T(8,128)(2,1)} %add_convert_fusion.refs_1_.refs_2_.refs_3_) | copy-start | bytes 3145732
  185.9 78.5 %all-to-all-start.4 = ((bf16[8,30,8,512]{3,2,1,0:T(8,128)(2,1)}), bf16[8,30,8,512]{3,2,1,0:T(8,128)(2,1)S(1)}, u32[]{:S(2)}, u32[]{:S(2)}) async-start(bf16[8,30,8,512]{3,2,1,0:T(8,128)(2,1)} %fence.11), calls=%async_computation.4 | async-start | bytes 3932160 | tf_op jit(solution)/shard_map/all_to_all | solution.py:770
  197.2 30.9 %collective-permute-start.7 = (bf16[2,512,512]{2,1,0:T(8,128)(2,1)S(1)}, bf16[2,512,512]{2,1,0:T(8,128)(2,1)}, u32[]{:S(2)}, u32[]{:S(2)}) collective-permute-start(bf16[2,512,512]{2,1,0:T(8,128)(2,1)S(1)} %copy-done.6), channel_id=1, source_target_pairs={{0,2},{1,3},{2,0},{3,1},{4,6},{5,7},{6,4},{7,5},{8,10},{9,11},{10,... | collective-permute-start | bytes 3145736 | tf_op jit(solution)/shard_map/ppermute | solution.py:656
  231.7 44.8 %collective-permute-start.8 = (bf16[512,512]{1,0:T(8,128)(2,1)S(1)}, bf16[512,512]{1,0:T(8,128)(2,1)S(1)}, u32[]{:S(2)}, u32[]{:S(2)}) collective-permute-start(bf16[512,512]{1,0:T(8,128)(2,1)S(1)} %dynamic-slice_convert_fusion.refs_2_.refs_4_), channel_id=1, source_target_pairs={{0,4},{4,0},{8,12},{12,8},{16,20},{20,16},{24,28},{28,24},{1,5},{5... | collective-permute-start | bytes 1572872 | tf_op jit(solution)/shard_map/ppermute | solution.py:684
  268.0 9.3 %copy-start.5 = (f32[2,512,512]{2,1,0:T(8,128)S(1)}, f32[2,512,512]{2,1,0:T(8,128)}, u32[]{:S(2)}) copy-start(f32[2,512,512]{2,1,0:T(8,128)} %copy-done.4) | copy-start | bytes 6291460
  269.9 25.3 %all-to-all-start.5 = ((bf16[8,64,640]{2,1,0:T(8,128)(2,1)}), bf16[8,64,640]{2,1,0:T(8,128)(2,1)}, u32[]{:S(2)}, u32[]{:S(2)}) async-start(bf16[8,64,640]{2,1,0:T(8,128)(2,1)} %broadcast_in_dim.50), calls=%async_computation.5 | async-start | bytes 1310720 | tf_op jit(solution)/shard_map/all_to_all | solution.py:680
  274.6 114.7 %all-gather.7.cloned.1.call-start = ((), (), s32[]{:S(2)}) async-start(), calls=%async_computation.9 | async-start | bytes 4325376 | tf_op jit(solution)/shard_map/all_gather | solution.py:870
  278.6 14.2 %collective-permute-start.9 = (bf16[256,512]{1,0:T(8,128)(2,1)S(1)}, bf16[256,512]{1,0:T(8,128)(2,1)S(1)}, u32[]{:S(2)}, u32[]{:S(2)}) collective-permute-start(bf16[256,512]{1,0:T(8,128)(2,1)S(1)} %dynamic-slice_convert_fusion.1), channel_id=1, source_target_pairs={{0,8},{4,12},{8,0},{12,4},{16,24},{20,28},{24,16},{28,20},{1,9},{5... | collective-permute-start | bytes 786440 | tf_op jit(solution)/shard_map/ppermute | solution.py:684
  292.9 17.0 %collective-permute-start.12 = (bf16[128,512]{1,0:T(8,128)(2,1)S(1)}, bf16[128,512]{1,0:T(8,128)(2,1)S(1)}, u32[]{:S(2)}, u32[]{:S(2)}) collective-permute-start(bf16[128,512]{1,0:T(8,128)(2,1)S(1)} %dynamic-slice_convert_fusion.2.refs_26_), channel_id=1, source_target_pairs={{0,16},{4,20},{8,24},{12,28},{16,0},{20,4},{24,8},{28,12},{1,17},{... | collective-permute-start | bytes 393224 | tf_op jit(solution)/shard_map/ppermute | solution.py:684
  312.8 2.9 collective-permute-start.10
  315.7 19.7 %copy-start.25 = (f32[3,8,512]{2,1,0:T(8,128)S(1)}, f32[3,8,512]{2,1,0:T(8,128)}, u32[]{:S(2)}) copy-start(f32[3,8,512]{2,1,0:T(8,128)} %get-tuple-element.104) | copy-start | bytes 147460
  315.7 19.7 %copy-start.26 = (f32[3,8,512]{2,1,0:T(8,128)S(1)}, f32[3,8,512]{2,1,0:T(8,128)}, u32[]{:S(2)}) copy-start(f32[3,8,512]{2,1,0:T(8,128)} %get-tuple-element.105) | copy-start | bytes 147460
  315.7 19.7 %copy-start.23 = (f32[4,8,512]{2,1,0:T(8,128)S(1)}, f32[4,8,512]{2,1,0:T(8,128)}, u32[]{:S(2)}) copy-start(f32[4,8,512]{2,1,0:T(8,128)} %get-tuple-element.106) | copy-start | bytes 196612
  315.7 19.7 %copy-start.24 = (f32[4,8,512]{2,1,0:T(8,128)S(1)}, f32[4,8,512]{2,1,0:T(8,128)}, u32[]{:S(2)}) copy-start(f32[4,8,512]{2,1,0:T(8,128)} %get-tuple-element.107) | copy-start | bytes 196612
  315.9 20.3 %copy-start.19 = (f32[5,8,512]{2,1,0:T(8,128)S(1)}, f32[5,8,512]{2,1,0:T(8,128)}, u32[]{:S(2)}) copy-start(f32[5,8,512]{2,1,0:T(8,128)} %get-tuple-element.97.refs_1_) | copy-start | bytes 245764
  315.9 20.3 %copy-start.20 = (f32[5,8,512]{2,1,0:T(8,128)S(1)}, f32[5,8,512]{2,1,0:T(8,128)}, u32[]{:S(2)}) copy-start(f32[5,8,512]{2,1,0:T(8,128)} %get-tuple-element.103) | copy-start | bytes 245764
  315.9 47.9 %copy-start.3 = (bf16[8,30,8,512]{3,2,1,0:T(8,128)(2,1)S(1)}, bf16[8,30,8,512]{3,2,1,0:T(8,128)(2,1)}, u32[]{:S(2)}) copy-start(bf16[8,30,8,512]{3,2,1,0:T(8,128)(2,1)} %copy-done.2) | copy-start | bytes 5898244
  315.9 15.0 %collective-permute-start.11 = (bf16[512,512]{1,0:T(8,128)(2,1)S(1)}, bf16[512,512]{1,0:T(8,128)(2,1)S(1)}, u32[]{:S(2)}, u32[]{:S(2)}) collective-permute-start(bf16[512,512]{1,0:T(8,128)(2,1)S(1)} %fusion.1), channel_id=1, source_target_pairs={{0,2},{1,3},{2,0},{3,1},{4,6},{5,7},{6,4},{7,5},{8,10},{9,11},{10,... | collective-permute-start | bytes 1572872 | tf_op jit(solution)/shard_map/ppermute | solution.py:656
  331.9 23.4 %all-to-all-start.6 = ((bf16[8,64,512]{2,1,0:T(8,128)(2,1)}), bf16[8,64,512]{2,1,0:T(8,128)(2,1)S(1)}, u32[]{:S(2)}, u32[]{:S(2)}) async-start(bf16[8,64,512]{2,1,0:T(8,128)(2,1)} %bitcast.44), calls=%async_computation.6 | async-start | bytes 1048576 | tf_op jit(solution)/shard_map/all_to_all | solution.py:770
  336.3 1.3 collective-permute-start.18
  337.5 19.9 %collective-permute-start.19 = (f32[12,512]{1,0:T(8,128)S(1)}, f32[12,512]{1,0:T(8,128)S(1)}, u32[]{:S(2)}, u32[]{:S(2)}) collective-permute-start(f32[12,512]{1,0:T(8,128)S(1)} %add.198), channel_id=1, source_target_pairs={{0,2},{1,3},{2,0},{3,1},{4,6},{5,7},{6,4},{7,5},{8,10},{9,11},{10,... | collective-permute-start | bytes 73736 | tf_op jit(solution)/shard_map/ppermute | solution.py:656
  357.3 1.6 collective-permute-start.13
  357.4 4.7 %collective-permute-start.20 = (f32[12,512]{1,0:T(8,128)S(1)}, f32[12,512]{1,0:T(8,128)S(1)}, u32[]{:S(2)}, u32[]{:S(2)}) collective-permute-start(f32[12,512]{1,0:T(8,128)S(1)} %add.199), channel_id=1, source_target_pairs={{0,4},{4,0},{8,12},{12,8},{16,20},{20,16},{24,28},{28,24},{1,5},{5... | collective-permute-start | bytes 73736 | tf_op jit(solution)/shard_map/ppermute | solution.py:684
  359.0 3.7 collective-permute-start.14
  362.1 4.2 collective-permute-start.21
  362.6 10.1 %collective-permute-start.15 = (f32[8,128]{1,0:T(8,128)S(1)}, f32[8,128]{1,0:T(8,128)S(1)}, u32[]{:S(2)}, u32[]{:S(2)}) collective-permute-start(f32[8,128]{1,0:T(8,128)S(1)} %fusion.5), channel_id=1, source_target_pairs={{0,4},{4,0},{8,12},{12,8},{16,20},{20,16},{24,28},{28,24},{1,5},{5... | collective-permute-start | bytes 12296 | tf_op jit(solution)/shard_map/ppermute | solution.py:684
  364.5 10.4 %copy-start.1 = (bf16[8,20,8,512]{3,2,1,0:T(8,128)(2,1)S(1)}, bf16[8,20,8,512]{3,2,1,0:T(8,128)(2,1)}, u32[]{:S(2)}) copy-start(bf16[8,20,8,512]{3,2,1,0:T(8,128)(2,1)} %copy-done) | copy-start | bytes 3932164
  366.4 18.5 %collective-permute-start.22 = (f32[12,512]{1,0:T(8,128)S(1)}, f32[12,512]{1,0:T(8,128)S(1)}, u32[]{:S(2)}, u32[]{:S(2)}) collective-permute-start(f32[12,512]{1,0:T(8,128)S(1)} %add.201), channel_id=1, source_target_pairs={{0,16},{4,20},{8,24},{12,28},{16,0},{20,4},{24,8},{28,12},{1,17},{... | collective-permute-start | bytes 73736 | tf_op jit(solution)/shard_map/ppermute | solution.py:684
  368.3 33.8 %all-to-all-start.7 = ((bf16[8,64,512]{2,1,0:T(8,128)(2,1)}), bf16[8,64,512]{2,1,0:T(8,128)(2,1)S(1)}, u32[]{:S(2)}, u32[]{:S(2)}) async-start(bf16[8,64,512]{2,1,0:T(8,128)(2,1)} %broadcast_in_dim.53), calls=%async_computation.7 | async-start | bytes 1048576 | tf_op jit(solution)/shard_map/all_to_all | solution.py:680
  372.8 15.8 %copy-start.15 = (f32[12,512]{1,0:T(8,128)S(1)}, f32[12,512]{1,0:T(8,128)}, u32[]{:S(2)}) copy-start(f32[12,512]{1,0:T(8,128)} %refs_25_.1) | copy-start | bytes 73732
  372.8 15.8 %copy-start.27 = (f32[12,512]{1,0:T(8,128)S(1)}, f32[12,512]{1,0:T(8,128)}, u32[]{:S(2)}) copy-start(f32[12,512]{1,0:T(8,128)} %param.28) | copy-start | bytes 73732
  372.8 15.8 %copy-start.28 = (f32[12,512]{1,0:T(8,128)S(1)}, f32[12,512]{1,0:T(8,128)}, u32[]{:S(2)}) copy-start(f32[12,512]{1,0:T(8,128)} %param.29) | copy-start | bytes 73732
  372.8 8.4 %collective-permute-start.16 = (f32[8,128]{1,0:T(8,128)S(1)}, f32[8,128]{1,0:T(8,128)S(1)}, u32[]{:S(2)}, u32[]{:S(2)}) collective-permute-start(f32[8,128]{1,0:T(8,128)S(1)} %add.192), channel_id=1, source_target_pairs={{0,8},{4,12},{8,0},{12,4},{16,24},{20,28},{24,16},{28,20},{1,9},{5... | collective-permute-start | bytes 12296 | tf_op jit(solution)/shard_map/ppermute | solution.py:684
  381.2 5.5 %collective-permute-start.17 = (f32[8,128]{1,0:T(8,128)S(1)}, f32[8,128]{1,0:T(8,128)S(1)}, u32[]{:S(2)}, u32[]{:S(2)}) collective-permute-start(f32[8,128]{1,0:T(8,128)S(1)} %add.193), channel_id=1, source_target_pairs={{0,16},{4,20},{8,24},{12,28},{16,0},{20,4},{24,8},{28,12},{1,17},{... | collective-permute-start | bytes 12296 | tf_op jit(solution)/shard_map/ppermute | solution.py:684
  (18 other events, 54.5 us)
Sparse Core Ops, SparseCore 0:
  88.0 59.7 all-gather.4
  312.9 64.3 all-gather.6

commit v6 on v5

--- a/solution.py
+++ b/solution.py
@@ -123,9 +123,10 @@
     return a * share, share + a * bell * INV_SQRT_2PI
 
 
-def attn_fwd_kernel(count, batch, p_ref, r_ref, wq_ref, wk_ref, wv_ref, wo_ref, vec_ref,
+def attn_fwd_kernel(count, batch, owner_ref, p_ref, r_ref, w_ref, vec_ref, _,
                     x1_ref, q_ref, k_ref, v_ref, o_ref, pt_ref, q_held, k_held, v_held, o_held):
     total = count * LIVE
+    owner = owner_ref[0, 0]
 
     @pl.when(pl.program_id(0) == 0)
     def _():
@@ -136,9 +137,9 @@
     vec = vec_ref[...]
     xhat, _ = norm_parts(x)
     xn = (xhat * vec[0:1] + vec[1:2]).astype(BF)
-    hold(q_held, total, nn(xn, wq_ref[...]) + vec[4:5])
-    hold(k_held, total, nn(xn, wk_ref[...]))
-    hold(v_held, total, nn(xn, wv_ref[...]) + vec[5:6])
+    hold(q_held, total, nn(xn, w_ref[owner ^ 0]) + vec[4:5])
+    hold(k_held, total, nn(xn, w_ref[owner ^ 1]))
+    hold(v_held, total, nn(xn, w_ref[owner ^ 2]) + vec[5:6])
     masks = head_masks()
     live = lax.broadcasted_iota(jnp.int32, (ROWS, 1), 0) < LIVE
 
@@ -170,20 +171,21 @@
     lax.fori_loop(0, count // batch, body, 0)
     mixed = held_rows(o_held, total).astype(BF)
     o_ref[...] = mixed.reshape(LIVE, count, D)
-    x1_ref[...] = (x + nn(mixed, wo_ref[...]) + vec[6:7]).reshape(LIVE, count, D)
+    x1_ref[...] = (x + nn(mixed, w_ref[owner ^ 3]) + vec[6:7]).reshape(LIVE, count, D)
 
 
 def middle(rows, count, skip=0):
     return pl.BlockSpec((rows, count, D), lambda i: (0, i + skip, 0))
 
 
-def attn_fwd(patches, region_rows, weights, vec, count=16, batch=4):
+def attn_fwd(owner, patches, region_rows, weights, vec, after, count=16, batch=8):
     windows = patches.shape[1]
     array = jax.ShapeDtypeStruct
     return pl.pallas_call(
         partial(attn_fwd_kernel, count, batch),
         grid=(windows // count,),
-        in_specs=[middle(PATCH, count), block((count, D))] + [full((D, D))] * 4 + [full(vec.shape)],
+        in_specs=[pl.BlockSpec(memory_space=pltpu.SMEM), middle(PATCH, count), block((count, D)), full((4, D, D)),
+                  full(vec.shape), pl.BlockSpec(memory_space=pl.ANY)],
         out_specs=[middle(LIVE, count)] + [block((count, ROWS, D))] * 3
         + [middle(LIVE, count), block((count, 4, ROWS, STACK))],
         out_shape=[array((LIVE, windows, D), F32)] + [array((windows, ROWS, D), BF)] * 3
@@ -192,7 +194,7 @@
         compiler_params=pltpu.CompilerParams(vmem_limit_bytes=VMEM),
         cost_estimate=cost(16e9),
         name="window_attention_forward",
-    )(patches, region_rows, *weights, vec)
+    )(owner, patches, region_rows, weights, vec, after)
 
 
 def mlp_kernel(many, sources, cols, steps, lanes, last, *refs):
@@ -300,13 +302,14 @@
     )(x1, cot, *weights, vec, bias_first, *prev)
 
 
-def attn_bwd_kernel(count, batch, chunks, more, *refs):
+def attn_bwd_kernel(count, batch, chunks, more, owner_ref, *refs):
     p_ref, r_ref = refs[:2]
     refs = refs[:3] + refs[4:]
     dx1_refs = refs[3 : 3 + chunks]
-    q_ref, k_ref, v_ref, o_ref, pt_ref, wq_ref, wk_ref, wv_ref, wo_ref, vec_ref = refs[3 + chunks : 13 + chunks]
-    prev_refs = refs[13 + chunks : 17 + chunks] if more else ()
-    dp_ref, dr_ref, dw_ref, dv_ref, dq_held, dk_held, dvv_held, do_held = refs[13 + chunks + len(prev_refs) :]
+    q_ref, k_ref, v_ref, o_ref, pt_ref, w_ref, vec_ref = refs[3 + chunks : 10 + chunks]
+    owner = owner_ref[0, 0]
+    prev_refs = refs[10 + chunks : 14 + chunks] if more else ()
+    dp_ref, dr_ref, dw_ref, dv_ref, dq_held, dk_held, dvv_held, do_held = refs[10 + chunks + len(prev_refs) :]
     total = count * LIVE
 
     @pl.when(pl.program_id(0) == 0)
@@ -319,7 +322,7 @@
     gain = vec[0:1]
     dx1 = jnp.concatenate([ref[...] for ref in dx1_refs], axis=0).reshape(total, D)
     gb = dx1.astype(BF)
-    hold(do_held, total, nt(gb, wo_ref[...]))
+    hold(do_held, total, nt(gb, w_ref[owner ^ 3]))
     masks = head_masks()
 
     def body(step, carry):
@@ -351,7 +354,7 @@
     dq = dq_wide.astype(BF)
     dk = held_rows(dk_held, total).astype(BF)
     dv = dv_wide.astype(BF)
-    dn = nt(dq, wq_ref[...]) + nt(dk, wk_ref[...]) + nt(dv, wv_ref[...])
+    dn = nt(dq, w_ref[owner ^ 0]) + nt(dk, w_ref[owner ^ 1]) + nt(dv, w_ref[owner ^ 2])
     dx = (dx1 + norm_back(dn, xhat, scale, gain)).reshape(LIVE, count, D)
     dp_ref[...] = dx[:PATCH].astype(BF)
     dr_ref[...] = dx[PATCH]
@@ -367,21 +370,21 @@
     dv_ref[4] += fold(dx1)
 
 
-def attn_bwd(patches, region_rows, dx1_parts, saved, weights, vec, start, windows, after, prev=(), count=16, batch=4):
+def attn_bwd(owner, patches, region_rows, dx1_parts, saved, weights, vec, start, windows, after, prev=(), count=16, batch=4):
     skip = start // count
     array = jax.ShapeDtypeStruct
     sums = [full((4, D, D)), full((5, 8, D))]
     anywhere = pl.BlockSpec(memory_space=pl.ANY)
     rows = pl.BlockSpec((count, D), lambda i: (i + skip, 0))
-    before = 14 + len(dx1_parts)
+    before = 12 + len(dx1_parts)
     return pl.pallas_call(
         partial(attn_bwd_kernel, count, batch, len(dx1_parts), len(prev) > 0),
         grid=(windows // count,),
-        in_specs=[middle(PATCH, count, skip), rows, anywhere, anywhere]
+        in_specs=[pl.BlockSpec(memory_space=pltpu.SMEM), middle(PATCH, count, skip), rows, anywhere, anywhere]
         + [middle(part.shape[0], count, skip) for part in dx1_parts]
         + [pl.BlockSpec((count, ROWS, D), lambda i: (i + skip, 0, 0))] * 3
         + [middle(LIVE, count, skip), pl.BlockSpec((count, 4, ROWS, STACK), lambda i: (i + skip, 0, 0, 0))]
-        + [full((D, D))] * 4 + [full(vec.shape)] + ([anywhere] * 2 + sums)[: len(prev)],
+        + [full((4, D, D)), full(vec.shape)] + ([anywhere] * 2 + sums)[: len(prev)],
         out_specs=[middle(PATCH, count, skip), rows] + sums,
         out_shape=[array(patches.shape, BF), array(region_rows.shape, F32),
                    array((4, D, D), F32), array((5, 8, D), F32)],
@@ -390,21 +393,22 @@
         compiler_params=pltpu.CompilerParams(vmem_limit_bytes=VMEM),
         cost_estimate=cost(12e9),
         name="window_attention_backward",
-    )(patches, region_rows, *after, *dx1_parts, *saved, *weights, vec, *prev)
-
-
-def regional_fwd_kernel(canvas_ref, band_ref, ids_ref, band_ids_ref, wq_ref, wk_ref, wv_ref, wo_ref, vec_ref,
+    )(owner, patches, region_rows, *after, *dx1_parts, *saved, weights, vec, *prev)
+
+
+def regional_fwd_kernel(owner_ref, canvas_ref, band_ref, ids_ref, band_ids_ref, w_ref, vec_ref,
                         r1_ref, mixed_ref, level_ref, q_ref, k_ref, v_ref):
     vec = vec_ref[...]
+    owner = owner_ref[0, 0]
     xhat, _ = norm_parts(canvas_ref[...].astype(F32))
     low = (xhat * vec[0:1] + vec[1:2]).astype(BF)
-    q_ref[...] = (nn(low, wq_ref[...]) + vec[4:5]).astype(BF)
-    k_ref[...] = nn(low, wk_ref[...]).astype(BF)
-    v_ref[...] = (nn(low, wv_ref[...]) + vec[5:6]).astype(BF)
+    q_ref[...] = (nn(low, w_ref[owner ^ 0]) + vec[4:5]).astype(BF)
+    k_ref[...] = nn(low, w_ref[owner ^ 1]).astype(BF)
+    v_ref[...] = (nn(low, w_ref[owner ^ 2]) + vec[5:6]).astype(BF)
     band = band_ref[...].astype(F32)
     rows = band.shape[0]
     xhat, _ = norm_parts(band)
-    q = nn((xhat * vec[0:1] + vec[1:2]).astype(BF), wq_ref[...]) + vec[4:5]
+    q = nn((xhat * vec[0:1] + vec[1:2]).astype(BF), w_ref[owner ^ 0]) + vec[4:5]
     masks = head_masks()
     same = ids_ref[...] == band_ids_ref[...]
     scores, probs = [], []
@@ -421,7 +425,7 @@
     for g, p in enumerate(probs):
         lanes = slice(GROUP * g, GROUP * (g + 1))
         mixed_ref[:, lanes] = collect(tn(p, v_ref[:, lanes]), masks, rows)
-    r1_ref[...] = band + nn(mixed_ref[...].astype(BF), wo_ref[...]) + vec[6:7]
+    r1_ref[...] = band + nn(mixed_ref[...].astype(BF), w_ref[owner ^ 3]) + vec[6:7]
 
 
 def in_vmem(kernel, outs, name, *args, after=(), scratch=(), flops=2e9):
@@ -440,10 +444,10 @@
     )(*args, *after)
 
 
-def payload_kernel(dr_ref, mixed_ref, level_ref, wo_ref, grad_ref, extra_ref):
+def payload_kernel(owner_ref, dr_ref, mixed_ref, level_ref, w_ref, grad_ref, extra_ref):
     low = dr_ref[...].astype(BF)
     grad_ref[...] = low
-    both = nt(low, wo_ref[...]).astype(BF).astype(F32) * mixed_ref[...]
+    both = nt(low, w_ref[owner_ref[0, 0] ^ 3]).astype(BF).astype(F32) * mixed_ref[...]
     head = lax.broadcasted_iota(jnp.int32, (D, GROUP), 0) // HEAD_DIM
     lane = lax.broadcasted_iota(jnp.int32, (D, GROUP), 1)
     pick = ((head == lane) | (head + HEADS == lane)).astype(BF)
@@ -462,47 +466,57 @@
     extra_ref[...] = extra.astype(BF)
 
 
-def regional_bwd_kernel(own_rows, owner_ref, q_ref, k_ref, v_ref, grads_ref, qo_ref, ko_ref, vo_ref, own_ref, ids_ref, ids_row_ref,
-                        ids_own_ref, ids_own_row_ref, level_ref, delta_ref, level_own_ref, delta_own_ref,
-                        grads_own_ref, mixed_ref, band_grad_ref, dw_ref, wq_ref, wk_ref, wv_ref, wo_ref, vec_ref,
+def regional_bwd_kernel(own_rows, owner_ref, place_ref, q_ref, k_ref, v_ref, canvas_ref, grads_ref, extra_ref, ids_ref,
+                        ids_row_ref, ids_own_ref, ids_own_row_ref, mixed_ref, band_grad_ref, dw_ref, w_ref, vec_ref,
                         dr_ref, keep_ref, give_ref, gv_ref, sum_held):
     vec = vec_ref[...]
+    owner = owner_ref[0, 0]
+    mine = pl.ds(pl.multiple_of(place_ref[0, 0] * own_rows, own_rows), own_rows)
     masks = head_masks()
-    do = nt(grads_ref[...], wo_ref[...]).astype(BF).astype(F32)
-    do_own = nt(grads_own_ref[...], wo_ref[...]).astype(BF).astype(F32)
+    grads_own = grads_ref[mine]
+    do = nt(grads_ref[...], w_ref[owner ^ 3]).astype(BF).astype(F32)
+    do_own = nt(grads_own, w_ref[owner ^ 3]).astype(BF).astype(F32)
     same_own = ids_ref[...] == ids_own_row_ref[...]
     same = ids_own_ref[...] == ids_row_ref[...]
     lanes = [slice(GROUP * g, GROUP * (g + 1)) for g in range(4)]
+
+    def columns(rows):
+        term = rows.astype(F32).T
+        part = lambda n: term[n * HEADS : (n + 1) * HEADS]
+        wide = lambda x: [jnp.concatenate([x[h : h + 1] for h in range(4 * g, 4 * g + 4)], axis=1) for g in range(4)]
+        return wide(part(0) + part(1)), wide(part(2) + part(3) + part(4))
+
+    delta, level = columns(extra_ref[...])
+    delta_own, level_own = columns(extra_ref[mine])
     first, second = [], []
     dqs, dks, dvs = [], [], []
     for g in range(4):
-        q_wide = spread(qo_ref[:, lanes[g]].astype(F32), masks)
+        q_wide = spread(q_ref[mine, lanes[g]].astype(F32), masks)
         do_wide = spread(do_own[:, lanes[g]], masks)
         first.append((nt(k_ref[:, lanes[g]], q_wide), nt(v_ref[:, lanes[g]], do_wide)))
         q_wide = spread(q_ref[:, lanes[g]].astype(F32), masks)
         do_wide = spread(do[:, lanes[g]], masks)
-        second.append((nt(ko_ref[:, lanes[g]], q_wide), nt(vo_ref[:, lanes[g]], do_wide), q_wide, do_wide))
+        second.append((nt(k_ref[mine, lanes[g]], q_wide), nt(v_ref[mine, lanes[g]], do_wide), q_wide, do_wide))
     for g in range(4):
         s, dp = first[g]
-        p = jnp.where(same_own, jnp.exp(s * SCALE - level_own_ref[g : g + 1]), 0.0)
-        ds = (p * (dp - delta_own_ref[g : g + 1])).astype(BF)
+        p = jnp.where(same_own, jnp.exp(s * SCALE - level_own[g]), 0.0)
+        ds = (p * (dp - delta_own[g])).astype(BF)
         dqs.append(collect(tn(ds, k_ref[:, lanes[g]]), masks, own_rows) * SCALE)
         s, dp, q_wide, do_wide = second[g]
-        p = jnp.where(same, jnp.exp(s * SCALE - level_ref[g : g + 1]), 0.0)
-        ds = (p * (dp - delta_ref[g : g + 1])).astype(BF)
+        p = jnp.where(same, jnp.exp(s * SCALE - level[g]), 0.0)
+        ds = (p * (dp - delta[g])).astype(BF)
         dvs.append(nn(p.astype(BF), do_wide))
         dks.append(nn(ds, q_wide) * SCALE)
-    xhat, scale = norm_parts(own_ref[...].astype(F32))
+    xhat, scale = norm_parts(canvas_ref[mine].astype(F32))
     low = (xhat * vec[0:1] + vec[1:2]).astype(BF)
     dq_wide, dk_wide, dv_wide = (jnp.concatenate(x, axis=1) for x in (dqs, dks, dvs))
     dq, dk, dv = dq_wide.astype(BF), dk_wide.astype(BF), dv_wide.astype(BF)
-    dn = nt(dq, wq_ref[...]) + nt(dk, wk_ref[...]) + nt(dv, wv_ref[...])
-    dr_ref[...] = grads_own_ref[...].astype(F32) + norm_back(dn, xhat, scale, vec[0:1])
+    dn = nt(dq, w_ref[owner ^ 0]) + nt(dk, w_ref[owner ^ 1]) + nt(dv, w_ref[owner ^ 2])
+    dr_ref[...] = grads_own.astype(F32) + norm_back(dn, xhat, scale, vec[0:1])
     sum_held[0] = dw_ref[0] + tn(low, dq)
     sum_held[1] = dw_ref[1] + tn(low, dk)
     sum_held[2] = dw_ref[2] + tn(low, dv)
     sum_held[3] = dw_ref[3] + tn(mixed_ref[...].astype(BF), band_grad_ref[...])
-    owner = owner_ref[0, 0]
     for n in range(2):
         keep_ref[n] = sum_held[owner ^ (2 * n)].astype(BF)
         give_ref[n] = sum_held[owner ^ (2 * n + 1)].astype(BF)
@@ -771,7 +785,9 @@
 
     attn_pieces = jnp.stack(pieces_of_owners(attn_w[0].astype(BF)))
     mlp_w = pieces_of_owners(jnp.stack([mlp_in, mlp_out]).astype(BF))
-    weights = [lax.dynamic_index_in_dim(attn_pieces, opt_index ^ j, 0, keepdims=False) for j in range(OPT)]
+    owner = opt_index.reshape(1, 1)
+    if not one_kernel:
+        weights = [lax.dynamic_index_in_dim(attn_pieces, opt_index ^ j, 0, keepdims=False) for j in range(OPT)]
     canvas_blocks = share(regions[0])
     canvas = canvas_blocks.reshape(tokens, D)
     by_position = patch_cot[0].transpose(0, 2, 1, 3)
@@ -791,8 +807,7 @@
         region_rows, mixed, level, reg_q, reg_k, reg_v = in_vmem(
             regional_fwd_kernel,
             [((grid_cols, D), F32), ((grid_cols, D), F32), ((4, 4 * grid_cols), F32)] + [((tokens, D), BF)] * 3,
-            "regional_attention_forward", canvas, band, ids[:, None], repeat(band_ids), *weights, vec,
-            after=(mlp_w[2],))
+            "regional_attention_forward", owner, canvas, band, ids[:, None], repeat(band_ids), attn_pieces, vec)
         level = level.reshape(HEADS, grid_cols)
     else:
         region_rows, mixed, level, reg_q, reg_k, reg_v = regional_forward(
@@ -801,7 +816,7 @@
 
     windows = patches[0, 0].transpose(1, 0, 2)
     some = grid_cols // 2
-    x1, *saved = attn_fwd(windows, region_rows, weights, vec)
+    x1, *saved = attn_fwd(owner, windows, region_rows, attn_pieces, vec, mlp_w[2])
     last_cot = move(fence(last, x1))
     early_out, late_out, dx1_a, *grads_a = mlp(x1, 0, first_cot, mlp_w, vec, bias_first)
     moved_a = move(early_out)
@@ -814,18 +829,18 @@
     out_regions = moved_b[None, :, -1]
 
     dx1 = (dx1_a, dx1_b)
-    early = attn_bwd(windows, region_rows, dx1, saved, weights, vec, 0, some, (far, far))
+    early = attn_bwd(owner, windows, region_rows, dx1, saved, attn_pieces, vec, 0, some, (far, far))
     own_mlp = near[:2].astype(F32) + grads_b[0][:2].astype(F32) + fence(pair(far, 2), early[3]).astype(F32)
     keep, give = halving_step(own_mlp.reshape(2 * D, D), 1)
     d_patches, d_region, d_attn, d_vec_attn = attn_bwd(
-        windows, region_rows, dx1, saved, weights, vec, some, some, (give, moms), prev=early)
+        owner, windows, region_rows, dx1, saved, attn_pieces, vec, some, some, (give, moms), prev=early)
     d_patches = d_patches.transpose(1, 0, 2)[None, None]
-    gives, owner = [], opt_index.reshape(1, 1)
+    gives = []
     old_grams = in_vmem(old_grams_kernel, [((D, D), F32)] * 2, "momentum_grams", moms, after=(d_vec_attn,),
                          flops=4e9)
 
     band_grad, extra = in_vmem(payload_kernel, [((grid_cols, D), BF), ((grid_cols, GROUP), BF)],
-                               "regional_payload", d_region, mixed, level_wide, weights[3],
+                               "regional_payload", owner, d_region, mixed, level_wide, attn_pieces,
                                after=(give, moved_b))
     taken = fence(swap(give, 1), band_grad)
     for bit in bits()[1:]:
@@ -835,23 +850,18 @@
     payload = share(jnp.concatenate([band_grad, extra], axis=1)).reshape(grid_rows, dp_size, cols, D + GROUP)
     payload = payload.transpose(1, 0, 2, 3).reshape(tokens, D + GROUP)
     grads = payload[:, :D]
-    extra = payload[:, D:].astype(F32)
-    part = lambda n: extra[:, n * HEADS : (n + 1) * HEADS]
-    delta = (part(0) + part(1)).T
-    level = (part(2) + part(3) + part(4)).T
+    extra = payload[:, D:]
     if one_kernel:
-        wide = lambda x: x.reshape(4, -1)
-        own_columns = lambda x: wide(lax.dynamic_slice_in_dim(x, dp_index * own_count, own_count, 1))
         matrices = ((2, D, D), BF)
         d_regions, keep_attn, give_attn, d_vec_reg = in_vmem(
             partial(regional_bwd_kernel, own_count),
             [((own_count, D), F32), matrices, matrices, ((5, 8, D), F32)],
-            "regional_attention_backward", owner,
-            reg_q, reg_k, reg_v, grads, own_of(reg_q), own_of(reg_k), own_of(reg_v),
-            own_of(canvas), ids[:, None], repeat(ids), own_ids[:, None], repeat(own_ids), wide(level), wide(delta),
-            own_columns(level), own_columns(delta), own_of(grads), mixed, band_grad, d_attn, *weights, vec,
+            "regional_attention_backward", owner, dp_index.reshape(1, 1), reg_q, reg_k, reg_v, canvas, grads, extra,
+            ids[:, None], repeat(ids), own_ids[:, None], repeat(own_ids), mixed, band_grad, d_attn, attn_pieces, vec,
             after=tuple(gives[-1:]) + tuple(old_grams), scratch=[pltpu.VMEM((4, D, D), F32)], flops=4e9)
     else:
+        part = lambda n: extra[:, n * HEADS : (n + 1) * HEADS].astype(F32)
+        delta, level = (part(0) + part(1)).T, (part(2) + part(3) + part(4)).T
         d_regions, grad_attn, d_vec_reg = regional_backward(
             reg_q, reg_k, reg_v, grads, own_of, own_of(canvas), ids[:, None] == own_ids[None, :], level, delta,
             weights, vec, mixed, band_grad, d_attn)
@@ -866,26 +876,27 @@
     piece_attn = near[0].astype(F32) + keep_attn[0].astype(F32) + pair(far, 2).astype(F32)
     piece_attn = move(piece_attn.astype(BF).reshape(dp_size, D // dp_size, D))
     piece_attn = jnp.sum(piece_attn.astype(F32), axis=0).astype(BF)
-    own_attn = share(piece_attn).reshape(D, D)
+    shared_attn = share(piece_attn)
     all_mlp = lax.all_gather(piece_mlp, ("dp", "opt"), axis=0).reshape(dp_size, OPT, -1, D)
     *grams, own_mlp = in_vmem(partial(grams_kernel, order_of_halves(dp_size)),
                               [((D, D), F32)] * 4 + [((2, D, D), BF)], "mlp_grams", owner, moms, all_mlp, flops=4e9)
     grams = [old_grams[0], *grams[:2], old_grams[1], *grams[2:]]
+    own_attn = fence(shared_attn, own_mlp).reshape(D, D)
 
     d_vec_attn = jnp.sum(d_vec_attn + d_vec_reg, axis=1)
     d_vec_mlp = jnp.sum(grads_a[2] + grads_b[2], axis=1)
     d_bias_first = jnp.take(jnp.sum(grads_a[3] + grads_b[3], axis=1), order, axis=0)
     grad_vec = jnp.concatenate([d_vec_attn[:2], d_vec_mlp[:2], d_vec_attn[2:], d_vec_mlp[2:], d_bias_first])
-    grad_vec = grad_vec + pair(grad_vec, 1)
-    grad_vec = grad_vec + pair(grad_vec, 2)
-    grad_vec = sum_small_over_dp(grad_vec)
 
     squares = lambda x: jnp.sum(x.astype(F32) ** 2)
-    total = jnp.full((8, 128), squares(piece_attn) + squares(piece_mlp))
-    total = total + pair(total, 1)
-    total = total + pair(total, 2)
-    total = sum_small_over_dp(total)
-    grad_norm = jnp.sqrt(total[0, 0] + squares(grad_vec))
+    part = jnp.full((1, D), squares(piece_attn) + squares(piece_mlp))
+    sums = jnp.concatenate([grad_vec, part])
+    sums = sums + pair(sums, 1)
+    sums = sums + pair(sums, 2)
+    sums = sum_small_over_dp(sums)
+    grad_vec, total = sums[:-1], sums[-1]
+
+    grad_norm = jnp.sqrt(total[0] + squares(grad_vec))
     clip = jnp.minimum(1.0, CLIP_LIMIT / (grad_norm + 1e-06))
     attn_mom_new, new_attn, first_mom, new_first, second_mom, new_second = in_vmem(
         update_kernel, [((D, D), F32)] * 6, "matrix_updates", clip.reshape(1, 1), own_attn, attn_mom[0], attn_w[0],

time: 448 us -> 443 us (0.989)
  local copies, waits for them, and re-layouts: 32.9 us -> 24 us
  waiting for transfers between devices: 65.4 us -> 74.3 us
  other arithmetic: 27.8 us -> 22.1 us
    ppermute x14 -> x12, waiting for transfers between devices: 33.6 us -> 41.7 us  [pair(): return lax.ppermute(values, 'opt', [(i, i ^ bit) for i in range(OPT)])]
    dynamic_slice x6 -> x1, local copies, waits for them, and re-layouts: 6.58 us -> 0.08 us  [per_device(): lax.dynamic_slice_in_dim(x, dp_index * own_count, own_count, 0)]
    ppermute x9 -> x6, starting transfers between devices: 16.1 us -> 14.6 us  [swap(): lax.ppermute(x, 'dp', [(i, i ^ bit) for i in range(lax.axis_size('dp'))])]
    ppermute x9 -> x6, waiting for transfers between devices: 10.2 us -> 11.3 us  [swap(): lax.ppermute(x, 'dp', [(i, i ^ bit) for i in range(lax.axis_size('dp'))])]
  transfers between devices with their start and end apart: 33 -> 28, of which waited for: 17 -> 12; matrix products, arithmetic and copies ran while one was open for 11% -> 8% of each run, Pallas kernels for 46% -> 47%
where the time goes in v6:
time: 443 us; the launch traced here: 435 us
  Pallas kernels  234 us (53%)
  waiting for transfers between devices  74.3 us (17%)
  starting transfers between devices  62.2 us (14%)
  local copies, waits for them, and re-layouts  24 us (5%)
  other arithmetic  22.1 us (5%)
  between operations  18.7 us (4%)
    pallas_call x6, Pallas kernels, in_vmem(): pl.pallas_call(lambda *refs: kernel(*refs[:count], *refs[count + len(afte...  69.4 us
    pallas_call x2, Pallas kernels, mlp(): pl.pallas_call(partial(mlp_kernel, many, sources, cols, steps, lanes, len...  69.3 us
    pallas_call x2, Pallas kernels, attn_bwd(): pl.pallas_call(partial(attn_bwd_kernel, count, batch, len(dx1_parts), len...  60.3 us
    ppermute x12, waiting for transfers between devices, pair(): return lax.ppermute(values, 'opt', [(i, i ^ bit) for i in range(OPT)])  41.7 us
    pallas_call x1, Pallas kernels, attn_fwd(): pl.pallas_call(partial(attn_fwd_kernel, count, batch), grid=(windows // c...  34.8 us
    all_to_all x5, starting transfers between devices, per_device(): move = lambda x: lax.all_to_all(x, 'dp', 0, 0, tiled=True)  25.9 us
    all_to_all x5, waiting for transfers between devices, per_device(): move = lambda x: lax.all_to_all(x, 'dp', 0, 0, tiled=True)  21.3 us
    all_to_all x3, starting transfers between devices, share(): return lax.all_to_all(copies, 'dp', 0, 0, tiled=True)  15.8 us
  transfers between devices with their start and end apart: 28, of which 12 were waited for; matrix products, arithmetic and copies ran while one was open for 8% of the time, Pallas kernels for 47%

profile of v6, /device:TPU:0, one launch (start us, length us, event | category | flops | bytes accessed | tf_op | source)
XLA Modules:
  0.0 435.1 jit_solution(6050388499082669118)
XLA Ops:
  7.2 1.8 broadcast_in_dim.47
  9.0 7.3 %all-to-all-start = ((bf16[8,8,8,512]{3,2,1,0:T(8,128)(2,1)}), bf16[8,8,8,512]{3,2,1,0:T(8,128)(2,1)}, u32[]{:S(2)}, u32[]{:S(2)}) async-start(bf16[8,8,8,512]{3,2,1,0:T(8,128)(2,1)} %broadcast_in_dim.47), calls=%async_computation | async-start | bytes 1048576 | tf_op jit(solution)/shard_map/all_to_all | solution.py:694
  17.3 1.5 collective-permute-start.1
  20.9 11.6 %collective-permute-done.1 = bf16[512,512]{1,0:T(8,128)(2,1)} collective-permute-done((bf16[512,512]{1,0:T(8,128)(2,1)}, bf16[512,512]{1,0:T(8,128)(2,1)}, u32[]{:S(2)}, u32[]{:S(2)}) %collective-permute-start.1) | collective-permute-done | bytes 524320 | tf_op jit(solution)/shard_map/ppermute | solution.py:670
  34.1 1.5 slice.91.refs_0_
  36.4 1.5 pad_maximum_fusion.1.refs_0_
  37.9 6.0 %all-to-all-start.1 = ((bf16[8,30,8,512]{3,2,1,0:T(8,128)(2,1)}), bf16[8,30,8,512]{3,2,1,0:T(8,128)(2,1)}, u32[]{:S(2)}, u32[]{:S(2)}) async-start(bf16[8,30,8,512]{3,2,1,0:T(8,128)(2,1)} %fence.9), calls=%async_computation.1 | async-start | bytes 3932160 | tf_op jit(solution)/shard_map/all_to_all | solution.py:784
  43.9 1.5 dynamic-slice_bitcast_fusion.refs_2_
  45.4 3.1 pad_maximum_fusion.refs_5_.w_ref.refs_11_.refs_4_.refs_15_
  48.5 5.2 %regional_attention_forward.1 = (f32[64,512]{1,0:T(8,128)}, f32[64,512]{1,0:T(8,128)}, f32[4,256]{1,0:T(4,128)}, bf16[512,512]{1,0:T(8,128)(2,1)}, bf16[512,512]{1,0:T(8,128)(2,1)}, /*index=5*/bf16[512,512]{1,0:T(8,128)(2,1)}) custom-call(s32[1,1]{1,0:T(1,128)} %bitcast.refs_0_.owner_ref, bf16[512,512]{1,0:T(8,128)(2,1)} %bitcast.4.refs_1_.refs_5_, ...), custom_call_target="tpu_custom_call" | custom-call | flops 2000000000 | bytes 100000 | tf_op jit(solution)/shard_map/regional_attention_forward/pallas_call | solution.py:434
  53.7 34.8 %window_attention_forward.1 = (f32[50,64,512]{2,1,0:T(8,128)}, bf16[64,56,512]{2,1,0:T(8,128)(2,1)}, bf16[64,56,512]{2,1,0:T(8,128)(2,1)}, bf16[64,56,512]{2,1,0...) custom-call(s32[1,1]{1,0:T(1,128)} %bitcast.refs_0_.owner_ref, ...), custom_call_target="tpu_custom_call" | custom-call | flops 16000000000 | bytes 100000 | tf_op jit(solution)/shard_map/window_attention_forward/pallas_call | solution.py:184
  90.5 6.1 %all-to-all-start.3 = ((bf16[8,20,8,512]{3,2,1,0:T(8,128)(2,1)}), bf16[8,20,8,512]{3,2,1,0:T(8,128)(2,1)S(1)}, u32[]{:S(2)}, u32[]{:S(2)}) async-start(bf16[8,20,8,512]{3,2,1,0:T(8,128)(2,1)} %fence.10), calls=%async_computation.3 | async-start | bytes 2621440 | tf_op jit(solution)/shard_map/all_to_all | solution.py:784
  98.4 1.9 collective-permute-done.4.refs_3_
  101.5 39.9 %mlp_forward_backward.2 = (bf16[8,20,8,512]{3,2,1,0:T(8,128)(2,1)}, bf16[8,30,8,512]{3,2,1,0:T(8,128)(2,1)}, f32[30,64,512]{2,1,0:T(8,128)}, bf16[4,512,512]{2,1...) custom-call(f32[50,64,512]{2,1,0:T(8,128)} %get-tuple-element.68.refs_0_.refs_1_, ...), custom_call_target="tpu_custom_call" | custom-call | flops 12000000000 | bytes 100000 | tf_op jit(solution)/shard_map/mlp_forward_backward/pallas_call | solution.py:288
  141.4 6.3 %all-to-all-start.2 = ((bf16[8,20,8,512]{3,2,1,0:T(8,128)(2,1)}), bf16[8,20,8,512]{3,2,1,0:T(8,128)(2,1)S(1)}, u32[]{:S(2)}, u32[]{:S(2)}) async-start(bf16[8,20,8,512]{3,2,1,0:T(8,128)(2,1)} %get-tuple-element.69), calls=%async_computation.2 | async-start | bytes 2621440 | tf_op jit(solution)/shard_map/all_to_all | solution.py:784
  147.7 29.4 %mlp_forward_backward.3 = (bf16[8,30,8,512]{3,2,1,0:T(8,128)(2,1)}, f32[20,64,512]{2,1,0:T(8,128)}, bf16[4,512,512]{2,1,0:T(8,128)(2,1)}, bf16[4,512,512]{2,1,0:...) custom-call(f32[50,64,512]{2,1,0:T(8,128)} %get-tuple-element.68.refs_0_.refs_1_, ...), custom_call_target="tpu_custom_call", output_to_operand_aliasing={{0}: (8, {})} | custom-call | flops 8000000000 | bytes 100000 | tf_op jit(solution)/shard_map/mlp_forward_backward/pallas_call | solution.py:288
  177.1 2.2 all-to-all-done.2.refs_1_
  180.5 4.4 %collective-permute-done.6 = bf16[4,512,512]{2,1,0:T(8,128)(2,1)S(1)} collective-permute-done((bf16[4,512,512]{2,1,0:T(8,128)(2,1)}, bf16[4,512,512]{2,1,0:T(8,128)(2,1)S(1)}, u32[]{:S(2)}, u32[]{:S(2)}) %collective-permute-start.6) | collective-permute-done | bytes 2097184 | tf_op jit(solution)/shard_map/ppermute | solution.py:670
  184.9 1.4 add_convert_fusion.refs_1_.refs_2_.refs_3_
  186.5 3.9 all-to-all-start.4
  191.3 1.5 collective-permute-start.7
  192.8 29.5 %window_attention_backward.2 = (bf16[49,64,512]{2,1,0:T(8,128)(2,1)}, f32[64,512]{1,0:T(8,128)}, f32[4,512,512]{2,1,0:T(8,128)}, f32[5,8,512]{2,1,0:T(8,128)}) custom-call(s32[1,1]{1,0:T(1,128)} %bitcast.refs_0_.owner_ref, bf16[49,64,512]{2,1,0:T(8,128)(2,1)} %bitcast.73, f32[64,512]{1,0:T(8,128)} %get-tuple-element.67.r_ref.refs_1_, ...), custom_call_target="tpu_custom_call" | custom-call | flops 12000000000 | bytes 100000 | tf_op jit(solution)/shard_map/window_attention_backward/pallas_call | solution.py:380
  222.3 2.3 convert_add_fusion
  224.6 1.3 copy-done.4
  226.0 2.1 collective-permute-start.8
  228.1 30.8 %window_attention_backward.3 = (bf16[49,64,512]{2,1,0:T(8,128)(2,1)}, f32[64,512]{1,0:T(8,128)}, f32[4,512,512]{2,1,0:T(8,128)}, f32[5,8,512]{2,1,0:T(8,128)}) custom-call(s32[1,1]{1,0:T(1,128)} %bitcast.refs_0_.owner_ref, bf16[49,64,512]{2,1,0:T(8,128)(2,1)} %bitcast.74, ...), custom_call_target="tpu_custom_call", output_to_operand_aliasing={{0}: (14, {}), {1}: (15, {})} | custom-call | flops 12000000000 | bytes 100000 | tf_op jit(solution)/shard_map/window_attention_backward/pallas_call | solution.py:380
  259.0 1.3 copy-done.2
  260.2 2.9 regional_payload.1
  265.0 4.7 %all-to-all-start.5 = ((bf16[8,64,640]{2,1,0:T(8,128)(2,1)}), bf16[8,64,640]{2,1,0:T(8,128)(2,1)}, u32[]{:S(2)}, u32[]{:S(2)}) async-start(bf16[8,64,640]{2,1,0:T(8,128)(2,1)} %broadcast_in_dim.50), calls=%async_computation.5 | async-start | bytes 1310720 | tf_op jit(solution)/shard_map/all_to_all | solution.py:694
  274.1 2.0 collective-permute-start.9
  276.2 9.1 %momentum_grams.1 = (f32[512,512]{1,0:T(8,128)}, f32[512,512]{1,0:T(8,128)}) custom-call(f32[4,2,512,512]{3,2,1,0:T(8,128)} %bitcast.66, f32[5,8,512]{2,1,0:T(8,128)} %get-tuple-element.97.refs_1_), custom_call_target="tpu_custom_call" | custom-call | flops 4000000000 | bytes 100000 | tf_op jit(solution)/shard_map/momentum_grams/pallas_call | solution.py:434
  285.3 2.5 collective-permute-done.9
  288.0 2.3 collective-permute-start.12
  293.0 9.8 %regional_attention_backward.1 = (f32[64,512]{1,0:T(8,128)}, bf16[2,512,512]{2,1,0:T(8,128)(2,1)}, bf16[2,512,512]{2,1,0:T(8,128)(2,1)}, f32[5,8,512]{2,1,0:T(8,128)}) custom-call(s32[1,1]{1,0:T(1,128)} %bitcast.refs_0_.owner_ref, s32[1,1]{1,0:T(1,128)} %bitcast.27.refs_1_, bf16[512,512]{1,0:T(8,128)(2,1)} %get-tuple-element.88.refs_2_, ...), custom_call_target="tpu_custom_call" | custom-call | flops 4000000000 | bytes 100000 | tf_op jit(solution)/shard_map/regional_attention_backward/pallas_call | solution.py:434
  303.4 2.2 multiply_reduce_fusion
  305.7 2.9 collective-permute-done.10
  309.3 14.4 %collective-permute-done.11 = bf16[512,512]{1,0:T(8,128)(2,1)S(1)} collective-permute-done((bf16[512,512]{1,0:T(8,128)(2,1)S(1)}, bf16[512,512]{1,0:T(8,128)(2,1)S(1)}, u32[]{:S(2)}, u32[]{:S(2)}) %collective-permute-start.11) | collective-permute-done | bytes 524320 | tf_op jit(solution)/shard_map/ppermute | solution.py:670
  324.7 3.6 all-to-all-start.6
  329.2 19.1 %all-to-all-done.6 = bf16[8,64,512]{2,1,0:T(8,128)(2,1)S(1)} async-done(((bf16[8,64,512]{2,1,0:T(8,128)(2,1)}), bf16[8,64,512]{2,1,0:T(8,128)(2,1)S(1)}, u32[]{:S(2)}, u32[]{:S(2)}) %all-to-all-start.6) | async-done | bytes 524320 | tf_op jit(solution)/shard_map/all_to_all | solution.py:784
  352.1 4.2 collective-permute-done.14
  356.3 1.5 collective-permute-start.15
  358.6 3.9 all-to-all-start.7
  362.5 2.0 collective-permute-start.16
  365.2 8.7 %collective-permute-done.16 = f32[13,512]{1,0:T(8,128)S(1)} collective-permute-done((f32[13,512]{1,0:T(8,128)S(1)}, f32[13,512]{1,0:T(8,128)S(1)}, u32[]{:S(2)}, u32[]{:S(2)}) %collective-permute-start.16) | collective-permute-done | bytes 26656 | tf_op jit(solution)/shard_map/ppermute | solution.py:698
  373.9 4.6 %collective-permute-start.17 = (f32[13,512]{1,0:T(8,128)S(1)}, f32[13,512]{1,0:T(8,128)S(1)}, u32[]{:S(2)}, u32[]{:S(2)}) collective-permute-start(f32[13,512]{1,0:T(8,128)S(1)} %add.145), channel_id=1, source_target_pairs={{0,16},{4,20},{8,24},{12,28},{16,0},{20,4},{24,8},{28,12},{1,17},{... | collective-permute-start | bytes 79880 | tf_op jit(solution)/shard_map/ppermute | solution.py:698
  378.6 2.0 maximum_bitcast_fusion
  383.7 12.8 %mlp_grams.1 = (f32[512,512]{1,0:T(8,128)}, f32[512,512]{1,0:T(8,128)}, f32[512,512]{1,0:T(8,128)}, f32[512,512]{1,0:T(8,128)}, bf16[2,512,512]{2,1,0:T(8,128)(2,1)}) custom-call(s32[1,1]{1,0:T(1,128)} %bitcast.refs_0_.owner_ref, f32[4,2,512,512]{3,2,1,0:T(8,128)} %bitcast.67, bf16[8,4,128,512]{3,2,1,0:T(8,128)(2,1)} %bitcast.89), custom_call_target="tpu_custom_call" | custom-call | flops 4000000000 | bytes 100000 | tf_op jit(solution)/shard_map/mlp_grams/pallas_call | solution.py:434
  397.4 29.5 %matrix_updates.1 = (f32[512,512]{1,0:T(8,128)}, f32[512,512]{1,0:T(8,128)}, f32[512,512]{1,0:T(8,128)}, f32[512,512]{1,0:T(8,128)}, f32[512,512]{1,0:T(8,128)}, /*index=5*/f32[512,512]{1,0:T(8,128)}) custom-call(f32[1,1]{1,0:T(1,128)} %bitcast.39.refs_0_, bf16[512,512]{1,0:T(8,128)(2,1)} %bitcast.78, f32[512,512]{1,0:T(8,128)} %bitcast.90, ...), custom_call_target="tpu_custom_call" | custom-call | flops 12000000000 | bytes 100000 | tf_op jit(solution)/shard_map/matrix_updates/pallas_call | solution.py:434
  (176 shorter events, 31.8 us)
Async XLA Ops:
  7.2 9.0 %copy-start.16 = (f32[1,512,512]{2,1,0:T(8,128)S(1)}, f32[1,512,512]{2,1,0:T(8,128)}, u32[]{:S(2)}) copy-start(f32[1,512,512]{2,1,0:T(8,128)} %param.19) | copy-start | bytes 3145732
  9.0 28.9 %all-to-all-start = ((bf16[8,8,8,512]{3,2,1,0:T(8,128)(2,1)}), bf16[8,8,8,512]{3,2,1,0:T(8,128)(2,1)}, u32[]{:S(2)}, u32[]{:S(2)}) async-start(bf16[8,8,8,512]{3,2,1,0:T(8,128)(2,1)} %broadcast_in_dim.47), calls=%async_computation | async-start | bytes 1048576 | tf_op jit(solution)/shard_map/all_to_all | solution.py:694
  17.3 15.2 %copy-start.32 = (s32[1,8,64]{2,1,0:T(8,128)S(1)}, s32[1,8,64]{2,1,0:T(8,128)}, u32[]{:S(2)}) copy-start(s32[1,8,64]{2,1,0:T(8,128)} %param.18) | copy-start | bytes 6148
  17.3 16.8 %copy-start.7 = (bf16[1,8,8,49,512]{4,2,3,1,0:T(8,128)(2,1)S(1)}, bf16[1,8,8,49,512]{4,2,3,1,0:T(8,128)(2,1)}, u32[]{:S(2)}) copy-start(bf16[1,8,8,49,512]{4,2,3,1,0:T(8,128)(2,1)} %param.23) | copy-start | bytes 9633796
  17.3 15.2 %collective-permute-start.1 = (bf16[512,512]{1,0:T(8,128)(2,1)}, bf16[512,512]{1,0:T(8,128)(2,1)}, u32[]{:S(2)}, u32[]{:S(2)}) collective-permute-start(bf16[512,512]{1,0:T(8,128)(2,1)} %get-tuple-element.125), channel_id=1, source_target_pairs={{0,2},{1,3},{2,0},{3,1},{4,6},{5,7},{6,4},{7,5},{8,10},{9,11},{10,... | collective-permute-start | bytes 1572872 | tf_op jit(solution)/shard_map/ppermute | solution.py:670
  20.0 33.7 %collective-permute-start.3 = (bf16[2,512,512]{2,1,0:T(8,128)(2,1)}, bf16[2,512,512]{2,1,0:T(8,128)(2,1)}, u32[]{:S(2)}, u32[]{:S(2)}) collective-permute-start(bf16[2,512,512]{2,1,0:T(8,128)(2,1)} %pad_maximum_fusion.3.refs_2_), channel_id=1, source_target_pairs={{0,2},{1,3},{2,0},{3,1},{4,6},{5,7},{6,4},{7,5},{8,10},{9,11},{10,... | collective-permute-start | bytes 3145736 | tf_op jit(solution)/shard_map/ppermute | solution.py:670
  20.9 24.5 %collective-permute-start = (bf16[512,512]{1,0:T(8,128)(2,1)}, bf16[512,512]{1,0:T(8,128)(2,1)}, u32[]{:S(2)}, u32[]{:S(2)}) collective-permute-start(bf16[512,512]{1,0:T(8,128)(2,1)} %get-tuple-element.125), channel_id=1, source_target_pairs={{0,1},{1,0},{2,3},{3,2},{4,5},{5,4},{6,7},{7,6},{8,9},{9,8},{10,11... | collective-permute-start | bytes 1572872 | tf_op jit(solution)/shard_map/ppermute | solution.py:670
  32.5 12.9 %collective-permute-start.2 = (bf16[512,512]{1,0:T(8,128)(2,1)}, bf16[512,512]{1,0:T(8,128)(2,1)}, u32[]{:S(2)}, u32[]{:S(2)}) collective-permute-start(bf16[512,512]{1,0:T(8,128)(2,1)} %collective-permute-done.1), channel_id=1, source_target_pairs={{0,1},{1,0},{2,3},{3,2},{4,5},{5,4},{6,7},{7,6},{8,9},{9,8},{10,11... | collective-permute-start | bytes 1572872 | tf_op jit(solution)/shard_map/ppermute | solution.py:670
  37.9 52.6 %all-to-all-start.1 = ((bf16[8,30,8,512]{3,2,1,0:T(8,128)(2,1)}), bf16[8,30,8,512]{3,2,1,0:T(8,128)(2,1)}, u32[]{:S(2)}, u32[]{:S(2)}) async-start(bf16[8,30,8,512]{3,2,1,0:T(8,128)(2,1)} %fence.9), calls=%async_computation.1 | async-start | bytes 3932160 | tf_op jit(solution)/shard_map/all_to_all | solution.py:784
  43.9 184.2 %all-gather.5.cloned.1.call-start = ((), (), s32[]{:S(2)}) async-start(), calls=%async_computation.8 | async-start | bytes 10485760 | tf_op jit(solution)/shard_map/all_gather | solution.py:823
  90.5 6.6 %slice-start.1 = ((f32[12,512]{1,0:T(8,128)}), f32[4,512]{1,0:T(4,128)S(1)}, s32[]{:S(2)}) async-start(f32[12,512]{1,0:T(8,128)} %refs_16_.1), calls=%async_computation.11 | async-start | bytes 16384 | tf_op jit(solution)/shard_map/slice | solution.py:797
  90.5 50.8 %all-to-all-start.3 = ((bf16[8,20,8,512]{3,2,1,0:T(8,128)(2,1)}), bf16[8,20,8,512]{3,2,1,0:T(8,128)(2,1)S(1)}, u32[]{:S(2)}, u32[]{:S(2)}) async-start(bf16[8,20,8,512]{3,2,1,0:T(8,128)(2,1)} %fence.10), calls=%async_computation.3 | async-start | bytes 2621440 | tf_op jit(solution)/shard_map/all_to_all | solution.py:784
  96.6 3.6 collective-permute-start.4
  96.6 4.9 %collective-permute-start.5 = (bf16[2,512,512]{2,1,0:T(8,128)(2,1)}, bf16[2,512,512]{2,1,0:T(8,128)(2,1)}, u32[]{:S(2)}, u32[]{:S(2)}) collective-permute-start(bf16[2,512,512]{2,1,0:T(8,128)(2,1)} %collective-permute-done.3._.refs_4_), channel_id=1, source_target_pairs={{0,1},{1,0},{2,3},{3,2},{4,5},{5,4},{6,7},{7,6},{8,9},{9,8},{10,11... | collective-permute-start | bytes 3145736 | tf_op jit(solution)/shard_map/ppermute | solution.py:670
  141.4 6.3 %copy-start.13 = (bf16[8,20,8,512]{3,2,1,0:T(8,128)(2,1)}, bf16[8,20,8,512]{3,2,1,0:T(8,128)(2,1)S(1)}, u32[]{:S(2)}) copy-start(bf16[8,20,8,512]{3,2,1,0:T(8,128)(2,1)S(1)} %all-to-all-done.3.refs_1_) | copy-start | bytes 3932164
  141.4 38.0 %all-to-all-start.2 = ((bf16[8,20,8,512]{3,2,1,0:T(8,128)(2,1)}), bf16[8,20,8,512]{3,2,1,0:T(8,128)(2,1)S(1)}, u32[]{:S(2)}, u32[]{:S(2)}) async-start(bf16[8,20,8,512]{3,2,1,0:T(8,128)(2,1)} %get-tuple-element.69), calls=%async_computation.2 | async-start | bytes 2621440 | tf_op jit(solution)/shard_map/all_to_all | solution.py:784
  180.5 4.4 %collective-permute-start.6 = (bf16[4,512,512]{2,1,0:T(8,128)(2,1)}, bf16[4,512,512]{2,1,0:T(8,128)(2,1)S(1)}, u32[]{:S(2)}, u32[]{:S(2)}) collective-permute-start(bf16[4,512,512]{2,1,0:T(8,128)(2,1)} %fence.11), channel_id=1, source_target_pairs={{0,1},{1,0},{2,3},{3,2},{4,5},{5,4},{6,7},{7,6},{8,9},{9,8},{10,11... | collective-permute-start | bytes 6291464 | tf_op jit(solution)/shard_map/ppermute | solution.py:670
  186.5 72.5 %all-to-all-start.4 = ((bf16[8,30,8,512]{3,2,1,0:T(8,128)(2,1)}), bf16[8,30,8,512]{3,2,1,0:T(8,128)(2,1)S(1)}, u32[]{:S(2)}, u32[]{:S(2)}) async-start(bf16[8,30,8,512]{3,2,1,0:T(8,128)(2,1)} %fence.12), calls=%async_computation.4 | async-start | bytes 3932160 | tf_op jit(solution)/shard_map/all_to_all | solution.py:784
  191.3 31.0 %collective-permute-start.7 = (bf16[2,512,512]{2,1,0:T(8,128)(2,1)S(1)}, bf16[2,512,512]{2,1,0:T(8,128)(2,1)}, u32[]{:S(2)}, u32[]{:S(2)}) collective-permute-start(bf16[2,512,512]{2,1,0:T(8,128)(2,1)S(1)} %copy-done.6), channel_id=1, source_target_pairs={{0,2},{1,3},{2,0},{3,1},{4,6},{5,7},{6,4},{7,5},{8,10},{9,11},{10,... | collective-permute-start | bytes 3145736 | tf_op jit(solution)/shard_map/ppermute | solution.py:670
  226.0 46.1 %collective-permute-start.8 = (bf16[512,512]{1,0:T(8,128)(2,1)S(1)}, bf16[512,512]{1,0:T(8,128)(2,1)S(1)}, u32[]{:S(2)}, u32[]{:S(2)}) collective-permute-start(bf16[512,512]{1,0:T(8,128)(2,1)S(1)} %dynamic-slice_convert_fusion.refs_2_.refs_5_), channel_id=1, source_target_pairs={{0,4},{4,0},{8,12},{12,8},{16,20},{20,16},{24,28},{28,24},{1,5},{5... | collective-permute-start | bytes 1572872 | tf_op jit(solution)/shard_map/ppermute | solution.py:698
  263.1 9.8 %copy-start.5 = (f32[2,512,512]{2,1,0:T(8,128)S(1)}, f32[2,512,512]{2,1,0:T(8,128)}, u32[]{:S(2)}) copy-start(f32[2,512,512]{2,1,0:T(8,128)} %copy-done.4) | copy-start | bytes 6291460
  265.0 25.3 %all-to-all-start.5 = ((bf16[8,64,640]{2,1,0:T(8,128)(2,1)}), bf16[8,64,640]{2,1,0:T(8,128)(2,1)}, u32[]{:S(2)}, u32[]{:S(2)}) async-start(bf16[8,64,640]{2,1,0:T(8,128)(2,1)} %broadcast_in_dim.50), calls=%async_computation.5 | async-start | bytes 1310720 | tf_op jit(solution)/shard_map/all_to_all | solution.py:694
  269.7 114.1 %all-gather.7.cloned.1.call-start = ((), (), s32[]{:S(2)}) async-start(), calls=%async_computation.9 | async-start | bytes 4325376 | tf_op jit(solution)/shard_map/all_gather | solution.py:880
  274.1 13.7 %collective-permute-start.9 = (bf16[256,512]{1,0:T(8,128)(2,1)S(1)}, bf16[256,512]{1,0:T(8,128)(2,1)S(1)}, u32[]{:S(2)}, u32[]{:S(2)}) collective-permute-start(bf16[256,512]{1,0:T(8,128)(2,1)S(1)} %dynamic-slice_convert_fusion.1), channel_id=1, source_target_pairs={{0,8},{4,12},{8,0},{12,4},{16,24},{20,28},{24,16},{28,20},{1,9},{5... | collective-permute-start | bytes 786440 | tf_op jit(solution)/shard_map/ppermute | solution.py:698
  287.9 5.0 %copy-start.22 = (bf16[128,512]{1,0:T(8,128)(2,1)}, bf16[128,512]{1,0:T(8,128)(2,1)S(1)}, u32[]{:S(2)}) copy-start(bf16[128,512]{1,0:T(8,128)(2,1)S(1)} %dynamic-slice_convert_fusion.2.refs_17_) | copy-start | bytes 393220
  288.0 14.8 %collective-permute-start.12 = (bf16[128,512]{1,0:T(8,128)(2,1)S(1)}, bf16[128,512]{1,0:T(8,128)(2,1)S(1)}, u32[]{:S(2)}, u32[]{:S(2)}) collective-permute-start(bf16[128,512]{1,0:T(8,128)(2,1)S(1)} %dynamic-slice_convert_fusion.2.refs_17_), channel_id=1, source_target_pairs={{0,16},{4,20},{8,24},{12,28},{16,0},{20,4},{24,8},{28,12},{1,17},{... | collective-permute-start | bytes 393224 | tf_op jit(solution)/shard_map/ppermute | solution.py:698
  302.7 5.8 %copy-start.17 = (bf16[2,512,512]{2,1,0:T(8,128)(2,1)S(1)}, bf16[2,512,512]{2,1,0:T(8,128)(2,1)}, u32[]{:S(2)}) copy-start(bf16[2,512,512]{2,1,0:T(8,128)(2,1)} %get-tuple-element.107) | copy-start | bytes 3145732
  305.6 2.9 collective-permute-start.10
  308.6 19.8 %copy-start.28 = (f32[3,8,512]{2,1,0:T(8,128)S(1)}, f32[3,8,512]{2,1,0:T(8,128)}, u32[]{:S(2)}) copy-start(f32[3,8,512]{2,1,0:T(8,128)} %get-tuple-element.102) | copy-start | bytes 147460
  308.6 19.8 %copy-start.29 = (f32[3,8,512]{2,1,0:T(8,128)S(1)}, f32[3,8,512]{2,1,0:T(8,128)}, u32[]{:S(2)}) copy-start(f32[3,8,512]{2,1,0:T(8,128)} %get-tuple-element.103) | copy-start | bytes 147460
  308.6 19.9 %copy-start.26 = (f32[4,8,512]{2,1,0:T(8,128)S(1)}, f32[4,8,512]{2,1,0:T(8,128)}, u32[]{:S(2)}) copy-start(f32[4,8,512]{2,1,0:T(8,128)} %get-tuple-element.104) | copy-start | bytes 196612
  308.6 19.9 %copy-start.27 = (f32[4,8,512]{2,1,0:T(8,128)S(1)}, f32[4,8,512]{2,1,0:T(8,128)}, u32[]{:S(2)}) copy-start(f32[4,8,512]{2,1,0:T(8,128)} %get-tuple-element.105) | copy-start | bytes 196612
  308.7 20.4 %copy-start.23 = (f32[5,8,512]{2,1,0:T(8,128)S(1)}, f32[5,8,512]{2,1,0:T(8,128)}, u32[]{:S(2)}) copy-start(f32[5,8,512]{2,1,0:T(8,128)} %get-tuple-element.97.refs_1_) | copy-start | bytes 245764
  308.7 20.4 %copy-start.24 = (f32[5,8,512]{2,1,0:T(8,128)S(1)}, f32[5,8,512]{2,1,0:T(8,128)}, u32[]{:S(2)}) copy-start(f32[5,8,512]{2,1,0:T(8,128)} %get-tuple-element.101) | copy-start | bytes 245764
  308.7 15.0 %collective-permute-start.11 = (bf16[512,512]{1,0:T(8,128)(2,1)S(1)}, bf16[512,512]{1,0:T(8,128)(2,1)S(1)}, u32[]{:S(2)}, u32[]{:S(2)}) collective-permute-start(bf16[512,512]{1,0:T(8,128)(2,1)S(1)} %fusion.1), channel_id=1, source_target_pairs={{0,2},{1,3},{2,0},{3,1},{4,6},{5,7},{6,4},{7,5},{8,10},{9,11},{10,... | collective-permute-start | bytes 1572872 | tf_op jit(solution)/shard_map/ppermute | solution.py:670
  324.7 39.8 %copy-start.3 = (bf16[8,30,8,512]{3,2,1,0:T(8,128)(2,1)S(1)}, bf16[8,30,8,512]{3,2,1,0:T(8,128)(2,1)}, u32[]{:S(2)}) copy-start(bf16[8,30,8,512]{3,2,1,0:T(8,128)(2,1)} %copy-done.2) | copy-start | bytes 5898244
  324.7 23.5 %all-to-all-start.6 = ((bf16[8,64,512]{2,1,0:T(8,128)(2,1)}), bf16[8,64,512]{2,1,0:T(8,128)(2,1)S(1)}, u32[]{:S(2)}, u32[]{:S(2)}) async-start(bf16[8,64,512]{2,1,0:T(8,128)(2,1)} %bitcast.37), calls=%async_computation.6 | async-start | bytes 1048576 | tf_op jit(solution)/shard_map/all_to_all | solution.py:784
  350.3 1.3 collective-permute-start.13
  351.6 4.7 %collective-permute-start.14 = (f32[13,512]{1,0:T(8,128)S(1)}, f32[13,512]{1,0:T(8,128)S(1)}, u32[]{:S(2)}, u32[]{:S(2)}) collective-permute-start(f32[13,512]{1,0:T(8,128)S(1)} %add.142), channel_id=1, source_target_pairs={{0,2},{1,3},{2,0},{3,1},{4,6},{5,7},{6,4},{7,5},{8,10},{9,11},{10,... | collective-permute-start | bytes 79880 | tf_op jit(solution)/shard_map/ppermute | solution.py:670
  356.3 6.3 %collective-permute-start.15 = (f32[13,512]{1,0:T(8,128)S(1)}, f32[13,512]{1,0:T(8,128)S(1)}, u32[]{:S(2)}, u32[]{:S(2)}) collective-permute-start(f32[13,512]{1,0:T(8,128)S(1)} %add.143), channel_id=1, source_target_pairs={{0,4},{4,0},{8,12},{12,8},{16,20},{20,16},{24,28},{28,24},{1,5},{5... | collective-permute-start | bytes 79880 | tf_op jit(solution)/shard_map/ppermute | solution.py:698
  358.6 38.0 %all-to-all-start.7 = ((bf16[8,64,512]{2,1,0:T(8,128)(2,1)}), bf16[8,64,512]{2,1,0:T(8,128)(2,1)S(1)}, u32[]{:S(2)}, u32[]{:S(2)}) async-start(bf16[8,64,512]{2,1,0:T(8,128)(2,1)} %broadcast_in_dim.53), calls=%async_computation.7 | async-start | bytes 1048576 | tf_op jit(solution)/shard_map/all_to_all | solution.py:694
  362.5 16.1 %copy-start.1 = (bf16[8,20,8,512]{3,2,1,0:T(8,128)(2,1)S(1)}, bf16[8,20,8,512]{3,2,1,0:T(8,128)(2,1)}, u32[]{:S(2)}) copy-start(bf16[8,20,8,512]{3,2,1,0:T(8,128)(2,1)} %copy-done) | copy-start | bytes 3932164
  362.5 16.1 %slice-start = ((bf16[8,30,8,512]{3,2,1,0:T(8,128)(2,1)}), bf16[8,29,8,512]{3,2,1,0:T(8,128)(2,1)S(1)}, s32[]{:S(2)}) async-start(bf16[8,30,8,512]{3,2,1,0:T(8,128)(2,1)} %copy-done.2), calls=%async_computation.10 | async-start | bytes 3801088 | tf_op jit(solution)/shard_map/slice | solution.py:828
  362.5 11.3 %collective-permute-start.16 = (f32[13,512]{1,0:T(8,128)S(1)}, f32[13,512]{1,0:T(8,128)S(1)}, u32[]{:S(2)}, u32[]{:S(2)}) collective-permute-start(f32[13,512]{1,0:T(8,128)S(1)} %add.144), channel_id=1, source_target_pairs={{0,8},{4,12},{8,0},{12,4},{16,24},{20,28},{24,16},{28,20},{1,9},{5... | collective-permute-start | bytes 79880 | tf_op jit(solution)/shard_map/ppermute | solution.py:698
  373.9 9.2 %copy-start.20 = (f32[12,512]{1,0:T(8,128)S(1)}, f32[12,512]{1,0:T(8,128)}, u32[]{:S(2)}) copy-start(f32[12,512]{1,0:T(8,128)} %refs_16_.1) | copy-start | bytes 73732
  373.9 9.2 %copy-start.30 = (f32[12,512]{1,0:T(8,128)S(1)}, f32[12,512]{1,0:T(8,128)}, u32[]{:S(2)}) copy-start(f32[12,512]{1,0:T(8,128)} %param.28) | copy-start | bytes 73732
  373.9 9.2 %copy-start.31 = (f32[12,512]{1,0:T(8,128)S(1)}, f32[12,512]{1,0:T(8,128)}, u32[]{:S(2)}) copy-start(f32[12,512]{1,0:T(8,128)} %param.29) | copy-start | bytes 73732
  373.9 6.6 %collective-permute-start.17 = (f32[13,512]{1,0:T(8,128)S(1)}, f32[13,512]{1,0:T(8,128)S(1)}, u32[]{:S(2)}, u32[]{:S(2)}) collective-permute-start(f32[13,512]{1,0:T(8,128)S(1)} %add.145), channel_id=1, source_target_pairs={{0,16},{4,20},{8,24},{12,28},{16,0},{20,4},{24,8},{28,12},{1,17},{... | collective-permute-start | bytes 79880 | tf_op jit(solution)/shard_map/ppermute | solution.py:698
  (17 other events, 33.9 us)
Sparse Core Ops, SparseCore 0:
  88.6 59.6 all-gather.4
  305.7 65.9 all-gather.6
